TPU v7x, 32 devices: a whole 2x2x4 slice. The times are simulated.
32 devices in a mesh: dp: 8 (over z, y), fsdp: 4 (over x, core).
Axes of the slice: x: 2, y: 2, z: 4, core: 2. Of those that a mesh axis runs over, the one named last changes fastest.
Arguments:
- frames: bfloat16 [4, 48, 32, 1536], P('fsdp', 'dp'), may hold values from -6 to 6
- ln_gain: float32 [1536], replicated, may hold values from 0.5 to 1.5
- w_in: bfloat16 [1536, 3072], P(('dp', 'fsdp')), may hold values from -0.15625 to 0.15625
- depth_kernel: float32 [31, 1536], replicated, may hold values from -1 to 1
- bn_scale: float32 [1536], replicated, may hold values from 0.5 to 1.5
- bn_shift: float32 [1536], replicated, may hold values from -3 to 3
- w_out: bfloat16 [1536, 1536], P(('dp', 'fsdp')), may hold values from -0.15625 to 0.15625
- lengths: int32 [4, 8, 6], P('fsdp'), may hold values from 0 to 32, as said below
- destinations: int32 [4, 8, 6], P('fsdp'), may hold values from 0 to 7, as said below
- offsets: int32 [4, 8, 6], P('fsdp'), may hold values from 0 to 32, as said below
Outputs:
- encoded: bfloat16 [4, 16, 32, 1536], P('fsdp', 'dp')
Inputs may be any that keep to these rules, and one draw needn't show every extreme that they name: lengths: live slots come first in a loader and hold half of 32 to 32 frames; 0 marks an empty slot. In each group the busiest loader has all 6 slots live, the group has 16 live utterances, and one of them has 32 frames. destinations: within a group a loader sends at most one live utterance to a device, and every device receives exactly 2 live utterances. Empty slots hold 0. offsets: multiples of 32; the 2 live utterances received by one device have distinct offsets. Empty slots hold 0.
All inputs are finite; a program needn't handle non-finite values.
Results may differ from a plain program's by a relative error of at most 0.003.
Values may be sent and summed in bfloat16 or wider, within the bound.
No kernel may reach another device: no remote copies, remote signals or barrier semaphores. Data moves between devices by JAX's collectives and lax.ppermute only.
A program may use at most 128 MiB of HBM per device.

v0:
```python
import jax
import jax.numpy as jnp
from jax import lax
from jax.sharding import PartitionSpec as P


def conv_module(blocks, utt_lengths, ln_gain, depth_kernel, bn_scale, bn_shift, full_in, full_out):
    block_count, frames_len, feature_width = blocks.shape
    wide_rows = blocks.reshape(block_count * frames_len, feature_width).astype(jnp.float32)
    row_mean = jnp.mean(wide_rows, axis=1, keepdims=True)
    centred = wide_rows - row_mean
    row_var = jnp.mean(centred * centred, axis=1, keepdims=True)
    normed = (centred * lax.rsqrt(row_var + 1e-05) * ln_gain).astype(jnp.bfloat16)
    glu_in = jnp.dot(normed, full_in, preferred_element_type=jnp.float32)
    gated_units = glu_in[:, :feature_width] * jax.nn.sigmoid(glu_in[:, feature_width:])
    gated_units = gated_units.reshape(block_count, frames_len, feature_width)
    valid_mask = jnp.arange(frames_len, dtype=jnp.int32)[None, :] < utt_lengths[:, None]
    gated_units = jnp.where(valid_mask[:, :, None], gated_units, jnp.zeros((), gated_units.dtype))
    side_reach = (depth_kernel.shape[0] - 1) // 2
    padded = jnp.pad(gated_units, ((0, 0), (side_reach, side_reach), (0, 0)))
    convolved = padded[:, 0:frames_len, :] * depth_kernel[0]
    for kernel_tap in range(1, depth_kernel.shape[0]):
        convolved = (
            convolved
            + padded[:, kernel_tap : kernel_tap + frames_len, :] * depth_kernel[kernel_tap]
        )
    shifted = convolved * bn_scale + bn_shift
    activated = (shifted * jax.nn.sigmoid(shifted)).astype(jnp.bfloat16)
    activated = activated.reshape(block_count * frames_len, feature_width)
    mixed_out = wide_rows + jnp.dot(activated, full_out, preferred_element_type=jnp.float32)
    mixed_out = mixed_out.reshape(block_count, frames_len, feature_width)
    mixed_out = jnp.where(valid_mask[:, :, None], mixed_out, jnp.zeros((), mixed_out.dtype))
    return mixed_out.astype(jnp.bfloat16)


def shards(
    frames, ln_gain, w_in, depth_kernel, bn_scale, bn_shift, w_out, lengths, destinations, offsets
):
    dp_count = lax.axis_size("dp")
    dp_index = lax.axis_index("dp")
    tab_len = lengths[0]
    tab_dest = destinations[0]
    tab_off = offsets[0]
    slot_count = tab_len.shape[1]
    recv_count = slot_count // 3
    frame_slots = frames.shape[2]
    own_len = lax.dynamic_index_in_dim(tab_len, dp_index, 0, keepdims=False)
    own_dest = lax.dynamic_index_in_dim(tab_dest, dp_index, 0, keepdims=False)
    slot_ids = jnp.arange(slot_count, dtype=jnp.int32)
    peer_ids = jnp.arange(dp_count, dtype=jnp.int32)
    send_table = ((own_dest[None, :] == peer_ids[:, None]) & (own_len[None, :] > 0)).astype(
        jnp.int32
    )
    send_slot = jnp.sum(send_table * slot_ids[None, :], axis=1)
    send_live = jnp.sum(send_table, axis=1) > 0
    key_table = jnp.where(tab_len > 0, tab_dest * recv_count + tab_off // frame_slots, -1)
    targets = dp_index * recv_count + jnp.arange(recv_count, dtype=jnp.int32)
    pick_table = (key_table[None, :, :] == targets[:, None, None]).astype(jnp.int32)
    recv_source = jnp.sum(pick_table * peer_ids[None, :, None], axis=(1, 2))
    full_in, full_out = (
        lax.all_gather(w_in, ("dp", "fsdp"), axis=0, tiled=True),
        lax.all_gather(w_out, ("dp", "fsdp"), axis=0, tiled=True),
    )
    local_out = conv_module(
        frames[0], own_len, ln_gain, depth_kernel, bn_scale, bn_shift, full_in, full_out
    )
    chosen = jnp.take(local_out, send_slot, axis=0)
    arrived = lax.all_to_all(
        jnp.where(send_live[:, None, None], chosen, jnp.zeros((), local_out.dtype)),
        "dp",
        split_axis=0,
        concat_axis=0,
        tiled=True,
    )
    result = jnp.take(arrived, recv_source, axis=0)
    return result[None]


def solution(mesh):
    return jax.shard_map(
        shards,
        mesh=mesh,
        in_specs=(
            P("fsdp", "dp", None, None),
            P(),
            P(("dp", "fsdp"), None),
            P(),
            P(),
            P(),
            P(("dp", "fsdp"), None),
            P("fsdp", None, None),
            P("fsdp", None, None),
            P("fsdp", None, None),
        ),
        out_specs=P("fsdp", "dp", None, None),
        check_vma=False,
    )
```

profile of v0, /device:TPU:0, one launch (start us, length us, event | category | flops | bytes accessed | tf_op | source)
XLA Modules:
  0.0 198.7 jit_solution(9312479826987872869)
XLA Ops:
  6.6 0.7 all-gather.3.cloned.1.call-update
  7.3 0.7 all-gather.5.cloned.1.call-update
  8.0 1.2 convert_reduce_fusion
  9.3 0.1 div.31
  9.3 0.3 multiply_reduce_fusion
  9.7 0.1 rsqrt.12
  9.7 0.3 dynamic-slice_reduce_fusion
  10.0 0.3 dynamic-slice_reduce_fusion.1
  10.3 0.2 convert_reduce_fusion.1
  10.5 0.2 slice_reduce_fusion.29
  10.7 0.3 slice_reduce_fusion.30
  11.1 0.4 fusion.68
  11.5 83.5 %all-gather.3.cloned.1.call-done = bf16[1536,3072]{1,0:T(8,128)(2,1)} async-done(((bf16[48,3072]{1,0:T(8,128)(2,1)}), bf16[1536,3072]{1,0:T(8,128)(2,1)}) %all-gather.3.cloned.1.call-update) | async-done | bytes 9437200 | tf_op jit(solution)/shard_map/all_gather | solution.py:61
  95.1 5.7 %fusion.78 = f32[192,3072]{1,0:T(8,128)S(1)} fusion(bf16[192,1536]{1,0:T(8,128)(2,1)S(1)} %fusion.68, bf16[1536,3072]{1,0:T(8,128)(2,1)} %all-gather.3.cloned.1.call-done), kind=kOutput, calls=%fused_computation.176 | convolution fusion | flops 1811939328 | bytes 12386304 | tf_op jit(solution)/shard_map/dot_general | solution.py:14
  100.7 0.3 fusion.65
  101.1 0.1 broadcast_select_fusion
  101.2 0.5 copy-done.5
  101.8 4.5 %multiply_convert_fusion = bf16[6,32,1536]{2,1,0:T(8,128)(2,1)S(1)} fusion(f32[6,32,1536]{2,1,0:T(8,128)S(1)} %broadcast_select_fusion, f32[1536]{0:T(1024)S(1)} %copy-done.5, f32[1536]{0:T(1024)S(1)} %copy-done.6, f32[1536]{0:T(1024)S(1)} %get-tuple-element.34, f32[1536]{0:T(1024)S(1)} %get-tuple-element.35, f32[1536]{0:T(1024)S(1)} %get-tuple-element.6, ...), kind=kLoop, calls=%fused_computation.105 | loop fusion | flops 20054016 | bytes 1972224 | tf_op jit(solution)/shard_map/convert_element_type | solution.py:28
  106.3 53.9 %all-gather.5.cloned.1.call-done = bf16[1536,1536]{1,0:T(8,128)(2,1)} async-done(((bf16[48,1536]{1,0:T(8,128)(2,1)}), bf16[1536,1536]{1,0:T(8,128)(2,1)}) %all-gather.5.cloned.1.call-update) | async-done | bytes 4718608 | tf_op jit(solution)/shard_map/all_gather | solution.py:62
  160.2 3.4 %convolution_add_fusion = bf16[192,1536]{1,0:T(8,128)(2,1)S(1)} fusion(bf16[192,1536]{1,0:T(8,128)(2,1)S(1)} %bitcast.31, bf16[1536,1536]{1,0:T(8,128)(2,1)} %all-gather.5.cloned.1.call-done, bf16[192,1536]{1,0:T(8,128)(2,1)S(1)} %bitcast.28), kind=kOutput, calls=%fused_computation.32 | convolution fusion | flops 906854400 | bytes 6488064 | tf_op jit(solution)/shard_map/dot_general | solution.py:30
  163.6 0.2 select_convert_fusion
  163.8 0.6 gather_fusion
  164.4 1.0 select_select_fusion
  165.5 4.4 %all-to-all-start = ((bf16[8,32,1536]{2,1,0:T(8,128)(2,1)}), bf16[8,32,1536]{2,1,0:T(8,128)(2,1)S(1)}, u32[]{:S(2)}, u32[]{:S(2)}) async-start(bf16[8,32,1536]{2,1,0:T(8,128)(2,1)} %select_select_fusion), calls=%async_computation | async-start | bytes 1572864 | tf_op jit(solution)/shard_map/all_to_all | solution.py:68
  169.9 0.1 copy.24
  170.0 0.1 copy.23
  170.1 0.1 copy.25
  170.2 0.1 copy.29
  170.3 0.2 fusion.69
  170.5 20.0 %all-to-all-done = bf16[8,32,1536]{2,1,0:T(8,128)(2,1)S(1)} async-done(((bf16[8,32,1536]{2,1,0:T(8,128)(2,1)}), bf16[8,32,1536]{2,1,0:T(8,128)(2,1)S(1)}, u32[]{:S(2)}, u32[]{:S(2)}) %all-to-all-start) | async-done | bytes 786464 | tf_op jit(solution)/shard_map/all_to_all | solution.py:68
  190.5 0.6 gather_fusion.1
  191.1 0.8 bitcast_select_fusion
  (29 shorter events, 0.3 us)
Async XLA Ops:
  6.5 2.8 %copy-start = (bf16[1,6,32,1536]{3,2,1,0:T(8,128)(2,1)S(1)}, bf16[1,6,32,1536]{3,2,1,0:T(8,128)(2,1)}, u32[]{:S(2)}) copy-start(bf16[1,6,32,1536]{3,2,1,0:T(8,128)(2,1)} %param.10) | copy-start | bytes 1769476
  6.5 3.2 %copy-start.3 = (s32[1,8,6]{1,0,2:T(1,128)S(1)}, s32[1,8,6]{1,0,2:T(1,128)}, u32[]{:S(2)}) copy-start(s32[1,8,6]{1,0,2:T(1,128)} %param.17) | copy-start | bytes 580
  6.5 3.5 %copy-start.2 = (s32[1,8,6]{1,0,2:T(1,128)S(1)}, s32[1,8,6]{1,0,2:T(1,128)}, u32[]{:S(2)}) copy-start(s32[1,8,6]{1,0,2:T(1,128)} %param.18) | copy-start | bytes 580
  6.5 3.9 %copy-start.1 = (f32[31,1536]{1,0:T(8,128)S(1)}, f32[31,1536]{1,0:T(8,128)}, u32[]{:S(2)}) copy-start(f32[31,1536]{1,0:T(8,128)} %param.13) | copy-start | bytes 571396
  6.5 4.6 %copy-start.4 = (f32[1536]{0:T(1024)S(1)}, f32[1536]{0:T(1024)}, u32[]{:S(2)}) copy-start(f32[1536]{0:T(1024)} %param.11) | copy-start | bytes 18436
  6.5 88.5 %all-gather.3.cloned.1.call-start = ((), (), s32[]{:S(2)}) async-start(), calls=%async_computation.1 | async-start | bytes 9732096 | tf_op jit(solution)/shard_map/all_gather | solution.py:61
  7.3 152.9 %all-gather.5.cloned.1.call-start = ((), (), s32[]{:S(2)}) async-start(), calls=%async_computation.2 | async-start | bytes 4866048 | tf_op jit(solution)/shard_map/all_gather | solution.py:62
  101.1 0.7 copy-start.5
  101.1 0.7 copy-start.6
  165.5 4.6 %copy-start.7 = (s32[1,8,6]{1,0,2:T(1,128)S(1)}, s32[1,8,6]{1,0,2:T(1,128)}, u32[]{:S(2)}) copy-start(s32[1,8,6]{1,0,2:T(1,128)} %param.19) | copy-start | bytes 580
  165.5 25.0 %all-to-all-start = ((bf16[8,32,1536]{2,1,0:T(8,128)(2,1)}), bf16[8,32,1536]{2,1,0:T(8,128)(2,1)S(1)}, u32[]{:S(2)}, u32[]{:S(2)}) async-start(bf16[8,32,1536]{2,1,0:T(8,128)(2,1)} %select_select_fusion), calls=%async_computation | async-start | bytes 1572864 | tf_op jit(solution)/shard_map/all_to_all | solution.py:68
Sparse Core Ops, SparseCore 0:
  10.3 84.7 all-gather.2
  98.0 62.2 all-gather.4
where the time goes:
time: 199 us
  waiting for transfers between devices  159 us (80%)
  between operations  13.6 us (7%)
  other arithmetic  9.35 us (5%)
  matrix products  9.09 us (5%)
  starting transfers between devices  4.53 us (2%)
  local copies, waits for them, and re-layouts  3.27 us (2%)
    all_gather x1, waiting for transfers between devices, shards(): lax.all_gather(w_in, ('dp', 'fsdp'), axis=0, tiled=True)  83.5 us
    all_gather x1, waiting for transfers between devices, shards(): lax.all_gather(w_out, ('dp', 'fsdp'), axis=0, tiled=True)  53.9 us
    all_to_all x1, waiting for transfers between devices, shards(): lax.all_to_all(jnp.where(send_live[:, None, None], chosen, jnp.zeros((),...  20 us
    dot_general x1, matrix products, conv_module(): glu_in = jnp.dot(normed, full_in, preferred_element_type=jnp.float32)  5.67 us
    convert_element_type x1, other arithmetic, conv_module(): activated = (shifted * jax.nn.sigmoid(shifted)).astype(jnp.bfloat16)  4.52 us
    all_to_all x1, starting transfers between devices, shards(): lax.all_to_all(jnp.where(send_live[:, None, None], chosen, jnp.zeros((),...  4.45 us
  transfers between devices with their start and end apart: 3, of which 3 were waited for; matrix products, arithmetic and copies ran while one was open for 7% of the time, Pallas kernels for 0%

commit v1 on v0

v1 whole, which is shorter than its diff:
```python
import functools

import jax
import jax.numpy as jnp
from jax import lax
from jax.experimental import pallas as pl
from jax.experimental.pallas import tpu as pltpu
from jax.sharding import PartitionSpec as P

ANY = pl.BlockSpec(memory_space=pl.ANY)
SMEM = pl.BlockSpec(memory_space=pltpu.SMEM)
VMEM = pl.BlockSpec(memory_space=pltpu.VMEM)
BF16 = jnp.bfloat16
F32 = jnp.float32


def call(kernel, out_shape, in_specs, out_specs, scratch, flops=0, moved=0):
    return pl.pallas_call(
        kernel,
        out_shape=out_shape,
        in_specs=in_specs,
        out_specs=out_specs,
        scratch_shapes=scratch,
        cost_estimate=pl.CostEstimate(flops=flops, bytes_accessed=moved, transcendentals=0),
        compiler_params=pltpu.CompilerParams(vmem_limit_bytes=48 * 1024 * 1024),
    )


def send_kernel(place, tab_len, tab_dest, frames, *refs):
    outs, sems = refs[:-1], refs[-1]
    me = place[0]
    copies = []
    for number, out in enumerate(outs):
        target = jnp.bitwise_xor(me, number + 1)

        def look(slot, found):
            hit = jnp.logical_and(tab_dest[me, slot] == target, tab_len[me, slot] > 0)
            return jnp.where(hit, slot, found)

        slot = lax.fori_loop(0, frames.shape[0], look, jnp.int32(0))
        copy = pltpu.make_async_copy(frames.at[slot], out, sems.at[number])
        copy.start()
        copies.append(copy)
    for copy in copies:
        copy.wait()


def norm_kernel(recv, place, tab_len, tab_dest, tab_off, gain, frames, *refs):
    arrived = refs[: tab_len.shape[0] - 1]
    kept, normed, lens, block, sems = refs[tab_len.shape[0] - 1 :]
    slots, long = frames.shape[0], frames.shape[1]
    me = place[0]
    for number in range(recv):

        def look(at, found):
            source, slot = at // slots, lax.rem(at, slots)
            length = tab_len[source, slot]
            hit = jnp.logical_and(
                jnp.logical_and(tab_dest[source, slot] == me, length > 0),
                tab_off[source, slot] == number * long,
            )
            return (
                jnp.where(hit, source, found[0]),
                jnp.where(hit, slot, found[1]),
                jnp.where(hit, length, found[2]),
            )

        zero = jnp.int32(0)
        source, slot, length = lax.fori_loop(
            0, tab_len.shape[0] * slots, look, (zero, zero, zero)
        )
        lens[number] = length
        shift = jnp.bitwise_xor(source, me)

        @pl.when(shift == 0)
        def _():
            pltpu.make_async_copy(frames.at[slot], block.at[number], sems.at[number]).start()

        for other, ref in enumerate(arrived):

            @pl.when(shift == other + 1)
            def _():
                pltpu.make_async_copy(ref, block.at[number], sems.at[number]).start()

    for number in range(recv):
        pltpu.make_async_copy(frames.at[0], block.at[number], sems.at[number]).wait()
        rows = block[number]
        kept[number] = rows
        wide = rows.astype(F32)
        mean = jnp.mean(wide, axis=1, keepdims=True)
        centred = wide - mean
        var = jnp.mean(centred * centred, axis=1, keepdims=True)
        value = centred * lax.rsqrt(var + 1e-05) * gain[...]
        steps = lax.broadcasted_iota(jnp.int32, value.shape, 0)
        normed[number] = jnp.where(steps < lens[number], value, 0.0).astype(BF16)


def glu_conv_kernel(parts, pieces, where, taps, scale, shift, *refs):
    normed, weights = refs[:parts], refs[parts : parts + pieces]
    outs = refs[parts + pieces : 2 * parts + pieces]
    rows_buf, w_buf, glu_buf, pad_buf, row_sems, w_sems = refs[2 * parts + pieces :]
    recv, long, width = normed[0].shape
    tall = recv * long
    depth = weights[0].shape[1]
    copies = []
    for number, ref in enumerate(normed):
        for slot in range(recv):
            copies.append(
                pltpu.make_async_copy(
                    ref.at[slot],
                    rows_buf.at[pl.ds(number * tall + slot * long, long)],
                    row_sems.at[number * recv + slot],
                )
            )
    for number, ref in enumerate(weights):
        for inner in range(ref.shape[0]):
            start = where[number, inner] * depth
            if depth % 16 == 0:
                start = pl.multiple_of(start, 16)
            else:
                start = 0
            copies.append(
                pltpu.make_async_copy(
                    ref.at[inner], w_buf.at[pl.ds(start, depth)], w_sems.at[number, inner]
                )
            )
    for copy in copies:
        copy.start()
    for copy in copies:
        copy.wait()
    glu_in = jnp.dot(rows_buf[...], w_buf[...], preferred_element_type=F32)
    chans = glu_in.shape[1] // 2
    glu_buf[...] = glu_in[:, :chans] * jax.nn.sigmoid(glu_in[:, chans:])
    reach = (taps.shape[0] - 1) // 2
    pad_buf[...] = jnp.zeros(pad_buf.shape, F32)
    for number, out in enumerate(outs):

        def utterance(slot, carry):
            start = pl.multiple_of(number * tall + slot * long, long)
            pad_buf[pl.ds(16, long), :] = glu_buf[pl.ds(start, long), :]
            total = pad_buf[pl.ds(16 - reach, long), :] * taps[0:1, :]
            for tap in range(1, taps.shape[0]):
                total = total + pad_buf[pl.ds(16 - reach + tap, long), :] * taps[tap : tap + 1, :]
            moved = total * scale[...] + shift[...]
            out[slot] = (moved * jax.nn.sigmoid(moved)).astype(BF16)
            return carry

        lax.fori_loop(0, recv, utterance, 0)


def mix_kernel(parts, pieces, where, lens, chip, kept, *refs):
    acts, weights = refs[:parts], refs[parts : parts + pieces]
    out, w_buf, w_sems = refs[parts + pieces :]
    recv, long, width = kept.shape
    depth = weights[0].shape[1]
    chans = acts[0].shape[2]
    copies = []
    for number, ref in enumerate(weights):
        for inner in range(ref.shape[0]):
            start = where[number, inner] * depth
            if depth % 16 == 0:
                start = pl.multiple_of(start, 16)
            else:
                start = 0
            copies.append(
                pltpu.make_async_copy(
                    ref.at[inner], w_buf.at[pl.ds(start, depth)], w_sems.at[number, inner]
                )
            )
    for copy in copies:
        copy.start()
    for copy in copies:
        copy.wait()
    total = kept[...].reshape(recv * long, width).astype(F32)
    for number, ref in enumerate(acts):
        first = jnp.bitwise_xor(chip[0], number) * chans
        total = total + jnp.dot(
            ref[...].reshape(recv * long, chans),
            w_buf[pl.ds(pl.multiple_of(first, 16), chans), :],
            preferred_element_type=F32,
        )
    total = total.reshape(recv, long, width)
    for number in range(recv):
        steps = lax.broadcasted_iota(jnp.int32, (long, width), 0)
        out[number] = jnp.where(steps < lens[number], total[number], 0.0).astype(out.dtype)


def shards(
    frames, ln_gain, w_in, depth_kernel, bn_scale, bn_shift, w_out, lengths, destinations, offsets
):
    dp_count, fsdp_count = lax.axis_size("dp"), lax.axis_size("fsdp")
    chips = (fsdp_count // 2) ** 2
    planes = dp_count * fsdp_count // (2 * chips)
    dp_index = lax.axis_index("dp")
    number = dp_index * fsdp_count + lax.axis_index("fsdp")
    core = number % 2
    chip = (number // 2) % chips
    plane = number // (2 * chips)
    all_devices = range(dp_count * fsdp_count)
    slots = lengths.shape[2]
    recv = slots // 3
    _, _, long, width = frames.shape
    depth = w_in.shape[0]
    chans = width // chips
    taps = depth_kernel.shape[0]

    def swap(array, mask):
        return lax.ppermute(array, ("dp", "fsdp"), [(at, at ^ mask) for at in all_devices])

    def climb(array):
        step = 2 * chips
        return lax.ppermute(
            array, ("dp", "fsdp"), [(at, (at + step) % len(all_devices)) for at in all_devices]
        )

    place = dp_index.astype(jnp.int32)[None]
    tab_len, tab_dest, tab_off = lengths[0], destinations[0], offsets[0]
    block = jax.ShapeDtypeStruct((long, width), BF16)
    chosen = call(
        send_kernel,
        [block] * (dp_count - 1),
        [SMEM, SMEM, SMEM, ANY],
        [ANY] * (dp_count - 1),
        [pltpu.SemaphoreType.DMA((dp_count - 1,))],
    )(place, tab_len, tab_dest, frames[0])
    arrived = [
        lax.ppermute(part, "dp", [(at, at ^ (mask + 1)) for at in range(dp_count)])
        for mask, part in enumerate(chosen)
    ]

    halves = w_in.reshape(depth, 2, width)

    def columns(owner):
        part = lax.dynamic_slice_in_dim(halves, owner * chans, chans, 2)
        return part.reshape(depth, 2 * chans)

    ring = jnp.stack(
        [columns(chip)] + [swap(columns(chip ^ mask), 2 * mask) for mask in range(1, chips)]
    )
    in_own = [ring]
    out_ring = w_out
    out_own = [out_ring]
    for _ in range(planes - 1):
        out_ring = climb(out_ring)
        out_own.append(out_ring)
    for _ in range(planes - 1):
        ring = climb(ring)
        in_own.append(ring)
    in_parts = in_own + [swap(part, 1) for part in in_own]

    out_stack = jnp.stack(out_own)
    out_plane = [out_stack] + [swap(out_stack, 2 * mask) for mask in range(1, chips)]
    out_parts = out_plane + [swap(part, 1) for part in out_plane]

    ring_plane = (plane - jnp.arange(planes)) % planes
    ring_chip = chip ^ jnp.arange(chips)
    rows_of = (ring_plane[:, None] * chips + ring_chip[None, :]) * 2
    in_where = jnp.concatenate([rows_of + core, rows_of + (1 - core)], 0).astype(jnp.int32)
    out_where = jnp.concatenate([rows_of.T + core, rows_of.T + (1 - core)], 0).astype(jnp.int32)
    if depth % 16:
        flat_in = jnp.concatenate(in_parts, 0)
        flat_out = jnp.concatenate(out_parts, 0)
        in_parts = [jnp.zeros_like(flat_in).at[in_where.reshape(-1)].set(flat_in)]
        out_parts = [jnp.zeros_like(flat_out).at[out_where.reshape(-1)].set(flat_out)]
        in_parts = [in_parts[0].reshape(1, width, 2 * chans)]
        out_parts = [out_parts[0].reshape(1, width, width)]
        in_where = out_where = jnp.zeros((1, 1), jnp.int32)

    utts = jax.ShapeDtypeStruct((recv, long, width), BF16)
    kept, normed, lens = call(
        functools.partial(norm_kernel, recv),
        [utts, utts, jax.ShapeDtypeStruct((recv,), jnp.int32)],
        [SMEM, SMEM, SMEM, SMEM, VMEM] + [ANY] * dp_count,
        [VMEM, VMEM, SMEM],
        [pltpu.VMEM((recv, long, width), BF16), pltpu.SemaphoreType.DMA((recv,))],
    )(place, tab_len, tab_dest, tab_off, ln_gain[None], frames[0], *arrived)

    all_normed = [normed] + [swap(normed, 2 * mask) for mask in range(1, chips)]

    def own_channels(array):
        return lax.dynamic_slice_in_dim(array, chip * chans, chans, array.ndim - 1)

    acts = call(
        functools.partial(glu_conv_kernel, chips, len(in_parts)),
        [jax.ShapeDtypeStruct((recv, long, chans), BF16)] * chips,
        [SMEM, VMEM, VMEM, VMEM] + [ANY] * (chips + len(in_parts)),
        [VMEM] * chips,
        [
            pltpu.VMEM((chips * recv * long, width), BF16),
            pltpu.VMEM((width, 2 * chans), BF16),
            pltpu.VMEM((chips * recv * long, chans), F32),
            pltpu.VMEM((long + 32, chans), F32),
            pltpu.SemaphoreType.DMA((chips * recv,)),
            pltpu.SemaphoreType.DMA(in_where.shape),
        ],
        flops=4 * chips * recv * long * width * chans,
        moved=4 * width * chans,
    )(
        in_where,
        own_channels(depth_kernel),
        own_channels(bn_scale[None]),
        own_channels(bn_shift[None]),
        *all_normed,
        *in_parts,
    )

    back = [acts[0]] + [swap(acts[mask], 2 * mask) for mask in range(1, chips)]
    result = call(
        functools.partial(mix_kernel, chips, len(out_parts)),
        utts,
        [SMEM, SMEM, SMEM, VMEM] + [VMEM] * chips + [ANY] * len(out_parts),
        VMEM,
        [pltpu.VMEM((width, width), BF16), pltpu.SemaphoreType.DMA(out_where.shape)],
        flops=2 * recv * long * width * width,
        moved=2 * width * width,
    )(out_where, lens, chip.astype(jnp.int32)[None], kept, *back, *out_parts)
    return result[None]


def solution(mesh):
    return jax.shard_map(
        shards,
        mesh=mesh,
        in_specs=(
            P("fsdp", "dp", None, None),
            P(),
            P(("dp", "fsdp"), None),
            P(),
            P(),
            P(),
            P(("dp", "fsdp"), None),
            P("fsdp", None, None),
            P("fsdp", None, None),
            P("fsdp", None, None),
        ),
        out_specs=P("fsdp", "dp", None, None),
        check_vma=False,
    )
```

time: 199 us -> 132 us (0.66)
  waiting for transfers between devices: 159 us -> 51.3 us
  starting transfers between devices: 4.53 us -> 43.3 us
  Pallas kernels: 0 us -> 23.6 us
  between operations: 13.6 us -> 0.32 us
  local copies, waits for them, and re-layouts: 3.27 us -> 12.7 us
  other arithmetic: 9.35 us -> 0.22 us
  matrix products: 9.09 us -> 0 us
    all_gather x2 -> x0, waiting for transfers between devices: 137 us -> none  [the longest x1 83.5 us: shards(): lax.all_gather(w_in, ('dp', 'fsdp'), axis=0, tiled=True)]
    ppermute x0 -> x33, waiting for transfers between devices: none -> 51.3 us  [the longest x20 28.4 us: swap(): lax.ppermute(array, ('dp', 'fsdp'), [(at, at ^ mask) for at in all_devices])]
    ppermute x0 -> x33, starting transfers between devices: none -> 43.3 us  [the longest x6 16 us: climb(): lax.ppermute(array, ('dp', 'fsdp'), [(at, (at + step) % len(all_devices))...]
    pallas_call x0 -> x4, Pallas kernels: none -> 23.6 us  [the longest x1 9.86 us: shards(): call(functools.partial(mix_kernel, chips, len(out_parts)), utts, [SMEM, S...]
    all_to_all x1 -> x0, waiting for transfers between devices: 20 us -> none  [shards(): lax.all_to_all(jnp.where(send_live[:, None, None], chosen, jnp.zeros((),...]
    dot_general x2 -> x0, matrix products: 9.09 us -> none  [the longest x1 5.67 us: conv_module(): glu_in = jnp.dot(normed, full_in, preferred_element_type=jnp.float32)]
    unnamed x19 -> x52, local copies, waits for them, and re-layouts: 0.81 us -> 9.69 us
    convert_element_type x3 -> x0, other arithmetic: 5.09 us -> none  [the longest x1 4.52 us: conv_module(): activated = (shifted * jax.nn.sigmoid(shifted)).astype(jnp.bfloat16)]
  transfers between devices with their start and end apart: 3 -> 33, of which waited for: 3 -> 10; matrix products, arithmetic and copies ran while one was open for 7% -> 2% of each run, Pallas kernels for 0% -> 10%
where the time goes in v1:
time: 132 us; the launch traced here: 131 us
  waiting for transfers between devices  51.3 us (39%)
  starting transfers between devices  43.3 us (33%)
  Pallas kernels  23.6 us (18%)
  local copies, waits for them, and re-layouts  12.7 us (10%)
    ppermute x20, waiting for transfers between devices, swap(): lax.ppermute(array, ('dp', 'fsdp'), [(at, at ^ mask) for at in all_devices])  28.4 us
    ppermute x6, starting transfers between devices, climb(): lax.ppermute(array, ('dp', 'fsdp'), [(at, (at + step) % len(all_devices))...  16 us
    ppermute x20, starting transfers between devices, swap(): lax.ppermute(array, ('dp', 'fsdp'), [(at, at ^ mask) for at in all_devices])  15.8 us
    ppermute x6, waiting for transfers between devices, climb(): lax.ppermute(array, ('dp', 'fsdp'), [(at, (at + step) % len(all_devices))...  14 us
    ppermute x7, starting transfers between devices, shards(): lax.ppermute(part, 'dp', [(at, at ^ mask + 1) for at in range(dp_count)])  11.4 us
    pallas_call x1, Pallas kernels, shards(): call(functools.partial(mix_kernel, chips, len(out_parts)), utts, [SMEM, S...  9.86 us
    unnamed x52, local copies, waits for them, and re-layouts  9.69 us
    ppermute x7, waiting for transfers between devices, shards(): lax.ppermute(part, 'dp', [(at, at ^ mask + 1) for at in range(dp_count)])  8.89 us
  transfers between devices with their start and end apart: 33, of which 10 were waited for; matrix products, arithmetic and copies ran while one was open for 2% of the time, Pallas kernels for 10%

profile of v1, /device:TPU:0, one launch (start us, length us, event | category | flops | bytes accessed | tf_op | source)
XLA Modules:
  0.0 131.4 jit_solution(3104912395741770450)
XLA Ops:
  0.0 1.2 reshape.35
  1.5 3.0 %collective-permute-start.10 = (bf16[48,768]{1,0:T(8,128)(2,1)S(1)}, bf16[48,768]{1,0:T(8,128)(2,1)S(1)}, u32[]{:S(2)}, u32[]{:S(2)}) collective-permute-start(bf16[48,768]{1,0:T(8,128)(2,1)S(1)} %bitcast.38), channel_id=1, source_target_pairs={{0,2},{1,3},{2,0},{3,1},{4,6},{5,7},{6,4},{7,5},{8,10},{9,11},{10,... | collective-permute-start | bytes 221192 | tf_op jit(solution)/shard_map/ppermute | solution.py:208
  4.5 1.6 %collective-permute-start.11 = (bf16[48,768]{1,0:T(8,128)(2,1)S(1)}, bf16[48,768]{1,0:T(8,128)(2,1)S(1)}, u32[]{:S(2)}, u32[]{:S(2)}) collective-permute-start(bf16[48,768]{1,0:T(8,128)(2,1)S(1)} %bitcast.37), channel_id=1, source_target_pairs={{0,4},{1,5},{2,6},{3,7},{4,0},{5,1},{6,2},{7,3},{8,12},{9,13},{10,... | collective-permute-start | bytes 221192 | tf_op jit(solution)/shard_map/ppermute | solution.py:208
  6.3 2.2 %shard_map.100 = (bf16[32,1536]{1,0:T(8,128)(2,1)S(1)}, bf16[32,1536]{1,0:T(8,128)(2,1)S(1)}, bf16[32,1536]{1,0:T(8,128)(2,1)S(1)}, bf16[32,1536]{1,0:T(8,128)(2...) custom-call(s32[1]{0:T(128)} %bitcast.place, ...), custom_call_target="tpu_custom_call" | custom-call | tf_op jit(solution)/shard_map/pallas_call | solution.py:219
  9.1 1.6 %collective-permute-start.1 = (bf16[32,1536]{1,0:T(8,128)(2,1)S(1)}, bf16[32,1536]{1,0:T(8,128)(2,1)S(1)}, u32[]{:S(2)}, u32[]{:S(2)}) collective-permute-start(bf16[32,1536]{1,0:T(8,128)(2,1)S(1)} %get-tuple-element.20), channel_id=1, source_target_pairs={{0,8},{4,12},{8,0},{12,4},{16,24},{20,28},{24,16},{28,20},{1,9},{5... | collective-permute-start | bytes 294920 | tf_op jit(solution)/shard_map/ppermute | solution.py:227
  10.7 1.3 %collective-permute-start.2 = (bf16[32,1536]{1,0:T(8,128)(2,1)S(1)}, bf16[32,1536]{1,0:T(8,128)(2,1)S(1)}, u32[]{:S(2)}, u32[]{:S(2)}) collective-permute-start(bf16[32,1536]{1,0:T(8,128)(2,1)S(1)} %get-tuple-element.21), channel_id=1, source_target_pairs={{0,12},{4,8},{8,4},{12,0},{16,28},{20,24},{24,20},{28,16},{1,13},{... | collective-permute-start | bytes 294920 | tf_op jit(solution)/shard_map/ppermute | solution.py:227
  12.7 1.6 %collective-permute-start.23 = (bf16[48,1536]{1,0:T(8,128)(2,1)S(1)}, bf16[48,1536]{1,0:T(8,128)(2,1)S(1)}, u32[]{:S(2)}, u32[]{:S(2)}) collective-permute-start(bf16[48,1536]{1,0:T(8,128)(2,1)S(1)} %copy-done.18), channel_id=1, source_target_pairs={{0,8},{1,9},{2,10},{3,11},{4,12},{5,13},{6,14},{7,15},{8,16},{9,17... | collective-permute-start | bytes 442376 | tf_op jit(solution)/shard_map/ppermute | solution.py:212
  14.3 3.1 %collective-permute-done.12 = bf16[48,768]{1,0:T(8,128)(2,1)S(1)} collective-permute-done((bf16[48,768]{1,0:T(8,128)(2,1)S(1)}, bf16[48,768]{1,0:T(8,128)(2,1)S(1)}, u32[]{:S(2)}, u32[]{:S(2)}) %collective-permute-start.12) | collective-permute-done | bytes 73760 | tf_op jit(solution)/shard_map/ppermute | solution.py:208
  17.4 3.0 %collective-permute-start.3 = (bf16[32,1536]{1,0:T(8,128)(2,1)S(1)}, bf16[32,1536]{1,0:T(8,128)(2,1)S(1)}, u32[]{:S(2)}, u32[]{:S(2)}) collective-permute-start(bf16[32,1536]{1,0:T(8,128)(2,1)S(1)} %get-tuple-element.22), channel_id=1, source_target_pairs={{0,16},{4,20},{8,24},{12,28},{16,0},{20,4},{24,8},{28,12},{1,17},{... | collective-permute-start | bytes 294920 | tf_op jit(solution)/shard_map/ppermute | solution.py:227
  20.8 3.5 %collective-permute-start.5 = (bf16[32,1536]{1,0:T(8,128)(2,1)S(1)}, bf16[32,1536]{1,0:T(8,128)(2,1)S(1)}, u32[]{:S(2)}, u32[]{:S(2)}) collective-permute-start(bf16[32,1536]{1,0:T(8,128)(2,1)S(1)} %get-tuple-element.24), channel_id=1, source_target_pairs={{0,24},{4,28},{8,16},{12,20},{16,8},{20,12},{24,0},{28,4},{1,25},{... | collective-permute-start | bytes 294920 | tf_op jit(solution)/shard_map/ppermute | solution.py:227
  24.3 0.9 collective-permute-start.6
  25.3 6.4 %collective-permute-done.3.refs_3_ = bf16[32,1536]{1,0:T(8,128)(2,1)S(1)} collective-permute-done((bf16[32,1536]{1,0:T(8,128)(2,1)S(1)}, bf16[32,1536]{1,0:T(8,128)(2,1)S(1)}, u32[]{:S(2)}, u32[]{:S(2)}) %collective-permute-start.3) | collective-permute-done | bytes 98336 | tf_op jit(solution)/shard_map/ppermute | solution.py:227
  31.9 2.5 %collective-permute-done.4.refs_4_ = bf16[32,1536]{1,0:T(8,128)(2,1)S(1)} collective-permute-done((bf16[32,1536]{1,0:T(8,128)(2,1)S(1)}, bf16[32,1536]{1,0:T(8,128)(2,1)S(1)}, u32[]{:S(2)}, u32[]{:S(2)}) %collective-permute-start.4) | collective-permute-done | bytes 98336 | tf_op jit(solution)/shard_map/ppermute | solution.py:227
  34.4 4.0 %shard_map.101 = (bf16[2,32,1536]{2,1,0:T(8,128)(2,1)S(1)}, bf16[2,32,1536]{2,1,0:T(8,128)(2,1)S(1)}, s32[2]{0:T(128)S(1)}) custom-call(s32[1]{0:T(128)} %bitcast.place, s32[8,6]{1,0:T(8,128)S(1)} %bitcast.23, s32[8,6]{1,0:T(8,128)S(1)} %bitcast.25, s32[8,6]{1,0:T(8,128)S(1)} %bitcast.26, f32[1,1536]{1,0:T(1,128)S(1)} %broadcast_in_dim.17.gain, ...), custom_call_target="tpu_custom_call" | custom-call | tf_op jit(solution)/shard_map/pallas_call | solution.py:270
  39.0 4.7 %collective-permute-done.24 = bf16[48,1536]{1,0:T(8,128)(2,1)S(1)} collective-permute-done((bf16[48,1536]{1,0:T(8,128)(2,1)S(1)}, bf16[48,1536]{1,0:T(8,128)(2,1)S(1)}, u32[]{:S(2)}, u32[]{:S(2)}) %collective-permute-start.24) | collective-permute-done | bytes 147488 | tf_op jit(solution)/shard_map/ppermute | solution.py:212
  43.7 10.6 %collective-permute-start.25 = (bf16[48,1536]{1,0:T(8,128)(2,1)S(1)}, bf16[48,1536]{1,0:T(8,128)(2,1)S(1)}, u32[]{:S(2)}, u32[]{:S(2)}) collective-permute-start(bf16[48,1536]{1,0:T(8,128)(2,1)S(1)} %collective-permute-done.24), channel_id=1, source_target_pairs={{0,8},{1,9},{2,10},{3,11},{4,12},{5,13},{6,14},{7,15},{8,16},{9,17... | collective-permute-start | bytes 442376 | tf_op jit(solution)/shard_map/ppermute | solution.py:212
  55.2 1.9 %collective-permute-start.9 = (bf16[2,32,1536]{2,1,0:T(8,128)(2,1)S(1)}, bf16[2,32,1536]{2,1,0:T(8,128)(2,1)S(1)}, u32[]{:S(2)}, u32[]{:S(2)}) collective-permute-start(bf16[2,32,1536]{2,1,0:T(8,128)(2,1)S(1)} %get-tuple-element.28.refs_0_), channel_id=1, source_target_pairs={{0,6},{1,7},{2,4},{3,5},{4,2},{5,3},{6,0},{7,1},{8,14},{9,15},{10,... | collective-permute-start | bytes 589832 | tf_op jit(solution)/shard_map/ppermute | solution.py:208
  57.2 3.8 %collective-permute-start.14 = (bf16[4,48,768]{2,1,0:T(8,128)(2,1)S(1)}, bf16[4,48,768]{2,1,0:T(8,128)(2,1)}, u32[]{:S(2)}, u32[]{:S(2)}) collective-permute-start(bf16[4,48,768]{2,1,0:T(8,128)(2,1)S(1)} %collective-permute-done.13.refs_5_), channel_id=1, source_target_pairs={{0,8},{1,9},{2,10},{3,11},{4,12},{5,13},{6,14},{7,15},{8,16},{9,17... | collective-permute-start | bytes 884744 | tf_op jit(solution)/shard_map/ppermute | solution.py:212
  61.1 4.7 %collective-permute-done.8.refs_2_ = bf16[2,32,1536]{2,1,0:T(8,128)(2,1)S(1)} collective-permute-done((bf16[2,32,1536]{2,1,0:T(8,128)(2,1)S(1)}, bf16[2,32,1536]{2,1,0:T(8,128)(2,1)S(1)}, u32[]{:S(2)}, u32[]{:S(2)}) %collective-permute-start.8) | collective-permute-done | bytes 196640 | tf_op jit(solution)/shard_map/ppermute | solution.py:208
  66.5 1.4 %collective-permute-start.26 = (bf16[4,48,1536]{2,1,0:T(8,128)(2,1)S(1)}, bf16[4,48,1536]{2,1,0:T(8,128)(2,1)S(1)}, u32[]{:S(2)}, u32[]{:S(2)}) collective-permute-start(bf16[4,48,1536]{2,1,0:T(8,128)(2,1)S(1)} %pad_maximum_fusion.refs_4_), channel_id=1, source_target_pairs={{0,2},{1,3},{2,0},{3,1},{4,6},{5,7},{6,4},{7,5},{8,10},{9,11},{10,... | collective-permute-start | bytes 1769480 | tf_op jit(solution)/shard_map/ppermute | solution.py:208
  68.6 1.0 collective-permute-start.27
  70.3 1.1 collective-permute-start.28
  72.1 9.3 %collective-permute-done.15.refs_7_ = bf16[4,48,768]{2,1,0:T(8,128)(2,1)} collective-permute-done((bf16[4,48,768]{2,1,0:T(8,128)(2,1)}, bf16[4,48,768]{2,1,0:T(8,128)(2,1)}, u32[]{:S(2)}, u32[]{:S(2)}) %collective-permute-start.15) | collective-permute-done | bytes 294944 | tf_op jit(solution)/shard_map/ppermute | solution.py:212
  82.7 13.3 %collective-permute-done.27.refs_6_ = bf16[4,48,1536]{2,1,0:T(8,128)(2,1)S(1)} collective-permute-done((bf16[4,48,1536]{2,1,0:T(8,128)(2,1)S(1)}, bf16[4,48,1536]{2,1,0:T(8,128)(2,1)S(1)}, u32[]{:S(2)}, u32[]{:S(2)}) %collective-permute-start.27) | collective-permute-done | bytes 589856 | tf_op jit(solution)/shard_map/ppermute | solution.py:208
  98.2 1.0 copy-done.3
  99.2 1.0 copy-done.5
  100.1 1.0 copy-done.7
  104.8 7.6 %shard_map.102 = (bf16[2,32,384]{2,1,0:T(8,128)(2,1)S(1)}, bf16[2,32,384]{2,1,0:T(8,128)(2,1)S(1)}, bf16[2,32,384]{2,1,0:T(8,128)(2,1)S(1)}, bf16[2,32,384]{2,1,0:T(8,128)(2,1)S(1)}) custom-call(s32[8,4]{1,0:T(8,128)S(1)} %pad_add_fusion.1.where, f32[31,384]{1,0:T(8,128)S(1)} %constant_dynamic-slice_fusion.4.taps, f32[1,384]{1,0:T(1,128)S(1)} %dynamic_slice.22.scale, ...), custom_call_target="tpu_custom_call" | custom-call | flops 603979776 | bytes 2359296 | tf_op jit(solution)/shard_map/pallas_call | solution.py:283
  114.0 2.6 %collective-permute-done.20.refs_1_ = bf16[2,32,384]{2,1,0:T(8,128)(2,1)S(1)} collective-permute-done((bf16[2,32,384]{2,1,0:T(8,128)(2,1)S(1)}, bf16[2,32,384]{2,1,0:T(8,128)(2,1)S(1)}, u32[]{:S(2)}, u32[]{:S(2)}) %collective-permute-start.20) | collective-permute-done | bytes 49184 | tf_op jit(solution)/shard_map/ppermute | solution.py:208
  116.6 1.0 collective-permute-start.22
  117.5 4.0 %collective-permute-done.22.refs_3_ = bf16[2,32,384]{2,1,0:T(8,128)(2,1)S(1)} collective-permute-done((bf16[2,32,384]{2,1,0:T(8,128)(2,1)S(1)}, bf16[2,32,384]{2,1,0:T(8,128)(2,1)S(1)}, u32[]{:S(2)}, u32[]{:S(2)}) %collective-permute-start.22) | collective-permute-done | bytes 49184 | tf_op jit(solution)/shard_map/ppermute | solution.py:208
  121.6 9.9 %shard_map.103 = bf16[2,32,1536]{2,1,0:T(8,128)(2,1)} custom-call(s32[8,4]{1,0:T(8,128)S(1)} %pad_add_fusion.where, s32[2]{0:T(128)S(1)} %get-tuple-element.26.lens, s32[1]{0:T(128)} %bitcast.5.chip, bf16[2,32,1536]{2,1,0:T(8,128)(2,1)S(1)} %copy-done.9, bf16[2,32,384]{2,1,0:T(8,128)(2,1)S(1)} %get-tuple-element.29.refs_0_, ...), custom_call_target="tpu_custom_call" | custom-call | flops 301989888 | bytes 4718592 | tf_op jit(solution)/shard_map/pallas_call | solution.py:308
  (105 shorter events, 15.6 us)
Async XLA Ops:
  1.5 10.6 %collective-permute-start.10 = (bf16[48,768]{1,0:T(8,128)(2,1)S(1)}, bf16[48,768]{1,0:T(8,128)(2,1)S(1)}, u32[]{:S(2)}, u32[]{:S(2)}) collective-permute-start(bf16[48,768]{1,0:T(8,128)(2,1)S(1)} %bitcast.38), channel_id=1, source_target_pairs={{0,2},{1,3},{2,0},{3,1},{4,6},{5,7},{6,4},{7,5},{8,10},{9,11},{10,... | collective-permute-start | bytes 221192 | tf_op jit(solution)/shard_map/ppermute | solution.py:208
  4.5 8.2 %collective-permute-start.11 = (bf16[48,768]{1,0:T(8,128)(2,1)S(1)}, bf16[48,768]{1,0:T(8,128)(2,1)S(1)}, u32[]{:S(2)}, u32[]{:S(2)}) collective-permute-start(bf16[48,768]{1,0:T(8,128)(2,1)S(1)} %bitcast.37), channel_id=1, source_target_pairs={{0,4},{1,5},{2,6},{3,7},{4,0},{5,1},{6,2},{7,3},{8,12},{9,13},{10,... | collective-permute-start | bytes 221192 | tf_op jit(solution)/shard_map/ppermute | solution.py:208
  8.5 11.9 %collective-permute-start = (bf16[32,1536]{1,0:T(8,128)(2,1)S(1)}, bf16[32,1536]{1,0:T(8,128)(2,1)S(1)}, u32[]{:S(2)}, u32[]{:S(2)}) collective-permute-start(bf16[32,1536]{1,0:T(8,128)(2,1)S(1)} %get-tuple-element.19), channel_id=1, source_target_pairs={{0,4},{4,0},{8,12},{12,8},{16,20},{20,16},{24,28},{28,24},{1,5},{5... | collective-permute-start | bytes 294920 | tf_op jit(solution)/shard_map/ppermute | solution.py:227
  9.1 11.7 %collective-permute-start.1 = (bf16[32,1536]{1,0:T(8,128)(2,1)S(1)}, bf16[32,1536]{1,0:T(8,128)(2,1)S(1)}, u32[]{:S(2)}, u32[]{:S(2)}) collective-permute-start(bf16[32,1536]{1,0:T(8,128)(2,1)S(1)} %get-tuple-element.20), channel_id=1, source_target_pairs={{0,8},{4,12},{8,0},{12,4},{16,24},{20,28},{24,16},{28,20},{1,9},{5... | collective-permute-start | bytes 294920 | tf_op jit(solution)/shard_map/ppermute | solution.py:227
  10.7 13.6 %collective-permute-start.2 = (bf16[32,1536]{1,0:T(8,128)(2,1)S(1)}, bf16[32,1536]{1,0:T(8,128)(2,1)S(1)}, u32[]{:S(2)}, u32[]{:S(2)}) collective-permute-start(bf16[32,1536]{1,0:T(8,128)(2,1)S(1)} %get-tuple-element.21), channel_id=1, source_target_pairs={{0,12},{4,8},{8,4},{12,0},{16,28},{20,24},{24,20},{28,16},{1,13},{... | collective-permute-start | bytes 294920 | tf_op jit(solution)/shard_map/ppermute | solution.py:227
  12.1 5.3 %collective-permute-start.12 = (bf16[48,768]{1,0:T(8,128)(2,1)S(1)}, bf16[48,768]{1,0:T(8,128)(2,1)S(1)}, u32[]{:S(2)}, u32[]{:S(2)}) collective-permute-start(bf16[48,768]{1,0:T(8,128)(2,1)S(1)} %bitcast.39), channel_id=1, source_target_pairs={{0,6},{1,7},{2,4},{3,5},{4,2},{5,3},{6,0},{7,1},{8,14},{9,15},{10,... | collective-permute-start | bytes 221192 | tf_op jit(solution)/shard_map/ppermute | solution.py:208
  12.7 19.1 %collective-permute-start.23 = (bf16[48,1536]{1,0:T(8,128)(2,1)S(1)}, bf16[48,1536]{1,0:T(8,128)(2,1)S(1)}, u32[]{:S(2)}, u32[]{:S(2)}) collective-permute-start(bf16[48,1536]{1,0:T(8,128)(2,1)S(1)} %copy-done.18), channel_id=1, source_target_pairs={{0,8},{1,9},{2,10},{3,11},{4,12},{5,13},{6,14},{7,15},{8,16},{9,17... | collective-permute-start | bytes 442376 | tf_op jit(solution)/shard_map/ppermute | solution.py:212
  17.4 14.4 %collective-permute-start.3 = (bf16[32,1536]{1,0:T(8,128)(2,1)S(1)}, bf16[32,1536]{1,0:T(8,128)(2,1)S(1)}, u32[]{:S(2)}, u32[]{:S(2)}) collective-permute-start(bf16[32,1536]{1,0:T(8,128)(2,1)S(1)} %get-tuple-element.22), channel_id=1, source_target_pairs={{0,16},{4,20},{8,24},{12,28},{16,0},{20,4},{24,8},{28,12},{1,17},{... | collective-permute-start | bytes 294920 | tf_op jit(solution)/shard_map/ppermute | solution.py:227
  20.4 14.0 %collective-permute-start.4 = (bf16[32,1536]{1,0:T(8,128)(2,1)S(1)}, bf16[32,1536]{1,0:T(8,128)(2,1)S(1)}, u32[]{:S(2)}, u32[]{:S(2)}) collective-permute-start(bf16[32,1536]{1,0:T(8,128)(2,1)S(1)} %get-tuple-element.23), channel_id=1, source_target_pairs={{0,20},{4,16},{8,28},{12,24},{16,4},{20,0},{24,12},{28,8},{1,21},{... | collective-permute-start | bytes 294920 | tf_op jit(solution)/shard_map/ppermute | solution.py:227
  20.8 13.5 %collective-permute-start.5 = (bf16[32,1536]{1,0:T(8,128)(2,1)S(1)}, bf16[32,1536]{1,0:T(8,128)(2,1)S(1)}, u32[]{:S(2)}, u32[]{:S(2)}) collective-permute-start(bf16[32,1536]{1,0:T(8,128)(2,1)S(1)} %get-tuple-element.24), channel_id=1, source_target_pairs={{0,24},{4,28},{8,16},{12,20},{16,8},{20,12},{24,0},{28,4},{1,25},{... | collective-permute-start | bytes 294920 | tf_op jit(solution)/shard_map/ppermute | solution.py:227
  24.3 10.0 %collective-permute-start.6 = (bf16[32,1536]{1,0:T(8,128)(2,1)S(1)}, bf16[32,1536]{1,0:T(8,128)(2,1)S(1)}, u32[]{:S(2)}, u32[]{:S(2)}) collective-permute-start(bf16[32,1536]{1,0:T(8,128)(2,1)S(1)} %get-tuple-element.25), channel_id=1, source_target_pairs={{0,28},{4,24},{8,20},{12,16},{16,12},{20,8},{24,4},{28,0},{1,29},{... | collective-permute-start | bytes 294920 | tf_op jit(solution)/shard_map/ppermute | solution.py:227
  31.7 25.4 %collective-permute-start.13 = (bf16[4,48,768]{2,1,0:T(8,128)(2,1)S(1)}, bf16[4,48,768]{2,1,0:T(8,128)(2,1)S(1)}, u32[]{:S(2)}, u32[]{:S(2)}) collective-permute-start(bf16[4,48,768]{2,1,0:T(8,128)(2,1)S(1)} %pad_maximum_fusion.1.refs_4_), channel_id=1, source_target_pairs={{0,8},{1,9},{2,10},{3,11},{4,12},{5,13},{6,14},{7,15},{8,16},{9,17... | collective-permute-start | bytes 884744 | tf_op jit(solution)/shard_map/ppermute | solution.py:212
  31.8 11.9 %collective-permute-start.24 = (bf16[48,1536]{1,0:T(8,128)(2,1)S(1)}, bf16[48,1536]{1,0:T(8,128)(2,1)S(1)}, u32[]{:S(2)}, u32[]{:S(2)}) collective-permute-start(bf16[48,1536]{1,0:T(8,128)(2,1)S(1)} %collective-permute-done.23), channel_id=1, source_target_pairs={{0,8},{1,9},{2,10},{3,11},{4,12},{5,13},{6,14},{7,15},{8,16},{9,17... | collective-permute-start | bytes 442376 | tf_op jit(solution)/shard_map/ppermute | solution.py:212
  38.4 16.8 %collective-permute-start.7 = (bf16[2,32,1536]{2,1,0:T(8,128)(2,1)S(1)}, bf16[2,32,1536]{2,1,0:T(8,128)(2,1)S(1)}, u32[]{:S(2)}, u32[]{:S(2)}) collective-permute-start(bf16[2,32,1536]{2,1,0:T(8,128)(2,1)S(1)} %get-tuple-element.28.refs_0_), channel_id=1, source_target_pairs={{0,2},{1,3},{2,0},{3,1},{4,6},{5,7},{6,4},{7,5},{8,10},{9,11},{10,... | collective-permute-start | bytes 589832 | tf_op jit(solution)/shard_map/ppermute | solution.py:208
  43.7 17.3 %collective-permute-start.25 = (bf16[48,1536]{1,0:T(8,128)(2,1)S(1)}, bf16[48,1536]{1,0:T(8,128)(2,1)S(1)}, u32[]{:S(2)}, u32[]{:S(2)}) collective-permute-start(bf16[48,1536]{1,0:T(8,128)(2,1)S(1)} %collective-permute-done.24), channel_id=1, source_target_pairs={{0,8},{1,9},{2,10},{3,11},{4,12},{5,13},{6,14},{7,15},{8,16},{9,17... | collective-permute-start | bytes 442376 | tf_op jit(solution)/shard_map/ppermute | solution.py:212
  54.3 15.3 %collective-permute-start.16 = (bf16[4,48,768]{2,1,0:T(8,128)(2,1)S(1)}, bf16[4,48,768]{2,1,0:T(8,128)(2,1)S(1)}, u32[]{:S(2)}, u32[]{:S(2)}) collective-permute-start(bf16[4,48,768]{2,1,0:T(8,128)(2,1)S(1)} %pad_maximum_fusion.1.refs_4_), channel_id=1, source_target_pairs={{0,1},{1,0},{2,3},{3,2},{4,5},{5,4},{6,7},{7,6},{8,9},{9,8},{10,11... | collective-permute-start | bytes 884744 | tf_op jit(solution)/shard_map/ppermute | solution.py:208
  54.3 11.5 %collective-permute-start.8 = (bf16[2,32,1536]{2,1,0:T(8,128)(2,1)S(1)}, bf16[2,32,1536]{2,1,0:T(8,128)(2,1)S(1)}, u32[]{:S(2)}, u32[]{:S(2)}) collective-permute-start(bf16[2,32,1536]{2,1,0:T(8,128)(2,1)S(1)} %get-tuple-element.28.refs_0_), channel_id=1, source_target_pairs={{0,4},{1,5},{2,6},{3,7},{4,0},{5,1},{6,2},{7,3},{8,12},{9,13},{10,... | collective-permute-start | bytes 589832 | tf_op jit(solution)/shard_map/ppermute | solution.py:208
  55.2 12.7 %collective-permute-start.9 = (bf16[2,32,1536]{2,1,0:T(8,128)(2,1)S(1)}, bf16[2,32,1536]{2,1,0:T(8,128)(2,1)S(1)}, u32[]{:S(2)}, u32[]{:S(2)}) collective-permute-start(bf16[2,32,1536]{2,1,0:T(8,128)(2,1)S(1)} %get-tuple-element.28.refs_0_), channel_id=1, source_target_pairs={{0,6},{1,7},{2,4},{3,5},{4,2},{5,3},{6,0},{7,1},{8,14},{9,15},{10,... | collective-permute-start | bytes 589832 | tf_op jit(solution)/shard_map/ppermute | solution.py:208
  57.2 14.2 %collective-permute-start.14 = (bf16[4,48,768]{2,1,0:T(8,128)(2,1)S(1)}, bf16[4,48,768]{2,1,0:T(8,128)(2,1)}, u32[]{:S(2)}, u32[]{:S(2)}) collective-permute-start(bf16[4,48,768]{2,1,0:T(8,128)(2,1)S(1)} %collective-permute-done.13.refs_5_), channel_id=1, source_target_pairs={{0,8},{1,9},{2,10},{3,11},{4,12},{5,13},{6,14},{7,15},{8,16},{9,17... | collective-permute-start | bytes 884744 | tf_op jit(solution)/shard_map/ppermute | solution.py:212
  61.0 10.4 %collective-permute-start.17 = (bf16[4,48,768]{2,1,0:T(8,128)(2,1)S(1)}, bf16[4,48,768]{2,1,0:T(8,128)(2,1)S(1)}, u32[]{:S(2)}, u32[]{:S(2)}) collective-permute-start(bf16[4,48,768]{2,1,0:T(8,128)(2,1)S(1)} %collective-permute-done.13.refs_5_), channel_id=1, source_target_pairs={{0,1},{1,0},{2,3},{3,2},{4,5},{5,4},{6,7},{7,6},{8,9},{9,8},{10,11... | collective-permute-start | bytes 884744 | tf_op jit(solution)/shard_map/ppermute | solution.py:208
  66.5 16.2 %collective-permute-start.26 = (bf16[4,48,1536]{2,1,0:T(8,128)(2,1)S(1)}, bf16[4,48,1536]{2,1,0:T(8,128)(2,1)S(1)}, u32[]{:S(2)}, u32[]{:S(2)}) collective-permute-start(bf16[4,48,1536]{2,1,0:T(8,128)(2,1)S(1)} %pad_maximum_fusion.refs_4_), channel_id=1, source_target_pairs={{0,2},{1,3},{2,0},{3,1},{4,6},{5,7},{6,4},{7,5},{8,10},{9,11},{10,... | collective-permute-start | bytes 1769480 | tf_op jit(solution)/shard_map/ppermute | solution.py:208
  68.6 27.4 %collective-permute-start.27 = (bf16[4,48,1536]{2,1,0:T(8,128)(2,1)S(1)}, bf16[4,48,1536]{2,1,0:T(8,128)(2,1)S(1)}, u32[]{:S(2)}, u32[]{:S(2)}) collective-permute-start(bf16[4,48,1536]{2,1,0:T(8,128)(2,1)S(1)} %pad_maximum_fusion.refs_4_), channel_id=1, source_target_pairs={{0,4},{1,5},{2,6},{3,7},{4,0},{5,1},{6,2},{7,3},{8,12},{9,13},{10,... | collective-permute-start | bytes 1769480 | tf_op jit(solution)/shard_map/ppermute | solution.py:208
  70.3 25.7 %collective-permute-start.28 = (bf16[4,48,1536]{2,1,0:T(8,128)(2,1)S(1)}, bf16[4,48,1536]{2,1,0:T(8,128)(2,1)S(1)}, u32[]{:S(2)}, u32[]{:S(2)}) collective-permute-start(bf16[4,48,1536]{2,1,0:T(8,128)(2,1)S(1)} %pad_maximum_fusion.refs_4_), channel_id=1, source_target_pairs={{0,6},{1,7},{2,4},{3,5},{4,2},{5,3},{6,0},{7,1},{8,14},{9,15},{10,... | collective-permute-start | bytes 1769480 | tf_op jit(solution)/shard_map/ppermute | solution.py:208
  71.4 10.0 %collective-permute-start.15 = (bf16[4,48,768]{2,1,0:T(8,128)(2,1)}, bf16[4,48,768]{2,1,0:T(8,128)(2,1)}, u32[]{:S(2)}, u32[]{:S(2)}) collective-permute-start(bf16[4,48,768]{2,1,0:T(8,128)(2,1)} %collective-permute-done.14.refs_6_), channel_id=1, source_target_pairs={{0,8},{1,9},{2,10},{3,11},{4,12},{5,13},{6,14},{7,15},{8,16},{9,17... | collective-permute-start | bytes 884744 | tf_op jit(solution)/shard_map/ppermute | solution.py:212
  72.1 9.3 %collective-permute-start.18 = (bf16[4,48,768]{2,1,0:T(8,128)(2,1)}, bf16[4,48,768]{2,1,0:T(8,128)(2,1)}, u32[]{:S(2)}, u32[]{:S(2)}) collective-permute-start(bf16[4,48,768]{2,1,0:T(8,128)(2,1)} %collective-permute-done.14.refs_6_), channel_id=1, source_target_pairs={{0,1},{1,0},{2,3},{3,2},{4,5},{5,4},{6,7},{7,6},{8,9},{9,8},{10,11... | collective-permute-start | bytes 884744 | tf_op jit(solution)/shard_map/ppermute | solution.py:208
  81.4 31.7 %collective-permute-start.29 = (bf16[4,48,1536]{2,1,0:T(8,128)(2,1)S(1)}, bf16[4,48,1536]{2,1,0:T(8,128)(2,1)S(1)}, u32[]{:S(2)}, u32[]{:S(2)}) collective-permute-start(bf16[4,48,1536]{2,1,0:T(8,128)(2,1)S(1)} %pad_maximum_fusion.refs_4_), channel_id=1, source_target_pairs={{0,1},{1,0},{2,3},{3,2},{4,5},{5,4},{6,7},{7,6},{8,9},{9,8},{10,11... | collective-permute-start | bytes 1769480 | tf_op jit(solution)/shard_map/ppermute | solution.py:208
  81.4 16.8 %collective-permute-start.19 = (bf16[4,48,768]{2,1,0:T(8,128)(2,1)}, bf16[4,48,768]{2,1,0:T(8,128)(2,1)S(1)}, u32[]{:S(2)}, u32[]{:S(2)}) collective-permute-start(bf16[4,48,768]{2,1,0:T(8,128)(2,1)} %collective-permute-done.15.refs_7_), channel_id=1, source_target_pairs={{0,1},{1,0},{2,3},{3,2},{4,5},{5,4},{6,7},{7,6},{8,9},{9,8},{10,11... | collective-permute-start | bytes 884744 | tf_op jit(solution)/shard_map/ppermute | solution.py:208
  82.7 38.9 %collective-permute-start.30 = (bf16[4,48,1536]{2,1,0:T(8,128)(2,1)S(1)}, bf16[4,48,1536]{2,1,0:T(8,128)(2,1)S(1)}, u32[]{:S(2)}, u32[]{:S(2)}) collective-permute-start(bf16[4,48,1536]{2,1,0:T(8,128)(2,1)S(1)} %collective-permute-done.26.refs_5_), channel_id=1, source_target_pairs={{0,1},{1,0},{2,3},{3,2},{4,5},{5,4},{6,7},{7,6},{8,9},{9,8},{10,11... | collective-permute-start | bytes 1769480 | tf_op jit(solution)/shard_map/ppermute | solution.py:208
  96.0 25.6 %collective-permute-start.31 = (bf16[4,48,1536]{2,1,0:T(8,128)(2,1)S(1)}, bf16[4,48,1536]{2,1,0:T(8,128)(2,1)S(1)}, u32[]{:S(2)}, u32[]{:S(2)}) collective-permute-start(bf16[4,48,1536]{2,1,0:T(8,128)(2,1)S(1)} %collective-permute-done.27.refs_6_), channel_id=1, source_target_pairs={{0,1},{1,0},{2,3},{3,2},{4,5},{5,4},{6,7},{7,6},{8,9},{9,8},{10,11... | collective-permute-start | bytes 1769480 | tf_op jit(solution)/shard_map/ppermute | solution.py:208
  96.0 25.6 %collective-permute-start.32 = (bf16[4,48,1536]{2,1,0:T(8,128)(2,1)S(1)}, bf16[4,48,1536]{2,1,0:T(8,128)(2,1)S(1)}, u32[]{:S(2)}, u32[]{:S(2)}) collective-permute-start(bf16[4,48,1536]{2,1,0:T(8,128)(2,1)S(1)} %collective-permute-done.28.refs_7_), channel_id=1, source_target_pairs={{0,1},{1,0},{2,3},{3,2},{4,5},{5,4},{6,7},{7,6},{8,9},{9,8},{10,11... | collective-permute-start | bytes 1769480 | tf_op jit(solution)/shard_map/ppermute | solution.py:208
  113.1 4.4 %collective-permute-start.21 = (bf16[2,32,384]{2,1,0:T(8,128)(2,1)S(1)}, bf16[2,32,384]{2,1,0:T(8,128)(2,1)S(1)}, u32[]{:S(2)}, u32[]{:S(2)}) collective-permute-start(bf16[2,32,384]{2,1,0:T(8,128)(2,1)S(1)} %get-tuple-element.31), channel_id=1, source_target_pairs={{0,4},{1,5},{2,6},{3,7},{4,0},{5,1},{6,2},{7,3},{8,12},{9,13},{10,... | collective-permute-start | bytes 147464 | tf_op jit(solution)/shard_map/ppermute | solution.py:208
  116.6 5.0 %collective-permute-start.22 = (bf16[2,32,384]{2,1,0:T(8,128)(2,1)S(1)}, bf16[2,32,384]{2,1,0:T(8,128)(2,1)S(1)}, u32[]{:S(2)}, u32[]{:S(2)}) collective-permute-start(bf16[2,32,384]{2,1,0:T(8,128)(2,1)S(1)} %get-tuple-element.32), channel_id=1, source_target_pairs={{0,6},{1,7},{2,4},{3,5},{4,2},{5,3},{6,0},{7,1},{8,14},{9,15},{10,... | collective-permute-start | bytes 147464 | tf_op jit(solution)/shard_map/ppermute | solution.py:208
  (24 other events, 209.4 us)

commit v2 on v0

v2 whole, which is shorter than its diff:
```python
import functools
import math

import jax
import jax.numpy as jnp
from jax import lax
from jax.experimental import pallas as pl
from jax.experimental.pallas import tpu as pltpu
from jax.sharding import PartitionSpec as P

SMEM = pl.BlockSpec(memory_space=pltpu.SMEM)
VMEM = pl.BlockSpec(memory_space=pltpu.VMEM)
BF16 = jnp.bfloat16
F32 = jnp.float32


def call(kernel, out_shape, in_specs, out_specs, operands, scratch=(), flops=0):
    shapes = list(operands) + list(jax.tree.leaves(out_shape)) + list(scratch)
    total = sum(math.prod(shape.shape) * shape.dtype.itemsize for shape in shapes)
    return pl.pallas_call(
        kernel,
        out_shape=out_shape,
        in_specs=in_specs,
        out_specs=out_specs,
        scratch_shapes=[pltpu.VMEM(shape.shape, shape.dtype) for shape in scratch],
        cost_estimate=pl.CostEstimate(flops=flops, bytes_accessed=total, transcendentals=0),
        compiler_params=pltpu.CompilerParams(
            vmem_limit_bytes=min(total + total // 2 + 4 * 2**20, 60 * 2**20)
        ),
    )(*operands)


def like(dtype, *shape):
    return jax.ShapeDtypeStruct(shape, dtype)


def send_kernel(place, tab_len, tab_dest, frames, out):
    me = place[0]
    slots = frames.shape[0]

    def send(target, carry):
        found = jnp.int32(0)
        for slot in range(slots):
            hit = jnp.logical_and(tab_dest[me, slot] == target, tab_len[me, slot] > 0)
            found = jnp.where(hit, slot, found)
        out[target] = frames[found]
        return carry

    lax.fori_loop(0, out.shape[0], send, 0)


def table_kernel(
    long, planes, place, chip, tab_len, tab_dest, tab_off, taps, scale, shift, sources, lens, table
):
    source_count, slots = tab_len.shape
    me = place[0]

    def look(source, carry):
        for slot in range(slots):

            @pl.when(jnp.logical_and(tab_dest[source, slot] == me, tab_len[source, slot] > 0))
            def _():
                number = tab_off[source, slot] // long
                sources[number] = source
                lens[number] = tab_len[source, slot]

        return carry

    lax.fori_loop(0, source_count, look, 0)
    width, chans = scale.shape[1], table.shape[1]
    chips = width // chans
    run = chans // planes
    whole = jnp.concatenate([taps[...], scale[...], shift[...]], axis=0)
    for owner in range(chips):

        @pl.when(chip[0] == owner)
        def _():
            starts = [(plane * chips + owner) * run for plane in range(planes)]
            table[...] = jnp.concatenate([whole[:, at : at + run] for at in starts], axis=1)


def norm_kernel(sources, lens, gain, arrived, kept, normed):
    for number in range(kept.shape[0]):
        rows = arrived[sources[number]]
        kept[number] = rows
        wide = rows.astype(F32)
        mean = jnp.mean(wide, axis=1, keepdims=True)
        centred = wide - mean
        var = jnp.mean(centred * centred, axis=1, keepdims=True)
        value = centred * lax.rsqrt(var + 1e-05) * gain[...]
        steps = lax.broadcasted_iota(jnp.int32, value.shape, 0)
        normed[number] = jnp.where(steps < lens[number], value, 0.0).astype(BF16)


def split_kernel(planes, chip, weights, *refs):
    outs, buf = refs[:-1], refs[-1]
    chips = len(outs)
    width = weights.shape[1] // 2
    run = width // (planes * chips)
    for owner in range(chips):
        parts = [
            weights[:, pl.ds(half * width + (plane * chips + owner) * run, run)]
            for half in range(2)
            for plane in range(planes)
        ]
        buf[owner] = jnp.concatenate(parts, axis=1)
    for number, out in enumerate(outs):
        out[...] = buf[jnp.bitwise_xor(chip[0], number)]


def conv_rows(block, taps):
    long, chans = block.shape
    count = taps.shape[0]
    front = (count - 1) // 2
    groups = long // 8
    pieces = [block[8 * at : 8 * at + 8, :] for at in range(groups)]
    total = None
    for residue in range(8):
        rows = []
        for at in range(groups + 1):
            value = None
            for step in range(-(count // 8) - 1, count // 8 + 2):
                tap = 8 * step + residue + front - 16
                source = at + step - 2
                if 0 <= tap < count and 0 <= source < groups:
                    term = pieces[source] * taps[tap : tap + 1, :]
                    value = term if value is None else value + term
            rows.append(jnp.zeros((8, chans), F32) if value is None else value)
        whole = jnp.concatenate(rows, axis=0)[residue : residue + long, :]
        total = whole if total is None else total + whole
    return total


def main_kernel(parts, pieces, where, kept, table, *refs):
    normed, weights = refs[:parts], refs[parts : parts + pieces]
    own, outs = refs[parts + pieces], refs[parts + pieces + 1 : 2 * parts + pieces]
    rows_buf, in_buf, out_buf, glu_buf, act_buf = refs[2 * parts + pieces :]
    recv, long, width = kept.shape
    tall = recv * long
    chans = table.shape[1]
    taps = table[: table.shape[0] - 2, :]
    scale, shift = table[table.shape[0] - 2 : table.shape[0] - 1, :], table[table.shape[0] - 1 :, :]
    for number, ref in enumerate(normed):
        rows_buf[pl.ds(number * tall, tall), :] = ref[...].reshape(tall, width)
    if pieces == 2:
        w_in, w_out = weights
    else:
        w_in, w_out = in_buf, out_buf
        depth, wide = weights[0].shape[1:]
        for number, ref in enumerate(weights):
            for inner in range(parts):
                start = pl.multiple_of(where[number, inner] * depth, 16)
                in_buf[pl.ds(start, depth), :] = ref[inner]
            start = pl.multiple_of(where[number, parts] * depth, 16)
            for half in range(width // wide):
                out_buf[pl.ds(start, depth), half * wide : half * wide + wide] = ref[parts + half]
    glu_in = jnp.dot(rows_buf[...], w_in[...], preferred_element_type=F32)
    glu_buf[...] = glu_in[:, :chans] * jax.nn.sigmoid(glu_in[:, chans:])

    def utterance(at, carry):
        start = pl.multiple_of(at * long, long)
        moved = conv_rows(glu_buf[pl.ds(start, long), :], taps) * scale + shift
        act_buf[pl.ds(start, long), :] = (moved * jax.nn.sigmoid(moved)).astype(BF16)
        return carry

    lax.fori_loop(0, parts * recv, utterance, 0)
    batch = min(parts, 4)
    for first in range(0, parts, batch):
        mixed = jnp.dot(
            act_buf[pl.ds(first * tall, batch * tall), :],
            w_out[...],
            preferred_element_type=F32,
        )
        for number in range(first, first + batch):
            part = mixed[(number - first) * tall : (number - first + 1) * tall, :]
            part = part.reshape(recv, long, width)
            if number == 0:
                own[...] = kept[...].astype(F32) + part
            else:
                outs[number - 1][...] = part.astype(BF16)


def shards(
    frames, ln_gain, w_in, depth_kernel, bn_scale, bn_shift, w_out, lengths, destinations, offsets
):
    dp_count, fsdp_count = lax.axis_size("dp"), lax.axis_size("fsdp")
    chips = (fsdp_count // 2) ** 2
    planes = dp_count * fsdp_count // (2 * chips)
    dp_index = lax.axis_index("dp")
    number = dp_index * fsdp_count + lax.axis_index("fsdp")
    core = number % 2
    chip = (number // 2) % chips
    plane = number // (2 * chips)
    devices = dp_count * fsdp_count
    recv = lengths.shape[2] // 3
    _, _, long, width = frames.shape
    depth = w_in.shape[0]
    chans = width // chips
    wide = 2 * chans
    run = 2 * depth
    taps = depth_kernel.shape[0]

    def swap(array, mask):
        return lax.ppermute(array, ("dp", "fsdp"), [(at, at ^ mask) for at in range(devices)])

    def climb(array):
        pairs = [(at, (at + 2 * chips) % devices) for at in range(devices)]
        return lax.ppermute(array, ("dp", "fsdp"), pairs)

    place = dp_index.astype(jnp.int32)[None]
    chip_place = chip.astype(jnp.int32)[None]
    tab_len, tab_dest, tab_off = lengths[0], destinations[0], offsets[0]

    if depth % 16 == 0:
        split = call(
            functools.partial(split_kernel, planes),
            [like(BF16, depth, wide)] * chips,
            [SMEM, VMEM],
            [VMEM] * chips,
            (chip_place, w_in),
            [like(BF16, chips, depth, wide)],
        )
    else:
        by_owner = w_in.reshape(depth, 2, planes, chips, run).transpose(3, 0, 1, 2, 4)
        by_owner = by_owner.reshape(chips, depth, wide)
        split = [
            lax.dynamic_index_in_dim(by_owner, chip ^ mask, 0, keepdims=False)
            for mask in range(chips)
        ]
    columns = [split[0]] + [swap(split[mask], 2 * mask) for mask in range(1, chips)]
    halves = [w_out[:, at : at + wide] for at in range(0, width, wide)]
    ring = jnp.stack(columns + halves)

    send = call(
        send_kernel,
        like(BF16, dp_count, long, width),
        [SMEM, SMEM, SMEM, VMEM],
        VMEM,
        (place, tab_len, tab_dest, frames[0]),
    )
    ring, send = lax.optimization_barrier((ring, send))
    arrived = lax.all_to_all(send, "dp", split_axis=0, concat_axis=0, tiled=True)
    sources, lens, table = call(
        functools.partial(table_kernel, long, planes),
        [like(jnp.int32, recv), like(jnp.int32, recv), like(F32, taps + 2, chans)],
        [SMEM] * 5 + [VMEM] * 3,
        [SMEM, SMEM, VMEM],
        (place, chip_place, tab_len, tab_dest, tab_off)
        + (depth_kernel, bn_scale[None], bn_shift[None]),
    )

    rings = [ring]
    for _ in range(planes - 1):
        rings.append(climb(rings[-1]))
    pieces = rings + [swap(part, 1) for part in rings]

    ring_plane = (plane - jnp.arange(planes)) % planes
    ring_chip = chip ^ jnp.arange(chips)
    in_rows = (ring_plane[:, None] * chips + ring_chip[None, :]) * 2
    where = jnp.concatenate([in_rows, ring_plane[:, None] * 2], 1)
    where = jnp.concatenate([where + core, where + 1 - core], 0).astype(jnp.int32)
    if depth % 16:
        together = jnp.stack(pieces)
        flat = together[:, :chips].reshape(-1, depth, wide)
        all_in = jnp.zeros_like(flat).at[where[:, :chips].reshape(-1)].set(flat)
        flat = together[:, chips:].transpose(0, 2, 1, 3).reshape(-1, depth, width)
        all_out = jnp.zeros_like(flat).at[where[:, chips]].set(flat)
        pieces = [all_in.reshape(width, wide), all_out.reshape(chans, width)]

    utts = like(BF16, recv, long, width)
    kept, normed = call(
        norm_kernel,
        [utts, utts],
        [SMEM, SMEM, VMEM, VMEM],
        [VMEM, VMEM],
        (sources, lens, ln_gain[None], arrived),
    )
    normed = [normed] + [swap(normed, 2 * mask) for mask in range(1, chips)]

    tall = chips * recv * long
    own, *partial_sums = call(
        functools.partial(main_kernel, chips, len(pieces)),
        [like(F32, recv, long, width)] + [utts] * (chips - 1),
        [SMEM] + [VMEM] * (2 + chips + len(pieces)),
        [VMEM] * chips,
        (where, kept, table, *normed, *pieces),
        [
            like(BF16, tall, width),
            like(BF16, width, wide),
            like(BF16, chans, width),
            like(F32, tall, chans),
            like(BF16, tall, chans),
        ],
        flops=6 * tall * width * chans,
    )
    for mask, part in enumerate(partial_sums, 1):
        own = own + swap(part, 2 * mask).astype(F32)
    live = jnp.arange(long, dtype=jnp.int32)[None, :, None] < lens[:, None, None]
    return jnp.where(live, own, 0.0).astype(BF16)[None]


def solution(mesh):
    return jax.shard_map(
        shards,
        mesh=mesh,
        in_specs=(
            P("fsdp", "dp", None, None),
            P(),
            P(("dp", "fsdp"), None),
            P(),
            P(),
            P(),
            P(("dp", "fsdp"), None),
            P("fsdp", None, None),
            P("fsdp", None, None),
            P("fsdp", None, None),
        ),
        out_specs=P("fsdp", "dp", None, None),
        check_vma=False,
    )
```

time: 199 us -> 90.7 us (0.46)
  waiting for transfers between devices: 159 us -> 50.1 us
  starting transfers between devices: 4.53 us -> 24.5 us
  between operations: 13.6 us -> 0.13 us
  matrix products: 9.09 us -> 0 us
  Pallas kernels: 0 us -> 8.89 us
  other arithmetic: 9.35 us -> 1.04 us
  local copies, waits for them, and re-layouts: 3.27 us -> 5.61 us
    all_gather x2 -> x0, waiting for transfers between devices: 137 us -> none  [the longest x1 83.5 us: shards(): lax.all_gather(w_in, ('dp', 'fsdp'), axis=0, tiled=True)]
    ppermute x0 -> x16, waiting for transfers between devices: none -> 48.9 us  [the longest x3 31 us: climb(): return lax.ppermute(array, ('dp', 'fsdp'), pairs)]
    ppermute x0 -> x16, starting transfers between devices: none -> 19.5 us  [the longest x13 12.4 us: swap(): lax.ppermute(array, ('dp', 'fsdp'), [(at, at ^ mask) for at in range(devi...]
    all_to_all x1, waiting for transfers between devices: 20 us -> 1.21 us  [shards(): lax.all_to_all(send, 'dp', split_axis=0, concat_axis=0, tiled=True)]
    dot_general x2 -> x0, matrix products: 9.09 us -> none  [the longest x1 5.67 us: conv_module(): glu_in = jnp.dot(normed, full_in, preferred_element_type=jnp.float32)]
    pallas_call x0 -> x5, Pallas kernels: none -> 8.89 us  [call(): pl.pallas_call(kernel, out_shape=out_shape, in_specs=in_specs, out_specs=...]
    convert_element_type x3 -> x0, other arithmetic: 5.09 us -> none  [the longest x1 4.52 us: conv_module(): activated = (shifted * jax.nn.sigmoid(shifted)).astype(jnp.bfloat16)]
    unnamed x19 -> x28, local copies, waits for them, and re-layouts: 0.81 us -> 5.58 us
  transfers between devices with their start and end apart: 3 -> 17, of which waited for: 3 -> 10; matrix products, arithmetic and copies ran while one was open for 7% -> 1% of each run, Pallas kernels for 0% -> 5%
where the time goes in v2:
time: 90.7 us; the launch traced here: 90.3 us
  waiting for transfers between devices  50.1 us (55%)
  starting transfers between devices  24.5 us (27%)
  Pallas kernels  8.89 us (10%)
  local copies, waits for them, and re-layouts  5.61 us (6%)
  other arithmetic  1.04 us (1%)
    ppermute x3, waiting for transfers between devices, climb(): return lax.ppermute(array, ('dp', 'fsdp'), pairs)  31 us
    ppermute x13, waiting for transfers between devices, swap(): lax.ppermute(array, ('dp', 'fsdp'), [(at, at ^ mask) for at in range(devi...  17.9 us
    ppermute x13, starting transfers between devices, swap(): lax.ppermute(array, ('dp', 'fsdp'), [(at, at ^ mask) for at in range(devi...  12.4 us
    pallas_call x5, Pallas kernels, call(): pl.pallas_call(kernel, out_shape=out_shape, in_specs=in_specs, out_specs=...  8.89 us
    ppermute x3, starting transfers between devices, climb(): return lax.ppermute(array, ('dp', 'fsdp'), pairs)  7.14 us
    unnamed x28, local copies, waits for them, and re-layouts  5.58 us
    all_to_all x1, starting transfers between devices, shards(): lax.all_to_all(send, 'dp', split_axis=0, concat_axis=0, tiled=True)  4.95 us
  transfers between devices with their start and end apart: 17, of which 10 were waited for; matrix products, arithmetic and copies ran while one was open for 1% of the time, Pallas kernels for 5%

profile of v2, /device:TPU:0, one launch (start us, length us, event | category | flops | bytes accessed | tf_op | source)
XLA Modules:
  0.0 90.3 jit_solution(12323540578760864214)
XLA Ops:
  0.0 1.0 %copy-done.1 = bf16[48,3072]{1,0:T(8,128)(2,1)S(1)} copy-done((bf16[48,3072]{1,0:T(8,128)(2,1)S(1)}, bf16[48,3072]{1,0:T(8,128)(2,1)}, u32[]{:S(2)}) %copy-start.1) | copy-done | bytes 294936
  1.2 3.0 %collective-permute-start = (bf16[48,768]{1,0:T(8,128)(2,1)S(1)}, bf16[48,768]{1,0:T(8,128)(2,1)S(1)}, u32[]{:S(2)}, u32[]{:S(2)}) collective-permute-start(bf16[48,768]{1,0:T(8,128)(2,1)S(1)} %get-tuple-element.23), channel_id=1, source_target_pairs={{0,2},{1,3},{2,0},{3,1},{4,6},{5,7},{6,4},{7,5},{8,10},{9,11},{10,... | collective-permute-start | bytes 221192 | tf_op jit(solution)/shard_map/ppermute | solution.py:204
  4.2 1.5 %collective-permute-start.1 = (bf16[48,768]{1,0:T(8,128)(2,1)S(1)}, bf16[48,768]{1,0:T(8,128)(2,1)S(1)}, u32[]{:S(2)}, u32[]{:S(2)}) collective-permute-start(bf16[48,768]{1,0:T(8,128)(2,1)S(1)} %get-tuple-element.24), channel_id=1, source_target_pairs={{0,4},{1,5},{2,6},{3,7},{4,0},{5,1},{6,2},{7,3},{8,12},{9,13},{10,... | collective-permute-start | bytes 221192 | tf_op jit(solution)/shard_map/ppermute | solution.py:204
  5.7 0.7 copy-done.7
  6.5 0.6 copy-done.8
  7.2 1.1 %copy-done = bf16[1,6,32,1536]{3,2,1,0:T(8,128)(2,1)S(1)} copy-done((bf16[1,6,32,1536]{3,2,1,0:T(8,128)(2,1)S(1)}, bf16[1,6,32,1536]{3,2,1,0:T(8,128)(2,1)}, u32[]{:S(2)}) %copy-start) | copy-done | bytes 589848
  8.2 1.7 %shard_map.102 = bf16[8,32,1536]{2,1,0:T(8,128)(2,1)} custom-call(s32[1]{0:T(128)} %bitcast.place, s32[8,6]{1,0:T(8,128)S(1)} %bitcast.21, s32[8,6]{1,0:T(8,128)S(1)} %bitcast.23, bf16[6,32,1536]{2,1,0:T(8,128)(2,1)S(1)} %bitcast.20), custom_call_target="tpu_custom_call" | custom-call | bytes 1376644 | tf_op jit(solution)/shard_map/pallas_call | solution.py:20
  10.0 0.9 %collective-permute-done.2 = bf16[48,768]{1,0:T(8,128)(2,1)S(1)} collective-permute-done((bf16[48,768]{1,0:T(8,128)(2,1)S(1)}, bf16[48,768]{1,0:T(8,128)(2,1)S(1)}, u32[]{:S(2)}, u32[]{:S(2)}) %collective-permute-start.2) | collective-permute-done | bytes 73760 | tf_op jit(solution)/shard_map/ppermute | solution.py:204
  11.0 2.0 %collective-permute-start.6 = (bf16[6,48,768]{2,1,0:T(8,128)(2,1)S(1)}, bf16[6,48,768]{2,1,0:T(8,128)(2,1)S(1)}, u32[]{:S(2)}, u32[]{:S(2)}) collective-permute-start(bf16[6,48,768]{2,1,0:T(8,128)(2,1)S(1)} %bitcast_dynamic-update-slice_fusion.refs_4_), channel_id=1, source_target_pairs={{0,8},{1,9},{2,10},{3,11},{4,12},{5,13},{6,14},{7,15},{8,16},{9,17... | collective-permute-start | bytes 1327112 | tf_op jit(solution)/shard_map/ppermute | solution.py:208
  13.0 5.0 %all-to-all-start = ((bf16[8,32,1536]{2,1,0:T(8,128)(2,1)}), bf16[8,32,1536]{2,1,0:T(8,128)(2,1)S(1)}, u32[]{:S(2)}, u32[]{:S(2)}) async-start(bf16[8,32,1536]{2,1,0:T(8,128)(2,1)} %shard_map.102), calls=%async_computation | async-start | bytes 1572864 | tf_op jit(solution)/shard_map/all_to_all | solution.py:242
  18.0 8.2 %collective-permute-done.6.refs_5_ = bf16[6,48,768]{2,1,0:T(8,128)(2,1)S(1)} collective-permute-done((bf16[6,48,768]{2,1,0:T(8,128)(2,1)S(1)}, bf16[6,48,768]{2,1,0:T(8,128)(2,1)S(1)}, u32[]{:S(2)}, u32[]{:S(2)}) %collective-permute-start.6) | collective-permute-done | bytes 442400 | tf_op jit(solution)/shard_map/ppermute | solution.py:208
  26.2 2.2 %collective-permute-start.7 = (bf16[6,48,768]{2,1,0:T(8,128)(2,1)S(1)}, bf16[6,48,768]{2,1,0:T(8,128)(2,1)S(1)}, u32[]{:S(2)}, u32[]{:S(2)}) collective-permute-start(bf16[6,48,768]{2,1,0:T(8,128)(2,1)S(1)} %collective-permute-done.6.refs_5_), channel_id=1, source_target_pairs={{0,8},{1,9},{2,10},{3,11},{4,12},{5,13},{6,14},{7,15},{8,16},{9,17... | collective-permute-start | bytes 1327112 | tf_op jit(solution)/shard_map/ppermute | solution.py:208
  28.4 18.2 %collective-permute-done.7.refs_6_ = bf16[6,48,768]{2,1,0:T(8,128)(2,1)S(1)} collective-permute-done((bf16[6,48,768]{2,1,0:T(8,128)(2,1)S(1)}, bf16[6,48,768]{2,1,0:T(8,128)(2,1)S(1)}, u32[]{:S(2)}, u32[]{:S(2)}) %collective-permute-start.7) | collective-permute-done | bytes 442400 | tf_op jit(solution)/shard_map/ppermute | solution.py:208
  46.6 2.9 %collective-permute-start.8 = (bf16[6,48,768]{2,1,0:T(8,128)(2,1)S(1)}, bf16[6,48,768]{2,1,0:T(8,128)(2,1)S(1)}, u32[]{:S(2)}, u32[]{:S(2)}) collective-permute-start(bf16[6,48,768]{2,1,0:T(8,128)(2,1)S(1)} %collective-permute-done.7.refs_6_), channel_id=1, source_target_pairs={{0,8},{1,9},{2,10},{3,11},{4,12},{5,13},{6,14},{7,15},{8,16},{9,17... | collective-permute-start | bytes 1327112 | tf_op jit(solution)/shard_map/ppermute | solution.py:208
  49.6 0.6 copy-done.4
  50.2 0.7 copy-done.5
  50.9 0.7 copy-done.6
  51.6 1.9 %shard_map.100 = (s32[2]{0:T(128)S(1)}, s32[2]{0:T(128)S(1)}, f32[33,384]{1,0:T(8,128)S(1)}) custom-call(s32[1]{0:T(128)} %bitcast.place, s32[1]{0:T(128)} %bitcast.1.chip, s32[8,6]{1,0:T(8,128)S(1)} %bitcast.22, s32[8,6]{1,0:T(8,128)S(1)} %bitcast.24, s32[8,6]{1,0:T(8,128)S(1)} %bitcast.25, f32[31,1536]{1,0:T(8,128)S(1)} %copy-done.2, ...), custom_call_target="tpu_custom_call" | custom-call | bytes 254040 | tf_op jit(solution)/shard_map/pallas_call | solution.py:20
  54.3 4.6 %collective-permute-done.8.refs_7_ = bf16[6,48,768]{2,1,0:T(8,128)(2,1)S(1)} collective-permute-done((bf16[6,48,768]{2,1,0:T(8,128)(2,1)S(1)}, bf16[6,48,768]{2,1,0:T(8,128)(2,1)S(1)}, u32[]{:S(2)}, u32[]{:S(2)}) %collective-permute-start.8) | collective-permute-done | bytes 442400 | tf_op jit(solution)/shard_map/ppermute | solution.py:208
  59.0 1.2 %all-to-all-done.arrived = bf16[8,32,1536]{2,1,0:T(8,128)(2,1)S(1)} async-done(((bf16[8,32,1536]{2,1,0:T(8,128)(2,1)}), bf16[8,32,1536]{2,1,0:T(8,128)(2,1)S(1)}, u32[]{:S(2)}, u32[]{:S(2)}) %all-to-all-start) | async-done | bytes 786464 | tf_op jit(solution)/shard_map/all_to_all | solution.py:242
  60.2 0.8 shard_map.103
  61.0 2.6 %collective-permute-start.5 = (bf16[2,32,1536]{2,1,0:T(8,128)(2,1)S(1)}, bf16[2,32,1536]{2,1,0:T(8,128)(2,1)S(1)}, u32[]{:S(2)}, u32[]{:S(2)}) collective-permute-start(bf16[2,32,1536]{2,1,0:T(8,128)(2,1)S(1)} %get-tuple-element.29.refs_0_), channel_id=1, source_target_pairs={{0,6},{1,7},{2,4},{3,5},{4,2},{5,3},{6,0},{7,1},{8,14},{9,15},{10,... | collective-permute-start | bytes 589832 | tf_op jit(solution)/shard_map/ppermute | solution.py:204
  64.0 0.5 collective-permute-start.3
  64.6 5.1 %collective-permute-done.5.refs_3_ = bf16[2,32,1536]{2,1,0:T(8,128)(2,1)S(1)} collective-permute-done((bf16[2,32,1536]{2,1,0:T(8,128)(2,1)S(1)}, bf16[2,32,1536]{2,1,0:T(8,128)(2,1)S(1)}, u32[]{:S(2)}, u32[]{:S(2)}) %collective-permute-start.5) | collective-permute-done | bytes 196640 | tf_op jit(solution)/shard_map/ppermute | solution.py:204
  69.7 3.2 %collective-permute-done.4.refs_2_ = bf16[2,32,1536]{2,1,0:T(8,128)(2,1)S(1)} collective-permute-done((bf16[2,32,1536]{2,1,0:T(8,128)(2,1)S(1)}, bf16[2,32,1536]{2,1,0:T(8,128)(2,1)S(1)}, u32[]{:S(2)}, u32[]{:S(2)}) %collective-permute-start.4) | collective-permute-done | bytes 196640 | tf_op jit(solution)/shard_map/ppermute | solution.py:204
  73.1 4.2 %shard_map.104 = (f32[2,32,1536]{2,1,0:T(8,128)S(1)}, bf16[2,32,1536]{2,1,0:T(8,128)(2,1)S(1)}, bf16[2,32,1536]{2,1,0:T(8,128)(2,1)S(1)}, bf16[2,32,1536]{2,1,0:T(8,128)(2,1)S(1)}) custom-call(s32[8,5]{1,0:T(8,128)S(1)} %pad_add_fusion.where, bf16[2,32,1536]{2,1,0:T(8,128)(2,1)S(1)} %get-tuple-element.27.kept, f32[33,384]{1,0:T(8,128)S(1)} %get-tuple-element.28.table, ...), custom_call_target="tpu_custom_call" | custom-call | flops 905969664 | bytes 10471072 | tf_op jit(solution)/shard_map/pallas_call | solution.py:20
  77.3 1.6 %collective-permute-start.13 = (bf16[2,32,1536]{2,1,0:T(8,128)(2,1)S(1)}, bf16[2,32,1536]{2,1,0:T(8,128)(2,1)S(1)}, u32[]{:S(2)}, u32[]{:S(2)}) collective-permute-start(bf16[2,32,1536]{2,1,0:T(8,128)(2,1)S(1)} %get-tuple-element.32), channel_id=1, source_target_pairs={{0,2},{1,3},{2,0},{3,1},{4,6},{5,7},{6,4},{7,5},{8,10},{9,11},{10,... | collective-permute-start | bytes 589832 | tf_op jit(solution)/shard_map/ppermute | solution.py:204
  78.9 0.7 collective-permute-start.14
  79.6 1.3 %collective-permute-start.15 = (bf16[2,32,1536]{2,1,0:T(8,128)(2,1)S(1)}, bf16[2,32,1536]{2,1,0:T(8,128)(2,1)S(1)}, u32[]{:S(2)}, u32[]{:S(2)}) collective-permute-start(bf16[2,32,1536]{2,1,0:T(8,128)(2,1)S(1)} %get-tuple-element.34), channel_id=1, source_target_pairs={{0,6},{1,7},{2,4},{3,5},{4,2},{5,3},{6,0},{7,1},{8,14},{9,15},{10,... | collective-permute-start | bytes 589832 | tf_op jit(solution)/shard_map/ppermute | solution.py:204
  81.0 4.2 %collective-permute-done.13 = bf16[2,32,1536]{2,1,0:T(8,128)(2,1)S(1)} collective-permute-done((bf16[2,32,1536]{2,1,0:T(8,128)(2,1)S(1)}, bf16[2,32,1536]{2,1,0:T(8,128)(2,1)S(1)}, u32[]{:S(2)}, u32[]{:S(2)}) %collective-permute-start.13) | collective-permute-done | bytes 196640 | tf_op jit(solution)/shard_map/ppermute | solution.py:204
  85.2 4.3 %collective-permute-done.14 = bf16[2,32,1536]{2,1,0:T(8,128)(2,1)S(1)} collective-permute-done((bf16[2,32,1536]{2,1,0:T(8,128)(2,1)S(1)}, bf16[2,32,1536]{2,1,0:T(8,128)(2,1)S(1)}, u32[]{:S(2)}, u32[]{:S(2)}) %collective-permute-start.14) | collective-permute-done | bytes 196640 | tf_op jit(solution)/shard_map/ppermute | solution.py:204
  89.5 0.8 fusion
  (46 shorter events, 2.1 us)
Async XLA Ops:
  0.0 1.0 %copy-start.1 = (bf16[48,3072]{1,0:T(8,128)(2,1)S(1)}, bf16[48,3072]{1,0:T(8,128)(2,1)}, u32[]{:S(2)}) copy-start(bf16[48,3072]{1,0:T(8,128)(2,1)} %weights.1) | copy-start | bytes 884740
  1.2 8.8 %collective-permute-start = (bf16[48,768]{1,0:T(8,128)(2,1)S(1)}, bf16[48,768]{1,0:T(8,128)(2,1)S(1)}, u32[]{:S(2)}, u32[]{:S(2)}) collective-permute-start(bf16[48,768]{1,0:T(8,128)(2,1)S(1)} %get-tuple-element.23), channel_id=1, source_target_pairs={{0,2},{1,3},{2,0},{3,1},{4,6},{5,7},{6,4},{7,5},{8,10},{9,11},{10,... | collective-permute-start | bytes 221192 | tf_op jit(solution)/shard_map/ppermute | solution.py:204
  4.2 5.8 %collective-permute-start.1 = (bf16[48,768]{1,0:T(8,128)(2,1)S(1)}, bf16[48,768]{1,0:T(8,128)(2,1)S(1)}, u32[]{:S(2)}, u32[]{:S(2)}) collective-permute-start(bf16[48,768]{1,0:T(8,128)(2,1)S(1)} %get-tuple-element.24), channel_id=1, source_target_pairs={{0,4},{1,5},{2,6},{3,7},{4,0},{5,1},{6,2},{7,3},{8,12},{9,13},{10,... | collective-permute-start | bytes 221192 | tf_op jit(solution)/shard_map/ppermute | solution.py:204
  5.7 5.3 %collective-permute-start.2 = (bf16[48,768]{1,0:T(8,128)(2,1)S(1)}, bf16[48,768]{1,0:T(8,128)(2,1)S(1)}, u32[]{:S(2)}, u32[]{:S(2)}) collective-permute-start(bf16[48,768]{1,0:T(8,128)(2,1)S(1)} %get-tuple-element.25), channel_id=1, source_target_pairs={{0,6},{1,7},{2,4},{3,5},{4,2},{5,3},{6,0},{7,1},{8,14},{9,15},{10,... | collective-permute-start | bytes 221192 | tf_op jit(solution)/shard_map/ppermute | solution.py:204
  5.7 0.7 copy-start.7
  6.4 0.7 copy-start.8
  7.2 1.1 %copy-start = (bf16[1,6,32,1536]{3,2,1,0:T(8,128)(2,1)S(1)}, bf16[1,6,32,1536]{3,2,1,0:T(8,128)(2,1)}, u32[]{:S(2)}) copy-start(bf16[1,6,32,1536]{3,2,1,0:T(8,128)(2,1)} %param.10) | copy-start | bytes 1769476
  10.0 1.0 %copy-start.3 = (bf16[48,1536]{1,0:T(8,128)(2,1)S(1)}, bf16[48,1536]{1,0:T(8,128)(2,1)}, u32[]{:S(2)}) copy-start(bf16[48,1536]{1,0:T(8,128)(2,1)} %param.16) | copy-start | bytes 442372
  11.0 15.2 %collective-permute-start.6 = (bf16[6,48,768]{2,1,0:T(8,128)(2,1)S(1)}, bf16[6,48,768]{2,1,0:T(8,128)(2,1)S(1)}, u32[]{:S(2)}, u32[]{:S(2)}) collective-permute-start(bf16[6,48,768]{2,1,0:T(8,128)(2,1)S(1)} %bitcast_dynamic-update-slice_fusion.refs_4_), channel_id=1, source_target_pairs={{0,8},{1,9},{2,10},{3,11},{4,12},{5,13},{6,14},{7,15},{8,16},{9,17... | collective-permute-start | bytes 1327112 | tf_op jit(solution)/shard_map/ppermute | solution.py:208
  13.0 36.5 %copy-start.9 = (s32[1,8,6]{1,0,2:T(1,128)S(1)}, s32[1,8,6]{1,0,2:T(1,128)}, u32[]{:S(2)}) copy-start(s32[1,8,6]{1,0,2:T(1,128)} %param.19) | copy-start | bytes 580
  13.0 38.6 %copy-start.2 = (f32[31,1536]{1,0:T(8,128)S(1)}, f32[31,1536]{1,0:T(8,128)}, u32[]{:S(2)}) copy-start(f32[31,1536]{1,0:T(8,128)} %taps.1) | copy-start | bytes 571396
  13.0 47.2 %all-to-all-start = ((bf16[8,32,1536]{2,1,0:T(8,128)(2,1)}), bf16[8,32,1536]{2,1,0:T(8,128)(2,1)S(1)}, u32[]{:S(2)}, u32[]{:S(2)}) async-start(bf16[8,32,1536]{2,1,0:T(8,128)(2,1)} %shard_map.102), calls=%async_computation | async-start | bytes 1572864 | tf_op jit(solution)/shard_map/all_to_all | solution.py:242
  26.2 20.4 %collective-permute-start.7 = (bf16[6,48,768]{2,1,0:T(8,128)(2,1)S(1)}, bf16[6,48,768]{2,1,0:T(8,128)(2,1)S(1)}, u32[]{:S(2)}, u32[]{:S(2)}) collective-permute-start(bf16[6,48,768]{2,1,0:T(8,128)(2,1)S(1)} %collective-permute-done.6.refs_5_), channel_id=1, source_target_pairs={{0,8},{1,9},{2,10},{3,11},{4,12},{5,13},{6,14},{7,15},{8,16},{9,17... | collective-permute-start | bytes 1327112 | tf_op jit(solution)/shard_map/ppermute | solution.py:208
  46.6 12.3 %collective-permute-start.8 = (bf16[6,48,768]{2,1,0:T(8,128)(2,1)S(1)}, bf16[6,48,768]{2,1,0:T(8,128)(2,1)S(1)}, u32[]{:S(2)}, u32[]{:S(2)}) collective-permute-start(bf16[6,48,768]{2,1,0:T(8,128)(2,1)S(1)} %collective-permute-done.7.refs_6_), channel_id=1, source_target_pairs={{0,8},{1,9},{2,10},{3,11},{4,12},{5,13},{6,14},{7,15},{8,16},{9,17... | collective-permute-start | bytes 1327112 | tf_op jit(solution)/shard_map/ppermute | solution.py:208
  49.5 0.7 copy-start.4
  50.2 0.7 copy-start.5
  50.9 0.7 copy-start.6
  53.5 10.0 %collective-permute-start.9 = (bf16[6,48,768]{2,1,0:T(8,128)(2,1)S(1)}, bf16[6,48,768]{2,1,0:T(8,128)(2,1)S(1)}, u32[]{:S(2)}, u32[]{:S(2)}) collective-permute-start(bf16[6,48,768]{2,1,0:T(8,128)(2,1)S(1)} %bitcast_dynamic-update-slice_fusion.refs_4_), channel_id=1, source_target_pairs={{0,1},{1,0},{2,3},{3,2},{4,5},{5,4},{6,7},{7,6},{8,9},{9,8},{10,11... | collective-permute-start | bytes 1327112 | tf_op jit(solution)/shard_map/ppermute | solution.py:204
  53.6 10.4 %collective-permute-start.10 = (bf16[6,48,768]{2,1,0:T(8,128)(2,1)S(1)}, bf16[6,48,768]{2,1,0:T(8,128)(2,1)S(1)}, u32[]{:S(2)}, u32[]{:S(2)}) collective-permute-start(bf16[6,48,768]{2,1,0:T(8,128)(2,1)S(1)} %collective-permute-done.6.refs_5_), channel_id=1, source_target_pairs={{0,1},{1,0},{2,3},{3,2},{4,5},{5,4},{6,7},{7,6},{8,9},{9,8},{10,11... | collective-permute-start | bytes 1327112 | tf_op jit(solution)/shard_map/ppermute | solution.py:204
  54.1 10.5 %collective-permute-start.11 = (bf16[6,48,768]{2,1,0:T(8,128)(2,1)S(1)}, bf16[6,48,768]{2,1,0:T(8,128)(2,1)}, u32[]{:S(2)}, u32[]{:S(2)}) collective-permute-start(bf16[6,48,768]{2,1,0:T(8,128)(2,1)S(1)} %collective-permute-done.7.refs_6_), channel_id=1, source_target_pairs={{0,1},{1,0},{2,3},{3,2},{4,5},{5,4},{6,7},{7,6},{8,9},{9,8},{10,11... | collective-permute-start | bytes 1327112 | tf_op jit(solution)/shard_map/ppermute | solution.py:204
  58.9 14.2 %collective-permute-start.12 = (bf16[6,48,768]{2,1,0:T(8,128)(2,1)S(1)}, bf16[6,48,768]{2,1,0:T(8,128)(2,1)}, u32[]{:S(2)}, u32[]{:S(2)}) collective-permute-start(bf16[6,48,768]{2,1,0:T(8,128)(2,1)S(1)} %collective-permute-done.8.refs_7_), channel_id=1, source_target_pairs={{0,1},{1,0},{2,3},{3,2},{4,5},{5,4},{6,7},{7,6},{8,9},{9,8},{10,11... | collective-permute-start | bytes 1327112 | tf_op jit(solution)/shard_map/ppermute | solution.py:204
  61.0 8.8 %collective-permute-start.5 = (bf16[2,32,1536]{2,1,0:T(8,128)(2,1)S(1)}, bf16[2,32,1536]{2,1,0:T(8,128)(2,1)S(1)}, u32[]{:S(2)}, u32[]{:S(2)}) collective-permute-start(bf16[2,32,1536]{2,1,0:T(8,128)(2,1)S(1)} %get-tuple-element.29.refs_0_), channel_id=1, source_target_pairs={{0,6},{1,7},{2,4},{3,5},{4,2},{5,3},{6,0},{7,1},{8,14},{9,15},{10,... | collective-permute-start | bytes 589832 | tf_op jit(solution)/shard_map/ppermute | solution.py:204
  63.5 9.4 %collective-permute-start.4 = (bf16[2,32,1536]{2,1,0:T(8,128)(2,1)S(1)}, bf16[2,32,1536]{2,1,0:T(8,128)(2,1)S(1)}, u32[]{:S(2)}, u32[]{:S(2)}) collective-permute-start(bf16[2,32,1536]{2,1,0:T(8,128)(2,1)S(1)} %get-tuple-element.29.refs_0_), channel_id=1, source_target_pairs={{0,4},{1,5},{2,6},{3,7},{4,0},{5,1},{6,2},{7,3},{8,12},{9,13},{10,... | collective-permute-start | bytes 589832 | tf_op jit(solution)/shard_map/ppermute | solution.py:204
  64.0 9.1 %collective-permute-start.3 = (bf16[2,32,1536]{2,1,0:T(8,128)(2,1)S(1)}, bf16[2,32,1536]{2,1,0:T(8,128)(2,1)S(1)}, u32[]{:S(2)}, u32[]{:S(2)}) collective-permute-start(bf16[2,32,1536]{2,1,0:T(8,128)(2,1)S(1)} %get-tuple-element.29.refs_0_), channel_id=1, source_target_pairs={{0,2},{1,3},{2,0},{3,1},{4,6},{5,7},{6,4},{7,5},{8,10},{9,11},{10,... | collective-permute-start | bytes 589832 | tf_op jit(solution)/shard_map/ppermute | solution.py:204
  77.3 7.9 %collective-permute-start.13 = (bf16[2,32,1536]{2,1,0:T(8,128)(2,1)S(1)}, bf16[2,32,1536]{2,1,0:T(8,128)(2,1)S(1)}, u32[]{:S(2)}, u32[]{:S(2)}) collective-permute-start(bf16[2,32,1536]{2,1,0:T(8,128)(2,1)S(1)} %get-tuple-element.32), channel_id=1, source_target_pairs={{0,2},{1,3},{2,0},{3,1},{4,6},{5,7},{6,4},{7,5},{8,10},{9,11},{10,... | collective-permute-start | bytes 589832 | tf_op jit(solution)/shard_map/ppermute | solution.py:204
  78.9 10.6 %collective-permute-start.14 = (bf16[2,32,1536]{2,1,0:T(8,128)(2,1)S(1)}, bf16[2,32,1536]{2,1,0:T(8,128)(2,1)S(1)}, u32[]{:S(2)}, u32[]{:S(2)}) collective-permute-start(bf16[2,32,1536]{2,1,0:T(8,128)(2,1)S(1)} %get-tuple-element.33), channel_id=1, source_target_pairs={{0,4},{1,5},{2,6},{3,7},{4,0},{5,1},{6,2},{7,3},{8,12},{9,13},{10,... | collective-permute-start | bytes 589832 | tf_op jit(solution)/shard_map/ppermute | solution.py:204
  79.6 9.9 %collective-permute-start.15 = (bf16[2,32,1536]{2,1,0:T(8,128)(2,1)S(1)}, bf16[2,32,1536]{2,1,0:T(8,128)(2,1)S(1)}, u32[]{:S(2)}, u32[]{:S(2)}) collective-permute-start(bf16[2,32,1536]{2,1,0:T(8,128)(2,1)S(1)} %get-tuple-element.34), channel_id=1, source_target_pairs={{0,6},{1,7},{2,4},{3,5},{4,2},{5,3},{6,0},{7,1},{8,14},{9,15},{10,... | collective-permute-start | bytes 589832 | tf_op jit(solution)/shard_map/ppermute | solution.py:204

commit v3 on v2

v3 whole, which is shorter than its diff:
```python
import functools
import math

import jax
import jax.numpy as jnp
from jax import lax
from jax.experimental import pallas as pl
from jax.experimental.pallas import tpu as pltpu
from jax.sharding import PartitionSpec as P

QUAD = 4
SMEM = pl.BlockSpec(memory_space=pltpu.SMEM)
VMEM = pl.BlockSpec(memory_space=pltpu.VMEM)
BF16 = jnp.bfloat16
F32 = jnp.float32


def call(kernel, out_shape, in_specs, out_specs, operands, scratch=(), flops=0):
    shapes = list(operands) + list(jax.tree.leaves(out_shape)) + list(scratch)
    total = sum(math.prod(shape.shape) * shape.dtype.itemsize for shape in shapes)
    return pl.pallas_call(
        kernel,
        out_shape=out_shape,
        in_specs=in_specs,
        out_specs=out_specs,
        scratch_shapes=[pltpu.VMEM(shape.shape, shape.dtype) for shape in scratch],
        cost_estimate=pl.CostEstimate(flops=flops, bytes_accessed=total, transcendentals=0),
        compiler_params=pltpu.CompilerParams(
            vmem_limit_bytes=min(total + total // 2 + 4 * 2**20, 60 * 2**20)
        ),
    )(*operands)


def like(dtype, *shape):
    return jax.ShapeDtypeStruct(shape, dtype)


def send_kernel(place, tab_len, tab_dest, frames, *outs):
    me = place[0]
    for number, out in enumerate(outs):
        for far in range(out.shape[0]):
            target = jnp.bitwise_xor(me, far * QUAD + number)
            found = jnp.int32(0)
            for slot in range(frames.shape[0]):
                hit = jnp.logical_and(tab_dest[me, slot] == target, tab_len[me, slot] > 0)
                found = jnp.where(hit, slot, found)
            out[far] = frames[found]


def merge_kernel(place, tab_len, tab_dest, tab_off, *refs):
    arrived, outs = refs[:QUAD], refs[QUAD:]
    me = place[0]
    long = arrived[0].shape[1]
    for far, out in enumerate(outs, 1):
        for number, ref in enumerate(arrived):
            source = jnp.bitwise_xor(me, number)
            target = jnp.bitwise_xor(me, far * QUAD)
            start = jnp.int32(-1)
            for slot in range(tab_len.shape[1]):
                hit = jnp.logical_and(
                    tab_dest[source, slot] == target, tab_len[source, slot] > 0
                )
                start = jnp.where(hit, tab_off[source, slot], start)

            @pl.when(start >= 0)
            def _():
                out[start // long] = ref[far]


def table_kernel(
    long, highs, place, quad, tab_len, tab_dest, tab_off, taps, scale, shift, sources, lens, table
):
    source_count, slots = tab_len.shape
    me = place[0]

    def look(source, carry):
        for slot in range(slots):

            @pl.when(jnp.logical_and(tab_dest[source, slot] == me, tab_len[source, slot] > 0))
            def _():
                number = tab_off[source, slot] // long
                sources[number] = source
                lens[number] = tab_len[source, slot]

        return carry

    lax.fori_loop(0, source_count, look, 0)
    run = scale.shape[1] // (highs * QUAD)
    whole = jnp.concatenate([taps[...], scale[...], shift[...]], axis=0)
    for owner in range(QUAD):

        @pl.when(quad[0] == owner)
        def _():
            starts = [(high * QUAD + owner) * run for high in range(highs)]
            table[...] = jnp.concatenate([whole[:, at : at + run] for at in starts], axis=1)


def norm_kernel(place, sources, lens, gain, *refs):
    near, far, (kept, normed) = refs[:QUAD], refs[QUAD:-2], refs[-2:]
    for number in range(kept.shape[0]):
        shift = jnp.bitwise_xor(sources[number], place[0])
        for other, ref in enumerate(near):

            @pl.when(shift == other)
            def _():
                kept[number] = ref[0]

        for other, ref in enumerate(far, 1):

            @pl.when(shift // QUAD == other)
            def _():
                kept[number] = ref[number]

        wide = kept[number].astype(F32)
        mean = jnp.mean(wide, axis=1, keepdims=True)
        centred = wide - mean
        var = jnp.mean(centred * centred, axis=1, keepdims=True)
        value = centred * lax.rsqrt(var + 1e-05) * gain[...]
        steps = lax.broadcasted_iota(jnp.int32, value.shape, 0)
        normed[number] = jnp.where(steps < lens[number], value, 0.0).astype(BF16)


def split_kernel(highs, quad, weights, *refs):
    outs, buf = refs[:-1], refs[-1]
    width = weights.shape[1] // 2
    run = width // (highs * QUAD)
    for owner in range(QUAD):
        parts = [
            weights[:, pl.ds(half * width + (high * QUAD + owner) * run, run)]
            for half in range(2)
            for high in range(highs)
        ]
        buf[owner] = jnp.concatenate(parts, axis=1)
    for number, out in enumerate(outs):
        out[...] = buf[jnp.bitwise_xor(quad[0], number)]


def conv_rows(block, taps):
    long, chans = block.shape
    count = taps.shape[0]
    front = (count - 1) // 2
    groups = long // 8
    pieces = [block[8 * at : 8 * at + 8, :] for at in range(groups)]
    total = None
    for residue in range(8):
        rows = []
        for at in range(groups + 1):
            value = None
            for step in range(-(count // 8) - 1, count // 8 + 2):
                tap = 8 * step + residue + front - 16
                source = at + step - 2
                if 0 <= tap < count and 0 <= source < groups:
                    term = pieces[source] * taps[tap : tap + 1, :]
                    value = term if value is None else value + term
            rows.append(jnp.zeros((8, chans), F32) if value is None else value)
        whole = jnp.concatenate(rows, axis=0)[residue : residue + long, :]
        total = whole if total is None else total + whole
    return total


def main_kernel(pieces, where, kept, table, *refs):
    normed, weights = refs[:QUAD], refs[QUAD : QUAD + pieces]
    own, outs = refs[QUAD + pieces], refs[QUAD + pieces + 1 : 2 * QUAD + pieces]
    rows_buf, in_buf, out_buf, glu_buf, act_buf = refs[2 * QUAD + pieces :]
    recv, long, width = kept.shape
    tall = recv * long
    chans = table.shape[1]
    taps = table[: table.shape[0] - 2, :]
    scale, shift = table[table.shape[0] - 2 : table.shape[0] - 1, :], table[table.shape[0] - 1 :, :]
    for number, ref in enumerate(normed):
        rows_buf[pl.ds(number * tall, tall), :] = ref[...].reshape(tall, width)
    if pieces == 2:
        w_in, w_out = weights
    else:
        w_in, w_out = in_buf, out_buf
        depth, wide = weights[0].shape[1:]
        for number, ref in enumerate(weights):
            for inner in range(QUAD):
                start = pl.multiple_of(where[number, inner] * depth, 16)
                in_buf[pl.ds(start, depth), :] = ref[inner]
            start = pl.multiple_of(where[number, QUAD] * depth, 16)
            for half in range(width // wide):
                out_buf[pl.ds(start, depth), half * wide : half * wide + wide] = ref[QUAD + half]
    glu_in = jnp.dot(rows_buf[...], w_in[...], preferred_element_type=F32)
    glu_buf[...] = glu_in[:, :chans] * jax.nn.sigmoid(glu_in[:, chans:])

    def utterance(at, carry):
        start = pl.multiple_of(at * long, long)
        moved = conv_rows(glu_buf[pl.ds(start, long), :], taps) * scale + shift
        act_buf[pl.ds(start, long), :] = (moved * jax.nn.sigmoid(moved)).astype(BF16)
        return carry

    lax.fori_loop(0, QUAD * recv, utterance, 0)
    mixed = jnp.dot(act_buf[...], w_out[...], preferred_element_type=F32)
    mixed = mixed.reshape(QUAD, recv, long, width)
    own[...] = kept[...].astype(F32) + mixed[0]
    for number, out in enumerate(outs, 1):
        out[...] = mixed[number].astype(BF16)


def shards(
    frames, ln_gain, w_in, depth_kernel, bn_scale, bn_shift, w_out, lengths, destinations, offsets
):
    dp_count, fsdp_count = lax.axis_size("dp"), lax.axis_size("fsdp")
    devices = dp_count * fsdp_count
    highs = dp_count // QUAD
    dp_index = lax.axis_index("dp")
    quad = dp_index % QUAD
    line = dp_index // QUAD * fsdp_count + lax.axis_index("fsdp")
    slots = lengths.shape[2]
    recv = slots // 3
    _, _, long, width = frames.shape
    depth = w_in.shape[0]
    chans = width // QUAD
    wide = 2 * chans
    taps = depth_kernel.shape[0]

    def swap(array, high=0, quad=0, fsdp=0):
        mask = (high * QUAD + quad) * fsdp_count + fsdp
        return lax.ppermute(array, ("dp", "fsdp"), [(at, at ^ mask) for at in range(devices)])

    def quad_swap(arrays):
        return [arrays[0]] + [swap(arrays[mask], quad=mask) for mask in range(1, QUAD)]

    place = dp_index.astype(jnp.int32)[None]
    quad_place = quad.astype(jnp.int32)[None]
    tab_len, tab_dest, tab_off = lengths[0], destinations[0], offsets[0]

    if depth % 16 == 0:
        split = call(
            functools.partial(split_kernel, highs),
            [like(BF16, depth, wide)] * QUAD,
            [SMEM, VMEM],
            [VMEM] * QUAD,
            (quad_place, w_in),
            [like(BF16, QUAD, depth, wide)],
        )
    else:
        by_owner = w_in.reshape(depth, 2, highs, QUAD, chans // highs).transpose(3, 0, 1, 2, 4)
        by_owner = by_owner.reshape(QUAD, depth, wide)
        split = [
            lax.dynamic_index_in_dim(by_owner, quad ^ mask, 0, keepdims=False)
            for mask in range(QUAD)
        ]
    halves = [w_out[:, at : at + wide] for at in range(0, width, wide)]
    pieces = [jnp.stack(quad_swap(split) + halves)]
    shifts = [0]
    bits = [1 << at for at in range((highs * fsdp_count).bit_length() - 1)]
    high_bits = [bit for bit in reversed(bits) if bit >= fsdp_count]
    chip_bits = [bit for bit in reversed(bits) if 1 < bit < fsdp_count]
    for bit in high_bits:
        pieces = pieces + [swap(part, high=bit // fsdp_count) for part in pieces]
        shifts = shifts + [shift ^ bit for shift in shifts]

    near = call(
        send_kernel,
        [like(BF16, highs, long, width)] * QUAD,
        [SMEM, SMEM, SMEM, VMEM],
        [VMEM] * QUAD,
        (place, tab_len, tab_dest, frames[0]),
    )
    near = quad_swap(near)
    utts = like(BF16, recv, long, width)
    far = call(
        merge_kernel,
        [utts] * (highs - 1),
        [SMEM] * 4 + [VMEM] * QUAD,
        [VMEM] * (highs - 1),
        (place, tab_len, tab_dest, tab_off, *near),
    )
    far = [swap(part, high=mask) for mask, part in enumerate(far, 1)]
    pieces[1:], _ = lax.optimization_barrier((pieces[1:], far))
    chip_first = [swap(pieces[0], fsdp=bit) for bit in chip_bits[:1]]
    early = [swap(part, fsdp=1) for part in pieces[:1] + chip_first]
    far, _ = lax.optimization_barrier((far, early))
    sources, lens, table = call(
        functools.partial(table_kernel, long, highs),
        [like(jnp.int32, recv), like(jnp.int32, recv), like(F32, taps + 2, chans)],
        [SMEM] * 5 + [VMEM] * 3,
        [SMEM, SMEM, VMEM],
        (place, quad_place, tab_len, tab_dest, tab_off)
        + (depth_kernel, bn_scale[None], bn_shift[None]),
    )
    kept, normed = call(
        norm_kernel,
        [utts, utts],
        [SMEM] * 3 + [VMEM] * (QUAD + highs),
        [VMEM, VMEM],
        (place, sources, lens, ln_gain[None], *near, *far),
    )
    for bit in chip_bits:
        first = chip_first if bit == chip_bits[0] else []
        pieces = pieces + first + [swap(part, fsdp=bit) for part in pieces[len(first) :]]
        shifts = shifts + [shift ^ bit for shift in shifts]
    ends = len(shifts) // 2 + 1
    normed = quad_swap([normed] * QUAD)
    pieces[ends:], _ = lax.optimization_barrier((pieces[ends:], normed[1]))
    cored = [swap(part, fsdp=1) for part in pieces]
    cored[0], cored[len(shifts) // 2] = early[0], early[-1]
    pieces = pieces + cored
    shifts = shifts + [shift ^ 1 for shift in shifts]
    out_rows = line ^ jnp.array(shifts)
    in_rows = out_rows // fsdp_count * QUAD
    in_rows = in_rows[:, None] + (quad ^ jnp.arange(QUAD))[None, :]
    in_rows = in_rows * fsdp_count + (out_rows % fsdp_count)[:, None]
    where = jnp.concatenate([in_rows, out_rows[:, None]], 1).astype(jnp.int32)
    if depth % 16:
        together = jnp.stack(pieces)
        flat = together[:, :QUAD].reshape(-1, depth, wide)
        all_in = jnp.zeros_like(flat).at[where[:, :QUAD].reshape(-1)].set(flat)
        flat = together[:, QUAD:].transpose(0, 2, 1, 3).reshape(-1, depth, width)
        all_out = jnp.zeros_like(flat).at[where[:, QUAD]].set(flat)
        pieces = [all_in.reshape(width, wide), all_out.reshape(chans, width)]

    tall = QUAD * recv * long
    partial_sums = call(
        functools.partial(main_kernel, len(pieces)),
        [like(F32, recv, long, width)] + [utts] * (QUAD - 1),
        [SMEM] + [VMEM] * (2 + QUAD + len(pieces)),
        [VMEM] * QUAD,
        (where, kept, table, *normed, *pieces),
        [
            like(BF16, tall, width),
            like(BF16, width, wide),
            like(BF16, chans, width),
            like(F32, tall, chans),
            like(BF16, tall, chans),
        ],
        flops=6 * tall * width * chans,
    )
    own, *others = quad_swap(partial_sums)
    for part in others:
        own = own + part.astype(F32)
    live = jnp.arange(long, dtype=jnp.int32)[None, :, None] < lens[:, None, None]
    return jnp.where(live, own, 0.0).astype(BF16)[None]


def solution(mesh):
    return jax.shard_map(
        shards,
        mesh=mesh,
        in_specs=(
            P("fsdp", "dp", None, None),
            P(),
            P(("dp", "fsdp"), None),
            P(),
            P(),
            P(),
            P(("dp", "fsdp"), None),
            P("fsdp", None, None),
            P("fsdp", None, None),
            P("fsdp", None, None),
        ),
        out_specs=P("fsdp", "dp", None, None),
        check_vma=False,
    )
```

time: 90.7 us -> 84.9 us (0.936)
  starting transfers between devices: 24.5 us -> 19.6 us
  local copies, waits for them, and re-layouts: 5.61 us -> 4.36 us
  Pallas kernels: 8.89 us -> 10.1 us
    ppermute x13 -> x20, waiting for transfers between devices: 17.9 us -> 49.4 us  [swap(): lax.ppermute(array, ('dp', 'fsdp'), [(at, at ^ mask) for at in range(devi...]
    ppermute x3 -> x0, waiting for transfers between devices: 31 us -> none  [climb(): return lax.ppermute(array, ('dp', 'fsdp'), pairs)]
    ppermute x13 -> x20, starting transfers between devices: 12.4 us -> 19.6 us  [swap(): lax.ppermute(array, ('dp', 'fsdp'), [(at, at ^ mask) for at in range(devi...]
    ppermute x3 -> x0, starting transfers between devices: 7.14 us -> none  [climb(): return lax.ppermute(array, ('dp', 'fsdp'), pairs)]
    all_to_all x1 -> x0, starting transfers between devices: 4.95 us -> none  [shards(): lax.all_to_all(send, 'dp', split_axis=0, concat_axis=0, tiled=True)]
    unnamed x28 -> x34, local copies, waits for them, and re-layouts: 5.58 us -> 4.26 us
    pallas_call x5 -> x6, Pallas kernels: 8.89 us -> 10.1 us  [call(): pl.pallas_call(kernel, out_shape=out_shape, in_specs=in_specs, out_specs=...]
    all_to_all x1 -> x0, waiting for transfers between devices: 1.21 us -> none  [shards(): lax.all_to_all(send, 'dp', split_axis=0, concat_axis=0, tiled=True)]
  transfers between devices with their start and end apart: 17 -> 20, of which waited for: 10 -> 14; matrix products, arithmetic and copies ran while one was open for 1% -> 1% of each run, Pallas kernels for 5% -> 7%
where the time goes in v3:
time: 84.9 us; the launch traced here: 84.6 us
  waiting for transfers between devices  49.4 us (58%)
  starting transfers between devices  19.6 us (23%)
  Pallas kernels  10.1 us (12%)
  local copies, waits for them, and re-layouts  4.36 us (5%)
  other arithmetic  1.02 us (1%)
    ppermute x20, waiting for transfers between devices, swap(): lax.ppermute(array, ('dp', 'fsdp'), [(at, at ^ mask) for at in range(devi...  49.4 us
    ppermute x20, starting transfers between devices, swap(): lax.ppermute(array, ('dp', 'fsdp'), [(at, at ^ mask) for at in range(devi...  19.6 us
    pallas_call x6, Pallas kernels, call(): pl.pallas_call(kernel, out_shape=out_shape, in_specs=in_specs, out_specs=...  10.1 us
    unnamed x34, local copies, waits for them, and re-layouts  4.26 us
  transfers between devices with their start and end apart: 20, of which 14 were waited for; matrix products, arithmetic and copies ran while one was open for 1% of the time, Pallas kernels for 7%

profile of v3, /device:TPU:0, one launch (start us, length us, event | category | flops | bytes accessed | tf_op | source)
XLA Modules:
  0.0 84.6 jit_solution(16908598880478773302)
XLA Ops:
  0.0 1.0 %copy-done.1 = bf16[48,3072]{1,0:T(8,128)(2,1)S(1)} copy-done((bf16[48,3072]{1,0:T(8,128)(2,1)S(1)}, bf16[48,3072]{1,0:T(8,128)(2,1)}, u32[]{:S(2)}) %copy-start.1) | copy-done | bytes 294936
  1.1 3.0 %collective-permute-start.4 = (bf16[48,768]{1,0:T(8,128)(2,1)S(1)}, bf16[48,768]{1,0:T(8,128)(2,1)S(1)}, u32[]{:S(2)}, u32[]{:S(2)}) collective-permute-start(bf16[48,768]{1,0:T(8,128)(2,1)S(1)} %get-tuple-element.32), channel_id=1, source_target_pairs={{0,4},{1,5},{2,6},{3,7},{4,0},{5,1},{6,2},{7,3},{8,12},{9,13},{10,... | collective-permute-start | bytes 221192 | tf_op jit(solution)/shard_map/ppermute | solution.py:220
  4.1 1.6 %collective-permute-start.5 = (bf16[48,768]{1,0:T(8,128)(2,1)S(1)}, bf16[48,768]{1,0:T(8,128)(2,1)S(1)}, u32[]{:S(2)}, u32[]{:S(2)}) collective-permute-start(bf16[48,768]{1,0:T(8,128)(2,1)S(1)} %get-tuple-element.33), channel_id=1, source_target_pairs={{0,8},{1,9},{2,10},{3,11},{4,12},{5,13},{6,14},{7,15},{8,0},{9,1},... | collective-permute-start | bytes 221192 | tf_op jit(solution)/shard_map/ppermute | solution.py:220
  5.7 0.7 collective-permute-done.4
  6.5 2.6 %collective-permute-done.5 = bf16[48,768]{1,0:T(8,128)(2,1)S(1)} collective-permute-done((bf16[48,768]{1,0:T(8,128)(2,1)S(1)}, bf16[48,768]{1,0:T(8,128)(2,1)S(1)}, u32[]{:S(2)}, u32[]{:S(2)}) %collective-permute-start.5) | collective-permute-done | bytes 73760 | tf_op jit(solution)/shard_map/ppermute | solution.py:220
  9.1 1.9 %collective-permute-done.6 = bf16[48,768]{1,0:T(8,128)(2,1)S(1)} collective-permute-done((bf16[48,768]{1,0:T(8,128)(2,1)S(1)}, bf16[48,768]{1,0:T(8,128)(2,1)S(1)}, u32[]{:S(2)}, u32[]{:S(2)}) %collective-permute-start.6) | collective-permute-done | bytes 73760 | tf_op jit(solution)/shard_map/ppermute | solution.py:220
  11.0 1.6 %collective-permute-start.8 = (bf16[6,48,768]{2,1,0:T(8,128)(2,1)S(1)}, bf16[6,48,768]{2,1,0:T(8,128)(2,1)S(1)}, u32[]{:S(2)}, u32[]{:S(2)}) collective-permute-start(bf16[6,48,768]{2,1,0:T(8,128)(2,1)S(1)} %bitcast_dynamic-update-slice_fusion.refs_4_), channel_id=1, source_target_pairs={{0,2},{1,3},{2,0},{3,1},{4,6},{5,7},{6,4},{7,5},{8,10},{9,11},{10,... | collective-permute-start | bytes 1327112 | tf_op jit(solution)/shard_map/ppermute | solution.py:220
  12.6 2.6 %collective-permute-start.13 = (bf16[6,48,768]{2,1,0:T(8,128)(2,1)S(1)}, bf16[6,48,768]{2,1,0:T(8,128)(2,1)S(1)}, u32[]{:S(2)}, u32[]{:S(2)}) collective-permute-start(bf16[6,48,768]{2,1,0:T(8,128)(2,1)S(1)} %bitcast_dynamic-update-slice_fusion.refs_4_), channel_id=1, source_target_pairs={{0,16},{1,17},{2,18},{3,19},{4,20},{5,21},{6,22},{7,23},{8,24},{9,... | collective-permute-start | bytes 1327112 | tf_op jit(solution)/shard_map/ppermute | solution.py:220
  15.4 0.8 shard_map.110
  16.7 1.0 %collective-permute-start.1 = (bf16[2,32,1536]{2,1,0:T(8,128)(2,1)S(1)}, bf16[2,32,1536]{2,1,0:T(8,128)(2,1)S(1)}, u32[]{:S(2)}, u32[]{:S(2)}) collective-permute-start(bf16[2,32,1536]{2,1,0:T(8,128)(2,1)S(1)} %get-tuple-element.29), channel_id=1, source_target_pairs={{0,8},{1,9},{2,10},{3,11},{4,12},{5,13},{6,14},{7,15},{8,0},{9,1},... | collective-permute-start | bytes 589832 | tf_op jit(solution)/shard_map/ppermute | solution.py:220
  17.7 2.0 %collective-permute-start.2 = (bf16[2,32,1536]{2,1,0:T(8,128)(2,1)S(1)}, bf16[2,32,1536]{2,1,0:T(8,128)(2,1)S(1)}, u32[]{:S(2)}, u32[]{:S(2)}) collective-permute-start(bf16[2,32,1536]{2,1,0:T(8,128)(2,1)S(1)} %get-tuple-element.30), channel_id=1, source_target_pairs={{0,12},{1,13},{2,14},{3,15},{4,8},{5,9},{6,10},{7,11},{8,4},{9,5},... | collective-permute-start | bytes 589832 | tf_op jit(solution)/shard_map/ppermute | solution.py:220
  19.7 4.2 %collective-permute-done.refs_1_ = bf16[2,32,1536]{2,1,0:T(8,128)(2,1)S(1)} collective-permute-done((bf16[2,32,1536]{2,1,0:T(8,128)(2,1)S(1)}, bf16[2,32,1536]{2,1,0:T(8,128)(2,1)S(1)}, u32[]{:S(2)}, u32[]{:S(2)}) %collective-permute-start) | collective-permute-done | bytes 196640 | tf_op jit(solution)/shard_map/ppermute | solution.py:220
  24.5 4.5 %collective-permute-done.1.refs_2_ = bf16[2,32,1536]{2,1,0:T(8,128)(2,1)S(1)} collective-permute-done((bf16[2,32,1536]{2,1,0:T(8,128)(2,1)S(1)}, bf16[2,32,1536]{2,1,0:T(8,128)(2,1)S(1)}, u32[]{:S(2)}, u32[]{:S(2)}) %collective-permute-start.1) | collective-permute-done | bytes 196640 | tf_op jit(solution)/shard_map/ppermute | solution.py:220
  29.0 7.7 %collective-permute-done.2.refs_3_ = bf16[2,32,1536]{2,1,0:T(8,128)(2,1)S(1)} collective-permute-done((bf16[2,32,1536]{2,1,0:T(8,128)(2,1)S(1)}, bf16[2,32,1536]{2,1,0:T(8,128)(2,1)S(1)}, u32[]{:S(2)}, u32[]{:S(2)}) %collective-permute-start.2) | collective-permute-done | bytes 196640 | tf_op jit(solution)/shard_map/ppermute | solution.py:220
  36.7 0.8 shard_map.111
  38.4 0.7 copy-done.8
  39.1 1.9 %shard_map.109 = (s32[2]{0:T(128)S(1)}, s32[2]{0:T(128)S(1)}, f32[33,384]{1,0:T(8,128)S(1)}) custom-call(s32[1]{0:T(128)} %bitcast.place, s32[1]{0:T(128)} %bitcast.1.quad, s32[8,6]{1,0:T(8,128)S(1)} %bitcast.25, s32[8,6]{1,0:T(8,128)S(1)} %bitcast.28, s32[8,6]{1,0:T(8,128)S(1)} %bitcast.30, f32[31,1536]{1,0:T(8,128)S(1)} %copy-done.4, ...), custom_call_target="tpu_custom_call" | custom-call | bytes 254040 | tf_op jit(solution)/shard_map/pallas_call | solution.py:21
  41.0 4.4 %collective-permute-done.3.refs_4_ = bf16[2,32,1536]{2,1,0:T(8,128)(2,1)} collective-permute-done((bf16[2,32,1536]{2,1,0:T(8,128)(2,1)S(1)}, bf16[2,32,1536]{2,1,0:T(8,128)(2,1)}, u32[]{:S(2)}, u32[]{:S(2)}) %collective-permute-start.3) | collective-permute-done | bytes 196640 | tf_op jit(solution)/shard_map/ppermute | solution.py:220
  46.0 2.1 %shard_map.113 = (bf16[2,32,1536]{2,1,0:T(8,128)(2,1)S(1)}, bf16[2,32,1536]{2,1,0:T(8,128)(2,1)}) custom-call(s32[1]{0:T(128)} %bitcast.place, s32[2]{0:T(128)S(1)} %get-tuple-element.26.sources, s32[2]{0:T(128)S(1)} %get-tuple-element.25.lens, f32[1,1536]{1,0:T(1,128)S(1)} %broadcast_in_dim.44.gain, bf16[2,32,1536]{2,1,0:T(8,128)(2,1)S(1)} %get-tuple-element.27.refs_0_, ...), custom_call_target="tpu_custom_call" | custom-call | bytes 1382420 | tf_op jit(solution)/shard_map/pallas_call | solution.py:21
  49.4 4.4 %collective-permute-done.14.refs_7_ = bf16[6,48,768]{2,1,0:T(8,128)(2,1)S(1)} collective-permute-done((bf16[6,48,768]{2,1,0:T(8,128)(2,1)S(1)}, bf16[6,48,768]{2,1,0:T(8,128)(2,1)S(1)}, u32[]{:S(2)}, u32[]{:S(2)}) %collective-permute-start.14) | collective-permute-done | bytes 442400 | tf_op jit(solution)/shard_map/ppermute | solution.py:220
  53.7 1.0 %collective-permute-done.10.refs_1_ = bf16[2,32,1536]{2,1,0:T(8,128)(2,1)S(1)} collective-permute-done((bf16[2,32,1536]{2,1,0:T(8,128)(2,1)}, bf16[2,32,1536]{2,1,0:T(8,128)(2,1)S(1)}, u32[]{:S(2)}, u32[]{:S(2)}) %collective-permute-start.10) | collective-permute-done | bytes 196640 | tf_op jit(solution)/shard_map/ppermute | solution.py:220
  54.7 2.0 %collective-permute-start.11 = (bf16[2,32,1536]{2,1,0:T(8,128)(2,1)}, bf16[2,32,1536]{2,1,0:T(8,128)(2,1)}, u32[]{:S(2)}, u32[]{:S(2)}) collective-permute-start(bf16[2,32,1536]{2,1,0:T(8,128)(2,1)} %get-tuple-element.38.refs_0_), channel_id=1, source_target_pairs={{0,8},{1,9},{2,10},{3,11},{4,12},{5,13},{6,14},{7,15},{8,0},{9,1},... | collective-permute-start | bytes 589832 | tf_op jit(solution)/shard_map/ppermute | solution.py:220
  56.9 6.7 %collective-permute-done.12.refs_3_ = bf16[2,32,1536]{2,1,0:T(8,128)(2,1)} collective-permute-done((bf16[2,32,1536]{2,1,0:T(8,128)(2,1)}, bf16[2,32,1536]{2,1,0:T(8,128)(2,1)}, u32[]{:S(2)}, u32[]{:S(2)}) %collective-permute-start.12) | collective-permute-done | bytes 196640 | tf_op jit(solution)/shard_map/ppermute | solution.py:220
  63.6 2.9 %collective-permute-done.11.refs_2_ = bf16[2,32,1536]{2,1,0:T(8,128)(2,1)} collective-permute-done((bf16[2,32,1536]{2,1,0:T(8,128)(2,1)}, bf16[2,32,1536]{2,1,0:T(8,128)(2,1)}, u32[]{:S(2)}, u32[]{:S(2)}) %collective-permute-start.11) | collective-permute-done | bytes 196640 | tf_op jit(solution)/shard_map/ppermute | solution.py:220
  66.5 0.9 %copy-done.3 = bf16[2,32,1536]{2,1,0:T(8,128)(2,1)S(1)} copy-done((bf16[2,32,1536]{2,1,0:T(8,128)(2,1)S(1)}, bf16[2,32,1536]{2,1,0:T(8,128)(2,1)}, u32[]{:S(2)}) %copy-start.3) | copy-done | bytes 196632
  67.5 4.4 %shard_map.114 = (f32[2,32,1536]{2,1,0:T(8,128)S(1)}, bf16[2,32,1536]{2,1,0:T(8,128)(2,1)S(1)}, bf16[2,32,1536]{2,1,0:T(8,128)(2,1)S(1)}, bf16[2,32,1536]{2,1,0:T(8,128)(2,1)S(1)}) custom-call(s32[8,5]{1,0:T(8,128)S(1)} %pad_add_fusion.where, bf16[2,32,1536]{2,1,0:T(8,128)(2,1)S(1)} %copy-done.3, f32[33,384]{1,0:T(8,128)S(1)} %get-tuple-element.37.table, ...), custom_call_target="tpu_custom_call" | custom-call | flops 905969664 | bytes 10471072 | tf_op jit(solution)/shard_map/pallas_call | solution.py:21
  71.8 1.5 %collective-permute-start.17 = (bf16[2,32,1536]{2,1,0:T(8,128)(2,1)S(1)}, bf16[2,32,1536]{2,1,0:T(8,128)(2,1)S(1)}, u32[]{:S(2)}, u32[]{:S(2)}) collective-permute-start(bf16[2,32,1536]{2,1,0:T(8,128)(2,1)S(1)} %get-tuple-element.42), channel_id=1, source_target_pairs={{0,4},{1,5},{2,6},{3,7},{4,0},{5,1},{6,2},{7,3},{8,12},{9,13},{10,... | collective-permute-start | bytes 589832 | tf_op jit(solution)/shard_map/ppermute | solution.py:220
  73.4 2.0 %collective-permute-start.19 = (bf16[2,32,1536]{2,1,0:T(8,128)(2,1)S(1)}, bf16[2,32,1536]{2,1,0:T(8,128)(2,1)S(1)}, u32[]{:S(2)}, u32[]{:S(2)}) collective-permute-start(bf16[2,32,1536]{2,1,0:T(8,128)(2,1)S(1)} %get-tuple-element.44), channel_id=1, source_target_pairs={{0,12},{1,13},{2,14},{3,15},{4,8},{5,9},{6,10},{7,11},{8,4},{9,5},... | collective-permute-start | bytes 589832 | tf_op jit(solution)/shard_map/ppermute | solution.py:220
  75.5 3.4 %collective-permute-done.17 = bf16[2,32,1536]{2,1,0:T(8,128)(2,1)S(1)} collective-permute-done((bf16[2,32,1536]{2,1,0:T(8,128)(2,1)S(1)}, bf16[2,32,1536]{2,1,0:T(8,128)(2,1)S(1)}, u32[]{:S(2)}, u32[]{:S(2)}) %collective-permute-start.17) | collective-permute-done | bytes 196640 | tf_op jit(solution)/shard_map/ppermute | solution.py:220
  78.8 2.4 %collective-permute-done.18 = bf16[2,32,1536]{2,1,0:T(8,128)(2,1)S(1)} collective-permute-done((bf16[2,32,1536]{2,1,0:T(8,128)(2,1)S(1)}, bf16[2,32,1536]{2,1,0:T(8,128)(2,1)S(1)}, u32[]{:S(2)}, u32[]{:S(2)}) %collective-permute-start.18) | collective-permute-done | bytes 196640 | tf_op jit(solution)/shard_map/ppermute | solution.py:220
  81.2 2.6 %collective-permute-done.19 = bf16[2,32,1536]{2,1,0:T(8,128)(2,1)S(1)} collective-permute-done((bf16[2,32,1536]{2,1,0:T(8,128)(2,1)S(1)}, bf16[2,32,1536]{2,1,0:T(8,128)(2,1)S(1)}, u32[]{:S(2)}, u32[]{:S(2)}) %collective-permute-start.19) | collective-permute-done | bytes 196640 | tf_op jit(solution)/shard_map/ppermute | solution.py:220
  83.8 0.8 fusion
  (60 shorter events, 4.4 us)
Async XLA Ops:
  0.0 1.0 %copy-start.1 = (bf16[48,3072]{1,0:T(8,128)(2,1)S(1)}, bf16[48,3072]{1,0:T(8,128)(2,1)}, u32[]{:S(2)}) copy-start(bf16[48,3072]{1,0:T(8,128)(2,1)} %weights.1) | copy-start | bytes 884740
  1.0 14.4 %copy-start = (bf16[1,6,32,1536]{3,2,1,0:T(8,128)(2,1)S(1)}, bf16[1,6,32,1536]{3,2,1,0:T(8,128)(2,1)}, u32[]{:S(2)}) copy-start(bf16[1,6,32,1536]{3,2,1,0:T(8,128)(2,1)} %param.11) | copy-start | bytes 1769476
  1.1 5.4 %collective-permute-start.4 = (bf16[48,768]{1,0:T(8,128)(2,1)S(1)}, bf16[48,768]{1,0:T(8,128)(2,1)S(1)}, u32[]{:S(2)}, u32[]{:S(2)}) collective-permute-start(bf16[48,768]{1,0:T(8,128)(2,1)S(1)} %get-tuple-element.32), channel_id=1, source_target_pairs={{0,4},{1,5},{2,6},{3,7},{4,0},{5,1},{6,2},{7,3},{8,12},{9,13},{10,... | collective-permute-start | bytes 221192 | tf_op jit(solution)/shard_map/ppermute | solution.py:220
  4.1 5.0 %collective-permute-start.5 = (bf16[48,768]{1,0:T(8,128)(2,1)S(1)}, bf16[48,768]{1,0:T(8,128)(2,1)S(1)}, u32[]{:S(2)}, u32[]{:S(2)}) collective-permute-start(bf16[48,768]{1,0:T(8,128)(2,1)S(1)} %get-tuple-element.33), channel_id=1, source_target_pairs={{0,8},{1,9},{2,10},{3,11},{4,12},{5,13},{6,14},{7,15},{8,0},{9,1},... | collective-permute-start | bytes 221192 | tf_op jit(solution)/shard_map/ppermute | solution.py:220
  5.7 5.3 %collective-permute-start.6 = (bf16[48,768]{1,0:T(8,128)(2,1)S(1)}, bf16[48,768]{1,0:T(8,128)(2,1)S(1)}, u32[]{:S(2)}, u32[]{:S(2)}) collective-permute-start(bf16[48,768]{1,0:T(8,128)(2,1)S(1)} %get-tuple-element.34), channel_id=1, source_target_pairs={{0,12},{1,13},{2,14},{3,15},{4,8},{5,9},{6,10},{7,11},{8,4},{9,5},... | collective-permute-start | bytes 221192 | tf_op jit(solution)/shard_map/ppermute | solution.py:220
  6.5 4.5 %copy-start.5 = (bf16[48,1536]{1,0:T(8,128)(2,1)S(1)}, bf16[48,1536]{1,0:T(8,128)(2,1)}, u32[]{:S(2)}) copy-start(bf16[48,1536]{1,0:T(8,128)(2,1)} %param.17) | copy-start | bytes 442372
  11.0 4.2 %copy-start.9 = (s32[1,8,6]{1,0,2:T(1,128)S(1)}, s32[1,8,6]{1,0,2:T(1,128)}, u32[]{:S(2)}) copy-start(s32[1,8,6]{1,0,2:T(1,128)} %param.18) | copy-start | bytes 580
  11.0 4.2 %copy-start.10 = (s32[1,8,6]{1,0,2:T(1,128)S(1)}, s32[1,8,6]{1,0,2:T(1,128)}, u32[]{:S(2)}) copy-start(s32[1,8,6]{1,0,2:T(1,128)} %param.19) | copy-start | bytes 580
  11.0 12.8 %collective-permute-start.8 = (bf16[6,48,768]{2,1,0:T(8,128)(2,1)S(1)}, bf16[6,48,768]{2,1,0:T(8,128)(2,1)S(1)}, u32[]{:S(2)}, u32[]{:S(2)}) collective-permute-start(bf16[6,48,768]{2,1,0:T(8,128)(2,1)S(1)} %bitcast_dynamic-update-slice_fusion.refs_4_), channel_id=1, source_target_pairs={{0,2},{1,3},{2,0},{3,1},{4,6},{5,7},{6,4},{7,5},{8,10},{9,11},{10,... | collective-permute-start | bytes 1327112 | tf_op jit(solution)/shard_map/ppermute | solution.py:220
  12.6 32.8 %collective-permute-start.13 = (bf16[6,48,768]{2,1,0:T(8,128)(2,1)S(1)}, bf16[6,48,768]{2,1,0:T(8,128)(2,1)S(1)}, u32[]{:S(2)}, u32[]{:S(2)}) collective-permute-start(bf16[6,48,768]{2,1,0:T(8,128)(2,1)S(1)} %bitcast_dynamic-update-slice_fusion.refs_4_), channel_id=1, source_target_pairs={{0,16},{1,17},{2,18},{3,19},{4,20},{5,21},{6,22},{7,23},{8,24},{9,... | collective-permute-start | bytes 1327112 | tf_op jit(solution)/shard_map/ppermute | solution.py:220
  16.1 8.3 %copy-start.11 = (s32[1,8,6]{1,0,2:T(1,128)S(1)}, s32[1,8,6]{1,0,2:T(1,128)}, u32[]{:S(2)}) copy-start(s32[1,8,6]{1,0,2:T(1,128)} %param.20) | copy-start | bytes 580
  16.1 7.7 %collective-permute-start = (bf16[2,32,1536]{2,1,0:T(8,128)(2,1)S(1)}, bf16[2,32,1536]{2,1,0:T(8,128)(2,1)S(1)}, u32[]{:S(2)}, u32[]{:S(2)}) collective-permute-start(bf16[2,32,1536]{2,1,0:T(8,128)(2,1)S(1)} %get-tuple-element.28), channel_id=1, source_target_pairs={{0,4},{1,5},{2,6},{3,7},{4,0},{5,1},{6,2},{7,3},{8,12},{9,13},{10,... | collective-permute-start | bytes 589832 | tf_op jit(solution)/shard_map/ppermute | solution.py:220
  16.7 12.3 %collective-permute-start.1 = (bf16[2,32,1536]{2,1,0:T(8,128)(2,1)S(1)}, bf16[2,32,1536]{2,1,0:T(8,128)(2,1)S(1)}, u32[]{:S(2)}, u32[]{:S(2)}) collective-permute-start(bf16[2,32,1536]{2,1,0:T(8,128)(2,1)S(1)} %get-tuple-element.29), channel_id=1, source_target_pairs={{0,8},{1,9},{2,10},{3,11},{4,12},{5,13},{6,14},{7,15},{8,0},{9,1},... | collective-permute-start | bytes 589832 | tf_op jit(solution)/shard_map/ppermute | solution.py:220
  17.7 19.0 %collective-permute-start.2 = (bf16[2,32,1536]{2,1,0:T(8,128)(2,1)S(1)}, bf16[2,32,1536]{2,1,0:T(8,128)(2,1)S(1)}, u32[]{:S(2)}, u32[]{:S(2)}) collective-permute-start(bf16[2,32,1536]{2,1,0:T(8,128)(2,1)S(1)} %get-tuple-element.30), channel_id=1, source_target_pairs={{0,12},{1,13},{2,14},{3,15},{4,8},{5,9},{6,10},{7,11},{8,4},{9,5},... | collective-permute-start | bytes 589832 | tf_op jit(solution)/shard_map/ppermute | solution.py:220
  23.9 22.1 %collective-permute-start.7 = (bf16[6,48,768]{2,1,0:T(8,128)(2,1)S(1)}, bf16[6,48,768]{2,1,0:T(8,128)(2,1)S(1)}, u32[]{:S(2)}, u32[]{:S(2)}) collective-permute-start(bf16[6,48,768]{2,1,0:T(8,128)(2,1)S(1)} %bitcast_dynamic-update-slice_fusion.refs_4_), channel_id=1, source_target_pairs={{0,1},{1,0},{2,3},{3,2},{4,5},{5,4},{6,7},{7,6},{8,9},{9,8},{10,11... | collective-permute-start | bytes 1327112 | tf_op jit(solution)/shard_map/ppermute | solution.py:220
  23.9 22.1 %collective-permute-start.9 = (bf16[6,48,768]{2,1,0:T(8,128)(2,1)S(1)}, bf16[6,48,768]{2,1,0:T(8,128)(2,1)S(1)}, u32[]{:S(2)}, u32[]{:S(2)}) collective-permute-start(bf16[6,48,768]{2,1,0:T(8,128)(2,1)S(1)} %collective-permute-done.8.refs_6_), channel_id=1, source_target_pairs={{0,1},{1,0},{2,3},{3,2},{4,5},{5,4},{6,7},{7,6},{8,9},{9,8},{10,11... | collective-permute-start | bytes 1327112 | tf_op jit(solution)/shard_map/ppermute | solution.py:220
  36.7 2.4 %copy-start.4 = (f32[31,1536]{1,0:T(8,128)S(1)}, f32[31,1536]{1,0:T(8,128)}, u32[]{:S(2)}) copy-start(f32[31,1536]{1,0:T(8,128)} %taps.1) | copy-start | bytes 571396
  37.6 7.8 %collective-permute-start.3 = (bf16[2,32,1536]{2,1,0:T(8,128)(2,1)S(1)}, bf16[2,32,1536]{2,1,0:T(8,128)(2,1)}, u32[]{:S(2)}, u32[]{:S(2)}) collective-permute-start(bf16[2,32,1536]{2,1,0:T(8,128)(2,1)S(1)} %shard_map.111), channel_id=1, source_target_pairs={{0,16},{1,17},{2,18},{3,19},{4,20},{5,21},{6,22},{7,23},{8,24},{9,... | collective-permute-start | bytes 589832 | tf_op jit(solution)/shard_map/ppermute | solution.py:220
  37.7 0.7 copy-start.6
  37.7 0.7 copy-start.7
  38.4 0.7 copy-start.8
  39.1 6.9 %copy-start.12 = (s32[8]{0:T(128)S(1)}, s32[8]{0:T(128)}, u32[]{:S(2)}) copy-start(s32[8]{0:T(128)} %constant.58.clone) | copy-start | bytes 100
  45.4 8.3 %collective-permute-start.14 = (bf16[6,48,768]{2,1,0:T(8,128)(2,1)S(1)}, bf16[6,48,768]{2,1,0:T(8,128)(2,1)S(1)}, u32[]{:S(2)}, u32[]{:S(2)}) collective-permute-start(bf16[6,48,768]{2,1,0:T(8,128)(2,1)S(1)} %collective-permute-done.13.refs_5_), channel_id=1, source_target_pairs={{0,2},{1,3},{2,0},{3,1},{4,6},{5,7},{6,4},{7,5},{8,10},{9,11},{10,... | collective-permute-start | bytes 1327112 | tf_op jit(solution)/shard_map/ppermute | solution.py:220
  48.8 5.9 %collective-permute-start.10 = (bf16[2,32,1536]{2,1,0:T(8,128)(2,1)}, bf16[2,32,1536]{2,1,0:T(8,128)(2,1)S(1)}, u32[]{:S(2)}, u32[]{:S(2)}) collective-permute-start(bf16[2,32,1536]{2,1,0:T(8,128)(2,1)} %get-tuple-element.38.refs_0_), channel_id=1, source_target_pairs={{0,4},{1,5},{2,6},{3,7},{4,0},{5,1},{6,2},{7,3},{8,12},{9,13},{10,... | collective-permute-start | bytes 589832 | tf_op jit(solution)/shard_map/ppermute | solution.py:220
  49.4 7.6 %collective-permute-start.15 = (bf16[6,48,768]{2,1,0:T(8,128)(2,1)S(1)}, bf16[6,48,768]{2,1,0:T(8,128)(2,1)S(1)}, u32[]{:S(2)}, u32[]{:S(2)}) collective-permute-start(bf16[6,48,768]{2,1,0:T(8,128)(2,1)S(1)} %collective-permute-done.13.refs_5_), channel_id=1, source_target_pairs={{0,1},{1,0},{2,3},{3,2},{4,5},{5,4},{6,7},{7,6},{8,9},{9,8},{10,11... | collective-permute-start | bytes 1327112 | tf_op jit(solution)/shard_map/ppermute | solution.py:220
  54.7 11.8 %collective-permute-start.16 = (bf16[6,48,768]{2,1,0:T(8,128)(2,1)S(1)}, bf16[6,48,768]{2,1,0:T(8,128)(2,1)}, u32[]{:S(2)}, u32[]{:S(2)}) collective-permute-start(bf16[6,48,768]{2,1,0:T(8,128)(2,1)S(1)} %collective-permute-done.14.refs_7_), channel_id=1, source_target_pairs={{0,1},{1,0},{2,3},{3,2},{4,5},{5,4},{6,7},{7,6},{8,9},{9,8},{10,11... | collective-permute-start | bytes 1327112 | tf_op jit(solution)/shard_map/ppermute | solution.py:220
  54.7 8.9 %collective-permute-start.12 = (bf16[2,32,1536]{2,1,0:T(8,128)(2,1)}, bf16[2,32,1536]{2,1,0:T(8,128)(2,1)}, u32[]{:S(2)}, u32[]{:S(2)}) collective-permute-start(bf16[2,32,1536]{2,1,0:T(8,128)(2,1)} %get-tuple-element.38.refs_0_), channel_id=1, source_target_pairs={{0,12},{1,13},{2,14},{3,15},{4,8},{5,9},{6,10},{7,11},{8,4},{9,5},... | collective-permute-start | bytes 589832 | tf_op jit(solution)/shard_map/ppermute | solution.py:220
  54.7 11.8 %collective-permute-start.11 = (bf16[2,32,1536]{2,1,0:T(8,128)(2,1)}, bf16[2,32,1536]{2,1,0:T(8,128)(2,1)}, u32[]{:S(2)}, u32[]{:S(2)}) collective-permute-start(bf16[2,32,1536]{2,1,0:T(8,128)(2,1)} %get-tuple-element.38.refs_0_), channel_id=1, source_target_pairs={{0,8},{1,9},{2,10},{3,11},{4,12},{5,13},{6,14},{7,15},{8,0},{9,1},... | collective-permute-start | bytes 589832 | tf_op jit(solution)/shard_map/ppermute | solution.py:220
  66.5 0.9 %copy-start.3 = (bf16[2,32,1536]{2,1,0:T(8,128)(2,1)S(1)}, bf16[2,32,1536]{2,1,0:T(8,128)(2,1)}, u32[]{:S(2)}) copy-start(bf16[2,32,1536]{2,1,0:T(8,128)(2,1)} %copy-done.2) | copy-start | bytes 589828
  71.8 7.0 %collective-permute-start.17 = (bf16[2,32,1536]{2,1,0:T(8,128)(2,1)S(1)}, bf16[2,32,1536]{2,1,0:T(8,128)(2,1)S(1)}, u32[]{:S(2)}, u32[]{:S(2)}) collective-permute-start(bf16[2,32,1536]{2,1,0:T(8,128)(2,1)S(1)} %get-tuple-element.42), channel_id=1, source_target_pairs={{0,4},{1,5},{2,6},{3,7},{4,0},{5,1},{6,2},{7,3},{8,12},{9,13},{10,... | collective-permute-start | bytes 589832 | tf_op jit(solution)/shard_map/ppermute | solution.py:220
  73.4 7.8 %collective-permute-start.18 = (bf16[2,32,1536]{2,1,0:T(8,128)(2,1)S(1)}, bf16[2,32,1536]{2,1,0:T(8,128)(2,1)S(1)}, u32[]{:S(2)}, u32[]{:S(2)}) collective-permute-start(bf16[2,32,1536]{2,1,0:T(8,128)(2,1)S(1)} %get-tuple-element.43), channel_id=1, source_target_pairs={{0,8},{1,9},{2,10},{3,11},{4,12},{5,13},{6,14},{7,15},{8,0},{9,1},... | collective-permute-start | bytes 589832 | tf_op jit(solution)/shard_map/ppermute | solution.py:220
  73.4 10.4 %collective-permute-start.19 = (bf16[2,32,1536]{2,1,0:T(8,128)(2,1)S(1)}, bf16[2,32,1536]{2,1,0:T(8,128)(2,1)S(1)}, u32[]{:S(2)}, u32[]{:S(2)}) collective-permute-start(bf16[2,32,1536]{2,1,0:T(8,128)(2,1)S(1)} %get-tuple-element.44), channel_id=1, source_target_pairs={{0,12},{1,13},{2,14},{3,15},{4,8},{5,9},{6,10},{7,11},{8,4},{9,5},... | collective-permute-start | bytes 589832 | tf_op jit(solution)/shard_map/ppermute | solution.py:220
  (1 other events, 0.7 us)

commit v4 on v3

--- a/solution.py
+++ b/solution.py
@@ -35,64 +35,134 @@
     return jax.ShapeDtypeStruct(shape, dtype)
 
 
-def send_kernel(place, tab_len, tab_dest, frames, *outs):
+class Tables:
+    def __init__(self, ref, sources):
+        self.ref = ref
+        self.slots = ref.shape[0] // (3 * sources)
+        self.size = sources * self.slots
+
+    def live_for(self, source, slot, target):
+        at = source * self.slots + slot
+        return jnp.logical_and(self.ref[self.size + at] == target, self.ref[at] > 0)
+
+    def length(self, source, slot):
+        return self.ref[source * self.slots + slot]
+
+    def offset(self, source, slot):
+        return self.ref[2 * self.size + source * self.slots + slot]
+
+
+def own_columns(highs, weights, owner, width):
+    run = width // (highs * QUAD)
+    parts = [
+        weights[:, pl.ds(half * width + (high * QUAD + owner) * run, run)]
+        for half in range(2)
+        for high in range(highs)
+    ]
+    return jnp.concatenate(parts, axis=1)
+
+
+def send_kernel(sources, place, packed, weights, frames, *refs):
+    outs, buf = refs[:-1], refs[-1]
+    tables = Tables(packed, sources)
     me = place[0]
+    highs = sources // QUAD
+    long, width = frames.shape[1:]
+    wide = outs[0].shape[1]
+    for owner in range(QUAD):
+        buf[owner] = own_columns(highs, weights, owner, width)
     for number, out in enumerate(outs):
-        for far in range(out.shape[0]):
+        for far in range(highs):
             target = jnp.bitwise_xor(me, far * QUAD + number)
             found = jnp.int32(0)
-            for slot in range(frames.shape[0]):
-                hit = jnp.logical_and(tab_dest[me, slot] == target, tab_len[me, slot] > 0)
-                found = jnp.where(hit, slot, found)
-            out[far] = frames[found]
-
-
-def merge_kernel(place, tab_len, tab_dest, tab_off, *refs):
-    arrived, outs = refs[:QUAD], refs[QUAD:]
+            for slot in range(tables.slots):
+                found = jnp.where(tables.live_for(me, slot, target), slot, found)
+            for half in range(width // wide):
+                start = (far * (width // wide) + half) * long
+                out[start : start + long, :] = frames[found, :, half * wide : half * wide + wide]
+        start = highs * (width // wide) * long
+        out[start:, :] = buf[jnp.bitwise_xor(lax.rem(me, QUAD), number)]
+
+
+def fetch(out, number, ref, far):
+    long, width = out.shape[1:]
+    wide = ref.shape[1]
+    for half in range(width // wide):
+        start = (far * (width // wide) + half) * long
+        out[number, :, half * wide : half * wide + wide] = ref[start : start + long, :]
+
+
+def merge_kernel(sources, place, packed, last, *refs):
+    arrived, outs, piece = refs[:QUAD], refs[QUAD:-1], refs[-1]
+    tables = Tables(packed, sources)
     me = place[0]
-    long = arrived[0].shape[1]
+    depth, wide = piece.shape[1:]
     for far, out in enumerate(outs, 1):
+        long = out.shape[1]
         for number, ref in enumerate(arrived):
             source = jnp.bitwise_xor(me, number)
             target = jnp.bitwise_xor(me, far * QUAD)
             start = jnp.int32(-1)
-            for slot in range(tab_len.shape[1]):
-                hit = jnp.logical_and(
-                    tab_dest[source, slot] == target, tab_len[source, slot] > 0
-                )
-                start = jnp.where(hit, tab_off[source, slot], start)
+            for slot in range(tables.slots):
+                hit = tables.live_for(source, slot, target)
+                start = jnp.where(hit, tables.offset(source, slot), start)
 
             @pl.when(start >= 0)
             def _():
-                out[start // long] = ref[far]
-
-
-def table_kernel(
-    long, highs, place, quad, tab_len, tab_dest, tab_off, taps, scale, shift, sources, lens, table
-):
-    source_count, slots = tab_len.shape
+                fetch(out, start // long, ref, far)
+
+    for number, ref in enumerate(arrived):
+        piece[number] = ref[ref.shape[0] - depth :, :]
+    for half in range(piece.shape[0] - QUAD):
+        piece[QUAD + half] = last[:, half * wide : half * wide + wide]
+
+
+def split_kernel(highs, place, weights, *refs):
+    outs, buf = refs[:-1], refs[-1]
+    for owner in range(QUAD):
+        buf[owner] = own_columns(highs, weights, owner, weights.shape[1] // 3)
+    for number, out in enumerate(outs):
+        out[...] = buf[jnp.bitwise_xor(lax.rem(place[0], QUAD), number)]
+
+
+def stack_kernel(both, *refs):
+    columns, piece = refs[:-1], refs[-1]
+    wide = piece.shape[2]
+    last = both.at[:, both.shape[1] // 3 * 2 :]
+    for number, ref in enumerate(columns):
+        piece[number] = ref[...]
+    for half in range(piece.shape[0] - QUAD):
+        piece[QUAD + half] = last[:, half * wide : half * wide + wide]
+
+
+def table_kernel(source_count, long, place, packed, small, sources, lens, table, gain):
+    tables = Tables(packed, source_count)
+    highs = source_count // QUAD
     me = place[0]
 
     def look(source, carry):
-        for slot in range(slots):
-
-            @pl.when(jnp.logical_and(tab_dest[source, slot] == me, tab_len[source, slot] > 0))
+        for slot in range(tables.slots):
+
+            @pl.when(tables.live_for(source, slot, me))
             def _():
-                number = tab_off[source, slot] // long
+                number = tables.offset(source, slot) // long
                 sources[number] = source
-                lens[number] = tab_len[source, slot]
+                lens[number] = tables.length(source, slot)
 
         return carry
 
     lax.fori_loop(0, source_count, look, 0)
-    run = scale.shape[1] // (highs * QUAD)
-    whole = jnp.concatenate([taps[...], scale[...], shift[...]], axis=0)
+    count, width = small.shape
+    run = width // (highs * QUAD)
+    whole = small[...]
+    gain[...] = whole[count - 1 :, :]
     for owner in range(QUAD):
 
-        @pl.when(quad[0] == owner)
+        @pl.when(lax.rem(me, QUAD) == owner)
         def _():
             starts = [(high * QUAD + owner) * run for high in range(highs)]
-            table[...] = jnp.concatenate([whole[:, at : at + run] for at in starts], axis=1)
+            parts = [whole[: count - 1, at : at + run] for at in starts]
+            table[...] = jnp.concatenate(parts, axis=1)
 
 
 def norm_kernel(place, sources, lens, gain, *refs):
@@ -103,7 +173,7 @@
 
             @pl.when(shift == other)
             def _():
-                kept[number] = ref[0]
+                fetch(kept, number, ref, 0)
 
         for other, ref in enumerate(far, 1):
 
@@ -118,21 +188,6 @@
         value = centred * lax.rsqrt(var + 1e-05) * gain[...]
         steps = lax.broadcasted_iota(jnp.int32, value.shape, 0)
         normed[number] = jnp.where(steps < lens[number], value, 0.0).astype(BF16)
-
-
-def split_kernel(highs, quad, weights, *refs):
-    outs, buf = refs[:-1], refs[-1]
-    width = weights.shape[1] // 2
-    run = width // (highs * QUAD)
-    for owner in range(QUAD):
-        parts = [
-            weights[:, pl.ds(half * width + (high * QUAD + owner) * run, run)]
-            for half in range(2)
-            for high in range(highs)
-        ]
-        buf[owner] = jnp.concatenate(parts, axis=1)
-    for number, out in enumerate(outs):
-        out[...] = buf[jnp.bitwise_xor(quad[0], number)]
 
 
 def conv_rows(block, taps):
@@ -207,8 +262,7 @@
     dp_index = lax.axis_index("dp")
     quad = dp_index % QUAD
     line = dp_index // QUAD * fsdp_count + lax.axis_index("fsdp")
-    slots = lengths.shape[2]
-    recv = slots // 3
+    recv = lengths.shape[2] // 3
     _, _, long, width = frames.shape
     depth = w_in.shape[0]
     chans = width // QUAD
@@ -222,83 +276,86 @@
     def quad_swap(arrays):
         return [arrays[0]] + [swap(arrays[mask], quad=mask) for mask in range(1, QUAD)]
 
+    def gated(arrays, others):
+        return lax.optimization_barrier((arrays, others))[0]
+
     place = dp_index.astype(jnp.int32)[None]
-    quad_place = quad.astype(jnp.int32)[None]
-    tab_len, tab_dest, tab_off = lengths[0], destinations[0], offsets[0]
-
-    if depth % 16 == 0:
-        split = call(
+    packed = jnp.stack([lengths[0], destinations[0], offsets[0]]).reshape(-1)
+    small = jnp.concatenate([depth_kernel, bn_scale[None], bn_shift[None], ln_gain[None]])
+    count = width // wide
+    bits = [1 << at for at in range((highs * fsdp_count).bit_length() - 1)]
+    chip_bits = [bit for bit in reversed(bits) if 1 < bit < fsdp_count]
+
+    both = jnp.concatenate([w_in, w_out], axis=1)
+    far_rows = [swap(both, high=mask) for mask in range(1, highs)]
+
+    near = call(
+        functools.partial(send_kernel, dp_count),
+        [like(BF16, highs * count * long + depth, wide)] * QUAD,
+        [SMEM, SMEM, VMEM, VMEM],
+        [VMEM] * QUAD,
+        (place, packed, w_in, frames[0]),
+        [like(BF16, QUAD, depth, wide)],
+    )
+    near = quad_swap(near)
+    sources, lens, table, gain = call(
+        functools.partial(table_kernel, dp_count, long),
+        [like(jnp.int32, recv)] * 2 + [like(F32, taps + 2, chans), like(F32, 1, width)],
+        [SMEM] * 2 + [VMEM],
+        [SMEM, SMEM, VMEM, VMEM],
+        (place, packed, small),
+    )
+    utts = like(BF16, recv, long, width)
+    block = like(BF16, QUAD + count, depth, wide)
+    *far, piece = call(
+        functools.partial(merge_kernel, dp_count),
+        [utts] * (highs - 1) + [block],
+        [SMEM] * 2 + [VMEM] * (1 + QUAD),
+        [VMEM] * highs,
+        (gated(place, (lens, gain)), packed, w_out, *near),
+    )
+    pieces = [piece]
+    shifts = [mask * fsdp_count for mask in range(highs)]
+    far_rows = gated(far_rows, far)
+    far = [swap(part, high=mask) for mask, part in enumerate(far, 1)]
+    for part in far_rows:
+        columns = call(
             functools.partial(split_kernel, highs),
             [like(BF16, depth, wide)] * QUAD,
             [SMEM, VMEM],
             [VMEM] * QUAD,
-            (quad_place, w_in),
+            (place, part),
             [like(BF16, QUAD, depth, wide)],
         )
-    else:
-        by_owner = w_in.reshape(depth, 2, highs, QUAD, chans // highs).transpose(3, 0, 1, 2, 4)
-        by_owner = by_owner.reshape(QUAD, depth, wide)
-        split = [
-            lax.dynamic_index_in_dim(by_owner, quad ^ mask, 0, keepdims=False)
-            for mask in range(QUAD)
-        ]
-    halves = [w_out[:, at : at + wide] for at in range(0, width, wide)]
-    pieces = [jnp.stack(quad_swap(split) + halves)]
-    shifts = [0]
-    bits = [1 << at for at in range((highs * fsdp_count).bit_length() - 1)]
-    high_bits = [bit for bit in reversed(bits) if bit >= fsdp_count]
-    chip_bits = [bit for bit in reversed(bits) if 1 < bit < fsdp_count]
-    for bit in high_bits:
-        pieces = pieces + [swap(part, high=bit // fsdp_count) for part in pieces]
+        pieces.append(
+            call(
+                stack_kernel,
+                block,
+                [VMEM] * (1 + QUAD),
+                VMEM,
+                (part, *gated(quad_swap(columns), far)),
+            )
+        )
+    early = len(pieces)
+    cored = [swap(part, fsdp=1) for part in pieces]
+    far = gated(far, (pieces, cored[:1]))
+    for bit in chip_bits:
+        pieces = pieces + [swap(part, fsdp=bit) for part in pieces]
         shifts = shifts + [shift ^ bit for shift in shifts]
 
-    near = call(
-        send_kernel,
-        [like(BF16, highs, long, width)] * QUAD,
-        [SMEM, SMEM, SMEM, VMEM],
-        [VMEM] * QUAD,
-        (place, tab_len, tab_dest, frames[0]),
-    )
-    near = quad_swap(near)
-    utts = like(BF16, recv, long, width)
-    far = call(
-        merge_kernel,
-        [utts] * (highs - 1),
-        [SMEM] * 4 + [VMEM] * QUAD,
-        [VMEM] * (highs - 1),
-        (place, tab_len, tab_dest, tab_off, *near),
-    )
-    far = [swap(part, high=mask) for mask, part in enumerate(far, 1)]
-    pieces[1:], _ = lax.optimization_barrier((pieces[1:], far))
-    chip_first = [swap(pieces[0], fsdp=bit) for bit in chip_bits[:1]]
-    early = [swap(part, fsdp=1) for part in pieces[:1] + chip_first]
-    far, _ = lax.optimization_barrier((far, early))
-    sources, lens, table = call(
-        functools.partial(table_kernel, long, highs),
-        [like(jnp.int32, recv), like(jnp.int32, recv), like(F32, taps + 2, chans)],
-        [SMEM] * 5 + [VMEM] * 3,
-        [SMEM, SMEM, VMEM],
-        (place, quad_place, tab_len, tab_dest, tab_off)
-        + (depth_kernel, bn_scale[None], bn_shift[None]),
-    )
     kept, normed = call(
         norm_kernel,
         [utts, utts],
         [SMEM] * 3 + [VMEM] * (QUAD + highs),
         [VMEM, VMEM],
-        (place, sources, lens, ln_gain[None], *near, *far),
-    )
-    for bit in chip_bits:
-        first = chip_first if bit == chip_bits[0] else []
-        pieces = pieces + first + [swap(part, fsdp=bit) for part in pieces[len(first) :]]
-        shifts = shifts + [shift ^ bit for shift in shifts]
-    ends = len(shifts) // 2 + 1
+        (place, sources, lens, gain, *near, *far),
+    )
     normed = quad_swap([normed] * QUAD)
-    pieces[ends:], _ = lax.optimization_barrier((pieces[ends:], normed[1]))
-    cored = [swap(part, fsdp=1) for part in pieces]
-    cored[0], cored[len(shifts) // 2] = early[0], early[-1]
-    pieces = pieces + cored
+    late = pieces[early:]
+    crossed = swap(jnp.stack(gated(late, normed[1:3])), fsdp=1)
+    pieces = pieces + cored + [crossed[at] for at in range(len(late))]
     shifts = shifts + [shift ^ 1 for shift in shifts]
+
     out_rows = line ^ jnp.array(shifts)
     in_rows = out_rows // fsdp_count * QUAD
     in_rows = in_rows[:, None] + (quad ^ jnp.arange(QUAD))[None, :]

time: 84.9 us -> 88.9 us (1.047)
  waiting for transfers between devices: 49.4 us -> 53.8 us
  other arithmetic: 1.02 us -> 3.23 us
  Pallas kernels: 10.1 us -> 8.06 us
  local copies, waits for them, and re-layouts: 4.36 us -> 2.86 us
  starting transfers between devices: 19.6 us -> 20.5 us
    ppermute x20 -> x19, waiting for transfers between devices: 49.4 us -> 53.8 us  [swap(): lax.ppermute(array, ('dp', 'fsdp'), [(at, at ^ mask) for at in range(devi...]
    unnamed x34 -> x22, local copies, waits for them, and re-layouts: 4.26 us -> 1.36 us
    pallas_call x6 -> x7, Pallas kernels: 10.1 us -> 8.06 us  [call(): pl.pallas_call(kernel, out_shape=out_shape, in_specs=in_specs, out_specs=...]
    squeeze x0 -> x1, local copies, waits for them, and re-layouts: none -> 1.2 us  [shards(): pieces = pieces + cored + [crossed[at] for at in range(len(late))]]
    concatenate x0 -> x2, other arithmetic: none -> 1.18 us  [the longest x1 1.14 us: shards(): both = jnp.concatenate([w_in, w_out], axis=1)]
    another operation x0 -> x2, other arithmetic: none -> 1.02 us  [the longest x1 1.01 us: shards(): crossed = swap(jnp.stack(gated(late, normed[1:3])), fsdp=1)]
    ppermute x20 -> x19, starting transfers between devices: 19.6 us -> 20.5 us  [swap(): lax.ppermute(array, ('dp', 'fsdp'), [(at, at ^ mask) for at in range(devi...]
  transfers between devices with their start and end apart: 20 -> 19, of which waited for: 14 -> 12; matrix products, arithmetic and copies ran while one was open for 1% -> 2% of each run, Pallas kernels for 7% -> 5%
where the time goes in v4:
time: 88.9 us; the launch traced here: 88.7 us
  waiting for transfers between devices  53.8 us (61%)
  starting transfers between devices  20.5 us (23%)
  Pallas kernels  8.06 us (9%)
  other arithmetic  3.23 us (4%)
  local copies, waits for them, and re-layouts  2.86 us (3%)
    ppermute x19, waiting for transfers between devices, swap(): lax.ppermute(array, ('dp', 'fsdp'), [(at, at ^ mask) for at in range(devi...  53.8 us
    ppermute x19, starting transfers between devices, swap(): lax.ppermute(array, ('dp', 'fsdp'), [(at, at ^ mask) for at in range(devi...  20.5 us
    pallas_call x7, Pallas kernels, call(): pl.pallas_call(kernel, out_shape=out_shape, in_specs=in_specs, out_specs=...  8.06 us
  transfers between devices with their start and end apart: 19, of which 12 were waited for; matrix products, arithmetic and copies ran while one was open for 2% of the time, Pallas kernels for 5%

profile of v4, /device:TPU:0, one launch (start us, length us, event | category | flops | bytes accessed | tf_op | source)
XLA Modules:
  0.0 88.7 jit_solution(17141955432549537164)
XLA Ops:
  0.0 1.1 %pad_maximum_fusion.1 = bf16[48,4608]{1,0:T(8,128)(2,1)S(1)} fusion(bf16[48,1536]{1,0:T(8,128)(2,1)} %last.1, bf16[48,3072]{1,0:T(8,128)(2,1)} %weights.1), kind=kLoop, calls=%fused_computation.3 | loop fusion | flops 884736 | bytes 884736 | tf_op jit(solution)/shard_map/concatenate | solution.py:289
  1.2 4.1 %collective-permute-start.4 = (bf16[48,4608]{1,0:T(8,128)(2,1)S(1)}, bf16[48,4608]{1,0:T(8,128)(2,1)S(1)}, u32[]{:S(2)}, u32[]{:S(2)}) collective-permute-start(bf16[48,4608]{1,0:T(8,128)(2,1)S(1)} %pad_maximum_fusion.1), channel_id=1, source_target_pairs={{0,16},{1,17},{2,18},{3,19},{4,20},{5,21},{6,22},{7,23},{8,24},{9,... | collective-permute-start | bytes 1327112 | tf_op jit(solution)/shard_map/ppermute | solution.py:274
  5.5 0.7 shard_map.110
  6.3 1.6 %collective-permute-start = (bf16[176,768]{1,0:T(8,128)(2,1)S(1)}, bf16[176,768]{1,0:T(8,128)(2,1)S(1)}, u32[]{:S(2)}, u32[]{:S(2)}) collective-permute-start(bf16[176,768]{1,0:T(8,128)(2,1)S(1)} %get-tuple-element.38), channel_id=1, source_target_pairs={{0,4},{1,5},{2,6},{3,7},{4,0},{5,1},{6,2},{7,3},{8,12},{9,13},{10,... | collective-permute-start | bytes 811016 | tf_op jit(solution)/shard_map/ppermute | solution.py:274
  7.8 1.6 %collective-permute-start.1 = (bf16[176,768]{1,0:T(8,128)(2,1)S(1)}, bf16[176,768]{1,0:T(8,128)(2,1)S(1)}, u32[]{:S(2)}, u32[]{:S(2)}) collective-permute-start(bf16[176,768]{1,0:T(8,128)(2,1)S(1)} %get-tuple-element.39), channel_id=1, source_target_pairs={{0,8},{1,9},{2,10},{3,11},{4,12},{5,13},{6,14},{7,15},{8,0},{9,1},... | collective-permute-start | bytes 811016 | tf_op jit(solution)/shard_map/ppermute | solution.py:274
  9.9 0.7 copy-done.6
  10.6 1.8 %shard_map.109 = (s32[2]{0:T(128)S(1)}, s32[2]{0:T(128)S(1)}, f32[33,384]{1,0:T(8,128)S(1)}, f32[1,1536]{1,0:T(1,128)S(1)}) custom-call(s32[1]{0:T(128)} %bitcast.place, s32[144]{0:T(256)S(1)} %reshape.34.packed, f32[34,1536]{1,0:T(8,128)S(1)} %pad_maximum_fusion.2.small), custom_call_target="tpu_custom_call" | custom-call | bytes 266324 | tf_op jit(solution)/shard_map/pallas_call | solution.py:21
  12.4 2.5 %collective-permute-done.refs_1_ = bf16[176,768]{1,0:T(8,128)(2,1)S(1)} collective-permute-done((bf16[176,768]{1,0:T(8,128)(2,1)S(1)}, bf16[176,768]{1,0:T(8,128)(2,1)S(1)}, u32[]{:S(2)}, u32[]{:S(2)}) %collective-permute-start) | collective-permute-done | bytes 270368 | tf_op jit(solution)/shard_map/ppermute | solution.py:274
  14.8 10.7 %collective-permute-done.1.refs_2_ = bf16[176,768]{1,0:T(8,128)(2,1)S(1)} collective-permute-done((bf16[176,768]{1,0:T(8,128)(2,1)S(1)}, bf16[176,768]{1,0:T(8,128)(2,1)S(1)}, u32[]{:S(2)}, u32[]{:S(2)}) %collective-permute-start.1) | collective-permute-done | bytes 270368 | tf_op jit(solution)/shard_map/ppermute | solution.py:274
  25.6 4.0 %collective-permute-done.2.refs_3_ = bf16[176,768]{1,0:T(8,128)(2,1)S(1)} collective-permute-done((bf16[176,768]{1,0:T(8,128)(2,1)S(1)}, bf16[176,768]{1,0:T(8,128)(2,1)S(1)}, u32[]{:S(2)}, u32[]{:S(2)}) %collective-permute-start.2) | collective-permute-done | bytes 270368 | tf_op jit(solution)/shard_map/ppermute | solution.py:274
  29.6 0.7 shard_map.111
  31.0 1.1 %collective-permute-start.5 = (bf16[48,768]{1,0:T(8,128)(2,1)S(1)}, bf16[48,768]{1,0:T(8,128)(2,1)S(1)}, u32[]{:S(2)}, u32[]{:S(2)}) collective-permute-start(bf16[48,768]{1,0:T(8,128)(2,1)S(1)} %get-tuple-element.46), channel_id=1, source_target_pairs={{0,4},{1,5},{2,6},{3,7},{4,0},{5,1},{6,2},{7,3},{8,12},{9,13},{10,... | collective-permute-start | bytes 221192 | tf_op jit(solution)/shard_map/ppermute | solution.py:274
  32.2 2.9 %collective-permute-start.6 = (bf16[48,768]{1,0:T(8,128)(2,1)S(1)}, bf16[48,768]{1,0:T(8,128)(2,1)S(1)}, u32[]{:S(2)}, u32[]{:S(2)}) collective-permute-start(bf16[48,768]{1,0:T(8,128)(2,1)S(1)} %get-tuple-element.47), channel_id=1, source_target_pairs={{0,8},{1,9},{2,10},{3,11},{4,12},{5,13},{6,14},{7,15},{8,0},{9,1},... | collective-permute-start | bytes 221192 | tf_op jit(solution)/shard_map/ppermute | solution.py:274
  35.1 5.7 %collective-permute-done.3.refs_4_ = bf16[2,32,1536]{2,1,0:T(8,128)(2,1)S(1)} collective-permute-done((bf16[2,32,1536]{2,1,0:T(8,128)(2,1)S(1)}, bf16[2,32,1536]{2,1,0:T(8,128)(2,1)S(1)}, u32[]{:S(2)}, u32[]{:S(2)}) %collective-permute-start.3) | collective-permute-done | bytes 196640 | tf_op jit(solution)/shard_map/ppermute | solution.py:274
  40.7 1.5 %collective-permute-start.12 = (bf16[6,48,768]{2,1,0:T(8,128)(2,1)S(1)}, bf16[6,48,768]{2,1,0:T(8,128)(2,1)S(1)}, u32[]{:S(2)}, u32[]{:S(2)}) collective-permute-start(bf16[6,48,768]{2,1,0:T(8,128)(2,1)S(1)} %get-tuple-element.43.refs_4_), channel_id=1, source_target_pairs={{0,2},{1,3},{2,0},{3,1},{4,6},{5,7},{6,4},{7,5},{8,10},{9,11},{10,... | collective-permute-start | bytes 1327112 | tf_op jit(solution)/shard_map/ppermute | solution.py:274
  42.2 1.0 %collective-permute-done.7.refs_3_ = bf16[48,768]{1,0:T(8,128)(2,1)S(1)} collective-permute-done((bf16[48,768]{1,0:T(8,128)(2,1)S(1)}, bf16[48,768]{1,0:T(8,128)(2,1)S(1)}, u32[]{:S(2)}, u32[]{:S(2)}) %collective-permute-start.7) | collective-permute-done | bytes 73760 | tf_op jit(solution)/shard_map/ppermute | solution.py:274
  43.3 1.6 %collective-permute-start.13 = (bf16[6,48,768]{2,1,0:T(8,128)(2,1)S(1)}, bf16[6,48,768]{2,1,0:T(8,128)(2,1)S(1)}, u32[]{:S(2)}, u32[]{:S(2)}) collective-permute-start(bf16[6,48,768]{2,1,0:T(8,128)(2,1)S(1)} %shard_map.113.refs_5_), channel_id=1, source_target_pairs={{0,2},{1,3},{2,0},{3,1},{4,6},{5,7},{6,4},{7,5},{8,10},{9,11},{10,... | collective-permute-start | bytes 1327112 | tf_op jit(solution)/shard_map/ppermute | solution.py:274
  44.9 1.0 %shard_map.114 = (bf16[2,32,1536]{2,1,0:T(8,128)(2,1)S(1)}, bf16[2,32,1536]{2,1,0:T(8,128)(2,1)S(1)}) custom-call(s32[1]{0:T(128)} %bitcast.place, s32[2]{0:T(128)S(1)} %get-tuple-element.35.sources, s32[2]{0:T(128)S(1)} %get-tuple-element.34.lens, f32[1,1536]{1,0:T(1,128)S(1)} %get-tuple-element.36.gain, bf16[176,768]{1,0:T(8,128)(2,1)S(1)} %get-tuple-element.37.refs_0_, ...), custom_call_target="tpu_custom_call" | custom-call | bytes 1677332 | tf_op jit(solution)/shard_map/pallas_call | solution.py:21
  46.0 1.5 %collective-permute-start.9 = (bf16[2,32,1536]{2,1,0:T(8,128)(2,1)S(1)}, bf16[2,32,1536]{2,1,0:T(8,128)(2,1)S(1)}, u32[]{:S(2)}, u32[]{:S(2)}) collective-permute-start(bf16[2,32,1536]{2,1,0:T(8,128)(2,1)S(1)} %get-tuple-element.56.refs_0_), channel_id=1, source_target_pairs={{0,4},{1,5},{2,6},{3,7},{4,0},{5,1},{6,2},{7,3},{8,12},{9,13},{10,... | collective-permute-start | bytes 589832 | tf_op jit(solution)/shard_map/ppermute | solution.py:274
  47.4 6.4 %collective-permute-done.12.refs_6_ = bf16[6,48,768]{2,1,0:T(8,128)(2,1)S(1)} collective-permute-done((bf16[6,48,768]{2,1,0:T(8,128)(2,1)S(1)}, bf16[6,48,768]{2,1,0:T(8,128)(2,1)S(1)}, u32[]{:S(2)}, u32[]{:S(2)}) %collective-permute-start.12) | collective-permute-done | bytes 442400 | tf_op jit(solution)/shard_map/ppermute | solution.py:274
  53.8 8.2 %collective-permute-done.13.refs_7_ = bf16[6,48,768]{2,1,0:T(8,128)(2,1)S(1)} collective-permute-done((bf16[6,48,768]{2,1,0:T(8,128)(2,1)S(1)}, bf16[6,48,768]{2,1,0:T(8,128)(2,1)S(1)}, u32[]{:S(2)}, u32[]{:S(2)}) %collective-permute-start.13) | collective-permute-done | bytes 442400 | tf_op jit(solution)/shard_map/ppermute | solution.py:274
  62.0 1.0 %pad_maximum_fusion = bf16[2,6,48,768]{3,2,1,0:T(8,128)(2,1)} fusion(bf16[1,6,48,768]{3,2,1,0:T(8,128)(2,1)S(1)} %bitcast.13, bf16[1,6,48,768]{3,2,1,0:T(8,128)(2,1)S(1)} %bitcast.12), kind=kLoop, calls=%fused_computation | loop fusion | flops 442368 | bytes 1769472 | tf_op jit(solution)/shard_map/stack | solution.py:355
  64.0 1.8 %collective-permute-done.15 = bf16[2,6,48,768]{3,2,1,0:T(8,128)(2,1)} collective-permute-done((bf16[2,6,48,768]{3,2,1,0:T(8,128)(2,1)}, bf16[2,6,48,768]{3,2,1,0:T(8,128)(2,1)}, u32[]{:S(2)}, u32[]{:S(2)}) %collective-permute-start.15) | collective-permute-done | bytes 884768 | tf_op jit(solution)/shard_map/ppermute | solution.py:274
  65.8 1.2 %slice_bitcast_fusion = (bf16[6,48,768]{2,1,0:T(8,128)(2,1)S(1)}, bf16[6,48,768]{2,1,0:T(8,128)(2,1)S(1)}) fusion(bf16[2,6,48,768]{3,2,1,0:T(8,128)(2,1)} %collective-permute-done.15), kind=kLoop, calls=%fused_computation.1 | loop fusion | bytes 1769472 | tf_op jit(solution)/shard_map/squeeze | solution.py:356
  67.0 5.2 %collective-permute-done.11.refs_3_ = bf16[2,32,1536]{2,1,0:T(8,128)(2,1)S(1)} collective-permute-done((bf16[2,32,1536]{2,1,0:T(8,128)(2,1)S(1)}, bf16[2,32,1536]{2,1,0:T(8,128)(2,1)S(1)}, u32[]{:S(2)}, u32[]{:S(2)}) %collective-permute-start.11) | collective-permute-done | bytes 196640 | tf_op jit(solution)/shard_map/ppermute | solution.py:274
  72.2 3.7 %shard_map.115 = (f32[2,32,1536]{2,1,0:T(8,128)S(1)}, bf16[2,32,1536]{2,1,0:T(8,128)(2,1)S(1)}, bf16[2,32,1536]{2,1,0:T(8,128)(2,1)S(1)}, bf16[2,32,1536]{2,1,0:T(8,128)(2,1)S(1)}) custom-call(s32[8,5]{1,0:T(8,128)S(1)} %pad_add_fusion.1.where, bf16[2,32,1536]{2,1,0:T(8,128)(2,1)S(1)} %get-tuple-element.54.kept, f32[33,384]{1,0:T(8,128)S(1)} %get-tuple-element.55.table, ...), custom_call_target="tpu_custom_call" | custom-call | flops 905969664 | bytes 10471072 | tf_op jit(solution)/shard_map/pallas_call | solution.py:21
  75.9 1.4 %collective-permute-start.16 = (bf16[2,32,1536]{2,1,0:T(8,128)(2,1)S(1)}, bf16[2,32,1536]{2,1,0:T(8,128)(2,1)S(1)}, u32[]{:S(2)}, u32[]{:S(2)}) collective-permute-start(bf16[2,32,1536]{2,1,0:T(8,128)(2,1)S(1)} %get-tuple-element.60), channel_id=1, source_target_pairs={{0,4},{1,5},{2,6},{3,7},{4,0},{5,1},{6,2},{7,3},{8,12},{9,13},{10,... | collective-permute-start | bytes 589832 | tf_op jit(solution)/shard_map/ppermute | solution.py:274
  77.3 2.2 %collective-permute-start.18 = (bf16[2,32,1536]{2,1,0:T(8,128)(2,1)S(1)}, bf16[2,32,1536]{2,1,0:T(8,128)(2,1)S(1)}, u32[]{:S(2)}, u32[]{:S(2)}) collective-permute-start(bf16[2,32,1536]{2,1,0:T(8,128)(2,1)S(1)} %get-tuple-element.62), channel_id=1, source_target_pairs={{0,12},{1,13},{2,14},{3,15},{4,8},{5,9},{6,10},{7,11},{8,4},{9,5},... | collective-permute-start | bytes 589832 | tf_op jit(solution)/shard_map/ppermute | solution.py:274
  79.5 3.4 %collective-permute-done.16 = bf16[2,32,1536]{2,1,0:T(8,128)(2,1)S(1)} collective-permute-done((bf16[2,32,1536]{2,1,0:T(8,128)(2,1)S(1)}, bf16[2,32,1536]{2,1,0:T(8,128)(2,1)S(1)}, u32[]{:S(2)}, u32[]{:S(2)}) %collective-permute-start.16) | collective-permute-done | bytes 196640 | tf_op jit(solution)/shard_map/ppermute | solution.py:274
  82.9 2.2 %collective-permute-done.17 = bf16[2,32,1536]{2,1,0:T(8,128)(2,1)S(1)} collective-permute-done((bf16[2,32,1536]{2,1,0:T(8,128)(2,1)S(1)}, bf16[2,32,1536]{2,1,0:T(8,128)(2,1)S(1)}, u32[]{:S(2)}, u32[]{:S(2)}) %collective-permute-start.17) | collective-permute-done | bytes 196640 | tf_op jit(solution)/shard_map/ppermute | solution.py:274
  85.1 2.7 %collective-permute-done.18 = bf16[2,32,1536]{2,1,0:T(8,128)(2,1)S(1)} collective-permute-done((bf16[2,32,1536]{2,1,0:T(8,128)(2,1)S(1)}, bf16[2,32,1536]{2,1,0:T(8,128)(2,1)S(1)}, u32[]{:S(2)}, u32[]{:S(2)}) %collective-permute-start.18) | collective-permute-done | bytes 196640 | tf_op jit(solution)/shard_map/ppermute | solution.py:274
  87.9 0.8 fusion
  (53 shorter events, 2.6 us)
Async XLA Ops:
  0.0 5.5 %copy-start = (bf16[48,3072]{1,0:T(8,128)(2,1)S(1)}, bf16[48,3072]{1,0:T(8,128)(2,1)}, u32[]{:S(2)}) copy-start(bf16[48,3072]{1,0:T(8,128)(2,1)} %weights.1) | copy-start | bytes 884740
  0.0 5.3 %copy-start.7 = (s32[1,8,6]{1,0,2:T(1,128)S(1)}, s32[1,8,6]{1,0,2:T(1,128)}, u32[]{:S(2)}) copy-start(s32[1,8,6]{1,0,2:T(1,128)} %param.20) | copy-start | bytes 580
  0.0 5.3 %copy-start.8 = (s32[1,8,6]{1,0,2:T(1,128)S(1)}, s32[1,8,6]{1,0,2:T(1,128)}, u32[]{:S(2)}) copy-start(s32[1,8,6]{1,0,2:T(1,128)} %param.19) | copy-start | bytes 580
  0.0 5.3 %copy-start.9 = (s32[1,8,6]{1,0,2:T(1,128)S(1)}, s32[1,8,6]{1,0,2:T(1,128)}, u32[]{:S(2)}) copy-start(s32[1,8,6]{1,0,2:T(1,128)} %param.18) | copy-start | bytes 580
  0.0 5.5 %copy-start.2 = (bf16[1,6,32,1536]{3,2,1,0:T(8,128)(2,1)S(1)}, bf16[1,6,32,1536]{3,2,1,0:T(8,128)(2,1)}, u32[]{:S(2)}) copy-start(bf16[1,6,32,1536]{3,2,1,0:T(8,128)(2,1)} %param.11) | copy-start | bytes 1769476
  1.2 29.7 %collective-permute-start.4 = (bf16[48,4608]{1,0:T(8,128)(2,1)S(1)}, bf16[48,4608]{1,0:T(8,128)(2,1)S(1)}, u32[]{:S(2)}, u32[]{:S(2)}) collective-permute-start(bf16[48,4608]{1,0:T(8,128)(2,1)S(1)} %pad_maximum_fusion.1), channel_id=1, source_target_pairs={{0,16},{1,17},{2,18},{3,19},{4,20},{5,21},{6,22},{7,23},{8,24},{9,... | collective-permute-start | bytes 1327112 | tf_op jit(solution)/shard_map/ppermute | solution.py:274
  5.5 4.3 %copy-start.4 = (f32[1536]{0:T(1024)S(1)}, f32[1536]{0:T(1024)}, u32[]{:S(2)}) copy-start(f32[1536]{0:T(1024)} %param.12) | copy-start | bytes 18436
  5.5 5.0 %copy-start.3 = (f32[31,1536]{1,0:T(8,128)S(1)}, f32[31,1536]{1,0:T(8,128)}, u32[]{:S(2)}) copy-start(f32[31,1536]{1,0:T(8,128)} %param.14) | copy-start | bytes 571396
  6.3 8.6 %collective-permute-start = (bf16[176,768]{1,0:T(8,128)(2,1)S(1)}, bf16[176,768]{1,0:T(8,128)(2,1)S(1)}, u32[]{:S(2)}, u32[]{:S(2)}) collective-permute-start(bf16[176,768]{1,0:T(8,128)(2,1)S(1)} %get-tuple-element.38), channel_id=1, source_target_pairs={{0,4},{1,5},{2,6},{3,7},{4,0},{5,1},{6,2},{7,3},{8,12},{9,13},{10,... | collective-permute-start | bytes 811016 | tf_op jit(solution)/shard_map/ppermute | solution.py:274
  7.8 2.0 %copy-start.5 = (f32[1536]{0:T(1024)S(1)}, f32[1536]{0:T(1024)}, u32[]{:S(2)}) copy-start(f32[1536]{0:T(1024)} %param.15) | copy-start | bytes 18436
  7.8 17.7 %collective-permute-start.1 = (bf16[176,768]{1,0:T(8,128)(2,1)S(1)}, bf16[176,768]{1,0:T(8,128)(2,1)S(1)}, u32[]{:S(2)}, u32[]{:S(2)}) collective-permute-start(bf16[176,768]{1,0:T(8,128)(2,1)S(1)} %get-tuple-element.39), channel_id=1, source_target_pairs={{0,8},{1,9},{2,10},{3,11},{4,12},{5,13},{6,14},{7,15},{8,0},{9,1},... | collective-permute-start | bytes 811016 | tf_op jit(solution)/shard_map/ppermute | solution.py:274
  9.4 20.2 %collective-permute-start.2 = (bf16[176,768]{1,0:T(8,128)(2,1)S(1)}, bf16[176,768]{1,0:T(8,128)(2,1)S(1)}, u32[]{:S(2)}, u32[]{:S(2)}) collective-permute-start(bf16[176,768]{1,0:T(8,128)(2,1)S(1)} %get-tuple-element.40), channel_id=1, source_target_pairs={{0,12},{1,13},{2,14},{3,15},{4,8},{5,9},{6,10},{7,11},{8,4},{9,5},... | collective-permute-start | bytes 811016 | tf_op jit(solution)/shard_map/ppermute | solution.py:274
  9.8 0.7 copy-start.6
  10.6 19.0 %copy-start.1 = (bf16[48,1536]{1,0:T(8,128)(2,1)S(1)}, bf16[48,1536]{1,0:T(8,128)(2,1)}, u32[]{:S(2)}) copy-start(bf16[48,1536]{1,0:T(8,128)(2,1)} %last.1) | copy-start | bytes 442372
  30.3 10.4 %collective-permute-start.3 = (bf16[2,32,1536]{2,1,0:T(8,128)(2,1)S(1)}, bf16[2,32,1536]{2,1,0:T(8,128)(2,1)S(1)}, u32[]{:S(2)}, u32[]{:S(2)}) collective-permute-start(bf16[2,32,1536]{2,1,0:T(8,128)(2,1)S(1)} %get-tuple-element.42), channel_id=1, source_target_pairs={{0,16},{1,17},{2,18},{3,19},{4,20},{5,21},{6,22},{7,23},{8,24},{9,... | collective-permute-start | bytes 589832 | tf_op jit(solution)/shard_map/ppermute | solution.py:274
  30.9 14.0 %collective-permute-start.8 = (bf16[6,48,768]{2,1,0:T(8,128)(2,1)S(1)}, bf16[6,48,768]{2,1,0:T(8,128)(2,1)S(1)}, u32[]{:S(2)}, u32[]{:S(2)}) collective-permute-start(bf16[6,48,768]{2,1,0:T(8,128)(2,1)S(1)} %get-tuple-element.43.refs_4_), channel_id=1, source_target_pairs={{0,1},{1,0},{2,3},{3,2},{4,5},{5,4},{6,7},{7,6},{8,9},{9,8},{10,11... | collective-permute-start | bytes 1327112 | tf_op jit(solution)/shard_map/ppermute | solution.py:274
  31.0 11.2 %collective-permute-start.5 = (bf16[48,768]{1,0:T(8,128)(2,1)S(1)}, bf16[48,768]{1,0:T(8,128)(2,1)S(1)}, u32[]{:S(2)}, u32[]{:S(2)}) collective-permute-start(bf16[48,768]{1,0:T(8,128)(2,1)S(1)} %get-tuple-element.46), channel_id=1, source_target_pairs={{0,4},{1,5},{2,6},{3,7},{4,0},{5,1},{6,2},{7,3},{8,12},{9,13},{10,... | collective-permute-start | bytes 221192 | tf_op jit(solution)/shard_map/ppermute | solution.py:274
  32.2 10.1 %collective-permute-start.6 = (bf16[48,768]{1,0:T(8,128)(2,1)S(1)}, bf16[48,768]{1,0:T(8,128)(2,1)S(1)}, u32[]{:S(2)}, u32[]{:S(2)}) collective-permute-start(bf16[48,768]{1,0:T(8,128)(2,1)S(1)} %get-tuple-element.47), channel_id=1, source_target_pairs={{0,8},{1,9},{2,10},{3,11},{4,12},{5,13},{6,14},{7,15},{8,0},{9,1},... | collective-permute-start | bytes 221192 | tf_op jit(solution)/shard_map/ppermute | solution.py:274
  35.1 8.2 %collective-permute-start.7 = (bf16[48,768]{1,0:T(8,128)(2,1)S(1)}, bf16[48,768]{1,0:T(8,128)(2,1)S(1)}, u32[]{:S(2)}, u32[]{:S(2)}) collective-permute-start(bf16[48,768]{1,0:T(8,128)(2,1)S(1)} %get-tuple-element.48), channel_id=1, source_target_pairs={{0,12},{1,13},{2,14},{3,15},{4,8},{5,9},{6,10},{7,11},{8,4},{9,5},... | collective-permute-start | bytes 221192 | tf_op jit(solution)/shard_map/ppermute | solution.py:274
  40.7 13.1 %collective-permute-start.12 = (bf16[6,48,768]{2,1,0:T(8,128)(2,1)S(1)}, bf16[6,48,768]{2,1,0:T(8,128)(2,1)S(1)}, u32[]{:S(2)}, u32[]{:S(2)}) collective-permute-start(bf16[6,48,768]{2,1,0:T(8,128)(2,1)S(1)} %get-tuple-element.43.refs_4_), channel_id=1, source_target_pairs={{0,2},{1,3},{2,0},{3,1},{4,6},{5,7},{6,4},{7,5},{8,10},{9,11},{10,... | collective-permute-start | bytes 1327112 | tf_op jit(solution)/shard_map/ppermute | solution.py:274
  43.3 18.7 %collective-permute-start.13 = (bf16[6,48,768]{2,1,0:T(8,128)(2,1)S(1)}, bf16[6,48,768]{2,1,0:T(8,128)(2,1)S(1)}, u32[]{:S(2)}, u32[]{:S(2)}) collective-permute-start(bf16[6,48,768]{2,1,0:T(8,128)(2,1)S(1)} %shard_map.113.refs_5_), channel_id=1, source_target_pairs={{0,2},{1,3},{2,0},{3,1},{4,6},{5,7},{6,4},{7,5},{8,10},{9,11},{10,... | collective-permute-start | bytes 1327112 | tf_op jit(solution)/shard_map/ppermute | solution.py:274
  45.9 7.9 %collective-permute-start.10 = (bf16[2,32,1536]{2,1,0:T(8,128)(2,1)S(1)}, bf16[2,32,1536]{2,1,0:T(8,128)(2,1)S(1)}, u32[]{:S(2)}, u32[]{:S(2)}) collective-permute-start(bf16[2,32,1536]{2,1,0:T(8,128)(2,1)S(1)} %get-tuple-element.56.refs_0_), channel_id=1, source_target_pairs={{0,8},{1,9},{2,10},{3,11},{4,12},{5,13},{6,14},{7,15},{8,0},{9,1},... | collective-permute-start | bytes 589832 | tf_op jit(solution)/shard_map/ppermute | solution.py:274
  46.0 7.8 %collective-permute-start.9 = (bf16[2,32,1536]{2,1,0:T(8,128)(2,1)S(1)}, bf16[2,32,1536]{2,1,0:T(8,128)(2,1)S(1)}, u32[]{:S(2)}, u32[]{:S(2)}) collective-permute-start(bf16[2,32,1536]{2,1,0:T(8,128)(2,1)S(1)} %get-tuple-element.56.refs_0_), channel_id=1, source_target_pairs={{0,4},{1,5},{2,6},{3,7},{4,0},{5,1},{6,2},{7,3},{8,12},{9,13},{10,... | collective-permute-start | bytes 589832 | tf_op jit(solution)/shard_map/ppermute | solution.py:274
  63.0 0.7 copy-start.10
  63.0 2.8 %collective-permute-start.15 = (bf16[2,6,48,768]{3,2,1,0:T(8,128)(2,1)}, bf16[2,6,48,768]{3,2,1,0:T(8,128)(2,1)}, u32[]{:S(2)}, u32[]{:S(2)}) collective-permute-start(bf16[2,6,48,768]{3,2,1,0:T(8,128)(2,1)} %pad_maximum_fusion), channel_id=1, source_target_pairs={{0,1},{1,0},{2,3},{3,2},{4,5},{5,4},{6,7},{7,6},{8,9},{9,8},{10,11... | collective-permute-start | bytes 2654216 | tf_op jit(solution)/shard_map/ppermute | solution.py:274
  63.7 8.5 %collective-permute-start.14 = (bf16[6,48,768]{2,1,0:T(8,128)(2,1)S(1)}, bf16[6,48,768]{2,1,0:T(8,128)(2,1)S(1)}, u32[]{:S(2)}, u32[]{:S(2)}) collective-permute-start(bf16[6,48,768]{2,1,0:T(8,128)(2,1)S(1)} %shard_map.113.refs_5_), channel_id=1, source_target_pairs={{0,1},{1,0},{2,3},{3,2},{4,5},{5,4},{6,7},{7,6},{8,9},{9,8},{10,11... | collective-permute-start | bytes 1327112 | tf_op jit(solution)/shard_map/ppermute | solution.py:274
  64.0 8.2 %collective-permute-start.11 = (bf16[2,32,1536]{2,1,0:T(8,128)(2,1)S(1)}, bf16[2,32,1536]{2,1,0:T(8,128)(2,1)S(1)}, u32[]{:S(2)}, u32[]{:S(2)}) collective-permute-start(bf16[2,32,1536]{2,1,0:T(8,128)(2,1)S(1)} %get-tuple-element.56.refs_0_), channel_id=1, source_target_pairs={{0,12},{1,13},{2,14},{3,15},{4,8},{5,9},{6,10},{7,11},{8,4},{9,5},... | collective-permute-start | bytes 589832 | tf_op jit(solution)/shard_map/ppermute | solution.py:274
  75.9 7.0 %collective-permute-start.16 = (bf16[2,32,1536]{2,1,0:T(8,128)(2,1)S(1)}, bf16[2,32,1536]{2,1,0:T(8,128)(2,1)S(1)}, u32[]{:S(2)}, u32[]{:S(2)}) collective-permute-start(bf16[2,32,1536]{2,1,0:T(8,128)(2,1)S(1)} %get-tuple-element.60), channel_id=1, source_target_pairs={{0,4},{1,5},{2,6},{3,7},{4,0},{5,1},{6,2},{7,3},{8,12},{9,13},{10,... | collective-permute-start | bytes 589832 | tf_op jit(solution)/shard_map/ppermute | solution.py:274
  77.3 7.8 %collective-permute-start.17 = (bf16[2,32,1536]{2,1,0:T(8,128)(2,1)S(1)}, bf16[2,32,1536]{2,1,0:T(8,128)(2,1)S(1)}, u32[]{:S(2)}, u32[]{:S(2)}) collective-permute-start(bf16[2,32,1536]{2,1,0:T(8,128)(2,1)S(1)} %get-tuple-element.61), channel_id=1, source_target_pairs={{0,8},{1,9},{2,10},{3,11},{4,12},{5,13},{6,14},{7,15},{8,0},{9,1},... | collective-permute-start | bytes 589832 | tf_op jit(solution)/shard_map/ppermute | solution.py:274
  77.3 10.6 %collective-permute-start.18 = (bf16[2,32,1536]{2,1,0:T(8,128)(2,1)S(1)}, bf16[2,32,1536]{2,1,0:T(8,128)(2,1)S(1)}, u32[]{:S(2)}, u32[]{:S(2)}) collective-permute-start(bf16[2,32,1536]{2,1,0:T(8,128)(2,1)S(1)} %get-tuple-element.62), channel_id=1, source_target_pairs={{0,12},{1,13},{2,14},{3,15},{4,8},{5,9},{6,10},{7,11},{8,4},{9,5},... | collective-permute-start | bytes 589832 | tf_op jit(solution)/shard_map/ppermute | solution.py:274

commit v5 on v4

--- a/solution.py
+++ b/solution.py
@@ -52,7 +52,8 @@
         return self.ref[2 * self.size + source * self.slots + slot]
 
 
-def own_columns(highs, weights, owner, width):
+def own_columns(highs, weights, owner):
+    width = weights.shape[1] // 2
     run = width // (highs * QUAD)
     parts = [
         weights[:, pl.ds(half * width + (high * QUAD + owner) * run, run)]
@@ -62,77 +63,40 @@
     return jnp.concatenate(parts, axis=1)
 
 
-def send_kernel(sources, place, packed, weights, frames, *refs):
-    outs, buf = refs[:-1], refs[-1]
-    tables = Tables(packed, sources)
+def send_kernel(place, packed, frames, out):
+    tables = Tables(packed, out.shape[0])
     me = place[0]
-    highs = sources // QUAD
-    long, width = frames.shape[1:]
-    wide = outs[0].shape[1]
-    for owner in range(QUAD):
-        buf[owner] = own_columns(highs, weights, owner, width)
-    for number, out in enumerate(outs):
-        for far in range(highs):
-            target = jnp.bitwise_xor(me, far * QUAD + number)
-            found = jnp.int32(0)
-            for slot in range(tables.slots):
-                found = jnp.where(tables.live_for(me, slot, target), slot, found)
-            for half in range(width // wide):
-                start = (far * (width // wide) + half) * long
-                out[start : start + long, :] = frames[found, :, half * wide : half * wide + wide]
-        start = highs * (width // wide) * long
-        out[start:, :] = buf[jnp.bitwise_xor(lax.rem(me, QUAD), number)]
-
-
-def fetch(out, number, ref, far):
-    long, width = out.shape[1:]
-    wide = ref.shape[1]
-    for half in range(width // wide):
-        start = (far * (width // wide) + half) * long
-        out[number, :, half * wide : half * wide + wide] = ref[start : start + long, :]
-
-
-def merge_kernel(sources, place, packed, last, *refs):
-    arrived, outs, piece = refs[:QUAD], refs[QUAD:-1], refs[-1]
-    tables = Tables(packed, sources)
-    me = place[0]
-    depth, wide = piece.shape[1:]
-    for far, out in enumerate(outs, 1):
-        long = out.shape[1]
-        for number, ref in enumerate(arrived):
-            source = jnp.bitwise_xor(me, number)
-            target = jnp.bitwise_xor(me, far * QUAD)
-            start = jnp.int32(-1)
-            for slot in range(tables.slots):
-                hit = tables.live_for(source, slot, target)
-                start = jnp.where(hit, tables.offset(source, slot), start)
-
-            @pl.when(start >= 0)
-            def _():
-                fetch(out, start // long, ref, far)
-
-    for number, ref in enumerate(arrived):
-        piece[number] = ref[ref.shape[0] - depth :, :]
-    for half in range(piece.shape[0] - QUAD):
-        piece[QUAD + half] = last[:, half * wide : half * wide + wide]
+
+    def send(target, carry):
+        found = jnp.int32(0)
+        for slot in range(tables.slots):
+            found = jnp.where(tables.live_for(me, slot, target), slot, found)
+        out[target] = frames[found]
+        return carry
+
+    lax.fori_loop(0, out.shape[0], send, 0)
 
 
 def split_kernel(highs, place, weights, *refs):
     outs, buf = refs[:-1], refs[-1]
     for owner in range(QUAD):
-        buf[owner] = own_columns(highs, weights, owner, weights.shape[1] // 3)
+        buf[owner] = own_columns(highs, weights, owner)
     for number, out in enumerate(outs):
         out[...] = buf[jnp.bitwise_xor(lax.rem(place[0], QUAD), number)]
 
 
-def stack_kernel(both, *refs):
-    columns, piece = refs[:-1], refs[-1]
-    wide = piece.shape[2]
-    last = both.at[:, both.shape[1] // 3 * 2 :]
-    for number, ref in enumerate(columns):
-        piece[number] = ref[...]
-    for half in range(piece.shape[0] - QUAD):
-        piece[QUAD + half] = last[:, half * wide : half * wide + wide]
+def stack_kernel(*refs):
+    parts, out = refs[:-1], refs[-1]
+    wide = out.shape[2]
+    at = 0
+    for ref in parts:
+        if len(ref.shape) == 3:
+            out[at : at + ref.shape[0]] = ref[...]
+            at += ref.shape[0]
+        else:
+            for first in range(0, ref.shape[1], wide):
+                out[at] = ref[:, first : first + wide]
+                at += 1
 
 
 def table_kernel(source_count, long, place, packed, small, sources, lens, table, gain):
@@ -165,23 +129,11 @@
             table[...] = jnp.concatenate(parts, axis=1)
 
 
-def norm_kernel(place, sources, lens, gain, *refs):
-    near, far, (kept, normed) = refs[:QUAD], refs[QUAD:-2], refs[-2:]
+def norm_kernel(sources, lens, gain, arrived, kept, normed):
     for number in range(kept.shape[0]):
-        shift = jnp.bitwise_xor(sources[number], place[0])
-        for other, ref in enumerate(near):
-
-            @pl.when(shift == other)
-            def _():
-                fetch(kept, number, ref, 0)
-
-        for other, ref in enumerate(far, 1):
-
-            @pl.when(shift // QUAD == other)
-            def _():
-                kept[number] = ref[number]
-
-        wide = kept[number].astype(F32)
+        rows = arrived[sources[number]]
+        kept[number] = rows
+        wide = rows.astype(F32)
         mean = jnp.mean(wide, axis=1, keepdims=True)
         centred = wide - mean
         var = jnp.mean(centred * centred, axis=1, keepdims=True)
@@ -213,29 +165,32 @@
     return total
 
 
-def main_kernel(pieces, where, kept, table, *refs):
+def main_kernel(layout, where, kept, table, *refs):
+    pieces = max(len(layout), 2)
+    chans = table.shape[1]
+    taps = table[: table.shape[0] - 2, :]
+    scale, shift = table[table.shape[0] - 2 : table.shape[0] - 1, :], table[table.shape[0] - 1 :, :]
     normed, weights = refs[:QUAD], refs[QUAD : QUAD + pieces]
     own, outs = refs[QUAD + pieces], refs[QUAD + pieces + 1 : 2 * QUAD + pieces]
     rows_buf, in_buf, out_buf, glu_buf, act_buf = refs[2 * QUAD + pieces :]
     recv, long, width = kept.shape
     tall = recv * long
-    chans = table.shape[1]
-    taps = table[: table.shape[0] - 2, :]
-    scale, shift = table[table.shape[0] - 2 : table.shape[0] - 1, :], table[table.shape[0] - 1 :, :]
     for number, ref in enumerate(normed):
         rows_buf[pl.ds(number * tall, tall), :] = ref[...].reshape(tall, width)
-    if pieces == 2:
-        w_in, w_out = weights
-    else:
+    if layout:
         w_in, w_out = in_buf, out_buf
         depth, wide = weights[0].shape[1:]
-        for number, ref in enumerate(weights):
-            for inner in range(QUAD):
-                start = pl.multiple_of(where[number, inner] * depth, 16)
-                in_buf[pl.ds(start, depth), :] = ref[inner]
-            start = pl.multiple_of(where[number, QUAD] * depth, 16)
-            for half in range(width // wide):
-                out_buf[pl.ds(start, depth), half * wide : half * wide + wide] = ref[QUAD + half]
+        for ref, slabs in zip(weights, layout):
+            for at, (kind, other, number) in enumerate(slabs):
+                if kind == "in":
+                    start = pl.multiple_of(where[other, number] * depth, 16)
+                    in_buf[pl.ds(start, depth), :] = ref[at]
+                else:
+                    start = pl.multiple_of(where[other, QUAD] * depth, 16)
+                    first = number * wide
+                    out_buf[pl.ds(start, depth), first : first + wide] = ref[at]
+    else:
+        w_in, w_out = weights
     glu_in = jnp.dot(rows_buf[...], w_in[...], preferred_element_type=F32)
     glu_buf[...] = glu_in[:, :chans] * jax.nn.sigmoid(glu_in[:, chans:])
 
@@ -286,18 +241,14 @@
     bits = [1 << at for at in range((highs * fsdp_count).bit_length() - 1)]
     chip_bits = [bit for bit in reversed(bits) if 1 < bit < fsdp_count]
 
-    both = jnp.concatenate([w_in, w_out], axis=1)
-    far_rows = [swap(both, high=mask) for mask in range(1, highs)]
-
-    near = call(
-        functools.partial(send_kernel, dp_count),
-        [like(BF16, highs * count * long + depth, wide)] * QUAD,
-        [SMEM, SMEM, VMEM, VMEM],
-        [VMEM] * QUAD,
-        (place, packed, w_in, frames[0]),
-        [like(BF16, QUAD, depth, wide)],
-    )
-    near = quad_swap(near)
+    send = call(
+        send_kernel,
+        like(BF16, dp_count, long, width),
+        [SMEM, SMEM, VMEM],
+        VMEM,
+        (place, packed, frames[0]),
+    )
+    arrived = lax.all_to_all(send, "dp", split_axis=0, concat_axis=0, tiled=True)
     sources, lens, table, gain = call(
         functools.partial(table_kernel, dp_count, long),
         [like(jnp.int32, recv)] * 2 + [like(F32, taps + 2, chans), like(F32, 1, width)],
@@ -306,72 +257,90 @@
         (place, packed, small),
     )
     utts = like(BF16, recv, long, width)
-    block = like(BF16, QUAD + count, depth, wide)
-    *far, piece = call(
-        functools.partial(merge_kernel, dp_count),
-        [utts] * (highs - 1) + [block],
-        [SMEM] * 2 + [VMEM] * (1 + QUAD),
-        [VMEM] * highs,
-        (gated(place, (lens, gain)), packed, w_out, *near),
-    )
-    pieces = [piece]
-    shifts = [mask * fsdp_count for mask in range(highs)]
-    far_rows = gated(far_rows, far)
-    far = [swap(part, high=mask) for mask, part in enumerate(far, 1)]
-    for part in far_rows:
+    def stack(*parts):
+        slabs = sum(part.size // (depth * wide) for part in parts)
+        return call(
+            stack_kernel, like(BF16, slabs, depth, wide), [VMEM] * len(parts), VMEM, parts
+        )
+
+    def share_columns(rows):
         columns = call(
             functools.partial(split_kernel, highs),
             [like(BF16, depth, wide)] * QUAD,
             [SMEM, VMEM],
             [VMEM] * QUAD,
-            (place, part),
+            (place, rows),
             [like(BF16, QUAD, depth, wide)],
         )
-        pieces.append(
-            call(
-                stack_kernel,
-                block,
-                [VMEM] * (1 + QUAD),
-                VMEM,
-                (part, *gated(quad_swap(columns), far)),
-            )
-        )
-    early = len(pieces)
-    cored = [swap(part, fsdp=1) for part in pieces]
-    far = gated(far, (pieces, cored[:1]))
-    for bit in chip_bits:
-        pieces = pieces + [swap(part, fsdp=bit) for part in pieces]
-        shifts = shifts + [shift ^ bit for shift in shifts]
-
+        return stack(*quad_swap(columns))
+
+    ins = {0: share_columns(gated(w_in, send))}
+    far_in = [swap(ins[0], high=mask) for mask in range(1, highs)]
+    late_out = gated(w_out, ins[0])
+    outs = {0: w_out}
+
+    def share_chips(shifts):
+        for bit in chip_bits:
+            for shift in list(shifts):
+                ins[shift ^ bit] = swap(ins[shift], fsdp=bit)
+                outs[shift ^ bit] = swap(outs[shift], fsdp=bit)
+                shifts.append(shift ^ bit)
+
+    share_chips([0])
+    early_cores = [swap(ins[shift], fsdp=1) for shift in ins]
+    far_out = [swap(late_out, high=mask) for mask in range(1, highs)]
+    arrived = gated(arrived, early_cores)
     kept, normed = call(
         norm_kernel,
         [utts, utts],
-        [SMEM] * 3 + [VMEM] * (QUAD + highs),
+        [SMEM] * 2 + [VMEM] * 2,
         [VMEM, VMEM],
-        (place, sources, lens, gain, *near, *far),
-    )
+        (sources, lens, gain, arrived),
+    )
+    for mask, (rows, last) in enumerate(zip(far_in, far_out), 1):
+        outs[mask * fsdp_count] = last
+        ins[mask * fsdp_count] = rows
     normed = quad_swap([normed] * QUAD)
-    late = pieces[early:]
-    crossed = swap(jnp.stack(gated(late, normed[1:3])), fsdp=1)
-    pieces = pieces + cored + [crossed[at] for at in range(len(late))]
-    shifts = shifts + [shift ^ 1 for shift in shifts]
-
-    out_rows = line ^ jnp.array(shifts)
+    share_chips([mask * fsdp_count for mask in range(1, highs)])
+    early = [shift for shift in ins if shift < fsdp_count]
+    late = [shift for shift in ins if shift >= fsdp_count]
+    pieces = [ins[shift] for shift in early]
+    last = [ins[shift] for shift in late] + [outs[shift] for shift in outs]
+    pieces.append(stack(*gated(last, normed)))
+    pieces = pieces + early_cores + [swap(pieces[-1], fsdp=1)]
+    layout = []
+    for core in range(2):
+        for group in [[shift] for shift in early] + [late]:
+            layout.append([("in", at ^ core, number) for at in group for number in range(QUAD)])
+        layout[-1] += [("out", at ^ core, half) for at in outs for half in range(count)]
+
+    out_rows = line ^ jnp.arange(highs * fsdp_count)
     in_rows = out_rows // fsdp_count * QUAD
     in_rows = in_rows[:, None] + (quad ^ jnp.arange(QUAD))[None, :]
     in_rows = in_rows * fsdp_count + (out_rows % fsdp_count)[:, None]
     where = jnp.concatenate([in_rows, out_rows[:, None]], 1).astype(jnp.int32)
     if depth % 16:
-        together = jnp.stack(pieces)
-        flat = together[:, :QUAD].reshape(-1, depth, wide)
+        slabs = {
+            name: part[at]
+            for part, names in zip(pieces, layout)
+            for at, name in enumerate(names)
+        }
+        sides = range(highs * fsdp_count)
+        flat = jnp.stack([slabs["in", at, number] for at in sides for number in range(QUAD)])
         all_in = jnp.zeros_like(flat).at[where[:, :QUAD].reshape(-1)].set(flat)
-        flat = together[:, QUAD:].transpose(0, 2, 1, 3).reshape(-1, depth, width)
+        flat = jnp.stack(
+            [
+                jnp.concatenate([slabs["out", at, half] for half in range(count)], axis=1)
+                for at in sides
+            ]
+        )
         all_out = jnp.zeros_like(flat).at[where[:, QUAD]].set(flat)
         pieces = [all_in.reshape(width, wide), all_out.reshape(chans, width)]
+        layout = []
 
     tall = QUAD * recv * long
     partial_sums = call(
-        functools.partial(main_kernel, len(pieces)),
+        functools.partial(main_kernel, layout),
         [like(F32, recv, long, width)] + [utts] * (QUAD - 1),
         [SMEM] + [VMEM] * (2 + QUAD + len(pieces)),
         [VMEM] * QUAD,

time: 88.9 us -> 94 us (1.057)
  waiting for transfers between devices: 53.8 us -> 37.5 us
  starting transfers between devices: 20.5 us -> 32.6 us
  local copies, waits for them, and re-layouts: 2.86 us -> 12.3 us
  other arithmetic: 3.23 us -> 1.79 us
  Pallas kernels: 8.06 us -> 9.11 us
    ppermute x19 -> x18, waiting for transfers between devices: 53.8 us -> 37.5 us  [swap(): lax.ppermute(array, ('dp', 'fsdp'), [(at, at ^ mask) for at in range(devi...]
    unnamed x22 -> x40, local copies, waits for them, and re-layouts: 1.36 us -> 12.1 us
    all_to_all x0 -> x1, starting transfers between devices: none -> 7.42 us  [shards(): lax.all_to_all(send, 'dp', split_axis=0, concat_axis=0, tiled=True)]
    ppermute x19 -> x18, starting transfers between devices: 20.5 us -> 25.2 us  [swap(): lax.ppermute(array, ('dp', 'fsdp'), [(at, at ^ mask) for at in range(devi...]
    squeeze x1 -> x0, local copies, waits for them, and re-layouts: 1.2 us -> none  [shards(): pieces = pieces + cored + [crossed[at] for at in range(len(late))]]
    concatenate x1 -> x0, other arithmetic: 1.14 us -> none  [shards(): both = jnp.concatenate([w_in, w_out], axis=1)]
    pallas_call x7, Pallas kernels: 8.06 us -> 9.11 us  [call(): pl.pallas_call(kernel, out_shape=out_shape, in_specs=in_specs, out_specs=...]
    another operation x1 -> x0, other arithmetic: 1.01 us -> none  [shards(): crossed = swap(jnp.stack(gated(late, normed[1:3])), fsdp=1)]
  transfers between devices with their start and end apart: 19 -> 19, of which waited for: 12 -> 10; matrix products, arithmetic and copies ran while one was open for 2% -> 0% of each run, Pallas kernels for 5% -> 3%
where the time goes in v5:
time: 94 us; the launch traced here: 93.5 us
  waiting for transfers between devices  37.5 us (40%)
  starting transfers between devices  32.6 us (35%)
  local copies, waits for them, and re-layouts  12.3 us (13%)
  Pallas kernels  9.11 us (10%)
  other arithmetic  1.79 us (2%)
    ppermute x18, waiting for transfers between devices, swap(): lax.ppermute(array, ('dp', 'fsdp'), [(at, at ^ mask) for at in range(devi...  37.5 us
    ppermute x18, starting transfers between devices, swap(): lax.ppermute(array, ('dp', 'fsdp'), [(at, at ^ mask) for at in range(devi...  25.2 us
    unnamed x40, local copies, waits for them, and re-layouts  12.1 us
    pallas_call x7, Pallas kernels, call(): pl.pallas_call(kernel, out_shape=out_shape, in_specs=in_specs, out_specs=...  9.11 us
    all_to_all x1, starting transfers between devices, shards(): lax.all_to_all(send, 'dp', split_axis=0, concat_axis=0, tiled=True)  7.42 us
  transfers between devices with their start and end apart: 19, of which 10 were waited for; matrix products, arithmetic and copies ran while one was open for 0% of the time, Pallas kernels for 3%

profile of v5, /device:TPU:0, one launch (start us, length us, event | category | flops | bytes accessed | tf_op | source)
XLA Modules:
  0.0 93.5 jit_solution(1881719343344275332)
XLA Ops:
  0.9 1.1 %copy-done = bf16[1,6,32,1536]{3,2,1,0:T(8,128)(2,1)S(1)} copy-done((bf16[1,6,32,1536]{3,2,1,0:T(8,128)(2,1)S(1)}, bf16[1,6,32,1536]{3,2,1,0:T(8,128)(2,1)}, u32[]{:S(2)}) %copy-start) | copy-done | bytes 589848
  2.0 1.6 %shard_map.101 = bf16[8,32,1536]{2,1,0:T(8,128)(2,1)} custom-call(s32[1]{0:T(128)} %bitcast.place, s32[144]{0:T(256)S(1)} %reshape.70.packed, bf16[6,32,1536]{2,1,0:T(8,128)(2,1)S(1)} %bitcast.4), custom_call_target="tpu_custom_call" | custom-call | bytes 1376836 | tf_op jit(solution)/shard_map/pallas_call | solution.py:21
  3.7 7.4 %all-to-all-start = ((bf16[8,32,1536]{2,1,0:T(8,128)(2,1)}), bf16[8,32,1536]{2,1,0:T(8,128)(2,1)S(1)}, u32[]{:S(2)}, u32[]{:S(2)}) async-start(bf16[8,32,1536]{2,1,0:T(8,128)(2,1)} %shard_map.101), calls=%async_computation | async-start | bytes 1572864 | tf_op jit(solution)/shard_map/all_to_all | solution.py:251
  11.2 2.1 %collective-permute-start = (bf16[48,768]{1,0:T(8,128)(2,1)S(1)}, bf16[48,768]{1,0:T(8,128)(2,1)S(1)}, u32[]{:S(2)}, u32[]{:S(2)}) collective-permute-start(bf16[48,768]{1,0:T(8,128)(2,1)S(1)} %get-tuple-element.33), channel_id=1, source_target_pairs={{0,4},{1,5},{2,6},{3,7},{4,0},{5,1},{6,2},{7,3},{8,12},{9,13},{10,... | collective-permute-start | bytes 221192 | tf_op jit(solution)/shard_map/ppermute | solution.py:229
  13.3 1.5 %collective-permute-start.1 = (bf16[48,768]{1,0:T(8,128)(2,1)S(1)}, bf16[48,768]{1,0:T(8,128)(2,1)S(1)}, u32[]{:S(2)}, u32[]{:S(2)}) collective-permute-start(bf16[48,768]{1,0:T(8,128)(2,1)S(1)} %get-tuple-element.34), channel_id=1, source_target_pairs={{0,8},{1,9},{2,10},{3,11},{4,12},{5,13},{6,14},{7,15},{8,0},{9,1},... | collective-permute-start | bytes 221192 | tf_op jit(solution)/shard_map/ppermute | solution.py:229
  14.9 5.1 %collective-permute-done.refs_1_ = bf16[48,768]{1,0:T(8,128)(2,1)S(1)} collective-permute-done((bf16[48,768]{1,0:T(8,128)(2,1)S(1)}, bf16[48,768]{1,0:T(8,128)(2,1)S(1)}, u32[]{:S(2)}, u32[]{:S(2)}) %collective-permute-start) | collective-permute-done | bytes 73760 | tf_op jit(solution)/shard_map/ppermute | solution.py:229
  19.9 6.3 %collective-permute-done.1.refs_2_ = bf16[48,768]{1,0:T(8,128)(2,1)S(1)} collective-permute-done((bf16[48,768]{1,0:T(8,128)(2,1)S(1)}, bf16[48,768]{1,0:T(8,128)(2,1)S(1)}, u32[]{:S(2)}, u32[]{:S(2)}) %collective-permute-start.1) | collective-permute-done | bytes 73760 | tf_op jit(solution)/shard_map/ppermute | solution.py:229
  26.2 1.9 %collective-permute-done.2.refs_3_ = bf16[48,768]{1,0:T(8,128)(2,1)S(1)} collective-permute-done((bf16[48,768]{1,0:T(8,128)(2,1)S(1)}, bf16[48,768]{1,0:T(8,128)(2,1)S(1)}, u32[]{:S(2)}, u32[]{:S(2)}) %collective-permute-start.2) | collective-permute-done | bytes 73760 | tf_op jit(solution)/shard_map/ppermute | solution.py:229
  28.2 1.6 %collective-permute-start.4 = (bf16[4,48,768]{2,1,0:T(8,128)(2,1)S(1)}, bf16[4,48,768]{2,1,0:T(8,128)(2,1)S(1)}, u32[]{:S(2)}, u32[]{:S(2)}) collective-permute-start(bf16[4,48,768]{2,1,0:T(8,128)(2,1)S(1)} %shard_map.103.refs_4_), channel_id=1, source_target_pairs={{0,2},{1,3},{2,0},{3,1},{4,6},{5,7},{6,4},{7,5},{8,10},{9,11},{10,... | collective-permute-start | bytes 884744 | tf_op jit(solution)/shard_map/ppermute | solution.py:229
  29.7 4.4 %collective-permute-start.9 = (bf16[4,48,768]{2,1,0:T(8,128)(2,1)S(1)}, bf16[4,48,768]{2,1,0:T(8,128)(2,1)S(1)}, u32[]{:S(2)}, u32[]{:S(2)}) collective-permute-start(bf16[4,48,768]{2,1,0:T(8,128)(2,1)S(1)} %shard_map.103.refs_4_), channel_id=1, source_target_pairs={{0,16},{1,17},{2,18},{3,19},{4,20},{5,21},{6,22},{7,23},{8,24},{9,... | collective-permute-start | bytes 884744 | tf_op jit(solution)/shard_map/ppermute | solution.py:229
  34.1 0.9 collective-permute-done.4.refs_5_
  35.0 1.5 %collective-permute-start.11 = (bf16[48,1536]{1,0:T(8,128)(2,1)}, bf16[48,1536]{1,0:T(8,128)(2,1)S(1)}, u32[]{:S(2)}, u32[]{:S(2)}) collective-permute-start(bf16[48,1536]{1,0:T(8,128)(2,1)} %refs_2_), channel_id=1, source_target_pairs={{0,2},{1,3},{2,0},{3,1},{4,6},{5,7},{6,4},{7,5},{8,10},{9,11},{10,... | collective-permute-start | bytes 442376 | tf_op jit(solution)/shard_map/ppermute | solution.py:229
  36.6 5.0 %collective-permute-start.12 = (bf16[48,1536]{1,0:T(8,128)(2,1)}, bf16[48,1536]{1,0:T(8,128)(2,1)}, u32[]{:S(2)}, u32[]{:S(2)}) collective-permute-start(bf16[48,1536]{1,0:T(8,128)(2,1)} %refs_2_), channel_id=1, source_target_pairs={{0,16},{1,17},{2,18},{3,19},{4,20},{5,21},{6,22},{7,23},{8,24},{9,... | collective-permute-start | bytes 442376 | tf_op jit(solution)/shard_map/ppermute | solution.py:229
  41.6 8.0 %collective-permute-done.9.refs_0_ = bf16[4,48,768]{2,1,0:T(8,128)(2,1)S(1)} collective-permute-done((bf16[4,48,768]{2,1,0:T(8,128)(2,1)S(1)}, bf16[4,48,768]{2,1,0:T(8,128)(2,1)S(1)}, u32[]{:S(2)}, u32[]{:S(2)}) %collective-permute-start.9) | collective-permute-done | bytes 294944 | tf_op jit(solution)/shard_map/ppermute | solution.py:229
  50.2 1.8 %shard_map.100 = (s32[2]{0:T(128)S(1)}, s32[2]{0:T(128)S(1)}, f32[33,384]{1,0:T(8,128)S(1)}, f32[1,1536]{1,0:T(1,128)S(1)}) custom-call(s32[1]{0:T(128)} %bitcast.place, s32[144]{0:T(256)S(1)} %reshape.70.packed, f32[34,1536]{1,0:T(8,128)S(1)} %pad_maximum_fusion.small), custom_call_target="tpu_custom_call" | custom-call | bytes 266324 | tf_op jit(solution)/shard_map/pallas_call | solution.py:21
  54.1 2.0 %collective-permute-start.7 = (bf16[2,32,1536]{2,1,0:T(8,128)(2,1)S(1)}, bf16[2,32,1536]{2,1,0:T(8,128)(2,1)S(1)}, u32[]{:S(2)}, u32[]{:S(2)}) collective-permute-start(bf16[2,32,1536]{2,1,0:T(8,128)(2,1)S(1)} %get-tuple-element.39.refs_0_), channel_id=1, source_target_pairs={{0,8},{1,9},{2,10},{3,11},{4,12},{5,13},{6,14},{7,15},{8,0},{9,1},... | collective-permute-start | bytes 589832 | tf_op jit(solution)/shard_map/ppermute | solution.py:229
  56.8 1.5 %collective-permute-start.6 = (bf16[2,32,1536]{2,1,0:T(8,128)(2,1)S(1)}, bf16[2,32,1536]{2,1,0:T(8,128)(2,1)S(1)}, u32[]{:S(2)}, u32[]{:S(2)}) collective-permute-start(bf16[2,32,1536]{2,1,0:T(8,128)(2,1)S(1)} %get-tuple-element.39.refs_0_), channel_id=1, source_target_pairs={{0,4},{1,5},{2,6},{3,7},{4,0},{5,1},{6,2},{7,3},{8,12},{9,13},{10,... | collective-permute-start | bytes 589832 | tf_op jit(solution)/shard_map/ppermute | solution.py:229
  58.9 1.5 %collective-permute-start.13 = (bf16[48,1536]{1,0:T(8,128)(2,1)}, bf16[48,1536]{1,0:T(8,128)(2,1)S(1)}, u32[]{:S(2)}, u32[]{:S(2)}) collective-permute-start(bf16[48,1536]{1,0:T(8,128)(2,1)} %collective-permute-done.12.refs_4_), channel_id=1, source_target_pairs={{0,2},{1,3},{2,0},{3,1},{4,6},{5,7},{6,4},{7,5},{8,10},{9,11},{10,... | collective-permute-start | bytes 442376 | tf_op jit(solution)/shard_map/ppermute | solution.py:229
  60.4 3.9 %collective-permute-done.13.refs_5_ = bf16[48,1536]{1,0:T(8,128)(2,1)S(1)} collective-permute-done((bf16[48,1536]{1,0:T(8,128)(2,1)}, bf16[48,1536]{1,0:T(8,128)(2,1)S(1)}, u32[]{:S(2)}, u32[]{:S(2)}) %collective-permute-start.13) | collective-permute-done | bytes 147488 | tf_op jit(solution)/shard_map/ppermute | solution.py:229
  66.3 0.9 copy-done.13
  67.2 1.1 %shard_map.105.refs_6_ = bf16[16,48,768]{2,1,0:T(8,128)(2,1)S(1)} custom-call(bf16[4,48,768]{2,1,0:T(8,128)(2,1)S(1)} %collective-permute-done.9.refs_0_, bf16[4,48,768]{2,1,0:T(8,128)(2,1)S(1)} %collective-permute-done.10.refs_1_, bf16[48,1536]{1,0:T(8,128)(2,1)} %refs_2_, bf16[48,1536]{1,0:T(8,128)(2,1)S(1)} %copy-done.13, ...), custom_call_target="tpu_custom_call" | custom-call | bytes 2359296 | tf_op jit(solution)/shard_map/pallas_call | solution.py:21
  68.6 2.6 %collective-permute-done.14.refs_9_ = bf16[16,48,768]{2,1,0:T(8,128)(2,1)S(1)} collective-permute-done((bf16[16,48,768]{2,1,0:T(8,128)(2,1)S(1)}, bf16[16,48,768]{2,1,0:T(8,128)(2,1)S(1)}, u32[]{:S(2)}, u32[]{:S(2)}) %collective-permute-start.14) | collective-permute-done | bytes 1179680 | tf_op jit(solution)/shard_map/ppermute | solution.py:229
  71.2 0.9 copy-done.3
  72.1 0.9 copy-done.5
  73.1 0.9 copy-done.7
  74.0 0.9 copy-done.9
  74.9 0.9 copy-done.11
  76.7 3.7 %shard_map.106 = (f32[2,32,1536]{2,1,0:T(8,128)S(1)}, bf16[2,32,1536]{2,1,0:T(8,128)(2,1)S(1)}, bf16[2,32,1536]{2,1,0:T(8,128)(2,1)S(1)}, bf16[2,32,1536]{2,1,0:T(8,128)(2,1)S(1)}) custom-call(s32[8,5]{1,0:T(8,128)S(1)} %pad_add_fusion.1.where, bf16[2,32,1536]{2,1,0:T(8,128)(2,1)S(1)} %copy-done.3, f32[33,384]{1,0:T(8,128)S(1)} %copy-done.15, ...), custom_call_target="tpu_custom_call" | custom-call | flops 905969664 | bytes 10471072 | tf_op jit(solution)/shard_map/pallas_call | solution.py:21
  81.0 2.9 %collective-permute-start.17 = (bf16[2,32,1536]{2,1,0:T(8,128)(2,1)S(1)}, bf16[2,32,1536]{2,1,0:T(8,128)(2,1)S(1)}, u32[]{:S(2)}, u32[]{:S(2)}) collective-permute-start(bf16[2,32,1536]{2,1,0:T(8,128)(2,1)S(1)} %get-tuple-element.50), channel_id=1, source_target_pairs={{0,12},{1,13},{2,14},{3,15},{4,8},{5,9},{6,10},{7,11},{8,4},{9,5},... | collective-permute-start | bytes 589832 | tf_op jit(solution)/shard_map/ppermute | solution.py:229
  84.0 3.4 %collective-permute-done.15 = bf16[2,32,1536]{2,1,0:T(8,128)(2,1)S(1)} collective-permute-done((bf16[2,32,1536]{2,1,0:T(8,128)(2,1)S(1)}, bf16[2,32,1536]{2,1,0:T(8,128)(2,1)S(1)}, u32[]{:S(2)}, u32[]{:S(2)}) %collective-permute-start.15) | collective-permute-done | bytes 196640 | tf_op jit(solution)/shard_map/ppermute | solution.py:229
  87.4 1.4 %collective-permute-done.16 = bf16[2,32,1536]{2,1,0:T(8,128)(2,1)S(1)} collective-permute-done((bf16[2,32,1536]{2,1,0:T(8,128)(2,1)S(1)}, bf16[2,32,1536]{2,1,0:T(8,128)(2,1)S(1)}, u32[]{:S(2)}, u32[]{:S(2)}) %collective-permute-start.16) | collective-permute-done | bytes 196640 | tf_op jit(solution)/shard_map/ppermute | solution.py:229
  88.8 4.0 %collective-permute-done.17 = bf16[2,32,1536]{2,1,0:T(8,128)(2,1)S(1)} collective-permute-done((bf16[2,32,1536]{2,1,0:T(8,128)(2,1)S(1)}, bf16[2,32,1536]{2,1,0:T(8,128)(2,1)S(1)}, u32[]{:S(2)}, u32[]{:S(2)}) %collective-permute-start.17) | collective-permute-done | bytes 196640 | tf_op jit(solution)/shard_map/ppermute | solution.py:229
  (67 shorter events, 9.9 us)
Async XLA Ops:
  0.9 1.1 %copy-start = (bf16[1,6,32,1536]{3,2,1,0:T(8,128)(2,1)S(1)}, bf16[1,6,32,1536]{3,2,1,0:T(8,128)(2,1)}, u32[]{:S(2)}) copy-start(bf16[1,6,32,1536]{3,2,1,0:T(8,128)(2,1)} %param.10) | copy-start | bytes 1769476
  2.0 9.1 %copy-start.1 = (bf16[48,3072]{1,0:T(8,128)(2,1)S(1)}, bf16[48,3072]{1,0:T(8,128)(2,1)}, u32[]{:S(2)}) copy-start(bf16[48,3072]{1,0:T(8,128)(2,1)} %weights) | copy-start | bytes 884740
  3.6 32.9 %copy-start.17 = (f32[1536]{0:T(1024)S(1)}, f32[1536]{0:T(1024)}, u32[]{:S(2)}) copy-start(f32[1536]{0:T(1024)} %param.11) | copy-start | bytes 18436
  3.6 32.9 %copy-start.18 = (f32[1536]{0:T(1024)S(1)}, f32[1536]{0:T(1024)}, u32[]{:S(2)}) copy-start(f32[1536]{0:T(1024)} %param.14) | copy-start | bytes 18436
  3.6 32.9 %copy-start.19 = (f32[1536]{0:T(1024)S(1)}, f32[1536]{0:T(1024)}, u32[]{:S(2)}) copy-start(f32[1536]{0:T(1024)} %param.15) | copy-start | bytes 18436
  3.7 46.5 %copy-start.16 = (f32[31,1536]{1,0:T(8,128)S(1)}, f32[31,1536]{1,0:T(8,128)}, u32[]{:S(2)}) copy-start(f32[31,1536]{1,0:T(8,128)} %param.13) | copy-start | bytes 571396
  3.7 48.9 %all-to-all-start = ((bf16[8,32,1536]{2,1,0:T(8,128)(2,1)}), bf16[8,32,1536]{2,1,0:T(8,128)(2,1)S(1)}, u32[]{:S(2)}, u32[]{:S(2)}) async-start(bf16[8,32,1536]{2,1,0:T(8,128)(2,1)} %shard_map.101), calls=%async_computation | async-start | bytes 1572864 | tf_op jit(solution)/shard_map/all_to_all | solution.py:251
  11.2 8.7 %collective-permute-start = (bf16[48,768]{1,0:T(8,128)(2,1)S(1)}, bf16[48,768]{1,0:T(8,128)(2,1)S(1)}, u32[]{:S(2)}, u32[]{:S(2)}) collective-permute-start(bf16[48,768]{1,0:T(8,128)(2,1)S(1)} %get-tuple-element.33), channel_id=1, source_target_pairs={{0,4},{1,5},{2,6},{3,7},{4,0},{5,1},{6,2},{7,3},{8,12},{9,13},{10,... | collective-permute-start | bytes 221192 | tf_op jit(solution)/shard_map/ppermute | solution.py:229
  13.3 12.9 %collective-permute-start.1 = (bf16[48,768]{1,0:T(8,128)(2,1)S(1)}, bf16[48,768]{1,0:T(8,128)(2,1)S(1)}, u32[]{:S(2)}, u32[]{:S(2)}) collective-permute-start(bf16[48,768]{1,0:T(8,128)(2,1)S(1)} %get-tuple-element.34), channel_id=1, source_target_pairs={{0,8},{1,9},{2,10},{3,11},{4,12},{5,13},{6,14},{7,15},{8,0},{9,1},... | collective-permute-start | bytes 221192 | tf_op jit(solution)/shard_map/ppermute | solution.py:229
  14.8 13.4 %collective-permute-start.2 = (bf16[48,768]{1,0:T(8,128)(2,1)S(1)}, bf16[48,768]{1,0:T(8,128)(2,1)S(1)}, u32[]{:S(2)}, u32[]{:S(2)}) collective-permute-start(bf16[48,768]{1,0:T(8,128)(2,1)S(1)} %get-tuple-element.35), channel_id=1, source_target_pairs={{0,12},{1,13},{2,14},{3,15},{4,8},{5,9},{6,10},{7,11},{8,4},{9,5},... | collective-permute-start | bytes 221192 | tf_op jit(solution)/shard_map/ppermute | solution.py:229
  28.2 6.8 %collective-permute-start.4 = (bf16[4,48,768]{2,1,0:T(8,128)(2,1)S(1)}, bf16[4,48,768]{2,1,0:T(8,128)(2,1)S(1)}, u32[]{:S(2)}, u32[]{:S(2)}) collective-permute-start(bf16[4,48,768]{2,1,0:T(8,128)(2,1)S(1)} %shard_map.103.refs_4_), channel_id=1, source_target_pairs={{0,2},{1,3},{2,0},{3,1},{4,6},{5,7},{6,4},{7,5},{8,10},{9,11},{10,... | collective-permute-start | bytes 884744 | tf_op jit(solution)/shard_map/ppermute | solution.py:229
  29.7 19.8 %collective-permute-start.9 = (bf16[4,48,768]{2,1,0:T(8,128)(2,1)S(1)}, bf16[4,48,768]{2,1,0:T(8,128)(2,1)S(1)}, u32[]{:S(2)}, u32[]{:S(2)}) collective-permute-start(bf16[4,48,768]{2,1,0:T(8,128)(2,1)S(1)} %shard_map.103.refs_4_), channel_id=1, source_target_pairs={{0,16},{1,17},{2,18},{3,19},{4,20},{5,21},{6,22},{7,23},{8,24},{9,... | collective-permute-start | bytes 884744 | tf_op jit(solution)/shard_map/ppermute | solution.py:229
  34.1 18.4 %collective-permute-start.3 = (bf16[4,48,768]{2,1,0:T(8,128)(2,1)S(1)}, bf16[4,48,768]{2,1,0:T(8,128)(2,1)S(1)}, u32[]{:S(2)}, u32[]{:S(2)}) collective-permute-start(bf16[4,48,768]{2,1,0:T(8,128)(2,1)S(1)} %shard_map.103.refs_4_), channel_id=1, source_target_pairs={{0,1},{1,0},{2,3},{3,2},{4,5},{5,4},{6,7},{7,6},{8,9},{9,8},{10,11... | collective-permute-start | bytes 884744 | tf_op jit(solution)/shard_map/ppermute | solution.py:229
  35.0 17.6 %collective-permute-start.5 = (bf16[4,48,768]{2,1,0:T(8,128)(2,1)S(1)}, bf16[4,48,768]{2,1,0:T(8,128)(2,1)S(1)}, u32[]{:S(2)}, u32[]{:S(2)}) collective-permute-start(bf16[4,48,768]{2,1,0:T(8,128)(2,1)S(1)} %collective-permute-done.4.refs_5_), channel_id=1, source_target_pairs={{0,1},{1,0},{2,3},{3,2},{4,5},{5,4},{6,7},{7,6},{8,9},{9,8},{10,11... | collective-permute-start | bytes 884744 | tf_op jit(solution)/shard_map/ppermute | solution.py:229
  35.0 21.1 %collective-permute-start.11 = (bf16[48,1536]{1,0:T(8,128)(2,1)}, bf16[48,1536]{1,0:T(8,128)(2,1)S(1)}, u32[]{:S(2)}, u32[]{:S(2)}) collective-permute-start(bf16[48,1536]{1,0:T(8,128)(2,1)} %refs_2_), channel_id=1, source_target_pairs={{0,2},{1,3},{2,0},{3,1},{4,6},{5,7},{6,4},{7,5},{8,10},{9,11},{10,... | collective-permute-start | bytes 442376 | tf_op jit(solution)/shard_map/ppermute | solution.py:229
  36.6 22.3 %collective-permute-start.12 = (bf16[48,1536]{1,0:T(8,128)(2,1)}, bf16[48,1536]{1,0:T(8,128)(2,1)}, u32[]{:S(2)}, u32[]{:S(2)}) collective-permute-start(bf16[48,1536]{1,0:T(8,128)(2,1)} %refs_2_), channel_id=1, source_target_pairs={{0,16},{1,17},{2,18},{3,19},{4,20},{5,21},{6,22},{7,23},{8,24},{9,... | collective-permute-start | bytes 442376 | tf_op jit(solution)/shard_map/ppermute | solution.py:229
  49.6 14.7 %collective-permute-start.10 = (bf16[4,48,768]{2,1,0:T(8,128)(2,1)S(1)}, bf16[4,48,768]{2,1,0:T(8,128)(2,1)S(1)}, u32[]{:S(2)}, u32[]{:S(2)}) collective-permute-start(bf16[4,48,768]{2,1,0:T(8,128)(2,1)S(1)} %collective-permute-done.9.refs_0_), channel_id=1, source_target_pairs={{0,2},{1,3},{2,0},{3,1},{4,6},{5,7},{6,4},{7,5},{8,10},{9,11},{10,... | collective-permute-start | bytes 884744 | tf_op jit(solution)/shard_map/ppermute | solution.py:229
  54.1 10.2 %collective-permute-start.8 = (bf16[2,32,1536]{2,1,0:T(8,128)(2,1)S(1)}, bf16[2,32,1536]{2,1,0:T(8,128)(2,1)S(1)}, u32[]{:S(2)}, u32[]{:S(2)}) collective-permute-start(bf16[2,32,1536]{2,1,0:T(8,128)(2,1)S(1)} %get-tuple-element.39.refs_0_), channel_id=1, source_target_pairs={{0,12},{1,13},{2,14},{3,15},{4,8},{5,9},{6,10},{7,11},{8,4},{9,5},... | collective-permute-start | bytes 589832 | tf_op jit(solution)/shard_map/ppermute | solution.py:229
  54.1 10.9 %collective-permute-start.7 = (bf16[2,32,1536]{2,1,0:T(8,128)(2,1)S(1)}, bf16[2,32,1536]{2,1,0:T(8,128)(2,1)S(1)}, u32[]{:S(2)}, u32[]{:S(2)}) collective-permute-start(bf16[2,32,1536]{2,1,0:T(8,128)(2,1)S(1)} %get-tuple-element.39.refs_0_), channel_id=1, source_target_pairs={{0,8},{1,9},{2,10},{3,11},{4,12},{5,13},{6,14},{7,15},{8,0},{9,1},... | collective-permute-start | bytes 589832 | tf_op jit(solution)/shard_map/ppermute | solution.py:229
  56.8 8.9 %collective-permute-start.6 = (bf16[2,32,1536]{2,1,0:T(8,128)(2,1)S(1)}, bf16[2,32,1536]{2,1,0:T(8,128)(2,1)S(1)}, u32[]{:S(2)}, u32[]{:S(2)}) collective-permute-start(bf16[2,32,1536]{2,1,0:T(8,128)(2,1)S(1)} %get-tuple-element.39.refs_0_), channel_id=1, source_target_pairs={{0,4},{1,5},{2,6},{3,7},{4,0},{5,1},{6,2},{7,3},{8,12},{9,13},{10,... | collective-permute-start | bytes 589832 | tf_op jit(solution)/shard_map/ppermute | solution.py:229
  58.9 5.4 %collective-permute-start.13 = (bf16[48,1536]{1,0:T(8,128)(2,1)}, bf16[48,1536]{1,0:T(8,128)(2,1)S(1)}, u32[]{:S(2)}, u32[]{:S(2)}) collective-permute-start(bf16[48,1536]{1,0:T(8,128)(2,1)} %collective-permute-done.12.refs_4_), channel_id=1, source_target_pairs={{0,2},{1,3},{2,0},{3,1},{4,6},{5,7},{6,4},{7,5},{8,10},{9,11},{10,... | collective-permute-start | bytes 442376 | tf_op jit(solution)/shard_map/ppermute | solution.py:229
  66.3 0.9 copy-start.13
  68.3 2.9 %collective-permute-start.14 = (bf16[16,48,768]{2,1,0:T(8,128)(2,1)S(1)}, bf16[16,48,768]{2,1,0:T(8,128)(2,1)S(1)}, u32[]{:S(2)}, u32[]{:S(2)}) collective-permute-start(bf16[16,48,768]{2,1,0:T(8,128)(2,1)S(1)} %shard_map.105.refs_6_), channel_id=1, source_target_pairs={{0,1},{1,0},{2,3},{3,2},{4,5},{5,4},{6,7},{7,6},{8,9},{9,8},{10,11... | collective-permute-start | bytes 3538952 | tf_op jit(solution)/shard_map/ppermute | solution.py:229
  71.2 0.9 copy-start.3
  72.1 0.9 copy-start.5
  73.1 0.9 copy-start.7
  74.0 0.9 copy-start.9
  74.9 0.9 copy-start.11
  75.9 0.8 copy-start.15
  80.4 7.0 %collective-permute-start.15 = (bf16[2,32,1536]{2,1,0:T(8,128)(2,1)S(1)}, bf16[2,32,1536]{2,1,0:T(8,128)(2,1)S(1)}, u32[]{:S(2)}, u32[]{:S(2)}) collective-permute-start(bf16[2,32,1536]{2,1,0:T(8,128)(2,1)S(1)} %get-tuple-element.48), channel_id=1, source_target_pairs={{0,4},{1,5},{2,6},{3,7},{4,0},{5,1},{6,2},{7,3},{8,12},{9,13},{10,... | collective-permute-start | bytes 589832 | tf_op jit(solution)/shard_map/ppermute | solution.py:229
  81.0 7.8 %collective-permute-start.16 = (bf16[2,32,1536]{2,1,0:T(8,128)(2,1)S(1)}, bf16[2,32,1536]{2,1,0:T(8,128)(2,1)S(1)}, u32[]{:S(2)}, u32[]{:S(2)}) collective-permute-start(bf16[2,32,1536]{2,1,0:T(8,128)(2,1)S(1)} %get-tuple-element.49), channel_id=1, source_target_pairs={{0,8},{1,9},{2,10},{3,11},{4,12},{5,13},{6,14},{7,15},{8,0},{9,1},... | collective-permute-start | bytes 589832 | tf_op jit(solution)/shard_map/ppermute | solution.py:229
  81.0 11.8 %collective-permute-start.17 = (bf16[2,32,1536]{2,1,0:T(8,128)(2,1)S(1)}, bf16[2,32,1536]{2,1,0:T(8,128)(2,1)S(1)}, u32[]{:S(2)}, u32[]{:S(2)}) collective-permute-start(bf16[2,32,1536]{2,1,0:T(8,128)(2,1)S(1)} %get-tuple-element.50), channel_id=1, source_target_pairs={{0,12},{1,13},{2,14},{3,15},{4,8},{5,9},{6,10},{7,11},{8,4},{9,5},... | collective-permute-start | bytes 589832 | tf_op jit(solution)/shard_map/ppermute | solution.py:229
  (7 other events, 4.7 us)

commit v6 on v5

v6 whole, which is shorter than its diff:
```python
import functools
import math

import jax
import jax.numpy as jnp
from jax import lax
from jax.experimental import pallas as pl
from jax.experimental.pallas import tpu as pltpu
from jax.sharding import PartitionSpec as P

SMEM = pl.BlockSpec(memory_space=pltpu.SMEM)
VMEM = pl.BlockSpec(memory_space=pltpu.VMEM)
BF16 = jnp.bfloat16
F32 = jnp.float32


def call(kernel, out_shape, in_specs, out_specs, operands, scratch=(), flops=0):
    shapes = list(operands) + list(jax.tree.leaves(out_shape)) + list(scratch)
    total = sum(math.prod(shape.shape) * shape.dtype.itemsize for shape in shapes)
    return pl.pallas_call(
        kernel,
        out_shape=out_shape,
        in_specs=in_specs,
        out_specs=out_specs,
        scratch_shapes=[pltpu.VMEM(shape.shape, shape.dtype) for shape in scratch],
        cost_estimate=pl.CostEstimate(flops=flops, bytes_accessed=total, transcendentals=0),
        compiler_params=pltpu.CompilerParams(
            vmem_limit_bytes=min(total + total // 2 + 4 * 2**20, 60 * 2**20)
        ),
    )(*operands)


def like(dtype, *shape):
    return jax.ShapeDtypeStruct(shape, dtype)


class Tables:
    def __init__(self, ref, sources):
        self.ref = ref
        self.slots = ref.shape[0] // (3 * sources)
        self.size = sources * self.slots

    def live_for(self, source, slot, target):
        at = source * self.slots + slot
        return jnp.logical_and(self.ref[self.size + at] == target, self.ref[at] > 0)

    def length(self, source, slot):
        return self.ref[source * self.slots + slot]

    def offset(self, source, slot):
        return self.ref[2 * self.size + source * self.slots + slot]


def own_columns(planes, chips, weights, owner):
    width = weights.shape[1] // 2
    run = width // (planes * chips)
    parts = [
        weights[:, pl.ds(half * width + (plane * chips + owner) * run, run)]
        for half in range(2)
        for plane in range(planes)
    ]
    return jnp.concatenate(parts, axis=1)


def send_kernel(place, packed, frames, out):
    tables = Tables(packed, out.shape[0])
    me = place[0]

    def send(target, carry):
        found = jnp.int32(0)
        for slot in range(tables.slots):
            found = jnp.where(tables.live_for(me, slot, target), slot, found)
        out[target] = frames[found]
        return carry

    lax.fori_loop(0, out.shape[0], send, 0)


def split_kernel(planes, chip, weights, *refs):
    outs, buf = refs[:-1], refs[-1]
    for owner in range(len(outs)):
        buf[owner] = own_columns(planes, len(outs), weights, owner)
    for number, out in enumerate(outs):
        out[...] = buf[jnp.bitwise_xor(chip[0], number)]


def table_kernel(
    source_count, long, planes, chips, place, chip, packed, small, sources, lens, table, gain
):
    tables = Tables(packed, source_count)
    me = place[0]

    def look(source, carry):
        for slot in range(tables.slots):

            @pl.when(tables.live_for(source, slot, me))
            def _():
                number = tables.offset(source, slot) // long
                sources[number] = source
                lens[number] = tables.length(source, slot)

        return carry

    lax.fori_loop(0, source_count, look, 0)
    count, width = small.shape
    run = width // (planes * chips)
    whole = small[...]
    gain[...] = whole[count - 1 :, :]
    for owner in range(chips):

        @pl.when(chip[0] == owner)
        def _():
            starts = [(plane * chips + owner) * run for plane in range(planes)]
            parts = [whole[: count - 1, at : at + run] for at in starts]
            table[...] = jnp.concatenate(parts, axis=1)


def norm_kernel(sources, lens, gain, arrived, kept, normed):
    for number in range(kept.shape[0]):
        rows = arrived[sources[number]]
        kept[number] = rows
        wide = rows.astype(F32)
        mean = jnp.mean(wide, axis=1, keepdims=True)
        centred = wide - mean
        var = jnp.mean(centred * centred, axis=1, keepdims=True)
        value = centred * lax.rsqrt(var + 1e-05) * gain[...]
        steps = lax.broadcasted_iota(jnp.int32, value.shape, 0)
        normed[number] = jnp.where(steps < lens[number], value, 0.0).astype(BF16)


def conv_rows(block, taps):
    long, chans = block.shape
    count = taps.shape[0]
    front = (count - 1) // 2
    groups = long // 8
    pieces = [block[8 * at : 8 * at + 8, :] for at in range(groups)]
    total = None
    for residue in range(8):
        rows = []
        for at in range(groups + 1):
            value = None
            for step in range(-(count // 8) - 1, count // 8 + 2):
                tap = 8 * step + residue + front - 16
                source = at + step - 2
                if 0 <= tap < count and 0 <= source < groups:
                    term = pieces[source] * taps[tap : tap + 1, :]
                    value = term if value is None else value + term
            rows.append(jnp.zeros((8, chans), F32) if value is None else value)
        whole = jnp.concatenate(rows, axis=0)[residue : residue + long, :]
        total = whole if total is None else total + whole
    return total


def main_kernel(chips, layout, where, kept, table, *refs):
    pieces = max(len(layout), 2)
    chans = table.shape[1]
    taps = table[: table.shape[0] - 2, :]
    scale, shift = table[table.shape[0] - 2 : table.shape[0] - 1, :], table[table.shape[0] - 1 :, :]
    normed, weights = refs[:chips], refs[chips : chips + pieces]
    own, outs = refs[chips + pieces], refs[chips + pieces + 1 : 2 * chips + pieces]
    rows_buf, in_buf, out_buf, glu_buf, act_buf = refs[2 * chips + pieces :]
    recv, long, width = kept.shape
    tall = recv * long
    for number, ref in enumerate(normed):
        rows_buf[pl.ds(number * tall, tall), :] = ref[...].reshape(tall, width)
    if layout:
        w_in, w_out = in_buf, out_buf
        depth, wide = weights[0].shape[1:]
        for ref, slabs in zip(weights, layout):
            for at, (kind, other, number) in enumerate(slabs):
                if kind == "in":
                    start = pl.multiple_of(where[other, number] * depth, 16)
                    in_buf[pl.ds(start, depth), :] = ref[at]
                else:
                    start = pl.multiple_of(where[other, chips] * depth, 16)
                    first = number * wide
                    out_buf[pl.ds(start, depth), first : first + wide] = ref[at]
    else:
        w_in, w_out = weights
    glu_in = jnp.dot(rows_buf[...], w_in[...], preferred_element_type=F32)
    glu_buf[...] = glu_in[:, :chans] * jax.nn.sigmoid(glu_in[:, chans:])

    def utterance(at, carry):
        start = pl.multiple_of(at * long, long)
        moved = conv_rows(glu_buf[pl.ds(start, long), :], taps) * scale + shift
        act_buf[pl.ds(start, long), :] = (moved * jax.nn.sigmoid(moved)).astype(BF16)
        return carry

    lax.fori_loop(0, chips * recv, utterance, 0)
    batch = min(chips, 4)
    for first in range(0, chips, batch):
        act = act_buf[pl.ds(first * tall, batch * tall), :]
        mixed = jnp.dot(act, w_out[...], preferred_element_type=F32)
        mixed = mixed.reshape(batch, recv, long, width)
        for number in range(batch):
            if first + number == 0:
                own[...] = kept[...].astype(F32) + mixed[0]
            else:
                outs[first + number - 1][...] = mixed[number].astype(BF16)


def shards(
    frames, ln_gain, w_in, depth_kernel, bn_scale, bn_shift, w_out, lengths, destinations, offsets
):
    dp_count, fsdp_count = lax.axis_size("dp"), lax.axis_size("fsdp")
    devices = dp_count * fsdp_count
    chips = (fsdp_count // 2) ** 2
    planes = devices // (2 * chips)
    dp_index = lax.axis_index("dp")
    number = dp_index * fsdp_count + lax.axis_index("fsdp")
    core = number % 2
    chip = (number // 2) % chips
    plane = number // (2 * chips)
    recv = lengths.shape[2] // 3
    _, _, long, width = frames.shape
    depth = w_in.shape[0]
    chans = width // chips
    wide = 2 * chans
    count = width // wide
    taps = depth_kernel.shape[0]

    def swap(array, mask):
        return lax.ppermute(array, ("dp", "fsdp"), [(at, at ^ mask) for at in range(devices)])

    def chip_swap(arrays):
        return [arrays[0]] + [swap(arrays[mask], 2 * mask) for mask in range(1, chips)]

    def climb(array):
        pairs = [(at, (at + 2 * chips) % devices) for at in range(devices)]
        return lax.ppermute(array, ("dp", "fsdp"), pairs)

    def gated(arrays, others):
        return lax.optimization_barrier((arrays, others))[0]

    place = dp_index.astype(jnp.int32)[None]
    chip_place = chip.astype(jnp.int32)[None]
    packed = jnp.stack([lengths[0], destinations[0], offsets[0]]).reshape(-1)
    small = jnp.concatenate([depth_kernel, bn_scale[None], bn_shift[None], ln_gain[None]])

    first_out = jnp.stack([w_out[:, at : at + wide] for at in range(0, width, wide)])
    next_out = climb(first_out)

    if depth % 16 == 0:
        split = call(
            functools.partial(split_kernel, planes),
            [like(BF16, depth, wide)] * chips,
            [SMEM, VMEM],
            [VMEM] * chips,
            (chip_place, w_in),
            [like(BF16, chips, depth, wide)],
        )
    else:
        by_owner = w_in.reshape(depth, 2, planes, chips, 2 * depth).transpose(3, 0, 1, 2, 4)
        by_owner = by_owner.reshape(chips, depth, wide)
        split = [
            lax.dynamic_index_in_dim(by_owner, chip ^ mask, 0, keepdims=False)
            for mask in range(chips)
        ]
    columns = chip_swap(split)

    send = call(
        send_kernel,
        like(BF16, dp_count, long, width),
        [SMEM, SMEM, VMEM],
        VMEM,
        (place, packed, frames[0]),
    )
    arrived = lax.all_to_all(send, "dp", split_axis=0, concat_axis=0, tiled=True)
    columns = gated(columns, send)
    ring = jnp.concatenate([jnp.stack(columns), next_out])
    sources, lens, table, gain = call(
        functools.partial(table_kernel, dp_count, long, planes, chips),
        [like(jnp.int32, recv)] * 2 + [like(F32, taps + 2, chans), like(F32, 1, width)],
        [SMEM] * 3 + [VMEM],
        [SMEM, SMEM, VMEM, VMEM],
        (place, chip_place, packed, small),
    )

    pieces = [first_out, ring]
    for _ in range(planes - 2):
        pieces.append(climb(pieces[-1]))
    crossed = [swap(part, 1) for part in pieces[:-1]]
    utts = like(BF16, recv, long, width)
    kept, normed = call(
        norm_kernel,
        [utts, utts],
        [SMEM] * 2 + [VMEM] * 2,
        [VMEM, VMEM],
        (sources, lens, gain, gated(arrived, crossed)),
    )
    last = climb(gated(pieces[-1], normed)[:chips])
    normed = chip_swap([normed] * chips)
    crossed.append(swap(pieces[-1], 1))
    crossed.append(swap(gated(last, normed), 1))
    pieces = pieces + [last] + crossed

    layout = []
    for side in range(2):
        first = side * planes
        layout.append([("out", first, half) for half in range(count)])
        for step in range(planes):
            layout.append([("in", first + step, at) for at in range(chips)])
            if step + 1 < planes:
                layout[-1] += [("out", first + step + 1, half) for half in range(count)]
    ring_plane = (plane - jnp.arange(planes)) % planes
    in_rows = (ring_plane[:, None] * chips + (chip ^ jnp.arange(chips))[None, :]) * 2
    where = jnp.concatenate([in_rows, ring_plane[:, None] * 2], 1)
    where = jnp.concatenate([where + core, where + 1 - core], 0).astype(jnp.int32)
    if depth % 16:
        slabs = {
            name: part[at]
            for part, names in zip(pieces, layout)
            for at, name in enumerate(names)
        }
        sides = range(2 * planes)
        flat = jnp.stack([slabs["in", at, number] for at in sides for number in range(chips)])
        all_in = jnp.zeros_like(flat).at[where[:, :chips].reshape(-1)].set(flat)
        flat = jnp.stack(
            [
                jnp.concatenate([slabs["out", at, half] for half in range(count)], axis=1)
                for at in sides
            ]
        )
        all_out = jnp.zeros_like(flat).at[where[:, chips]].set(flat)
        pieces = [all_in.reshape(width, wide), all_out.reshape(chans, width)]
        layout = []

    tall = chips * recv * long
    partial_sums = call(
        functools.partial(main_kernel, chips, layout),
        [like(F32, recv, long, width)] + [utts] * (chips - 1),
        [SMEM] + [VMEM] * (2 + chips + len(pieces)),
        [VMEM] * chips,
        (where, kept, table, *normed, *pieces),
        [
            like(BF16, tall, width),
            like(BF16, width, wide),
            like(BF16, chans, width),
            like(F32, tall, chans),
            like(BF16, tall, chans),
        ],
        flops=6 * tall * width * chans,
    )
    own, *others = chip_swap(partial_sums)
    for part in others:
        own = own + part.astype(F32)
    live = jnp.arange(long, dtype=jnp.int32)[None, :, None] < lens[:, None, None]
    return jnp.where(live, own, 0.0).astype(BF16)[None]


def solution(mesh):
    return jax.shard_map(
        shards,
        mesh=mesh,
        in_specs=(
            P("fsdp", "dp", None, None),
            P(),
            P(("dp", "fsdp"), None),
            P(),
            P(),
            P(),
            P(("dp", "fsdp"), None),
            P("fsdp", None, None),
            P("fsdp", None, None),
            P("fsdp", None, None),
        ),
        out_specs=P("fsdp", "dp", None, None),
        check_vma=False,
    )
```

time: 94 us -> 88.9 us (0.946)
  waiting for transfers between devices: 37.5 us -> 49.7 us
  starting transfers between devices: 32.6 us -> 22.4 us
  local copies, waits for them, and re-layouts: 12.3 us -> 6.41 us
    ppermute x0 -> x4, waiting for transfers between devices: none -> 30.5 us  [climb(): return lax.ppermute(array, ('dp', 'fsdp'), pairs)]
    ppermute x18 -> x14, waiting for transfers between devices: 37.5 us -> 19.3 us  [swap(): lax.ppermute(array, ('dp', 'fsdp'), [(at, at ^ mask) for at in range(devi...]
    ppermute x18 -> x14, starting transfers between devices: 25.2 us -> 11 us  [swap(): lax.ppermute(array, ('dp', 'fsdp'), [(at, at ^ mask) for at in range(devi...]
    unnamed x40 -> x30, local copies, waits for them, and re-layouts: 12.1 us -> 4.45 us
    ppermute x0 -> x4, starting transfers between devices: none -> 6.63 us  [climb(): return lax.ppermute(array, ('dp', 'fsdp'), pairs)]
    all_to_all x1, starting transfers between devices: 7.42 us -> 4.82 us  [shards(): lax.all_to_all(send, 'dp', split_axis=0, concat_axis=0, tiled=True)]
    another operation x0 -> x1, local copies, waits for them, and re-layouts: none -> 1.01 us  [shards(): jnp.stack([w_out[:, at:at + wide] for at in range(0, width, wide)])]
    pallas_call x7 -> x5, Pallas kernels: 9.11 us -> 8.63 us  [call(): pl.pallas_call(kernel, out_shape=out_shape, in_specs=in_specs, out_specs=...]
  transfers between devices with their start and end apart: 19 -> 19, of which waited for: 10 -> 7; matrix products, arithmetic and copies ran while one was open for 0% -> 1% of each run, Pallas kernels for 3% -> 5%
where the time goes in v6:
time: 88.9 us; the launch traced here: 88.5 us
  waiting for transfers between devices  49.7 us (56%)
  starting transfers between devices  22.4 us (25%)
  Pallas kernels  8.63 us (10%)
  local copies, waits for them, and re-layouts  6.41 us (7%)
  other arithmetic  1.1 us (1%)
    ppermute x4, waiting for transfers between devices, climb(): return lax.ppermute(array, ('dp', 'fsdp'), pairs)  30.5 us
    ppermute x14, waiting for transfers between devices, swap(): lax.ppermute(array, ('dp', 'fsdp'), [(at, at ^ mask) for at in range(devi...  19.3 us
    ppermute x14, starting transfers between devices, swap(): lax.ppermute(array, ('dp', 'fsdp'), [(at, at ^ mask) for at in range(devi...  11 us
    pallas_call x5, Pallas kernels, call(): pl.pallas_call(kernel, out_shape=out_shape, in_specs=in_specs, out_specs=...  8.63 us
    ppermute x4, starting transfers between devices, climb(): return lax.ppermute(array, ('dp', 'fsdp'), pairs)  6.63 us
    all_to_all x1, starting transfers between devices, shards(): lax.all_to_all(send, 'dp', split_axis=0, concat_axis=0, tiled=True)  4.82 us
    unnamed x30, local copies, waits for them, and re-layouts  4.45 us
  transfers between devices with their start and end apart: 19, of which 7 were waited for; matrix products, arithmetic and copies ran while one was open for 1% of the time, Pallas kernels for 5%

profile of v6, /device:TPU:0, one launch (start us, length us, event | category | flops | bytes accessed | tf_op | source)
XLA Modules:
  0.0 88.5 jit_solution(1712188387996043559)
XLA Ops:
  0.0 1.0 %slice_bitcast_fusion.1 = (bf16[1,48,768]{2,1,0:T(8,128)(2,1)S(1)}, bf16[1,48,768]{2,1,0:T(8,128)(2,1)S(1)}) fusion(bf16[48,1536]{1,0:T(8,128)(2,1)} %param.16), kind=kLoop, calls=%fused_computation.9 | loop fusion | bytes 294912 | tf_op jit(solution)/shard_map/stack | solution.py:240
  1.0 3.1 %collective-permute-start.4 = (bf16[2,48,768]{2,1,0:T(8,128)(2,1)S(1)}, bf16[2,48,768]{2,1,0:T(8,128)(2,1)S(1)}, u32[]{:S(2)}, u32[]{:S(2)}) collective-permute-start(bf16[2,48,768]{2,1,0:T(8,128)(2,1)S(1)} %pad_maximum_fusion.1.refs_4_), channel_id=1, source_target_pairs={{0,8},{1,9},{2,10},{3,11},{4,12},{5,13},{6,14},{7,15},{8,16},{9,17... | collective-permute-start | bytes 442376 | tf_op jit(solution)/shard_map/ppermute | solution.py:230
  4.3 1.6 %collective-permute-start.1 = (bf16[48,768]{1,0:T(8,128)(2,1)S(1)}, bf16[48,768]{1,0:T(8,128)(2,1)S(1)}, u32[]{:S(2)}, u32[]{:S(2)}) collective-permute-start(bf16[48,768]{1,0:T(8,128)(2,1)S(1)} %get-tuple-element.30), channel_id=1, source_target_pairs={{0,2},{1,3},{2,0},{3,1},{4,6},{5,7},{6,4},{7,5},{8,10},{9,11},{10,... | collective-permute-start | bytes 221192 | tf_op jit(solution)/shard_map/ppermute | solution.py:223
  5.9 1.5 %collective-permute-start.2 = (bf16[48,768]{1,0:T(8,128)(2,1)S(1)}, bf16[48,768]{1,0:T(8,128)(2,1)S(1)}, u32[]{:S(2)}, u32[]{:S(2)}) collective-permute-start(bf16[48,768]{1,0:T(8,128)(2,1)S(1)} %get-tuple-element.31), channel_id=1, source_target_pairs={{0,4},{1,5},{2,6},{3,7},{4,0},{5,1},{6,2},{7,3},{8,12},{9,13},{10,... | collective-permute-start | bytes 221192 | tf_op jit(solution)/shard_map/ppermute | solution.py:223
  8.1 1.6 %shard_map.101 = bf16[8,32,1536]{2,1,0:T(8,128)(2,1)} custom-call(s32[1]{0:T(128)} %bitcast.place, s32[144]{0:T(256)S(1)} %reshape.80.packed, bf16[6,32,1536]{2,1,0:T(8,128)(2,1)S(1)} %bitcast.17), custom_call_target="tpu_custom_call" | custom-call | bytes 1376836 | tf_op jit(solution)/shard_map/pallas_call | solution.py:20
  9.8 4.8 %all-to-all-start = ((bf16[8,32,1536]{2,1,0:T(8,128)(2,1)}), bf16[8,32,1536]{2,1,0:T(8,128)(2,1)S(1)}, u32[]{:S(2)}, u32[]{:S(2)}) async-start(bf16[8,32,1536]{2,1,0:T(8,128)(2,1)} %shard_map.101), calls=%async_computation | async-start | bytes 1572864 | tf_op jit(solution)/shard_map/all_to_all | solution.py:268
  14.7 2.1 %collective-permute-start.6 = (bf16[6,48,768]{2,1,0:T(8,128)(2,1)S(1)}, bf16[6,48,768]{2,1,0:T(8,128)(2,1)S(1)}, u32[]{:S(2)}, u32[]{:S(2)}) collective-permute-start(bf16[6,48,768]{2,1,0:T(8,128)(2,1)S(1)} %constant_dynamic-update-slice_fusion.refs_5_), channel_id=1, source_target_pairs={{0,8},{1,9},{2,10},{3,11},{4,12},{5,13},{6,14},{7,15},{8,16},{9,17... | collective-permute-start | bytes 1327112 | tf_op jit(solution)/shard_map/ppermute | solution.py:230
  16.8 23.2 %collective-permute-done.6.refs_6_ = bf16[6,48,768]{2,1,0:T(8,128)(2,1)S(1)} collective-permute-done((bf16[6,48,768]{2,1,0:T(8,128)(2,1)S(1)}, bf16[6,48,768]{2,1,0:T(8,128)(2,1)S(1)}, u32[]{:S(2)}, u32[]{:S(2)}) %collective-permute-start.6) | collective-permute-done | bytes 442400 | tf_op jit(solution)/shard_map/ppermute | solution.py:230
  40.0 1.5 %collective-permute-start.11 = (bf16[6,48,768]{2,1,0:T(8,128)(2,1)S(1)}, bf16[6,48,768]{2,1,0:T(8,128)(2,1)S(1)}, u32[]{:S(2)}, u32[]{:S(2)}) collective-permute-start(bf16[6,48,768]{2,1,0:T(8,128)(2,1)S(1)} %collective-permute-done.6.refs_6_), channel_id=1, source_target_pairs={{0,8},{1,9},{2,10},{3,11},{4,12},{5,13},{6,14},{7,15},{8,16},{9,17... | collective-permute-start | bytes 1327112 | tf_op jit(solution)/shard_map/ppermute | solution.py:230
  41.7 0.7 copy-done.7
  42.4 0.7 copy-done.9
  43.2 1.8 %shard_map.100 = (s32[2]{0:T(128)S(1)}, s32[2]{0:T(128)S(1)}, f32[33,384]{1,0:T(8,128)S(1)}, f32[1,1536]{1,0:T(1,128)S(1)}) custom-call(s32[1]{0:T(128)} %bitcast.place, s32[1]{0:T(128)} %bitcast.1.chip, s32[144]{0:T(256)S(1)} %reshape.80.packed, f32[34,1536]{1,0:T(8,128)S(1)} %pad_maximum_fusion.small), custom_call_target="tpu_custom_call" | custom-call | bytes 266328 | tf_op jit(solution)/shard_map/pallas_call | solution.py:20
  45.0 0.6 copy-done.4
  45.6 0.7 copy-done.2
  46.3 0.8 shard_map.103
  47.1 7.3 %collective-permute-done.11.refs_7_ = bf16[6,48,768]{2,1,0:T(8,128)(2,1)S(1)} collective-permute-done((bf16[6,48,768]{2,1,0:T(8,128)(2,1)S(1)}, bf16[6,48,768]{2,1,0:T(8,128)(2,1)S(1)}, u32[]{:S(2)}, u32[]{:S(2)}) %collective-permute-start.11) | collective-permute-done | bytes 442400 | tf_op jit(solution)/shard_map/ppermute | solution.py:230
  54.4 0.7 slice.11
  55.2 2.5 %collective-permute-start.10 = (bf16[2,32,1536]{2,1,0:T(8,128)(2,1)S(1)}, bf16[2,32,1536]{2,1,0:T(8,128)(2,1)}, u32[]{:S(2)}, u32[]{:S(2)}) collective-permute-start(bf16[2,32,1536]{2,1,0:T(8,128)(2,1)S(1)} %get-tuple-element.40.refs_0_), channel_id=1, source_target_pairs={{0,6},{1,7},{2,4},{3,5},{4,2},{5,3},{6,0},{7,1},{8,14},{9,15},{10,... | collective-permute-start | bytes 589832 | tf_op jit(solution)/shard_map/ppermute | solution.py:223
  57.6 0.6 collective-permute-start.9
  58.2 0.5 collective-permute-start.8
  58.8 5.2 %collective-permute-done.10.refs_3_ = bf16[2,32,1536]{2,1,0:T(8,128)(2,1)} collective-permute-done((bf16[2,32,1536]{2,1,0:T(8,128)(2,1)S(1)}, bf16[2,32,1536]{2,1,0:T(8,128)(2,1)}, u32[]{:S(2)}, u32[]{:S(2)}) %collective-permute-start.10) | collective-permute-done | bytes 196640 | tf_op jit(solution)/shard_map/ppermute | solution.py:223
  64.0 3.7 %collective-permute-done.9.refs_2_ = bf16[2,32,1536]{2,1,0:T(8,128)(2,1)} collective-permute-done((bf16[2,32,1536]{2,1,0:T(8,128)(2,1)S(1)}, bf16[2,32,1536]{2,1,0:T(8,128)(2,1)}, u32[]{:S(2)}, u32[]{:S(2)}) %collective-permute-start.9) | collective-permute-done | bytes 196640 | tf_op jit(solution)/shard_map/ppermute | solution.py:223
  67.9 1.5 %collective-permute-done.14.refs_13_ = bf16[4,48,768]{2,1,0:T(8,128)(2,1)S(1)} collective-permute-done((bf16[4,48,768]{2,1,0:T(8,128)(2,1)S(1)}, bf16[4,48,768]{2,1,0:T(8,128)(2,1)S(1)}, u32[]{:S(2)}, u32[]{:S(2)}) %collective-permute-start.14) | collective-permute-done | bytes 294944 | tf_op jit(solution)/shard_map/ppermute | solution.py:223
  69.3 0.9 %copy-done.3 = bf16[2,48,768]{2,1,0:T(8,128)(2,1)S(1)} copy-done((bf16[2,48,768]{2,1,0:T(8,128)(2,1)S(1)}, bf16[2,48,768]{2,1,0:T(8,128)(2,1)}, u32[]{:S(2)}) %copy-start.3) | copy-done | bytes 147480
  70.3 0.8 copy-done.5
  71.1 4.2 %shard_map.104 = (f32[2,32,1536]{2,1,0:T(8,128)S(1)}, bf16[2,32,1536]{2,1,0:T(8,128)(2,1)S(1)}, bf16[2,32,1536]{2,1,0:T(8,128)(2,1)S(1)}, bf16[2,32,1536]{2,1,0:T(8,128)(2,1)S(1)}) custom-call(s32[8,5]{1,0:T(8,128)S(1)} %pad_add_fusion.1.where, bf16[2,32,1536]{2,1,0:T(8,128)(2,1)S(1)} %get-tuple-element.38.kept, f32[33,384]{1,0:T(8,128)S(1)} %copy-done.5, ...), custom_call_target="tpu_custom_call" | custom-call | flops 905969664 | bytes 10471072 | tf_op jit(solution)/shard_map/pallas_call | solution.py:20
  75.3 1.6 %collective-permute-start.15 = (bf16[2,32,1536]{2,1,0:T(8,128)(2,1)S(1)}, bf16[2,32,1536]{2,1,0:T(8,128)(2,1)S(1)}, u32[]{:S(2)}, u32[]{:S(2)}) collective-permute-start(bf16[2,32,1536]{2,1,0:T(8,128)(2,1)S(1)} %get-tuple-element.44), channel_id=1, source_target_pairs={{0,2},{1,3},{2,0},{3,1},{4,6},{5,7},{6,4},{7,5},{8,10},{9,11},{10,... | collective-permute-start | bytes 589832 | tf_op jit(solution)/shard_map/ppermute | solution.py:223
  76.9 0.8 collective-permute-start.16
  77.6 1.2 %collective-permute-start.17 = (bf16[2,32,1536]{2,1,0:T(8,128)(2,1)S(1)}, bf16[2,32,1536]{2,1,0:T(8,128)(2,1)S(1)}, u32[]{:S(2)}, u32[]{:S(2)}) collective-permute-start(bf16[2,32,1536]{2,1,0:T(8,128)(2,1)S(1)} %get-tuple-element.46), channel_id=1, source_target_pairs={{0,6},{1,7},{2,4},{3,5},{4,2},{5,3},{6,0},{7,1},{8,14},{9,15},{10,... | collective-permute-start | bytes 589832 | tf_op jit(solution)/shard_map/ppermute | solution.py:223
  78.9 4.2 %collective-permute-done.15 = bf16[2,32,1536]{2,1,0:T(8,128)(2,1)S(1)} collective-permute-done((bf16[2,32,1536]{2,1,0:T(8,128)(2,1)S(1)}, bf16[2,32,1536]{2,1,0:T(8,128)(2,1)S(1)}, u32[]{:S(2)}, u32[]{:S(2)}) %collective-permute-start.15) | collective-permute-done | bytes 196640 | tf_op jit(solution)/shard_map/ppermute | solution.py:223
  83.1 4.6 %collective-permute-done.16 = bf16[2,32,1536]{2,1,0:T(8,128)(2,1)S(1)} collective-permute-done((bf16[2,32,1536]{2,1,0:T(8,128)(2,1)S(1)}, bf16[2,32,1536]{2,1,0:T(8,128)(2,1)S(1)}, u32[]{:S(2)}, u32[]{:S(2)}) %collective-permute-start.16) | collective-permute-done | bytes 196640 | tf_op jit(solution)/shard_map/ppermute | solution.py:223
  87.7 0.8 fusion
  (59 shorter events, 1.7 us)
Async XLA Ops:
  0.0 4.1 %copy-start.1 = (bf16[48,3072]{1,0:T(8,128)(2,1)S(1)}, bf16[48,3072]{1,0:T(8,128)(2,1)}, u32[]{:S(2)}) copy-start(bf16[48,3072]{1,0:T(8,128)(2,1)} %weights.1) | copy-start | bytes 884740
  0.0 8.1 %copy-start = (bf16[1,6,32,1536]{3,2,1,0:T(8,128)(2,1)S(1)}, bf16[1,6,32,1536]{3,2,1,0:T(8,128)(2,1)}, u32[]{:S(2)}) copy-start(bf16[1,6,32,1536]{3,2,1,0:T(8,128)(2,1)} %param.10) | copy-start | bytes 1769476
  1.0 13.6 %collective-permute-start.4 = (bf16[2,48,768]{2,1,0:T(8,128)(2,1)S(1)}, bf16[2,48,768]{2,1,0:T(8,128)(2,1)S(1)}, u32[]{:S(2)}, u32[]{:S(2)}) collective-permute-start(bf16[2,48,768]{2,1,0:T(8,128)(2,1)S(1)} %pad_maximum_fusion.1.refs_4_), channel_id=1, source_target_pairs={{0,8},{1,9},{2,10},{3,11},{4,12},{5,13},{6,14},{7,15},{8,16},{9,17... | collective-permute-start | bytes 442376 | tf_op jit(solution)/shard_map/ppermute | solution.py:230
  4.1 3.8 %copy-start.11 = (s32[1,8,6]{1,0,2:T(1,128)S(1)}, s32[1,8,6]{1,0,2:T(1,128)}, u32[]{:S(2)}) copy-start(s32[1,8,6]{1,0,2:T(1,128)} %param.18) | copy-start | bytes 580
  4.1 3.8 %copy-start.12 = (s32[1,8,6]{1,0,2:T(1,128)S(1)}, s32[1,8,6]{1,0,2:T(1,128)}, u32[]{:S(2)}) copy-start(s32[1,8,6]{1,0,2:T(1,128)} %param.17) | copy-start | bytes 580
  4.3 3.6 %copy-start.10 = (s32[1,8,6]{1,0,2:T(1,128)S(1)}, s32[1,8,6]{1,0,2:T(1,128)}, u32[]{:S(2)}) copy-start(s32[1,8,6]{1,0,2:T(1,128)} %param.19) | copy-start | bytes 580
  4.3 10.2 %collective-permute-start.1 = (bf16[48,768]{1,0:T(8,128)(2,1)S(1)}, bf16[48,768]{1,0:T(8,128)(2,1)S(1)}, u32[]{:S(2)}, u32[]{:S(2)}) collective-permute-start(bf16[48,768]{1,0:T(8,128)(2,1)S(1)} %get-tuple-element.30), channel_id=1, source_target_pairs={{0,2},{1,3},{2,0},{3,1},{4,6},{5,7},{6,4},{7,5},{8,10},{9,11},{10,... | collective-permute-start | bytes 221192 | tf_op jit(solution)/shard_map/ppermute | solution.py:223
  5.9 8.7 %collective-permute-start.2 = (bf16[48,768]{1,0:T(8,128)(2,1)S(1)}, bf16[48,768]{1,0:T(8,128)(2,1)S(1)}, u32[]{:S(2)}, u32[]{:S(2)}) collective-permute-start(bf16[48,768]{1,0:T(8,128)(2,1)S(1)} %get-tuple-element.31), channel_id=1, source_target_pairs={{0,4},{1,5},{2,6},{3,7},{4,0},{5,1},{6,2},{7,3},{8,12},{9,13},{10,... | collective-permute-start | bytes 221192 | tf_op jit(solution)/shard_map/ppermute | solution.py:223
  7.4 7.2 %collective-permute-start.3 = (bf16[48,768]{1,0:T(8,128)(2,1)S(1)}, bf16[48,768]{1,0:T(8,128)(2,1)S(1)}, u32[]{:S(2)}, u32[]{:S(2)}) collective-permute-start(bf16[48,768]{1,0:T(8,128)(2,1)S(1)} %get-tuple-element.32), channel_id=1, source_target_pairs={{0,6},{1,7},{2,4},{3,5},{4,2},{5,3},{6,0},{7,1},{8,14},{9,15},{10,... | collective-permute-start | bytes 221192 | tf_op jit(solution)/shard_map/ppermute | solution.py:223
  9.8 36.5 %all-to-all-start = ((bf16[8,32,1536]{2,1,0:T(8,128)(2,1)}), bf16[8,32,1536]{2,1,0:T(8,128)(2,1)S(1)}, u32[]{:S(2)}, u32[]{:S(2)}) async-start(bf16[8,32,1536]{2,1,0:T(8,128)(2,1)} %shard_map.101), calls=%async_computation | async-start | bytes 1572864 | tf_op jit(solution)/shard_map/all_to_all | solution.py:268
  14.7 28.4 %copy-start.6 = (f32[31,1536]{1,0:T(8,128)S(1)}, f32[31,1536]{1,0:T(8,128)}, u32[]{:S(2)}) copy-start(f32[31,1536]{1,0:T(8,128)} %param.13) | copy-start | bytes 571396
  14.7 25.3 %collective-permute-start.6 = (bf16[6,48,768]{2,1,0:T(8,128)(2,1)S(1)}, bf16[6,48,768]{2,1,0:T(8,128)(2,1)S(1)}, u32[]{:S(2)}, u32[]{:S(2)}) collective-permute-start(bf16[6,48,768]{2,1,0:T(8,128)(2,1)S(1)} %constant_dynamic-update-slice_fusion.refs_5_), channel_id=1, source_target_pairs={{0,8},{1,9},{2,10},{3,11},{4,12},{5,13},{6,14},{7,15},{8,16},{9,17... | collective-permute-start | bytes 1327112 | tf_op jit(solution)/shard_map/ppermute | solution.py:230
  16.8 29.5 %collective-permute-start.5 = (bf16[6,48,768]{2,1,0:T(8,128)(2,1)S(1)}, bf16[6,48,768]{2,1,0:T(8,128)(2,1)S(1)}, u32[]{:S(2)}, u32[]{:S(2)}) collective-permute-start(bf16[6,48,768]{2,1,0:T(8,128)(2,1)S(1)} %constant_dynamic-update-slice_fusion.refs_5_), channel_id=1, source_target_pairs={{0,1},{1,0},{2,3},{3,2},{4,5},{5,4},{6,7},{7,6},{8,9},{9,8},{10,11... | collective-permute-start | bytes 1327112 | tf_op jit(solution)/shard_map/ppermute | solution.py:223
  40.0 6.3 %collective-permute-start.7 = (bf16[6,48,768]{2,1,0:T(8,128)(2,1)S(1)}, bf16[6,48,768]{2,1,0:T(8,128)(2,1)S(1)}, u32[]{:S(2)}, u32[]{:S(2)}) collective-permute-start(bf16[6,48,768]{2,1,0:T(8,128)(2,1)S(1)} %collective-permute-done.6.refs_6_), channel_id=1, source_target_pairs={{0,1},{1,0},{2,3},{3,2},{4,5},{5,4},{6,7},{7,6},{8,9},{9,8},{10,11... | collective-permute-start | bytes 1327112 | tf_op jit(solution)/shard_map/ppermute | solution.py:223
  40.0 14.4 %collective-permute-start.11 = (bf16[6,48,768]{2,1,0:T(8,128)(2,1)S(1)}, bf16[6,48,768]{2,1,0:T(8,128)(2,1)S(1)}, u32[]{:S(2)}, u32[]{:S(2)}) collective-permute-start(bf16[6,48,768]{2,1,0:T(8,128)(2,1)S(1)} %collective-permute-done.6.refs_6_), channel_id=1, source_target_pairs={{0,8},{1,9},{2,10},{3,11},{4,12},{5,13},{6,14},{7,15},{8,16},{9,17... | collective-permute-start | bytes 1327112 | tf_op jit(solution)/shard_map/ppermute | solution.py:230
  41.5 4.1 %collective-permute-start = (bf16[2,48,768]{2,1,0:T(8,128)(2,1)S(1)}, bf16[2,48,768]{2,1,0:T(8,128)(2,1)S(1)}, u32[]{:S(2)}, u32[]{:S(2)}) collective-permute-start(bf16[2,48,768]{2,1,0:T(8,128)(2,1)S(1)} %pad_maximum_fusion.1.refs_4_), channel_id=1, source_target_pairs={{0,1},{1,0},{2,3},{3,2},{4,5},{5,4},{6,7},{7,6},{8,9},{9,8},{10,11... | collective-permute-start | bytes 442376 | tf_op jit(solution)/shard_map/ppermute | solution.py:223
  41.7 0.7 copy-start.7
  41.7 0.7 copy-start.8
  42.4 0.7 copy-start.9
  45.0 0.6 copy-start.4
  45.6 0.7 copy-start.2
  55.1 12.7 %collective-permute-start.12 = (bf16[4,48,768]{2,1,0:T(8,128)(2,1)}, bf16[4,48,768]{2,1,0:T(8,128)(2,1)S(1)}, u32[]{:S(2)}, u32[]{:S(2)}) collective-permute-start(bf16[4,48,768]{2,1,0:T(8,128)(2,1)} %slice.11), channel_id=1, source_target_pairs={{0,8},{1,9},{2,10},{3,11},{4,12},{5,13},{6,14},{7,15},{8,16},{9,17... | collective-permute-start | bytes 884744 | tf_op jit(solution)/shard_map/ppermute | solution.py:230
  55.1 12.8 %collective-permute-start.13 = (bf16[6,48,768]{2,1,0:T(8,128)(2,1)S(1)}, bf16[6,48,768]{2,1,0:T(8,128)(2,1)S(1)}, u32[]{:S(2)}, u32[]{:S(2)}) collective-permute-start(bf16[6,48,768]{2,1,0:T(8,128)(2,1)S(1)} %collective-permute-done.11.refs_7_), channel_id=1, source_target_pairs={{0,1},{1,0},{2,3},{3,2},{4,5},{5,4},{6,7},{7,6},{8,9},{9,8},{10,11... | collective-permute-start | bytes 1327112 | tf_op jit(solution)/shard_map/ppermute | solution.py:223
  55.2 8.8 %collective-permute-start.10 = (bf16[2,32,1536]{2,1,0:T(8,128)(2,1)S(1)}, bf16[2,32,1536]{2,1,0:T(8,128)(2,1)}, u32[]{:S(2)}, u32[]{:S(2)}) collective-permute-start(bf16[2,32,1536]{2,1,0:T(8,128)(2,1)S(1)} %get-tuple-element.40.refs_0_), channel_id=1, source_target_pairs={{0,6},{1,7},{2,4},{3,5},{4,2},{5,3},{6,0},{7,1},{8,14},{9,15},{10,... | collective-permute-start | bytes 589832 | tf_op jit(solution)/shard_map/ppermute | solution.py:223
  57.6 10.1 %collective-permute-start.9 = (bf16[2,32,1536]{2,1,0:T(8,128)(2,1)S(1)}, bf16[2,32,1536]{2,1,0:T(8,128)(2,1)}, u32[]{:S(2)}, u32[]{:S(2)}) collective-permute-start(bf16[2,32,1536]{2,1,0:T(8,128)(2,1)S(1)} %get-tuple-element.40.refs_0_), channel_id=1, source_target_pairs={{0,4},{1,5},{2,6},{3,7},{4,0},{5,1},{6,2},{7,3},{8,12},{9,13},{10,... | collective-permute-start | bytes 589832 | tf_op jit(solution)/shard_map/ppermute | solution.py:223
  58.2 9.6 %collective-permute-start.8 = (bf16[2,32,1536]{2,1,0:T(8,128)(2,1)S(1)}, bf16[2,32,1536]{2,1,0:T(8,128)(2,1)}, u32[]{:S(2)}, u32[]{:S(2)}) collective-permute-start(bf16[2,32,1536]{2,1,0:T(8,128)(2,1)S(1)} %get-tuple-element.40.refs_0_), channel_id=1, source_target_pairs={{0,2},{1,3},{2,0},{3,1},{4,6},{5,7},{6,4},{7,5},{8,10},{9,11},{10,... | collective-permute-start | bytes 589832 | tf_op jit(solution)/shard_map/ppermute | solution.py:223
  67.8 1.6 %collective-permute-start.14 = (bf16[4,48,768]{2,1,0:T(8,128)(2,1)S(1)}, bf16[4,48,768]{2,1,0:T(8,128)(2,1)S(1)}, u32[]{:S(2)}, u32[]{:S(2)}) collective-permute-start(bf16[4,48,768]{2,1,0:T(8,128)(2,1)S(1)} %collective-permute-done.12.refs_8_), channel_id=1, source_target_pairs={{0,1},{1,0},{2,3},{3,2},{4,5},{5,4},{6,7},{7,6},{8,9},{9,8},{10,11... | collective-permute-start | bytes 884744 | tf_op jit(solution)/shard_map/ppermute | solution.py:223
  69.3 0.9 %copy-start.3 = (bf16[2,48,768]{2,1,0:T(8,128)(2,1)S(1)}, bf16[2,48,768]{2,1,0:T(8,128)(2,1)}, u32[]{:S(2)}) copy-start(bf16[2,48,768]{2,1,0:T(8,128)(2,1)} %copy-done.2) | copy-start | bytes 442372
  70.3 0.8 copy-start.5
  75.3 7.8 %collective-permute-start.15 = (bf16[2,32,1536]{2,1,0:T(8,128)(2,1)S(1)}, bf16[2,32,1536]{2,1,0:T(8,128)(2,1)S(1)}, u32[]{:S(2)}, u32[]{:S(2)}) collective-permute-start(bf16[2,32,1536]{2,1,0:T(8,128)(2,1)S(1)} %get-tuple-element.44), channel_id=1, source_target_pairs={{0,2},{1,3},{2,0},{3,1},{4,6},{5,7},{6,4},{7,5},{8,10},{9,11},{10,... | collective-permute-start | bytes 589832 | tf_op jit(solution)/shard_map/ppermute | solution.py:223
  76.9 10.9 %collective-permute-start.16 = (bf16[2,32,1536]{2,1,0:T(8,128)(2,1)S(1)}, bf16[2,32,1536]{2,1,0:T(8,128)(2,1)S(1)}, u32[]{:S(2)}, u32[]{:S(2)}) collective-permute-start(bf16[2,32,1536]{2,1,0:T(8,128)(2,1)S(1)} %get-tuple-element.45), channel_id=1, source_target_pairs={{0,4},{1,5},{2,6},{3,7},{4,0},{5,1},{6,2},{7,3},{8,12},{9,13},{10,... | collective-permute-start | bytes 589832 | tf_op jit(solution)/shard_map/ppermute | solution.py:223
  77.6 10.1 %collective-permute-start.17 = (bf16[2,32,1536]{2,1,0:T(8,128)(2,1)S(1)}, bf16[2,32,1536]{2,1,0:T(8,128)(2,1)S(1)}, u32[]{:S(2)}, u32[]{:S(2)}) collective-permute-start(bf16[2,32,1536]{2,1,0:T(8,128)(2,1)S(1)} %get-tuple-element.46), channel_id=1, source_target_pairs={{0,6},{1,7},{2,4},{3,5},{4,2},{5,3},{6,0},{7,1},{8,14},{9,15},{10,... | collective-permute-start | bytes 589832 | tf_op jit(solution)/shard_map/ppermute | solution.py:223

commit v7 on v4

--- a/solution.py
+++ b/solution.py
@@ -52,7 +52,8 @@
         return self.ref[2 * self.size + source * self.slots + slot]
 
 
-def own_columns(highs, weights, owner, width):
+def own_columns(highs, weights, owner):
+    width = weights.shape[1] // 2
     run = width // (highs * QUAD)
     parts = [
         weights[:, pl.ds(half * width + (high * QUAD + owner) * run, run)]
@@ -62,41 +63,22 @@
     return jnp.concatenate(parts, axis=1)
 
 
-def send_kernel(sources, place, packed, weights, frames, *refs):
-    outs, buf = refs[:-1], refs[-1]
+def send_kernel(sources, place, packed, frames, *outs):
     tables = Tables(packed, sources)
     me = place[0]
-    highs = sources // QUAD
-    long, width = frames.shape[1:]
-    wide = outs[0].shape[1]
-    for owner in range(QUAD):
-        buf[owner] = own_columns(highs, weights, owner, width)
     for number, out in enumerate(outs):
-        for far in range(highs):
+        for far in range(out.shape[0]):
             target = jnp.bitwise_xor(me, far * QUAD + number)
             found = jnp.int32(0)
             for slot in range(tables.slots):
                 found = jnp.where(tables.live_for(me, slot, target), slot, found)
-            for half in range(width // wide):
-                start = (far * (width // wide) + half) * long
-                out[start : start + long, :] = frames[found, :, half * wide : half * wide + wide]
-        start = highs * (width // wide) * long
-        out[start:, :] = buf[jnp.bitwise_xor(lax.rem(me, QUAD), number)]
-
-
-def fetch(out, number, ref, far):
-    long, width = out.shape[1:]
-    wide = ref.shape[1]
-    for half in range(width // wide):
-        start = (far * (width // wide) + half) * long
-        out[number, :, half * wide : half * wide + wide] = ref[start : start + long, :]
-
-
-def merge_kernel(sources, place, packed, last, *refs):
-    arrived, outs, piece = refs[:QUAD], refs[QUAD:-1], refs[-1]
+            out[far] = frames[found]
+
+
+def merge_kernel(sources, place, packed, *refs):
+    arrived, outs = refs[:QUAD], refs[QUAD:]
     tables = Tables(packed, sources)
     me = place[0]
-    depth, wide = piece.shape[1:]
     for far, out in enumerate(outs, 1):
         long = out.shape[1]
         for number, ref in enumerate(arrived):
@@ -109,30 +91,15 @@
 
             @pl.when(start >= 0)
             def _():
-                fetch(out, start // long, ref, far)
-
-    for number, ref in enumerate(arrived):
-        piece[number] = ref[ref.shape[0] - depth :, :]
-    for half in range(piece.shape[0] - QUAD):
-        piece[QUAD + half] = last[:, half * wide : half * wide + wide]
+                out[start // long] = ref[far]
 
 
 def split_kernel(highs, place, weights, *refs):
     outs, buf = refs[:-1], refs[-1]
     for owner in range(QUAD):
-        buf[owner] = own_columns(highs, weights, owner, weights.shape[1] // 3)
+        buf[owner] = own_columns(highs, weights, owner)
     for number, out in enumerate(outs):
         out[...] = buf[jnp.bitwise_xor(lax.rem(place[0], QUAD), number)]
-
-
-def stack_kernel(both, *refs):
-    columns, piece = refs[:-1], refs[-1]
-    wide = piece.shape[2]
-    last = both.at[:, both.shape[1] // 3 * 2 :]
-    for number, ref in enumerate(columns):
-        piece[number] = ref[...]
-    for half in range(piece.shape[0] - QUAD):
-        piece[QUAD + half] = last[:, half * wide : half * wide + wide]
 
 
 def table_kernel(source_count, long, place, packed, small, sources, lens, table, gain):
@@ -173,7 +140,7 @@
 
             @pl.when(shift == other)
             def _():
-                fetch(kept, number, ref, 0)
+                kept[number] = ref[0]
 
         for other, ref in enumerate(far, 1):
 
@@ -282,22 +249,36 @@
     place = dp_index.astype(jnp.int32)[None]
     packed = jnp.stack([lengths[0], destinations[0], offsets[0]]).reshape(-1)
     small = jnp.concatenate([depth_kernel, bn_scale[None], bn_shift[None], ln_gain[None]])
-    count = width // wide
     bits = [1 << at for at in range((highs * fsdp_count).bit_length() - 1)]
     chip_bits = [bit for bit in reversed(bits) if 1 < bit < fsdp_count]
 
-    both = jnp.concatenate([w_in, w_out], axis=1)
-    far_rows = [swap(both, high=mask) for mask in range(1, highs)]
+    if depth % 16 == 0:
+        split = call(
+            functools.partial(split_kernel, highs),
+            [like(BF16, depth, wide)] * QUAD,
+            [SMEM, VMEM],
+            [VMEM] * QUAD,
+            (place, w_in),
+            [like(BF16, QUAD, depth, wide)],
+        )
+    else:
+        by_owner = w_in.reshape(depth, 2, highs, QUAD, chans // highs).transpose(3, 0, 1, 2, 4)
+        by_owner = by_owner.reshape(QUAD, depth, wide)
+        split = [
+            lax.dynamic_index_in_dim(by_owner, quad ^ mask, 0, keepdims=False)
+            for mask in range(QUAD)
+        ]
+    columns = quad_swap(split)
 
     near = call(
         functools.partial(send_kernel, dp_count),
-        [like(BF16, highs * count * long + depth, wide)] * QUAD,
-        [SMEM, SMEM, VMEM, VMEM],
+        [like(BF16, highs, long, width)] * QUAD,
+        [SMEM, SMEM, VMEM],
         [VMEM] * QUAD,
-        (place, packed, w_in, frames[0]),
-        [like(BF16, QUAD, depth, wide)],
+        (place, packed, frames[0]),
     )
     near = quad_swap(near)
+    columns = gated(columns, near[1])
     sources, lens, table, gain = call(
         functools.partial(table_kernel, dp_count, long),
         [like(jnp.int32, recv)] * 2 + [like(F32, taps + 2, chans), like(F32, 1, width)],
@@ -306,43 +287,22 @@
         (place, packed, small),
     )
     utts = like(BF16, recv, long, width)
-    block = like(BF16, QUAD + count, depth, wide)
-    *far, piece = call(
+    far = call(
         functools.partial(merge_kernel, dp_count),
-        [utts] * (highs - 1) + [block],
-        [SMEM] * 2 + [VMEM] * (1 + QUAD),
-        [VMEM] * highs,
-        (gated(place, (lens, gain)), packed, w_out, *near),
-    )
-    pieces = [piece]
+        [utts] * (highs - 1),
+        [SMEM] * 2 + [VMEM] * QUAD,
+        [VMEM] * (highs - 1),
+        (gated(place, (lens, gain)), packed, *near),
+    )
+    far = [swap(part, high=mask) for mask, part in enumerate(far, 1)]
+
+    halves = [w_out[:, at : at + wide] for at in range(0, width, wide)]
+    pieces = [jnp.stack(columns + halves)]
     shifts = [mask * fsdp_count for mask in range(highs)]
-    far_rows = gated(far_rows, far)
-    far = [swap(part, high=mask) for mask, part in enumerate(far, 1)]
-    for part in far_rows:
-        columns = call(
-            functools.partial(split_kernel, highs),
-            [like(BF16, depth, wide)] * QUAD,
-            [SMEM, VMEM],
-            [VMEM] * QUAD,
-            (place, part),
-            [like(BF16, QUAD, depth, wide)],
-        )
-        pieces.append(
-            call(
-                stack_kernel,
-                block,
-                [VMEM] * (1 + QUAD),
-                VMEM,
-                (part, *gated(quad_swap(columns), far)),
-            )
-        )
-    early = len(pieces)
-    cored = [swap(part, fsdp=1) for part in pieces]
-    far = gated(far, (pieces, cored[:1]))
-    for bit in chip_bits:
-        pieces = pieces + [swap(part, fsdp=bit) for part in pieces]
-        shifts = shifts + [shift ^ bit for shift in shifts]
-
+    pieces += gated([swap(pieces[0], high=mask) for mask in range(1, highs)], far)
+    chip_first = [swap(pieces[0], fsdp=bit) for bit in chip_bits[:1]]
+    early = [swap(part, fsdp=1) for part in pieces[:1] + chip_first]
+    far = gated(far, early)
     kept, normed = call(
         norm_kernel,
         [utts, utts],
@@ -350,10 +310,16 @@
         [VMEM, VMEM],
         (place, sources, lens, gain, *near, *far),
     )
+    for bit in chip_bits:
+        first = chip_first if bit == chip_bits[0] else []
+        pieces = pieces + first + [swap(part, fsdp=bit) for part in pieces[len(first) :]]
+        shifts = shifts + [shift ^ bit for shift in shifts]
     normed = quad_swap([normed] * QUAD)
-    late = pieces[early:]
-    crossed = swap(jnp.stack(gated(late, normed[1:3])), fsdp=1)
-    pieces = pieces + cored + [crossed[at] for at in range(len(late))]
+    ends = len(shifts) // 2 + 1
+    pieces[ends:] = gated(pieces[ends:], normed)
+    cored = [swap(part, fsdp=1) for part in pieces]
+    cored[0], cored[len(shifts) // 2] = early[0], early[-1]
+    pieces = pieces + cored
     shifts = shifts + [shift ^ 1 for shift in shifts]
 
     out_rows = line ^ jnp.array(shifts)

time: 88.9 us -> 80.3 us (0.903)
  waiting for transfers between devices: 53.8 us -> 39.1 us
  starting transfers between devices: 20.5 us -> 25.8 us
  local copies, waits for them, and re-layouts: 2.86 us -> 5.27 us
  other arithmetic: 3.23 us -> 1.76 us
    ppermute x19 -> x20, waiting for transfers between devices: 53.8 us -> 39.1 us  [swap(): lax.ppermute(array, ('dp', 'fsdp'), [(at, at ^ mask) for at in range(devi...]
    ppermute x19 -> x20, starting transfers between devices: 20.5 us -> 25.8 us  [swap(): lax.ppermute(array, ('dp', 'fsdp'), [(at, at ^ mask) for at in range(devi...]
    unnamed x22 -> x29, local copies, waits for them, and re-layouts: 1.36 us -> 4.97 us
    squeeze x1 -> x0, local copies, waits for them, and re-layouts: 1.2 us -> none  [shards(): pieces = pieces + cored + [crossed[at] for at in range(len(late))]]
    concatenate x1 -> x0, other arithmetic: 1.14 us -> none  [shards(): both = jnp.concatenate([w_in, w_out], axis=1)]
    another operation x1 -> x0, other arithmetic: 1.01 us -> none  [shards(): crossed = swap(jnp.stack(gated(late, normed[1:3])), fsdp=1)]
    pallas_call x7 -> x6, Pallas kernels: 8.06 us -> 7.92 us  [call(): pl.pallas_call(kernel, out_shape=out_shape, in_specs=in_specs, out_specs=...]
  transfers between devices with their start and end apart: 19 -> 20, of which waited for: 12 -> 13; matrix products, arithmetic and copies ran while one was open for 2% -> 0% of each run, Pallas kernels for 5% -> 5%
where the time goes in v7:
time: 80.3 us; the launch traced here: 80 us
  waiting for transfers between devices  39.1 us (49%)
  starting transfers between devices  25.8 us (32%)
  Pallas kernels  7.92 us (10%)
  local copies, waits for them, and re-layouts  5.27 us (7%)
  other arithmetic  1.76 us (2%)
    ppermute x20, waiting for transfers between devices, swap(): lax.ppermute(array, ('dp', 'fsdp'), [(at, at ^ mask) for at in range(devi...  39.1 us
    ppermute x20, starting transfers between devices, swap(): lax.ppermute(array, ('dp', 'fsdp'), [(at, at ^ mask) for at in range(devi...  25.8 us
    pallas_call x6, Pallas kernels, call(): pl.pallas_call(kernel, out_shape=out_shape, in_specs=in_specs, out_specs=...  7.92 us
    unnamed x29, local copies, waits for them, and re-layouts  4.97 us
  transfers between devices with their start and end apart: 20, of which 13 were waited for; matrix products, arithmetic and copies ran while one was open for 0% of the time, Pallas kernels for 5%

profile of v7, /device:TPU:0, one launch (start us, length us, event | category | flops | bytes accessed | tf_op | source)
XLA Modules:
  0.0 80.0 jit_solution(8818770166879872519)
XLA Ops:
  0.7 0.7 pad_add_fusion
  1.6 1.1 %copy-done = bf16[1,6,32,1536]{3,2,1,0:T(8,128)(2,1)S(1)} copy-done((bf16[1,6,32,1536]{3,2,1,0:T(8,128)(2,1)S(1)}, bf16[1,6,32,1536]{3,2,1,0:T(8,128)(2,1)}, u32[]{:S(2)}) %copy-start) | copy-done | bytes 589848
  3.3 3.0 %collective-permute-start = (bf16[2,32,1536]{2,1,0:T(8,128)(2,1)S(1)}, bf16[2,32,1536]{2,1,0:T(8,128)(2,1)S(1)}, u32[]{:S(2)}, u32[]{:S(2)}) collective-permute-start(bf16[2,32,1536]{2,1,0:T(8,128)(2,1)S(1)} %get-tuple-element.35), channel_id=1, source_target_pairs={{0,4},{1,5},{2,6},{3,7},{4,0},{5,1},{6,2},{7,3},{8,12},{9,13},{10,... | collective-permute-start | bytes 589832 | tf_op jit(solution)/shard_map/ppermute | solution.py:241
  6.8 1.8 %collective-permute-start.5 = (bf16[48,768]{1,0:T(8,128)(2,1)S(1)}, bf16[48,768]{1,0:T(8,128)(2,1)S(1)}, u32[]{:S(2)}, u32[]{:S(2)}) collective-permute-start(bf16[48,768]{1,0:T(8,128)(2,1)S(1)} %get-tuple-element.41), channel_id=1, source_target_pairs={{0,8},{1,9},{2,10},{3,11},{4,12},{5,13},{6,14},{7,15},{8,0},{9,1},... | collective-permute-start | bytes 221192 | tf_op jit(solution)/shard_map/ppermute | solution.py:241
  8.7 1.4 %collective-permute-start.6 = (bf16[48,768]{1,0:T(8,128)(2,1)S(1)}, bf16[48,768]{1,0:T(8,128)(2,1)S(1)}, u32[]{:S(2)}, u32[]{:S(2)}) collective-permute-start(bf16[48,768]{1,0:T(8,128)(2,1)S(1)} %get-tuple-element.42), channel_id=1, source_target_pairs={{0,12},{1,13},{2,14},{3,15},{4,8},{5,9},{6,10},{7,11},{8,4},{9,5},... | collective-permute-start | bytes 221192 | tf_op jit(solution)/shard_map/ppermute | solution.py:241
  10.1 4.4 %collective-permute-done.4 = bf16[48,768]{1,0:T(8,128)(2,1)S(1)} collective-permute-done((bf16[48,768]{1,0:T(8,128)(2,1)S(1)}, bf16[48,768]{1,0:T(8,128)(2,1)S(1)}, u32[]{:S(2)}, u32[]{:S(2)}) %collective-permute-start.4) | collective-permute-done | bytes 73760 | tf_op jit(solution)/shard_map/ppermute | solution.py:241
  14.5 0.9 %copy-done.5 = bf16[48,1536]{1,0:T(8,128)(2,1)S(1)} copy-done((bf16[48,1536]{1,0:T(8,128)(2,1)S(1)}, bf16[48,1536]{1,0:T(8,128)(2,1)}, u32[]{:S(2)}) %copy-start.5) | copy-done | bytes 147480
  15.4 1.8 %collective-permute-start.8 = (bf16[6,48,768]{2,1,0:T(8,128)(2,1)S(1)}, bf16[6,48,768]{2,1,0:T(8,128)(2,1)S(1)}, u32[]{:S(2)}, u32[]{:S(2)}) collective-permute-start(bf16[6,48,768]{2,1,0:T(8,128)(2,1)S(1)} %bitcast_dynamic-update-slice_fusion.refs_4_), channel_id=1, source_target_pairs={{0,2},{1,3},{2,0},{3,1},{4,6},{5,7},{6,4},{7,5},{8,10},{9,11},{10,... | collective-permute-start | bytes 1327112 | tf_op jit(solution)/shard_map/ppermute | solution.py:241
  17.2 2.6 %collective-permute-start.13 = (bf16[6,48,768]{2,1,0:T(8,128)(2,1)S(1)}, bf16[6,48,768]{2,1,0:T(8,128)(2,1)S(1)}, u32[]{:S(2)}, u32[]{:S(2)}) collective-permute-start(bf16[6,48,768]{2,1,0:T(8,128)(2,1)S(1)} %bitcast_dynamic-update-slice_fusion.refs_4_), channel_id=1, source_target_pairs={{0,16},{1,17},{2,18},{3,19},{4,20},{5,21},{6,22},{7,23},{8,24},{9,... | collective-permute-start | bytes 1327112 | tf_op jit(solution)/shard_map/ppermute | solution.py:241
  19.8 1.6 %collective-permute-start.1 = (bf16[2,32,1536]{2,1,0:T(8,128)(2,1)S(1)}, bf16[2,32,1536]{2,1,0:T(8,128)(2,1)S(1)}, u32[]{:S(2)}, u32[]{:S(2)}) collective-permute-start(bf16[2,32,1536]{2,1,0:T(8,128)(2,1)S(1)} %get-tuple-element.36), channel_id=1, source_target_pairs={{0,8},{1,9},{2,10},{3,11},{4,12},{5,13},{6,14},{7,15},{8,0},{9,1},... | collective-permute-start | bytes 589832 | tf_op jit(solution)/shard_map/ppermute | solution.py:241
  21.3 1.4 %collective-permute-start.2 = (bf16[2,32,1536]{2,1,0:T(8,128)(2,1)S(1)}, bf16[2,32,1536]{2,1,0:T(8,128)(2,1)S(1)}, u32[]{:S(2)}, u32[]{:S(2)}) collective-permute-start(bf16[2,32,1536]{2,1,0:T(8,128)(2,1)S(1)} %get-tuple-element.37), channel_id=1, source_target_pairs={{0,12},{1,13},{2,14},{3,15},{4,8},{5,9},{6,10},{7,11},{8,4},{9,5},... | collective-permute-start | bytes 589832 | tf_op jit(solution)/shard_map/ppermute | solution.py:241
  23.5 2.5 %collective-permute-done.8.refs_6_ = bf16[6,48,768]{2,1,0:T(8,128)(2,1)S(1)} collective-permute-done((bf16[6,48,768]{2,1,0:T(8,128)(2,1)S(1)}, bf16[6,48,768]{2,1,0:T(8,128)(2,1)S(1)}, u32[]{:S(2)}, u32[]{:S(2)}) %collective-permute-start.8) | collective-permute-done | bytes 442400 | tf_op jit(solution)/shard_map/ppermute | solution.py:241
  26.1 1.8 %shard_map.109 = (s32[2]{0:T(128)S(1)}, s32[2]{0:T(128)S(1)}, f32[33,384]{1,0:T(8,128)S(1)}, f32[1,1536]{1,0:T(1,128)S(1)}) custom-call(s32[1]{0:T(128)} %bitcast.place, s32[144]{0:T(256)S(1)} %reshape.34.packed, f32[34,1536]{1,0:T(8,128)S(1)} %pad_maximum_fusion.small), custom_call_target="tpu_custom_call" | custom-call | bytes 266324 | tf_op jit(solution)/shard_map/pallas_call | solution.py:21
  27.9 5.8 %collective-permute-done.1.refs_2_ = bf16[2,32,1536]{2,1,0:T(8,128)(2,1)S(1)} collective-permute-done((bf16[2,32,1536]{2,1,0:T(8,128)(2,1)S(1)}, bf16[2,32,1536]{2,1,0:T(8,128)(2,1)S(1)}, u32[]{:S(2)}, u32[]{:S(2)}) %collective-permute-start.1) | collective-permute-done | bytes 196640 | tf_op jit(solution)/shard_map/ppermute | solution.py:241
  33.6 2.1 %collective-permute-done.2.refs_3_ = bf16[2,32,1536]{2,1,0:T(8,128)(2,1)S(1)} collective-permute-done((bf16[2,32,1536]{2,1,0:T(8,128)(2,1)S(1)}, bf16[2,32,1536]{2,1,0:T(8,128)(2,1)S(1)}, u32[]{:S(2)}, u32[]{:S(2)}) %collective-permute-start.2) | collective-permute-done | bytes 196640 | tf_op jit(solution)/shard_map/ppermute | solution.py:241
  36.4 4.2 %collective-permute-start.3 = (bf16[2,32,1536]{2,1,0:T(8,128)(2,1)S(1)}, bf16[2,32,1536]{2,1,0:T(8,128)(2,1)S(1)}, u32[]{:S(2)}, u32[]{:S(2)}) collective-permute-start(bf16[2,32,1536]{2,1,0:T(8,128)(2,1)S(1)} %shard_map.111), channel_id=1, source_target_pairs={{0,16},{1,17},{2,18},{3,19},{4,20},{5,21},{6,22},{7,23},{8,24},{9,... | collective-permute-start | bytes 589832 | tf_op jit(solution)/shard_map/ppermute | solution.py:241
  40.6 6.8 %collective-permute-done.3.refs_4_ = bf16[2,32,1536]{2,1,0:T(8,128)(2,1)S(1)} collective-permute-done((bf16[2,32,1536]{2,1,0:T(8,128)(2,1)S(1)}, bf16[2,32,1536]{2,1,0:T(8,128)(2,1)S(1)}, u32[]{:S(2)}, u32[]{:S(2)}) %collective-permute-start.3) | collective-permute-done | bytes 196640 | tf_op jit(solution)/shard_map/ppermute | solution.py:241
  48.7 0.9 %copy-done.3 = bf16[2,32,1536]{2,1,0:T(8,128)(2,1)S(1)} copy-done((bf16[2,32,1536]{2,1,0:T(8,128)(2,1)S(1)}, bf16[2,32,1536]{2,1,0:T(8,128)(2,1)}, u32[]{:S(2)}) %copy-start.3) | copy-done | bytes 196632
  49.6 1.0 %shard_map.113 = (bf16[2,32,1536]{2,1,0:T(8,128)(2,1)S(1)}, bf16[2,32,1536]{2,1,0:T(8,128)(2,1)S(1)}) custom-call(s32[1]{0:T(128)} %bitcast.place, s32[2]{0:T(128)S(1)} %get-tuple-element.32.sources, s32[2]{0:T(128)S(1)} %get-tuple-element.31.lens, f32[1,1536]{1,0:T(1,128)S(1)} %get-tuple-element.33.gain, ...), custom_call_target="tpu_custom_call" | custom-call | bytes 1382420 | tf_op jit(solution)/shard_map/pallas_call | solution.py:21
  50.9 1.7 %collective-permute-start.11 = (bf16[2,32,1536]{2,1,0:T(8,128)(2,1)S(1)}, bf16[2,32,1536]{2,1,0:T(8,128)(2,1)S(1)}, u32[]{:S(2)}, u32[]{:S(2)}) collective-permute-start(bf16[2,32,1536]{2,1,0:T(8,128)(2,1)S(1)} %get-tuple-element.50.refs_0_), channel_id=1, source_target_pairs={{0,8},{1,9},{2,10},{3,11},{4,12},{5,13},{6,14},{7,15},{8,0},{9,1},... | collective-permute-start | bytes 589832 | tf_op jit(solution)/shard_map/ppermute | solution.py:241
  52.7 1.5 %collective-permute-start.10 = (bf16[2,32,1536]{2,1,0:T(8,128)(2,1)S(1)}, bf16[2,32,1536]{2,1,0:T(8,128)(2,1)S(1)}, u32[]{:S(2)}, u32[]{:S(2)}) collective-permute-start(bf16[2,32,1536]{2,1,0:T(8,128)(2,1)S(1)} %get-tuple-element.50.refs_0_), channel_id=1, source_target_pairs={{0,4},{1,5},{2,6},{3,7},{4,0},{5,1},{6,2},{7,3},{8,12},{9,13},{10,... | collective-permute-start | bytes 589832 | tf_op jit(solution)/shard_map/ppermute | solution.py:241
  54.2 4.8 %collective-permute-done.14.refs_7_ = bf16[6,48,768]{2,1,0:T(8,128)(2,1)S(1)} collective-permute-done((bf16[6,48,768]{2,1,0:T(8,128)(2,1)S(1)}, bf16[6,48,768]{2,1,0:T(8,128)(2,1)S(1)}, u32[]{:S(2)}, u32[]{:S(2)}) %collective-permute-start.14) | collective-permute-done | bytes 442400 | tf_op jit(solution)/shard_map/ppermute | solution.py:241
  59.3 1.1 %collective-permute-done.11.refs_2_ = bf16[2,32,1536]{2,1,0:T(8,128)(2,1)S(1)} collective-permute-done((bf16[2,32,1536]{2,1,0:T(8,128)(2,1)S(1)}, bf16[2,32,1536]{2,1,0:T(8,128)(2,1)S(1)}, u32[]{:S(2)}, u32[]{:S(2)}) %collective-permute-start.11) | collective-permute-done | bytes 196640 | tf_op jit(solution)/shard_map/ppermute | solution.py:241
  60.4 1.0 %collective-permute-done.10.refs_1_ = bf16[2,32,1536]{2,1,0:T(8,128)(2,1)S(1)} collective-permute-done((bf16[2,32,1536]{2,1,0:T(8,128)(2,1)S(1)}, bf16[2,32,1536]{2,1,0:T(8,128)(2,1)S(1)}, u32[]{:S(2)}, u32[]{:S(2)}) %collective-permute-start.10) | collective-permute-done | bytes 196640 | tf_op jit(solution)/shard_map/ppermute | solution.py:241
  61.5 1.6 %collective-permute-done.16.refs_11_ = bf16[6,48,768]{2,1,0:T(8,128)(2,1)S(1)} collective-permute-done((bf16[6,48,768]{2,1,0:T(8,128)(2,1)S(1)}, bf16[6,48,768]{2,1,0:T(8,128)(2,1)S(1)}, u32[]{:S(2)}, u32[]{:S(2)}) %collective-permute-start.16) | collective-permute-done | bytes 442400 | tf_op jit(solution)/shard_map/ppermute | solution.py:241
  63.1 3.7 %shard_map.114 = (f32[2,32,1536]{2,1,0:T(8,128)S(1)}, bf16[2,32,1536]{2,1,0:T(8,128)(2,1)S(1)}, bf16[2,32,1536]{2,1,0:T(8,128)(2,1)S(1)}, bf16[2,32,1536]{2,1,0:T(8,128)(2,1)S(1)}) custom-call(s32[8,5]{1,0:T(8,128)S(1)} %pad_add_fusion.1.where, bf16[2,32,1536]{2,1,0:T(8,128)(2,1)S(1)} %get-tuple-element.48.kept, f32[33,384]{1,0:T(8,128)S(1)} %get-tuple-element.49.table, ...), custom_call_target="tpu_custom_call" | custom-call | flops 905969664 | bytes 10471072 | tf_op jit(solution)/shard_map/pallas_call | solution.py:21
  67.5 0.7 collective-permute-start.18
  68.2 2.2 %collective-permute-start.19 = (bf16[2,32,1536]{2,1,0:T(8,128)(2,1)S(1)}, bf16[2,32,1536]{2,1,0:T(8,128)(2,1)S(1)}, u32[]{:S(2)}, u32[]{:S(2)}) collective-permute-start(bf16[2,32,1536]{2,1,0:T(8,128)(2,1)S(1)} %get-tuple-element.56), channel_id=1, source_target_pairs={{0,12},{1,13},{2,14},{3,15},{4,8},{5,9},{6,10},{7,11},{8,4},{9,5},... | collective-permute-start | bytes 589832 | tf_op jit(solution)/shard_map/ppermute | solution.py:241
  70.4 3.4 %collective-permute-done.17 = bf16[2,32,1536]{2,1,0:T(8,128)(2,1)S(1)} collective-permute-done((bf16[2,32,1536]{2,1,0:T(8,128)(2,1)S(1)}, bf16[2,32,1536]{2,1,0:T(8,128)(2,1)S(1)}, u32[]{:S(2)}, u32[]{:S(2)}) %collective-permute-start.17) | collective-permute-done | bytes 196640 | tf_op jit(solution)/shard_map/ppermute | solution.py:241
  73.8 1.4 %collective-permute-done.18 = bf16[2,32,1536]{2,1,0:T(8,128)(2,1)S(1)} collective-permute-done((bf16[2,32,1536]{2,1,0:T(8,128)(2,1)S(1)}, bf16[2,32,1536]{2,1,0:T(8,128)(2,1)S(1)}, u32[]{:S(2)}, u32[]{:S(2)}) %collective-permute-start.18) | collective-permute-done | bytes 196640 | tf_op jit(solution)/shard_map/ppermute | solution.py:241
  75.3 4.0 %collective-permute-done.19 = bf16[2,32,1536]{2,1,0:T(8,128)(2,1)S(1)} collective-permute-done((bf16[2,32,1536]{2,1,0:T(8,128)(2,1)S(1)}, bf16[2,32,1536]{2,1,0:T(8,128)(2,1)S(1)}, u32[]{:S(2)}, u32[]{:S(2)}) %collective-permute-start.19) | collective-permute-done | bytes 196640 | tf_op jit(solution)/shard_map/ppermute | solution.py:241
  79.2 0.8 fusion
  (59 shorter events, 6.1 us)
Async XLA Ops:
  0.0 0.7 copy-start.10
  0.0 0.7 copy-start.9
  1.6 1.1 %copy-start = (bf16[1,6,32,1536]{3,2,1,0:T(8,128)(2,1)S(1)}, bf16[1,6,32,1536]{3,2,1,0:T(8,128)(2,1)}, u32[]{:S(2)}) copy-start(bf16[1,6,32,1536]{3,2,1,0:T(8,128)(2,1)} %param.11) | copy-start | bytes 1769476
  2.7 3.7 %copy-start.1 = (bf16[48,3072]{1,0:T(8,128)(2,1)S(1)}, bf16[48,3072]{1,0:T(8,128)(2,1)}, u32[]{:S(2)}) copy-start(bf16[48,3072]{1,0:T(8,128)(2,1)} %weights.1) | copy-start | bytes 884740
  3.3 11.1 %collective-permute-start = (bf16[2,32,1536]{2,1,0:T(8,128)(2,1)S(1)}, bf16[2,32,1536]{2,1,0:T(8,128)(2,1)S(1)}, u32[]{:S(2)}, u32[]{:S(2)}) collective-permute-start(bf16[2,32,1536]{2,1,0:T(8,128)(2,1)S(1)} %get-tuple-element.35), channel_id=1, source_target_pairs={{0,4},{1,5},{2,6},{3,7},{4,0},{5,1},{6,2},{7,3},{8,12},{9,13},{10,... | collective-permute-start | bytes 589832 | tf_op jit(solution)/shard_map/ppermute | solution.py:241
  6.5 7.9 %collective-permute-start.4 = (bf16[48,768]{1,0:T(8,128)(2,1)S(1)}, bf16[48,768]{1,0:T(8,128)(2,1)S(1)}, u32[]{:S(2)}, u32[]{:S(2)}) collective-permute-start(bf16[48,768]{1,0:T(8,128)(2,1)S(1)} %get-tuple-element.40), channel_id=1, source_target_pairs={{0,4},{1,5},{2,6},{3,7},{4,0},{5,1},{6,2},{7,3},{8,12},{9,13},{10,... | collective-permute-start | bytes 221192 | tf_op jit(solution)/shard_map/ppermute | solution.py:241
  6.8 7.6 %collective-permute-start.5 = (bf16[48,768]{1,0:T(8,128)(2,1)S(1)}, bf16[48,768]{1,0:T(8,128)(2,1)S(1)}, u32[]{:S(2)}, u32[]{:S(2)}) collective-permute-start(bf16[48,768]{1,0:T(8,128)(2,1)S(1)} %get-tuple-element.41), channel_id=1, source_target_pairs={{0,8},{1,9},{2,10},{3,11},{4,12},{5,13},{6,14},{7,15},{8,0},{9,1},... | collective-permute-start | bytes 221192 | tf_op jit(solution)/shard_map/ppermute | solution.py:241
  8.7 5.8 %collective-permute-start.6 = (bf16[48,768]{1,0:T(8,128)(2,1)S(1)}, bf16[48,768]{1,0:T(8,128)(2,1)S(1)}, u32[]{:S(2)}, u32[]{:S(2)}) collective-permute-start(bf16[48,768]{1,0:T(8,128)(2,1)S(1)} %get-tuple-element.42), channel_id=1, source_target_pairs={{0,12},{1,13},{2,14},{3,15},{4,8},{5,9},{6,10},{7,11},{8,4},{9,5},... | collective-permute-start | bytes 221192 | tf_op jit(solution)/shard_map/ppermute | solution.py:241
  14.4 0.9 %copy-start.5 = (bf16[48,1536]{1,0:T(8,128)(2,1)S(1)}, bf16[48,1536]{1,0:T(8,128)(2,1)}, u32[]{:S(2)}) copy-start(bf16[48,1536]{1,0:T(8,128)(2,1)} %param.17) | copy-start | bytes 442372
  15.4 10.7 %copy-start.4 = (f32[31,1536]{1,0:T(8,128)S(1)}, f32[31,1536]{1,0:T(8,128)}, u32[]{:S(2)}) copy-start(f32[31,1536]{1,0:T(8,128)} %param.14) | copy-start | bytes 571396
  15.4 7.4 %copy-start.6 = (f32[1536]{0:T(1024)S(1)}, f32[1536]{0:T(1024)}, u32[]{:S(2)}) copy-start(f32[1536]{0:T(1024)} %param.12) | copy-start | bytes 18436
  15.4 10.6 %collective-permute-start.8 = (bf16[6,48,768]{2,1,0:T(8,128)(2,1)S(1)}, bf16[6,48,768]{2,1,0:T(8,128)(2,1)S(1)}, u32[]{:S(2)}, u32[]{:S(2)}) collective-permute-start(bf16[6,48,768]{2,1,0:T(8,128)(2,1)S(1)} %bitcast_dynamic-update-slice_fusion.refs_4_), channel_id=1, source_target_pairs={{0,2},{1,3},{2,0},{3,1},{4,6},{5,7},{6,4},{7,5},{8,10},{9,11},{10,... | collective-permute-start | bytes 1327112 | tf_op jit(solution)/shard_map/ppermute | solution.py:241
  17.2 30.8 %collective-permute-start.13 = (bf16[6,48,768]{2,1,0:T(8,128)(2,1)S(1)}, bf16[6,48,768]{2,1,0:T(8,128)(2,1)S(1)}, u32[]{:S(2)}, u32[]{:S(2)}) collective-permute-start(bf16[6,48,768]{2,1,0:T(8,128)(2,1)S(1)} %bitcast_dynamic-update-slice_fusion.refs_4_), channel_id=1, source_target_pairs={{0,16},{1,17},{2,18},{3,19},{4,20},{5,21},{6,22},{7,23},{8,24},{9,... | collective-permute-start | bytes 1327112 | tf_op jit(solution)/shard_map/ppermute | solution.py:241
  19.8 3.0 %copy-start.7 = (f32[1536]{0:T(1024)S(1)}, f32[1536]{0:T(1024)}, u32[]{:S(2)}) copy-start(f32[1536]{0:T(1024)} %param.15) | copy-start | bytes 18436
  19.8 13.8 %collective-permute-start.1 = (bf16[2,32,1536]{2,1,0:T(8,128)(2,1)S(1)}, bf16[2,32,1536]{2,1,0:T(8,128)(2,1)S(1)}, u32[]{:S(2)}, u32[]{:S(2)}) collective-permute-start(bf16[2,32,1536]{2,1,0:T(8,128)(2,1)S(1)} %get-tuple-element.36), channel_id=1, source_target_pairs={{0,8},{1,9},{2,10},{3,11},{4,12},{5,13},{6,14},{7,15},{8,0},{9,1},... | collective-permute-start | bytes 589832 | tf_op jit(solution)/shard_map/ppermute | solution.py:241
  21.3 14.4 %collective-permute-start.2 = (bf16[2,32,1536]{2,1,0:T(8,128)(2,1)S(1)}, bf16[2,32,1536]{2,1,0:T(8,128)(2,1)S(1)}, u32[]{:S(2)}, u32[]{:S(2)}) collective-permute-start(bf16[2,32,1536]{2,1,0:T(8,128)(2,1)S(1)} %get-tuple-element.37), channel_id=1, source_target_pairs={{0,12},{1,13},{2,14},{3,15},{4,8},{5,9},{6,10},{7,11},{8,4},{9,5},... | collective-permute-start | bytes 589832 | tf_op jit(solution)/shard_map/ppermute | solution.py:241
  22.8 0.7 copy-start.8
  23.5 25.2 %collective-permute-start.7 = (bf16[6,48,768]{2,1,0:T(8,128)(2,1)S(1)}, bf16[6,48,768]{2,1,0:T(8,128)(2,1)S(1)}, u32[]{:S(2)}, u32[]{:S(2)}) collective-permute-start(bf16[6,48,768]{2,1,0:T(8,128)(2,1)S(1)} %bitcast_dynamic-update-slice_fusion.refs_4_), channel_id=1, source_target_pairs={{0,1},{1,0},{2,3},{3,2},{4,5},{5,4},{6,7},{7,6},{8,9},{9,8},{10,11... | collective-permute-start | bytes 1327112 | tf_op jit(solution)/shard_map/ppermute | solution.py:241
  26.0 22.7 %collective-permute-start.9 = (bf16[6,48,768]{2,1,0:T(8,128)(2,1)S(1)}, bf16[6,48,768]{2,1,0:T(8,128)(2,1)S(1)}, u32[]{:S(2)}, u32[]{:S(2)}) collective-permute-start(bf16[6,48,768]{2,1,0:T(8,128)(2,1)S(1)} %collective-permute-done.8.refs_6_), channel_id=1, source_target_pairs={{0,1},{1,0},{2,3},{3,2},{4,5},{5,4},{6,7},{7,6},{8,9},{9,8},{10,11... | collective-permute-start | bytes 1327112 | tf_op jit(solution)/shard_map/ppermute | solution.py:241
  36.4 11.0 %collective-permute-start.3 = (bf16[2,32,1536]{2,1,0:T(8,128)(2,1)S(1)}, bf16[2,32,1536]{2,1,0:T(8,128)(2,1)S(1)}, u32[]{:S(2)}, u32[]{:S(2)}) collective-permute-start(bf16[2,32,1536]{2,1,0:T(8,128)(2,1)S(1)} %shard_map.111), channel_id=1, source_target_pairs={{0,16},{1,17},{2,18},{3,19},{4,20},{5,21},{6,22},{7,23},{8,24},{9,... | collective-permute-start | bytes 589832 | tf_op jit(solution)/shard_map/ppermute | solution.py:241
  40.6 8.0 %copy-start.11 = (s32[8]{0:T(128)S(1)}, s32[8]{0:T(128)}, u32[]{:S(2)}) copy-start(s32[8]{0:T(128)} %constant.58.clone) | copy-start | bytes 100
  47.3 0.7 copy-start.2
  48.0 11.0 %collective-permute-start.14 = (bf16[6,48,768]{2,1,0:T(8,128)(2,1)S(1)}, bf16[6,48,768]{2,1,0:T(8,128)(2,1)S(1)}, u32[]{:S(2)}, u32[]{:S(2)}) collective-permute-start(bf16[6,48,768]{2,1,0:T(8,128)(2,1)S(1)} %collective-permute-done.13.refs_5_), channel_id=1, source_target_pairs={{0,2},{1,3},{2,0},{3,1},{4,6},{5,7},{6,4},{7,5},{8,10},{9,11},{10,... | collective-permute-start | bytes 1327112 | tf_op jit(solution)/shard_map/ppermute | solution.py:241
  48.7 0.9 %copy-start.3 = (bf16[2,32,1536]{2,1,0:T(8,128)(2,1)S(1)}, bf16[2,32,1536]{2,1,0:T(8,128)(2,1)}, u32[]{:S(2)}) copy-start(bf16[2,32,1536]{2,1,0:T(8,128)(2,1)} %copy-done.2) | copy-start | bytes 589828
  50.7 8.6 %collective-permute-start.12 = (bf16[2,32,1536]{2,1,0:T(8,128)(2,1)S(1)}, bf16[2,32,1536]{2,1,0:T(8,128)(2,1)S(1)}, u32[]{:S(2)}, u32[]{:S(2)}) collective-permute-start(bf16[2,32,1536]{2,1,0:T(8,128)(2,1)S(1)} %get-tuple-element.50.refs_0_), channel_id=1, source_target_pairs={{0,12},{1,13},{2,14},{3,15},{4,8},{5,9},{6,10},{7,11},{8,4},{9,5},... | collective-permute-start | bytes 589832 | tf_op jit(solution)/shard_map/ppermute | solution.py:241
  50.9 9.4 %collective-permute-start.11 = (bf16[2,32,1536]{2,1,0:T(8,128)(2,1)S(1)}, bf16[2,32,1536]{2,1,0:T(8,128)(2,1)S(1)}, u32[]{:S(2)}, u32[]{:S(2)}) collective-permute-start(bf16[2,32,1536]{2,1,0:T(8,128)(2,1)S(1)} %get-tuple-element.50.refs_0_), channel_id=1, source_target_pairs={{0,8},{1,9},{2,10},{3,11},{4,12},{5,13},{6,14},{7,15},{8,0},{9,1},... | collective-permute-start | bytes 589832 | tf_op jit(solution)/shard_map/ppermute | solution.py:241
  52.7 8.7 %collective-permute-start.10 = (bf16[2,32,1536]{2,1,0:T(8,128)(2,1)S(1)}, bf16[2,32,1536]{2,1,0:T(8,128)(2,1)S(1)}, u32[]{:S(2)}, u32[]{:S(2)}) collective-permute-start(bf16[2,32,1536]{2,1,0:T(8,128)(2,1)S(1)} %get-tuple-element.50.refs_0_), channel_id=1, source_target_pairs={{0,4},{1,5},{2,6},{3,7},{4,0},{5,1},{6,2},{7,3},{8,12},{9,13},{10,... | collective-permute-start | bytes 589832 | tf_op jit(solution)/shard_map/ppermute | solution.py:241
  54.2 7.3 %collective-permute-start.15 = (bf16[6,48,768]{2,1,0:T(8,128)(2,1)S(1)}, bf16[6,48,768]{2,1,0:T(8,128)(2,1)S(1)}, u32[]{:S(2)}, u32[]{:S(2)}) collective-permute-start(bf16[6,48,768]{2,1,0:T(8,128)(2,1)S(1)} %collective-permute-done.13.refs_5_), channel_id=1, source_target_pairs={{0,1},{1,0},{2,3},{3,2},{4,5},{5,4},{6,7},{7,6},{8,9},{9,8},{10,11... | collective-permute-start | bytes 1327112 | tf_op jit(solution)/shard_map/ppermute | solution.py:241
  61.4 1.8 %collective-permute-start.16 = (bf16[6,48,768]{2,1,0:T(8,128)(2,1)S(1)}, bf16[6,48,768]{2,1,0:T(8,128)(2,1)S(1)}, u32[]{:S(2)}, u32[]{:S(2)}) collective-permute-start(bf16[6,48,768]{2,1,0:T(8,128)(2,1)S(1)} %collective-permute-done.14.refs_7_), channel_id=1, source_target_pairs={{0,1},{1,0},{2,3},{3,2},{4,5},{5,4},{6,7},{7,6},{8,9},{9,8},{10,11... | collective-permute-start | bytes 1327112 | tf_op jit(solution)/shard_map/ppermute | solution.py:241
  66.8 7.0 %collective-permute-start.17 = (bf16[2,32,1536]{2,1,0:T(8,128)(2,1)S(1)}, bf16[2,32,1536]{2,1,0:T(8,128)(2,1)S(1)}, u32[]{:S(2)}, u32[]{:S(2)}) collective-permute-start(bf16[2,32,1536]{2,1,0:T(8,128)(2,1)S(1)} %get-tuple-element.54), channel_id=1, source_target_pairs={{0,4},{1,5},{2,6},{3,7},{4,0},{5,1},{6,2},{7,3},{8,12},{9,13},{10,... | collective-permute-start | bytes 589832 | tf_op jit(solution)/shard_map/ppermute | solution.py:241
  67.5 7.8 %collective-permute-start.18 = (bf16[2,32,1536]{2,1,0:T(8,128)(2,1)S(1)}, bf16[2,32,1536]{2,1,0:T(8,128)(2,1)S(1)}, u32[]{:S(2)}, u32[]{:S(2)}) collective-permute-start(bf16[2,32,1536]{2,1,0:T(8,128)(2,1)S(1)} %get-tuple-element.55), channel_id=1, source_target_pairs={{0,8},{1,9},{2,10},{3,11},{4,12},{5,13},{6,14},{7,15},{8,0},{9,1},... | collective-permute-start | bytes 589832 | tf_op jit(solution)/shard_map/ppermute | solution.py:241
  68.2 11.0 %collective-permute-start.19 = (bf16[2,32,1536]{2,1,0:T(8,128)(2,1)S(1)}, bf16[2,32,1536]{2,1,0:T(8,128)(2,1)S(1)}, u32[]{:S(2)}, u32[]{:S(2)}) collective-permute-start(bf16[2,32,1536]{2,1,0:T(8,128)(2,1)S(1)} %get-tuple-element.56), channel_id=1, source_target_pairs={{0,12},{1,13},{2,14},{3,15},{4,8},{5,9},{6,10},{7,11},{8,4},{9,5},... | collective-permute-start | bytes 589832 | tf_op jit(solution)/shard_map/ppermute | solution.py:241

commit v8 on v4

--- a/solution.py
+++ b/solution.py
@@ -52,7 +52,8 @@
         return self.ref[2 * self.size + source * self.slots + slot]
 
 
-def own_columns(highs, weights, owner, width):
+def own_columns(highs, weights, owner):
+    width = weights.shape[1] // 2
     run = width // (highs * QUAD)
     parts = [
         weights[:, pl.ds(half * width + (high * QUAD + owner) * run, run)]
@@ -70,7 +71,7 @@
     long, width = frames.shape[1:]
     wide = outs[0].shape[1]
     for owner in range(QUAD):
-        buf[owner] = own_columns(highs, weights, owner, width)
+        buf[owner] = own_columns(highs, weights, owner)
     for number, out in enumerate(outs):
         for far in range(highs):
             target = jnp.bitwise_xor(me, far * QUAD + number)
@@ -92,7 +93,7 @@
         out[number, :, half * wide : half * wide + wide] = ref[start : start + long, :]
 
 
-def merge_kernel(sources, place, packed, last, *refs):
+def merge_kernel(sources, place, packed, *refs):
     arrived, outs, piece = refs[:QUAD], refs[QUAD:-1], refs[-1]
     tables = Tables(packed, sources)
     me = place[0]
@@ -113,26 +114,20 @@
 
     for number, ref in enumerate(arrived):
         piece[number] = ref[ref.shape[0] - depth :, :]
-    for half in range(piece.shape[0] - QUAD):
-        piece[QUAD + half] = last[:, half * wide : half * wide + wide]
-
-
-def split_kernel(highs, place, weights, *refs):
-    outs, buf = refs[:-1], refs[-1]
-    for owner in range(QUAD):
-        buf[owner] = own_columns(highs, weights, owner, weights.shape[1] // 3)
-    for number, out in enumerate(outs):
-        out[...] = buf[jnp.bitwise_xor(lax.rem(place[0], QUAD), number)]
-
-
-def stack_kernel(both, *refs):
-    columns, piece = refs[:-1], refs[-1]
-    wide = piece.shape[2]
-    last = both.at[:, both.shape[1] // 3 * 2 :]
-    for number, ref in enumerate(columns):
-        piece[number] = ref[...]
-    for half in range(piece.shape[0] - QUAD):
-        piece[QUAD + half] = last[:, half * wide : half * wide + wide]
+
+
+def stack_kernel(*refs):
+    parts, out = refs[:-1], refs[-1]
+    wide = out.shape[2]
+    at = 0
+    for ref in parts:
+        if len(ref.shape) == 3:
+            out[at : at + ref.shape[0]] = ref[...]
+            at += ref.shape[0]
+        else:
+            for first in range(0, ref.shape[1], wide):
+                out[at] = ref[:, first : first + wide]
+                at += 1
 
 
 def table_kernel(source_count, long, place, packed, small, sources, lens, table, gain):
@@ -213,29 +208,32 @@
     return total
 
 
-def main_kernel(pieces, where, kept, table, *refs):
+def main_kernel(layout, where, kept, table, *refs):
+    pieces = max(len(layout), 2)
+    chans = table.shape[1]
+    taps = table[: table.shape[0] - 2, :]
+    scale, shift = table[table.shape[0] - 2 : table.shape[0] - 1, :], table[table.shape[0] - 1 :, :]
     normed, weights = refs[:QUAD], refs[QUAD : QUAD + pieces]
     own, outs = refs[QUAD + pieces], refs[QUAD + pieces + 1 : 2 * QUAD + pieces]
     rows_buf, in_buf, out_buf, glu_buf, act_buf = refs[2 * QUAD + pieces :]
     recv, long, width = kept.shape
     tall = recv * long
-    chans = table.shape[1]
-    taps = table[: table.shape[0] - 2, :]
-    scale, shift = table[table.shape[0] - 2 : table.shape[0] - 1, :], table[table.shape[0] - 1 :, :]
     for number, ref in enumerate(normed):
         rows_buf[pl.ds(number * tall, tall), :] = ref[...].reshape(tall, width)
-    if pieces == 2:
-        w_in, w_out = weights
-    else:
+    if layout:
         w_in, w_out = in_buf, out_buf
         depth, wide = weights[0].shape[1:]
-        for number, ref in enumerate(weights):
-            for inner in range(QUAD):
-                start = pl.multiple_of(where[number, inner] * depth, 16)
-                in_buf[pl.ds(start, depth), :] = ref[inner]
-            start = pl.multiple_of(where[number, QUAD] * depth, 16)
-            for half in range(width // wide):
-                out_buf[pl.ds(start, depth), half * wide : half * wide + wide] = ref[QUAD + half]
+        for ref, slabs in zip(weights, layout):
+            for at, (kind, other, number) in enumerate(slabs):
+                if kind == "in":
+                    start = pl.multiple_of(where[other, number] * depth, 16)
+                    in_buf[pl.ds(start, depth), :] = ref[at]
+                else:
+                    start = pl.multiple_of(where[other, QUAD] * depth, 16)
+                    first = number * wide
+                    out_buf[pl.ds(start, depth), first : first + wide] = ref[at]
+    else:
+        w_in, w_out = weights
     glu_in = jnp.dot(rows_buf[...], w_in[...], preferred_element_type=F32)
     glu_buf[...] = glu_in[:, :chans] * jax.nn.sigmoid(glu_in[:, chans:])
 
@@ -282,12 +280,21 @@
     place = dp_index.astype(jnp.int32)[None]
     packed = jnp.stack([lengths[0], destinations[0], offsets[0]]).reshape(-1)
     small = jnp.concatenate([depth_kernel, bn_scale[None], bn_shift[None], ln_gain[None]])
-    count = width // wide
     bits = [1 << at for at in range((highs * fsdp_count).bit_length() - 1)]
     chip_bits = [bit for bit in reversed(bits) if 1 < bit < fsdp_count]
 
-    both = jnp.concatenate([w_in, w_out], axis=1)
-    far_rows = [swap(both, high=mask) for mask in range(1, highs)]
+    count = width // wide
+
+    outs = {0: w_out}
+
+    def share_chips(parts, first):
+        for bit in chip_bits:
+            for shift in [shift for shift in parts if (shift >= fsdp_count) == first]:
+                parts[shift ^ bit] = swap(parts[shift], fsdp=bit)
+
+    for mask in range(1, highs):
+        outs[mask * fsdp_count] = swap(w_out, high=mask)
+    share_chips(outs, False)
 
     near = call(
         functools.partial(send_kernel, dp_count),
@@ -306,72 +313,80 @@
         (place, packed, small),
     )
     utts = like(BF16, recv, long, width)
-    block = like(BF16, QUAD + count, depth, wide)
-    *far, piece = call(
+    *far, own_in = call(
         functools.partial(merge_kernel, dp_count),
-        [utts] * (highs - 1) + [block],
-        [SMEM] * 2 + [VMEM] * (1 + QUAD),
+        [utts] * (highs - 1) + [like(BF16, QUAD, depth, wide)],
+        [SMEM] * 2 + [VMEM] * QUAD,
         [VMEM] * highs,
-        (gated(place, (lens, gain)), packed, w_out, *near),
-    )
-    pieces = [piece]
-    shifts = [mask * fsdp_count for mask in range(highs)]
-    far_rows = gated(far_rows, far)
+        (gated(place, (lens, gain, outs)), packed, *near),
+    )
     far = [swap(part, high=mask) for mask, part in enumerate(far, 1)]
-    for part in far_rows:
-        columns = call(
-            functools.partial(split_kernel, highs),
-            [like(BF16, depth, wide)] * QUAD,
-            [SMEM, VMEM],
-            [VMEM] * QUAD,
-            (place, part),
-            [like(BF16, QUAD, depth, wide)],
-        )
-        pieces.append(
-            call(
-                stack_kernel,
-                block,
-                [VMEM] * (1 + QUAD),
-                VMEM,
-                (part, *gated(quad_swap(columns), far)),
-            )
-        )
-    early = len(pieces)
-    cored = [swap(part, fsdp=1) for part in pieces]
-    far = gated(far, (pieces, cored[:1]))
-    for bit in chip_bits:
-        pieces = pieces + [swap(part, fsdp=bit) for part in pieces]
-        shifts = shifts + [shift ^ bit for shift in shifts]
-
+
+    ins = {0: own_in}
+    far_in = [swap(own_in, high=mask) for mask in range(1, highs)]
+    share_chips(ins, False)
+    early = list(ins)
+    share_chips(outs, True)
+    order = sorted(outs)
+    stacked = call(
+        stack_kernel,
+        like(BF16, len(order) * count, depth, wide),
+        [VMEM] * len(order),
+        VMEM,
+        [outs[shift] for shift in order],
+    )
+    crossed = {shift: swap(ins[shift], fsdp=1) for shift in early}
+    crossed_out = swap(stacked, fsdp=1)
+    for mask, part in enumerate(gated(far_in, far), 1):
+        ins[mask * fsdp_count] = part
     kept, normed = call(
         norm_kernel,
         [utts, utts],
         [SMEM] * 3 + [VMEM] * (QUAD + highs),
         [VMEM, VMEM],
-        (place, sources, lens, gain, *near, *far),
-    )
+        (place, sources, lens, gain, *near, *gated(far, (crossed, crossed_out))),
+    )
+    share_chips(ins, True)
     normed = quad_swap([normed] * QUAD)
-    late = pieces[early:]
-    crossed = swap(jnp.stack(gated(late, normed[1:3])), fsdp=1)
-    pieces = pieces + cored + [crossed[at] for at in range(len(late))]
-    shifts = shifts + [shift ^ 1 for shift in shifts]
-
-    out_rows = line ^ jnp.array(shifts)
+    chip_mask = (fsdp_count - 1) ^ 1
+    last = {at: ins[at] for at in ins if at & chip_mask and at not in early}
+    last = gated(last, normed)
+    for shift in ins:
+        if shift not in crossed:
+            crossed[shift] = swap(last.get(shift, ins[shift]), fsdp=1)
+    pieces = list(ins.values()) + [stacked]
+    layout = [[("in", shift, number) for number in range(QUAD)] for shift in ins]
+    layout.append([("out", shift, half) for shift in order for half in range(count)])
+    pieces += [crossed[shift] for shift in ins] + [crossed_out]
+    layout += [[(kind, shift ^ 1, at) for kind, shift, at in slabs] for slabs in layout]
+
+    out_rows = line ^ jnp.arange(highs * fsdp_count)
     in_rows = out_rows // fsdp_count * QUAD
     in_rows = in_rows[:, None] + (quad ^ jnp.arange(QUAD))[None, :]
     in_rows = in_rows * fsdp_count + (out_rows % fsdp_count)[:, None]
     where = jnp.concatenate([in_rows, out_rows[:, None]], 1).astype(jnp.int32)
     if depth % 16:
-        together = jnp.stack(pieces)
-        flat = together[:, :QUAD].reshape(-1, depth, wide)
+        slabs = {
+            name: part[at]
+            for part, names in zip(pieces, layout)
+            for at, name in enumerate(names)
+        }
+        sides = range(highs * fsdp_count)
+        flat = jnp.stack([slabs["in", at, number] for at in sides for number in range(QUAD)])
         all_in = jnp.zeros_like(flat).at[where[:, :QUAD].reshape(-1)].set(flat)
-        flat = together[:, QUAD:].transpose(0, 2, 1, 3).reshape(-1, depth, width)
+        flat = jnp.stack(
+            [
+                jnp.concatenate([slabs["out", at, half] for half in range(count)], axis=1)
+                for at in sides
+            ]
+        )
         all_out = jnp.zeros_like(flat).at[where[:, QUAD]].set(flat)
         pieces = [all_in.reshape(width, wide), all_out.reshape(chans, width)]
+        layout = []
 
     tall = QUAD * recv * long
     partial_sums = call(
-        functools.partial(main_kernel, len(pieces)),
+        functools.partial(main_kernel, layout),
         [like(F32, recv, long, width)] + [utts] * (QUAD - 1),
         [SMEM] + [VMEM] * (2 + QUAD + len(pieces)),
         [VMEM] * QUAD,

time: 88.9 us -> 84.5 us (0.951)
  waiting for transfers between devices: 53.8 us -> 47.4 us
  other arithmetic: 3.23 us -> 1.76 us
  starting transfers between devices: 20.5 us -> 21.9 us
  Pallas kernels: 8.06 us -> 9.36 us
    ppermute x19 -> x21, waiting for transfers between devices: 53.8 us -> 47.4 us  [swap(): lax.ppermute(array, ('dp', 'fsdp'), [(at, at ^ mask) for at in range(devi...]
    unnamed x22 -> x18, local copies, waits for them, and re-layouts: 1.36 us -> 3.41 us
    ppermute x19 -> x21, starting transfers between devices: 20.5 us -> 21.9 us  [swap(): lax.ppermute(array, ('dp', 'fsdp'), [(at, at ^ mask) for at in range(devi...]
    pallas_call x7 -> x6, Pallas kernels: 8.06 us -> 9.36 us  [call(): pl.pallas_call(kernel, out_shape=out_shape, in_specs=in_specs, out_specs=...]
    squeeze x1 -> x0, local copies, waits for them, and re-layouts: 1.2 us -> none  [shards(): pieces = pieces + cored + [crossed[at] for at in range(len(late))]]
    concatenate x1 -> x0, other arithmetic: 1.14 us -> none  [shards(): both = jnp.concatenate([w_in, w_out], axis=1)]
    another operation x1 -> x0, other arithmetic: 1.01 us -> none  [shards(): crossed = swap(jnp.stack(gated(late, normed[1:3])), fsdp=1)]
  transfers between devices with their start and end apart: 19 -> 21, of which waited for: 12 -> 13; matrix products, arithmetic and copies ran while one was open for 2% -> 1% of each run, Pallas kernels for 5% -> 6%
where the time goes in v8:
time: 84.5 us; the launch traced here: 84.2 us
  waiting for transfers between devices  47.4 us (56%)
  starting transfers between devices  21.9 us (26%)
  Pallas kernels  9.36 us (11%)
  local copies, waits for them, and re-layouts  3.62 us (4%)
  other arithmetic  1.76 us (2%)
    ppermute x21, waiting for transfers between devices, swap(): lax.ppermute(array, ('dp', 'fsdp'), [(at, at ^ mask) for at in range(devi...  47.4 us
    ppermute x21, starting transfers between devices, swap(): lax.ppermute(array, ('dp', 'fsdp'), [(at, at ^ mask) for at in range(devi...  21.9 us
    pallas_call x6, Pallas kernels, call(): pl.pallas_call(kernel, out_shape=out_shape, in_specs=in_specs, out_specs=...  9.36 us
    unnamed x18, local copies, waits for them, and re-layouts  3.41 us
  transfers between devices with their start and end apart: 21, of which 13 were waited for; matrix products, arithmetic and copies ran while one was open for 1% of the time, Pallas kernels for 6%

profile of v8, /device:TPU:0, one launch (start us, length us, event | category | flops | bytes accessed | tf_op | source)
XLA Modules:
  0.0 84.2 jit_solution(11390914522082092449)
XLA Ops:
  0.0 4.0 %collective-permute-start.4 = (bf16[48,1536]{1,0:T(8,128)(2,1)}, bf16[48,1536]{1,0:T(8,128)(2,1)S(1)}, u32[]{:S(2)}, u32[]{:S(2)}) collective-permute-start(bf16[48,1536]{1,0:T(8,128)(2,1)} %refs_0_.1), channel_id=1, source_target_pairs={{0,16},{1,17},{2,18},{3,19},{4,20},{5,21},{6,22},{7,23},{8,24},{9,... | collective-permute-start | bytes 442376 | tf_op jit(solution)/shard_map/ppermute | solution.py:272
  4.7 0.7 pad_add_fusion
  5.6 1.1 %copy-done = bf16[1,6,32,1536]{3,2,1,0:T(8,128)(2,1)S(1)} copy-done((bf16[1,6,32,1536]{3,2,1,0:T(8,128)(2,1)S(1)}, bf16[1,6,32,1536]{3,2,1,0:T(8,128)(2,1)}, u32[]{:S(2)}) %copy-start) | copy-done | bytes 589848
  6.7 1.0 %copy-done.1 = bf16[48,3072]{1,0:T(8,128)(2,1)S(1)} copy-done((bf16[48,3072]{1,0:T(8,128)(2,1)S(1)}, bf16[48,3072]{1,0:T(8,128)(2,1)}, u32[]{:S(2)}) %copy-start.1) | copy-done | bytes 294936
  7.7 0.7 shard_map.101
  8.4 1.6 %collective-permute-start = (bf16[176,768]{1,0:T(8,128)(2,1)S(1)}, bf16[176,768]{1,0:T(8,128)(2,1)S(1)}, u32[]{:S(2)}, u32[]{:S(2)}) collective-permute-start(bf16[176,768]{1,0:T(8,128)(2,1)S(1)} %get-tuple-element.29), channel_id=1, source_target_pairs={{0,4},{1,5},{2,6},{3,7},{4,0},{5,1},{6,2},{7,3},{8,12},{9,13},{10,... | collective-permute-start | bytes 811016 | tf_op jit(solution)/shard_map/ppermute | solution.py:272
  10.0 1.6 %collective-permute-start.1 = (bf16[176,768]{1,0:T(8,128)(2,1)S(1)}, bf16[176,768]{1,0:T(8,128)(2,1)S(1)}, u32[]{:S(2)}, u32[]{:S(2)}) collective-permute-start(bf16[176,768]{1,0:T(8,128)(2,1)S(1)} %get-tuple-element.30), channel_id=1, source_target_pairs={{0,8},{1,9},{2,10},{3,11},{4,12},{5,13},{6,14},{7,15},{8,0},{9,1},... | collective-permute-start | bytes 811016 | tf_op jit(solution)/shard_map/ppermute | solution.py:272
  11.9 1.5 %collective-permute-start.3 = (bf16[48,1536]{1,0:T(8,128)(2,1)S(1)}, bf16[48,1536]{1,0:T(8,128)(2,1)S(1)}, u32[]{:S(2)}, u32[]{:S(2)}) collective-permute-start(bf16[48,1536]{1,0:T(8,128)(2,1)S(1)} %copy-done.2), channel_id=1, source_target_pairs={{0,2},{1,3},{2,0},{3,1},{4,6},{5,7},{6,4},{7,5},{8,10},{9,11},{10,... | collective-permute-start | bytes 442376 | tf_op jit(solution)/shard_map/ppermute | solution.py:272
  14.8 1.8 %shard_map.100 = (s32[2]{0:T(128)S(1)}, s32[2]{0:T(128)S(1)}, f32[33,384]{1,0:T(8,128)S(1)}, f32[1,1536]{1,0:T(1,128)S(1)}) custom-call(s32[1]{0:T(128)} %bitcast.place, s32[144]{0:T(256)S(1)} %reshape.70.packed, f32[34,1536]{1,0:T(8,128)S(1)} %pad_maximum_fusion.small), custom_call_target="tpu_custom_call" | custom-call | bytes 266324 | tf_op jit(solution)/shard_map/pallas_call | solution.py:21
  16.6 1.8 %collective-permute-done.3.refs_1_ = bf16[48,1536]{1,0:T(8,128)(2,1)S(1)} collective-permute-done((bf16[48,1536]{1,0:T(8,128)(2,1)S(1)}, bf16[48,1536]{1,0:T(8,128)(2,1)S(1)}, u32[]{:S(2)}, u32[]{:S(2)}) %collective-permute-start.3) | collective-permute-done | bytes 147488 | tf_op jit(solution)/shard_map/ppermute | solution.py:272
  18.4 1.0 %collective-permute-done.1.refs_2_ = bf16[176,768]{1,0:T(8,128)(2,1)S(1)} collective-permute-done((bf16[176,768]{1,0:T(8,128)(2,1)S(1)}, bf16[176,768]{1,0:T(8,128)(2,1)S(1)}, u32[]{:S(2)}, u32[]{:S(2)}) %collective-permute-start.1) | collective-permute-done | bytes 270368 | tf_op jit(solution)/shard_map/ppermute | solution.py:272
  19.4 4.5 %collective-permute-done.2.refs_3_ = bf16[176,768]{1,0:T(8,128)(2,1)S(1)} collective-permute-done((bf16[176,768]{1,0:T(8,128)(2,1)S(1)}, bf16[176,768]{1,0:T(8,128)(2,1)S(1)}, u32[]{:S(2)}, u32[]{:S(2)}) %collective-permute-start.2) | collective-permute-done | bytes 270368 | tf_op jit(solution)/shard_map/ppermute | solution.py:272
  23.8 1.4 %shard_map.102 = (bf16[2,32,1536]{2,1,0:T(8,128)(2,1)}, bf16[4,48,768]{2,1,0:T(8,128)(2,1)S(1)}) custom-call(s32[1]{0:T(128)} %bitcast.place, s32[144]{0:T(256)S(1)} %reshape.70.packed, bf16[176,768]{1,0:T(8,128)(2,1)S(1)} %get-tuple-element.28.refs_0_, bf16[176,768]{1,0:T(8,128)(2,1)S(1)} %collective-permute-done.refs_1_, ...), custom_call_target="tpu_custom_call" | custom-call | bytes 1573444 | tf_op jit(solution)/shard_map/pallas_call | solution.py:21
  25.2 1.5 %collective-permute-start.7 = (bf16[4,48,768]{2,1,0:T(8,128)(2,1)S(1)}, bf16[4,48,768]{2,1,0:T(8,128)(2,1)S(1)}, u32[]{:S(2)}, u32[]{:S(2)}) collective-permute-start(bf16[4,48,768]{2,1,0:T(8,128)(2,1)S(1)} %get-tuple-element.34.refs_4_), channel_id=1, source_target_pairs={{0,2},{1,3},{2,0},{3,1},{4,6},{5,7},{6,4},{7,5},{8,10},{9,11},{10,... | collective-permute-start | bytes 884744 | tf_op jit(solution)/shard_map/ppermute | solution.py:272
  26.8 0.7 collective-permute-start.14
  27.5 2.3 %collective-permute-start.5 = (bf16[2,32,1536]{2,1,0:T(8,128)(2,1)}, bf16[2,32,1536]{2,1,0:T(8,128)(2,1)}, u32[]{:S(2)}, u32[]{:S(2)}) collective-permute-start(bf16[2,32,1536]{2,1,0:T(8,128)(2,1)} %get-tuple-element.33), channel_id=1, source_target_pairs={{0,16},{1,17},{2,18},{3,19},{4,20},{5,21},{6,22},{7,23},{8,24},{9,... | collective-permute-start | bytes 589832 | tf_op jit(solution)/shard_map/ppermute | solution.py:272
  29.8 3.1 %collective-permute-done.7.refs_5_ = bf16[4,48,768]{2,1,0:T(8,128)(2,1)S(1)} collective-permute-done((bf16[4,48,768]{2,1,0:T(8,128)(2,1)S(1)}, bf16[4,48,768]{2,1,0:T(8,128)(2,1)S(1)}, u32[]{:S(2)}, u32[]{:S(2)}) %collective-permute-start.7) | collective-permute-done | bytes 294944 | tf_op jit(solution)/shard_map/ppermute | solution.py:272
  32.9 19.0 %collective-permute-done.5.refs_4_ = bf16[2,32,1536]{2,1,0:T(8,128)(2,1)} collective-permute-done((bf16[2,32,1536]{2,1,0:T(8,128)(2,1)}, bf16[2,32,1536]{2,1,0:T(8,128)(2,1)}, u32[]{:S(2)}, u32[]{:S(2)}) %collective-permute-start.5) | collective-permute-done | bytes 196640 | tf_op jit(solution)/shard_map/ppermute | solution.py:272
  52.6 1.4 %shard_map.104 = (bf16[2,32,1536]{2,1,0:T(8,128)(2,1)S(1)}, bf16[2,32,1536]{2,1,0:T(8,128)(2,1)S(1)}) custom-call(s32[1]{0:T(128)} %bitcast.place, s32[2]{0:T(128)S(1)} %get-tuple-element.26.sources, s32[2]{0:T(128)S(1)} %get-tuple-element.25.lens, f32[1,1536]{1,0:T(1,128)S(1)} %get-tuple-element.27.gain, bf16[176,768]{1,0:T(8,128)(2,1)S(1)} %get-tuple-element.28.refs_0_, ...), custom_call_target="tpu_custom_call" | custom-call | bytes 1677332 | tf_op jit(solution)/shard_map/pallas_call | solution.py:21
  54.1 2.5 %collective-permute-start.12 = (bf16[2,32,1536]{2,1,0:T(8,128)(2,1)S(1)}, bf16[2,32,1536]{2,1,0:T(8,128)(2,1)S(1)}, u32[]{:S(2)}, u32[]{:S(2)}) collective-permute-start(bf16[2,32,1536]{2,1,0:T(8,128)(2,1)S(1)} %get-tuple-element.38.refs_0_), channel_id=1, source_target_pairs={{0,8},{1,9},{2,10},{3,11},{4,12},{5,13},{6,14},{7,15},{8,0},{9,1},... | collective-permute-start | bytes 589832 | tf_op jit(solution)/shard_map/ppermute | solution.py:272
  56.6 1.0 %collective-permute-start.11 = (bf16[2,32,1536]{2,1,0:T(8,128)(2,1)S(1)}, bf16[2,32,1536]{2,1,0:T(8,128)(2,1)S(1)}, u32[]{:S(2)}, u32[]{:S(2)}) collective-permute-start(bf16[2,32,1536]{2,1,0:T(8,128)(2,1)S(1)} %get-tuple-element.38.refs_0_), channel_id=1, source_target_pairs={{0,4},{1,5},{2,6},{3,7},{4,0},{5,1},{6,2},{7,3},{8,12},{9,13},{10,... | collective-permute-start | bytes 589832 | tf_op jit(solution)/shard_map/ppermute | solution.py:272
  57.6 3.0 %collective-permute-done.15.refs_7_ = bf16[4,48,768]{2,1,0:T(8,128)(2,1)S(1)} collective-permute-done((bf16[4,48,768]{2,1,0:T(8,128)(2,1)S(1)}, bf16[4,48,768]{2,1,0:T(8,128)(2,1)S(1)}, u32[]{:S(2)}, u32[]{:S(2)}) %collective-permute-start.15) | collective-permute-done | bytes 294944 | tf_op jit(solution)/shard_map/ppermute | solution.py:272
  60.6 2.3 %collective-permute-done.13.refs_3_ = bf16[2,32,1536]{2,1,0:T(8,128)(2,1)S(1)} collective-permute-done((bf16[2,32,1536]{2,1,0:T(8,128)(2,1)S(1)}, bf16[2,32,1536]{2,1,0:T(8,128)(2,1)S(1)}, u32[]{:S(2)}, u32[]{:S(2)}) %collective-permute-start.13) | collective-permute-done | bytes 196640 | tf_op jit(solution)/shard_map/ppermute | solution.py:272
  62.8 2.1 %collective-permute-done.12.refs_2_ = bf16[2,32,1536]{2,1,0:T(8,128)(2,1)S(1)} collective-permute-done((bf16[2,32,1536]{2,1,0:T(8,128)(2,1)S(1)}, bf16[2,32,1536]{2,1,0:T(8,128)(2,1)S(1)}, u32[]{:S(2)}, u32[]{:S(2)}) %collective-permute-start.12) | collective-permute-done | bytes 196640 | tf_op jit(solution)/shard_map/ppermute | solution.py:272
  65.5 1.4 %collective-permute-done.17.refs_12_ = bf16[4,48,768]{2,1,0:T(8,128)(2,1)S(1)} collective-permute-done((bf16[4,48,768]{2,1,0:T(8,128)(2,1)S(1)}, bf16[4,48,768]{2,1,0:T(8,128)(2,1)S(1)}, u32[]{:S(2)}, u32[]{:S(2)}) %collective-permute-start.17) | collective-permute-done | bytes 294944 | tf_op jit(solution)/shard_map/ppermute | solution.py:272
  67.0 4.0 %shard_map.105 = (f32[2,32,1536]{2,1,0:T(8,128)S(1)}, bf16[2,32,1536]{2,1,0:T(8,128)(2,1)S(1)}, bf16[2,32,1536]{2,1,0:T(8,128)(2,1)S(1)}, bf16[2,32,1536]{2,1,0:T(8,128)(2,1)S(1)}) custom-call(s32[8,5]{1,0:T(8,128)S(1)} %pad_add_fusion.1.where, bf16[2,32,1536]{2,1,0:T(8,128)(2,1)S(1)} %get-tuple-element.36.kept, f32[33,384]{1,0:T(8,128)S(1)} %get-tuple-element.37.table, ...), custom_call_target="tpu_custom_call" | custom-call | flops 905969664 | bytes 10471072 | tf_op jit(solution)/shard_map/pallas_call | solution.py:21
  71.0 1.1 %collective-permute-start.18 = (bf16[2,32,1536]{2,1,0:T(8,128)(2,1)S(1)}, bf16[2,32,1536]{2,1,0:T(8,128)(2,1)S(1)}, u32[]{:S(2)}, u32[]{:S(2)}) collective-permute-start(bf16[2,32,1536]{2,1,0:T(8,128)(2,1)S(1)} %get-tuple-element.42), channel_id=1, source_target_pairs={{0,4},{1,5},{2,6},{3,7},{4,0},{5,1},{6,2},{7,3},{8,12},{9,13},{10,... | collective-permute-start | bytes 589832 | tf_op jit(solution)/shard_map/ppermute | solution.py:272
  72.1 2.4 %collective-permute-start.20 = (bf16[2,32,1536]{2,1,0:T(8,128)(2,1)S(1)}, bf16[2,32,1536]{2,1,0:T(8,128)(2,1)S(1)}, u32[]{:S(2)}, u32[]{:S(2)}) collective-permute-start(bf16[2,32,1536]{2,1,0:T(8,128)(2,1)S(1)} %get-tuple-element.44), channel_id=1, source_target_pairs={{0,12},{1,13},{2,14},{3,15},{4,8},{5,9},{6,10},{7,11},{8,4},{9,5},... | collective-permute-start | bytes 589832 | tf_op jit(solution)/shard_map/ppermute | solution.py:272
  74.6 3.4 %collective-permute-done.18 = bf16[2,32,1536]{2,1,0:T(8,128)(2,1)S(1)} collective-permute-done((bf16[2,32,1536]{2,1,0:T(8,128)(2,1)S(1)}, bf16[2,32,1536]{2,1,0:T(8,128)(2,1)S(1)}, u32[]{:S(2)}, u32[]{:S(2)}) %collective-permute-start.18) | collective-permute-done | bytes 196640 | tf_op jit(solution)/shard_map/ppermute | solution.py:272
  78.0 1.9 %collective-permute-done.19 = bf16[2,32,1536]{2,1,0:T(8,128)(2,1)S(1)} collective-permute-done((bf16[2,32,1536]{2,1,0:T(8,128)(2,1)S(1)}, bf16[2,32,1536]{2,1,0:T(8,128)(2,1)S(1)}, u32[]{:S(2)}, u32[]{:S(2)}) %collective-permute-start.19) | collective-permute-done | bytes 196640 | tf_op jit(solution)/shard_map/ppermute | solution.py:272
  79.9 3.5 %collective-permute-done.20 = bf16[2,32,1536]{2,1,0:T(8,128)(2,1)S(1)} collective-permute-done((bf16[2,32,1536]{2,1,0:T(8,128)(2,1)S(1)}, bf16[2,32,1536]{2,1,0:T(8,128)(2,1)S(1)}, u32[]{:S(2)}, u32[]{:S(2)}) %collective-permute-start.20) | collective-permute-done | bytes 196640 | tf_op jit(solution)/shard_map/ppermute | solution.py:272
  83.4 0.8 fusion
  (48 shorter events, 4.0 us)
Async XLA Ops:
  0.0 14.2 %collective-permute-start.4 = (bf16[48,1536]{1,0:T(8,128)(2,1)}, bf16[48,1536]{1,0:T(8,128)(2,1)S(1)}, u32[]{:S(2)}, u32[]{:S(2)}) collective-permute-start(bf16[48,1536]{1,0:T(8,128)(2,1)} %refs_0_.1), channel_id=1, source_target_pairs={{0,16},{1,17},{2,18},{3,19},{4,20},{5,21},{6,22},{7,23},{8,24},{9,... | collective-permute-start | bytes 442376 | tf_op jit(solution)/shard_map/ppermute | solution.py:272
  4.0 0.7 copy-start.8
  4.0 0.7 copy-start.7
  5.6 1.1 %copy-start = (bf16[1,6,32,1536]{3,2,1,0:T(8,128)(2,1)S(1)}, bf16[1,6,32,1536]{3,2,1,0:T(8,128)(2,1)}, u32[]{:S(2)}) copy-start(bf16[1,6,32,1536]{3,2,1,0:T(8,128)(2,1)} %param.10) | copy-start | bytes 1769476
  6.7 1.0 %copy-start.1 = (bf16[48,3072]{1,0:T(8,128)(2,1)S(1)}, bf16[48,3072]{1,0:T(8,128)(2,1)}, u32[]{:S(2)}) copy-start(bf16[48,3072]{1,0:T(8,128)(2,1)} %weights.1) | copy-start | bytes 884740
  7.7 4.3 %copy-start.2 = (bf16[48,1536]{1,0:T(8,128)(2,1)S(1)}, bf16[48,1536]{1,0:T(8,128)(2,1)}, u32[]{:S(2)}) copy-start(bf16[48,1536]{1,0:T(8,128)(2,1)} %refs_0_.1) | copy-start | bytes 442372
  7.7 5.8 %copy-start.4 = (f32[1536]{0:T(1024)S(1)}, f32[1536]{0:T(1024)}, u32[]{:S(2)}) copy-start(f32[1536]{0:T(1024)} %param.11) | copy-start | bytes 18436
  7.7 7.1 %copy-start.3 = (f32[31,1536]{1,0:T(8,128)S(1)}, f32[31,1536]{1,0:T(8,128)}, u32[]{:S(2)}) copy-start(f32[31,1536]{1,0:T(8,128)} %param.13) | copy-start | bytes 571396
  8.4 10.0 %collective-permute-start = (bf16[176,768]{1,0:T(8,128)(2,1)S(1)}, bf16[176,768]{1,0:T(8,128)(2,1)S(1)}, u32[]{:S(2)}, u32[]{:S(2)}) collective-permute-start(bf16[176,768]{1,0:T(8,128)(2,1)S(1)} %get-tuple-element.29), channel_id=1, source_target_pairs={{0,4},{1,5},{2,6},{3,7},{4,0},{5,1},{6,2},{7,3},{8,12},{9,13},{10,... | collective-permute-start | bytes 811016 | tf_op jit(solution)/shard_map/ppermute | solution.py:272
  10.0 3.5 %copy-start.5 = (f32[1536]{0:T(1024)S(1)}, f32[1536]{0:T(1024)}, u32[]{:S(2)}) copy-start(f32[1536]{0:T(1024)} %param.14) | copy-start | bytes 18436
  10.0 9.4 %collective-permute-start.1 = (bf16[176,768]{1,0:T(8,128)(2,1)S(1)}, bf16[176,768]{1,0:T(8,128)(2,1)S(1)}, u32[]{:S(2)}, u32[]{:S(2)}) collective-permute-start(bf16[176,768]{1,0:T(8,128)(2,1)S(1)} %get-tuple-element.30), channel_id=1, source_target_pairs={{0,8},{1,9},{2,10},{3,11},{4,12},{5,13},{6,14},{7,15},{8,0},{9,1},... | collective-permute-start | bytes 811016 | tf_op jit(solution)/shard_map/ppermute | solution.py:272
  11.6 12.3 %collective-permute-start.2 = (bf16[176,768]{1,0:T(8,128)(2,1)S(1)}, bf16[176,768]{1,0:T(8,128)(2,1)S(1)}, u32[]{:S(2)}, u32[]{:S(2)}) collective-permute-start(bf16[176,768]{1,0:T(8,128)(2,1)S(1)} %get-tuple-element.31), channel_id=1, source_target_pairs={{0,12},{1,13},{2,14},{3,15},{4,8},{5,9},{6,10},{7,11},{8,4},{9,5},... | collective-permute-start | bytes 811016 | tf_op jit(solution)/shard_map/ppermute | solution.py:272
  11.9 6.5 %collective-permute-start.3 = (bf16[48,1536]{1,0:T(8,128)(2,1)S(1)}, bf16[48,1536]{1,0:T(8,128)(2,1)S(1)}, u32[]{:S(2)}, u32[]{:S(2)}) collective-permute-start(bf16[48,1536]{1,0:T(8,128)(2,1)S(1)} %copy-done.2), channel_id=1, source_target_pairs={{0,2},{1,3},{2,0},{3,1},{4,6},{5,7},{6,4},{7,5},{8,10},{9,11},{10,... | collective-permute-start | bytes 442376 | tf_op jit(solution)/shard_map/ppermute | solution.py:272
  13.5 0.7 copy-start.6
  14.2 12.5 %collective-permute-start.9 = (bf16[48,1536]{1,0:T(8,128)(2,1)S(1)}, bf16[48,1536]{1,0:T(8,128)(2,1)S(1)}, u32[]{:S(2)}, u32[]{:S(2)}) collective-permute-start(bf16[48,1536]{1,0:T(8,128)(2,1)S(1)} %collective-permute-done.4.refs_2_), channel_id=1, source_target_pairs={{0,2},{1,3},{2,0},{3,1},{4,6},{5,7},{6,4},{7,5},{8,10},{9,11},{10,... | collective-permute-start | bytes 442376 | tf_op jit(solution)/shard_map/ppermute | solution.py:272
  25.2 7.7 %collective-permute-start.7 = (bf16[4,48,768]{2,1,0:T(8,128)(2,1)S(1)}, bf16[4,48,768]{2,1,0:T(8,128)(2,1)S(1)}, u32[]{:S(2)}, u32[]{:S(2)}) collective-permute-start(bf16[4,48,768]{2,1,0:T(8,128)(2,1)S(1)} %get-tuple-element.34.refs_4_), channel_id=1, source_target_pairs={{0,2},{1,3},{2,0},{3,1},{4,6},{5,7},{6,4},{7,5},{8,10},{9,11},{10,... | collective-permute-start | bytes 884744 | tf_op jit(solution)/shard_map/ppermute | solution.py:272
  26.7 25.8 %collective-permute-start.10 = (bf16[8,48,768]{2,1,0:T(8,128)(2,1)S(1)}, bf16[8,48,768]{2,1,0:T(8,128)(2,1)S(1)}, u32[]{:S(2)}, u32[]{:S(2)}) collective-permute-start(bf16[8,48,768]{2,1,0:T(8,128)(2,1)S(1)} %shard_map.103.refs_8_), channel_id=1, source_target_pairs={{0,1},{1,0},{2,3},{3,2},{4,5},{5,4},{6,7},{7,6},{8,9},{9,8},{10,11... | collective-permute-start | bytes 1769480 | tf_op jit(solution)/shard_map/ppermute | solution.py:272
  26.8 25.2 %collective-permute-start.14 = (bf16[4,48,768]{2,1,0:T(8,128)(2,1)S(1)}, bf16[4,48,768]{2,1,0:T(8,128)(2,1)S(1)}, u32[]{:S(2)}, u32[]{:S(2)}) collective-permute-start(bf16[4,48,768]{2,1,0:T(8,128)(2,1)S(1)} %get-tuple-element.34.refs_4_), channel_id=1, source_target_pairs={{0,16},{1,17},{2,18},{3,19},{4,20},{5,21},{6,22},{7,23},{8,24},{9,... | collective-permute-start | bytes 884744 | tf_op jit(solution)/shard_map/ppermute | solution.py:272
  27.5 24.5 %collective-permute-start.5 = (bf16[2,32,1536]{2,1,0:T(8,128)(2,1)}, bf16[2,32,1536]{2,1,0:T(8,128)(2,1)}, u32[]{:S(2)}, u32[]{:S(2)}) collective-permute-start(bf16[2,32,1536]{2,1,0:T(8,128)(2,1)} %get-tuple-element.33), channel_id=1, source_target_pairs={{0,16},{1,17},{2,18},{3,19},{4,20},{5,21},{6,22},{7,23},{8,24},{9,... | collective-permute-start | bytes 589832 | tf_op jit(solution)/shard_map/ppermute | solution.py:272
  29.8 22.8 %collective-permute-start.6 = (bf16[4,48,768]{2,1,0:T(8,128)(2,1)S(1)}, bf16[4,48,768]{2,1,0:T(8,128)(2,1)S(1)}, u32[]{:S(2)}, u32[]{:S(2)}) collective-permute-start(bf16[4,48,768]{2,1,0:T(8,128)(2,1)S(1)} %get-tuple-element.34.refs_4_), channel_id=1, source_target_pairs={{0,1},{1,0},{2,3},{3,2},{4,5},{5,4},{6,7},{7,6},{8,9},{9,8},{10,11... | collective-permute-start | bytes 884744 | tf_op jit(solution)/shard_map/ppermute | solution.py:272
  32.9 19.6 %collective-permute-start.8 = (bf16[4,48,768]{2,1,0:T(8,128)(2,1)S(1)}, bf16[4,48,768]{2,1,0:T(8,128)(2,1)}, u32[]{:S(2)}, u32[]{:S(2)}) collective-permute-start(bf16[4,48,768]{2,1,0:T(8,128)(2,1)S(1)} %collective-permute-done.7.refs_5_), channel_id=1, source_target_pairs={{0,1},{1,0},{2,3},{3,2},{4,5},{5,4},{6,7},{7,6},{8,9},{9,8},{10,11... | collective-permute-start | bytes 884744 | tf_op jit(solution)/shard_map/ppermute | solution.py:272
  52.0 8.6 %collective-permute-start.15 = (bf16[4,48,768]{2,1,0:T(8,128)(2,1)S(1)}, bf16[4,48,768]{2,1,0:T(8,128)(2,1)S(1)}, u32[]{:S(2)}, u32[]{:S(2)}) collective-permute-start(bf16[4,48,768]{2,1,0:T(8,128)(2,1)S(1)} %collective-permute-done.14.refs_6_), channel_id=1, source_target_pairs={{0,2},{1,3},{2,0},{3,1},{4,6},{5,7},{6,4},{7,5},{8,10},{9,11},{10,... | collective-permute-start | bytes 884744 | tf_op jit(solution)/shard_map/ppermute | solution.py:272
  54.0 8.8 %collective-permute-start.13 = (bf16[2,32,1536]{2,1,0:T(8,128)(2,1)S(1)}, bf16[2,32,1536]{2,1,0:T(8,128)(2,1)S(1)}, u32[]{:S(2)}, u32[]{:S(2)}) collective-permute-start(bf16[2,32,1536]{2,1,0:T(8,128)(2,1)S(1)} %get-tuple-element.38.refs_0_), channel_id=1, source_target_pairs={{0,12},{1,13},{2,14},{3,15},{4,8},{5,9},{6,10},{7,11},{8,4},{9,5},... | collective-permute-start | bytes 589832 | tf_op jit(solution)/shard_map/ppermute | solution.py:272
  54.1 10.9 %collective-permute-start.12 = (bf16[2,32,1536]{2,1,0:T(8,128)(2,1)S(1)}, bf16[2,32,1536]{2,1,0:T(8,128)(2,1)S(1)}, u32[]{:S(2)}, u32[]{:S(2)}) collective-permute-start(bf16[2,32,1536]{2,1,0:T(8,128)(2,1)S(1)} %get-tuple-element.38.refs_0_), channel_id=1, source_target_pairs={{0,8},{1,9},{2,10},{3,11},{4,12},{5,13},{6,14},{7,15},{8,0},{9,1},... | collective-permute-start | bytes 589832 | tf_op jit(solution)/shard_map/ppermute | solution.py:272
  56.6 8.8 %collective-permute-start.11 = (bf16[2,32,1536]{2,1,0:T(8,128)(2,1)S(1)}, bf16[2,32,1536]{2,1,0:T(8,128)(2,1)S(1)}, u32[]{:S(2)}, u32[]{:S(2)}) collective-permute-start(bf16[2,32,1536]{2,1,0:T(8,128)(2,1)S(1)} %get-tuple-element.38.refs_0_), channel_id=1, source_target_pairs={{0,4},{1,5},{2,6},{3,7},{4,0},{5,1},{6,2},{7,3},{8,12},{9,13},{10,... | collective-permute-start | bytes 589832 | tf_op jit(solution)/shard_map/ppermute | solution.py:272
  57.6 8.0 %collective-permute-start.16 = (bf16[4,48,768]{2,1,0:T(8,128)(2,1)S(1)}, bf16[4,48,768]{2,1,0:T(8,128)(2,1)S(1)}, u32[]{:S(2)}, u32[]{:S(2)}) collective-permute-start(bf16[4,48,768]{2,1,0:T(8,128)(2,1)S(1)} %collective-permute-done.14.refs_6_), channel_id=1, source_target_pairs={{0,1},{1,0},{2,3},{3,2},{4,5},{5,4},{6,7},{7,6},{8,9},{9,8},{10,11... | collective-permute-start | bytes 884744 | tf_op jit(solution)/shard_map/ppermute | solution.py:272
  65.4 1.6 %collective-permute-start.17 = (bf16[4,48,768]{2,1,0:T(8,128)(2,1)S(1)}, bf16[4,48,768]{2,1,0:T(8,128)(2,1)S(1)}, u32[]{:S(2)}, u32[]{:S(2)}) collective-permute-start(bf16[4,48,768]{2,1,0:T(8,128)(2,1)S(1)} %collective-permute-done.15.refs_7_), channel_id=1, source_target_pairs={{0,1},{1,0},{2,3},{3,2},{4,5},{5,4},{6,7},{7,6},{8,9},{9,8},{10,11... | collective-permute-start | bytes 884744 | tf_op jit(solution)/shard_map/ppermute | solution.py:272
  71.0 7.0 %collective-permute-start.18 = (bf16[2,32,1536]{2,1,0:T(8,128)(2,1)S(1)}, bf16[2,32,1536]{2,1,0:T(8,128)(2,1)S(1)}, u32[]{:S(2)}, u32[]{:S(2)}) collective-permute-start(bf16[2,32,1536]{2,1,0:T(8,128)(2,1)S(1)} %get-tuple-element.42), channel_id=1, source_target_pairs={{0,4},{1,5},{2,6},{3,7},{4,0},{5,1},{6,2},{7,3},{8,12},{9,13},{10,... | collective-permute-start | bytes 589832 | tf_op jit(solution)/shard_map/ppermute | solution.py:272
  72.1 7.8 %collective-permute-start.19 = (bf16[2,32,1536]{2,1,0:T(8,128)(2,1)S(1)}, bf16[2,32,1536]{2,1,0:T(8,128)(2,1)S(1)}, u32[]{:S(2)}, u32[]{:S(2)}) collective-permute-start(bf16[2,32,1536]{2,1,0:T(8,128)(2,1)S(1)} %get-tuple-element.43), channel_id=1, source_target_pairs={{0,8},{1,9},{2,10},{3,11},{4,12},{5,13},{6,14},{7,15},{8,0},{9,1},... | collective-permute-start | bytes 589832 | tf_op jit(solution)/shard_map/ppermute | solution.py:272
  72.1 11.3 %collective-permute-start.20 = (bf16[2,32,1536]{2,1,0:T(8,128)(2,1)S(1)}, bf16[2,32,1536]{2,1,0:T(8,128)(2,1)S(1)}, u32[]{:S(2)}, u32[]{:S(2)}) collective-permute-start(bf16[2,32,1536]{2,1,0:T(8,128)(2,1)S(1)} %get-tuple-element.44), channel_id=1, source_target_pairs={{0,12},{1,13},{2,14},{3,15},{4,8},{5,9},{6,10},{7,11},{8,4},{9,5},... | collective-permute-start | bytes 589832 | tf_op jit(solution)/shard_map/ppermute | solution.py:272

commit v9 on v8

--- a/solution.py
+++ b/solution.py
@@ -64,56 +64,32 @@
 
 
 def send_kernel(sources, place, packed, weights, frames, *refs):
-    outs, buf = refs[:-1], refs[-1]
+    near, far, buf = refs[:QUAD], refs[QUAD:-1], refs[-1]
     tables = Tables(packed, sources)
     me = place[0]
     highs = sources // QUAD
     long, width = frames.shape[1:]
-    wide = outs[0].shape[1]
+    wide = near[0].shape[1]
     for owner in range(QUAD):
         buf[owner] = own_columns(highs, weights, owner)
-    for number, out in enumerate(outs):
-        for far in range(highs):
-            target = jnp.bitwise_xor(me, far * QUAD + number)
-            found = jnp.int32(0)
-            for slot in range(tables.slots):
-                found = jnp.where(tables.live_for(me, slot, target), slot, found)
+    for shift, out in enumerate(near + far):
+        target = jnp.bitwise_xor(me, shift)
+        found = jnp.int32(0)
+        for slot in range(tables.slots):
+            found = jnp.where(tables.live_for(me, slot, target), slot, found)
+        if shift >= QUAD:
+            out[...] = frames[found]
+        else:
             for half in range(width // wide):
-                start = (far * (width // wide) + half) * long
-                out[start : start + long, :] = frames[found, :, half * wide : half * wide + wide]
-        start = highs * (width // wide) * long
-        out[start:, :] = buf[jnp.bitwise_xor(lax.rem(me, QUAD), number)]
-
-
-def fetch(out, number, ref, far):
-    long, width = out.shape[1:]
-    wide = ref.shape[1]
-    for half in range(width // wide):
-        start = (far * (width // wide) + half) * long
-        out[number, :, half * wide : half * wide + wide] = ref[start : start + long, :]
-
-
-def merge_kernel(sources, place, packed, *refs):
-    arrived, outs, piece = refs[:QUAD], refs[QUAD:-1], refs[-1]
-    tables = Tables(packed, sources)
-    me = place[0]
-    depth, wide = piece.shape[1:]
-    for far, out in enumerate(outs, 1):
-        long = out.shape[1]
-        for number, ref in enumerate(arrived):
-            source = jnp.bitwise_xor(me, number)
-            target = jnp.bitwise_xor(me, far * QUAD)
-            start = jnp.int32(-1)
-            for slot in range(tables.slots):
-                hit = tables.live_for(source, slot, target)
-                start = jnp.where(hit, tables.offset(source, slot), start)
-
-            @pl.when(start >= 0)
-            def _():
-                fetch(out, start // long, ref, far)
-
+                first = half * wide
+                out[half * long : (half + 1) * long, :] = frames[found, :, first : first + wide]
+            out[width // wide * long :, :] = buf[jnp.bitwise_xor(lax.rem(me, QUAD), shift)]
+
+
+def columns_kernel(*refs):
+    arrived, piece = refs[:-1], refs[-1]
     for number, ref in enumerate(arrived):
-        piece[number] = ref[ref.shape[0] - depth :, :]
+        piece[number] = ref[ref.shape[0] - piece.shape[1] :, :]
 
 
 def stack_kernel(*refs):
@@ -161,20 +137,21 @@
 
 
 def norm_kernel(place, sources, lens, gain, *refs):
-    near, far, (kept, normed) = refs[:QUAD], refs[QUAD:-2], refs[-2:]
+    arrived, (kept, normed) = refs[:-2], refs[-2:]
+    long, width = kept.shape[1:]
     for number in range(kept.shape[0]):
         shift = jnp.bitwise_xor(sources[number], place[0])
-        for other, ref in enumerate(near):
+        for other, ref in enumerate(arrived):
 
             @pl.when(shift == other)
             def _():
-                fetch(kept, number, ref, 0)
-
-        for other, ref in enumerate(far, 1):
-
-            @pl.when(shift // QUAD == other)
-            def _():
-                kept[number] = ref[number]
+                if other >= QUAD:
+                    kept[number] = ref[...]
+                else:
+                    wide = ref.shape[1]
+                    for half in range(width // wide):
+                        rows = ref[half * long : (half + 1) * long, :]
+                        kept[number, :, half * wide : (half + 1) * wide] = rows
 
         wide = kept[number].astype(F32)
         mean = jnp.mean(wide, axis=1, keepdims=True)
@@ -285,6 +262,25 @@
 
     count = width // wide
 
+    sent = call(
+        functools.partial(send_kernel, dp_count),
+        [like(BF16, count * long + depth, wide)] * QUAD
+        + [like(BF16, long, width)] * (dp_count - QUAD),
+        [SMEM, SMEM, VMEM, VMEM],
+        [VMEM] * dp_count,
+        (place, packed, w_in, frames[0]),
+        [like(BF16, QUAD, depth, wide)],
+    )
+    sent = list(sent)
+    near = quad_swap(sent[:QUAD])
+    later = QUAD + 2
+    sent[later:] = gated(sent[later:], near[1])
+    far = [
+        swap(sent[shift], high=shift // QUAD, quad=shift % QUAD)
+        for shift in range(QUAD, dp_count)
+    ]
+
+    w_out = gated(w_out, sent[:later])
     outs = {0: w_out}
 
     def share_chips(parts, first):
@@ -295,16 +291,7 @@
     for mask in range(1, highs):
         outs[mask * fsdp_count] = swap(w_out, high=mask)
     share_chips(outs, False)
-
-    near = call(
-        functools.partial(send_kernel, dp_count),
-        [like(BF16, highs * count * long + depth, wide)] * QUAD,
-        [SMEM, SMEM, VMEM, VMEM],
-        [VMEM] * QUAD,
-        (place, packed, w_in, frames[0]),
-        [like(BF16, QUAD, depth, wide)],
-    )
-    near = quad_swap(near)
+    share_chips(outs, True)
     sources, lens, table, gain = call(
         functools.partial(table_kernel, dp_count, long),
         [like(jnp.int32, recv)] * 2 + [like(F32, taps + 2, chans), like(F32, 1, width)],
@@ -312,21 +299,19 @@
         [SMEM, SMEM, VMEM, VMEM],
         (place, packed, small),
     )
-    utts = like(BF16, recv, long, width)
-    *far, own_in = call(
-        functools.partial(merge_kernel, dp_count),
-        [utts] * (highs - 1) + [like(BF16, QUAD, depth, wide)],
-        [SMEM] * 2 + [VMEM] * QUAD,
-        [VMEM] * highs,
-        (gated(place, (lens, gain, outs)), packed, *near),
-    )
-    far = [swap(part, high=mask) for mask, part in enumerate(far, 1)]
-
+
+    own_in = call(
+        columns_kernel,
+        like(BF16, QUAD, depth, wide),
+        [VMEM] * QUAD,
+        VMEM,
+        gated(near, (lens, gain)),
+    )
     ins = {0: own_in}
-    far_in = [swap(own_in, high=mask) for mask in range(1, highs)]
+    for mask in range(1, highs):
+        ins[mask * fsdp_count] = swap(gated(own_in, far), high=mask)
     share_chips(ins, False)
-    early = list(ins)
-    share_chips(outs, True)
+    early = [shift for shift in ins if shift < fsdp_count]
     order = sorted(outs)
     stacked = call(
         stack_kernel,
@@ -337,23 +322,26 @@
     )
     crossed = {shift: swap(ins[shift], fsdp=1) for shift in early}
     crossed_out = swap(stacked, fsdp=1)
-    for mask, part in enumerate(gated(far_in, far), 1):
-        ins[mask * fsdp_count] = part
+    utts = like(BF16, recv, long, width)
     kept, normed = call(
         norm_kernel,
         [utts, utts],
-        [SMEM] * 3 + [VMEM] * (QUAD + highs),
+        [SMEM] * 3 + [VMEM] * (1 + dp_count),
         [VMEM, VMEM],
-        (place, sources, lens, gain, *near, *gated(far, (crossed, crossed_out))),
-    )
+        (place, sources, lens, gain, *near, *gated(far, crossed)),
+    )
+    for shift in ins:
+        if shift not in early:
+            ins[shift] = gated(ins[shift], normed)
     share_chips(ins, True)
     normed = quad_swap([normed] * QUAD)
     chip_mask = (fsdp_count - 1) ^ 1
     last = {at: ins[at] for at in ins if at & chip_mask and at not in early}
-    last = gated(last, normed)
     for shift in ins:
-        if shift not in crossed:
-            crossed[shift] = swap(last.get(shift, ins[shift]), fsdp=1)
+        if shift not in crossed and shift not in last:
+            crossed[shift] = swap(ins[shift], fsdp=1)
+    for shift, part in gated(last, (normed, crossed, crossed_out)).items():
+        crossed[shift] = swap(part, fsdp=1)
     pieces = list(ins.values()) + [stacked]
     layout = [[("in", shift, number) for number in range(QUAD)] for shift in ins]
     layout.append([("out", shift, half) for shift in order for half in range(count)])

time: 84.5 us -> 89.7 us (1.062)
  starting transfers between devices: 21.9 us -> 37.1 us
  waiting for transfers between devices: 47.4 us -> 35.6 us
  local copies, waits for them, and re-layouts: 3.62 us -> 7.45 us
  Pallas kernels: 9.36 us -> 7.27 us
    ppermute x21 -> x24, starting transfers between devices: 21.9 us -> 37.1 us  [swap(): lax.ppermute(array, ('dp', 'fsdp'), [(at, at ^ mask) for at in range(devi...]
    ppermute x21 -> x24, waiting for transfers between devices: 47.4 us -> 35.6 us  [swap(): lax.ppermute(array, ('dp', 'fsdp'), [(at, at ^ mask) for at in range(devi...]
    unnamed x18 -> x30, local copies, waits for them, and re-layouts: 3.41 us -> 7.24 us
    pallas_call x6, Pallas kernels: 9.36 us -> 7.27 us  [call(): pl.pallas_call(kernel, out_shape=out_shape, in_specs=in_specs, out_specs=...]
  transfers between devices with their start and end apart: 21 -> 24, of which waited for: 13 -> 13; matrix products, arithmetic and copies ran while one was open for 1% -> 0% of each run, Pallas kernels for 6% -> 3%
where the time goes in v9:
time: 89.7 us; the launch traced here: 89.3 us
  starting transfers between devices  37.1 us (41%)
  waiting for transfers between devices  35.6 us (40%)
  local copies, waits for them, and re-layouts  7.45 us (8%)
  Pallas kernels  7.27 us (8%)
  other arithmetic  1.75 us (2%)
    ppermute x24, starting transfers between devices, swap(): lax.ppermute(array, ('dp', 'fsdp'), [(at, at ^ mask) for at in range(devi...  37.1 us
    ppermute x24, waiting for transfers between devices, swap(): lax.ppermute(array, ('dp', 'fsdp'), [(at, at ^ mask) for at in range(devi...  35.6 us
    pallas_call x6, Pallas kernels, call(): pl.pallas_call(kernel, out_shape=out_shape, in_specs=in_specs, out_specs=...  7.27 us
    unnamed x30, local copies, waits for them, and re-layouts  7.24 us
  transfers between devices with their start and end apart: 24, of which 13 were waited for; matrix products, arithmetic and copies ran while one was open for 0% of the time, Pallas kernels for 3%

profile of v9, /device:TPU:0, one launch (start us, length us, event | category | flops | bytes accessed | tf_op | source)
XLA Modules:
  0.0 89.3 jit_solution(10777471760704463938)
XLA Ops:
  1.6 1.1 %copy-done = bf16[1,6,32,1536]{3,2,1,0:T(8,128)(2,1)S(1)} copy-done((bf16[1,6,32,1536]{3,2,1,0:T(8,128)(2,1)S(1)}, bf16[1,6,32,1536]{3,2,1,0:T(8,128)(2,1)}, u32[]{:S(2)}) %copy-start) | copy-done | bytes 589848
  2.7 1.0 %copy-done.1 = bf16[48,3072]{1,0:T(8,128)(2,1)S(1)} copy-done((bf16[48,3072]{1,0:T(8,128)(2,1)S(1)}, bf16[48,3072]{1,0:T(8,128)(2,1)}, u32[]{:S(2)}) %copy-start.1) | copy-done | bytes 294936
  4.5 4.0 %collective-permute-start.16 = (bf16[48,1536]{1,0:T(8,128)(2,1)S(1)}, bf16[48,1536]{1,0:T(8,128)(2,1)S(1)}, u32[]{:S(2)}, u32[]{:S(2)}) collective-permute-start(bf16[48,1536]{1,0:T(8,128)(2,1)S(1)} %copy-done.2), channel_id=1, source_target_pairs={{0,16},{1,17},{2,18},{3,19},{4,20},{5,21},{6,22},{7,23},{8,24},{9,... | collective-permute-start | bytes 442376 | tf_op jit(solution)/shard_map/ppermute | solution.py:249
  8.6 1.5 %collective-permute-start.15 = (bf16[48,1536]{1,0:T(8,128)(2,1)S(1)}, bf16[48,1536]{1,0:T(8,128)(2,1)S(1)}, u32[]{:S(2)}, u32[]{:S(2)}) collective-permute-start(bf16[48,1536]{1,0:T(8,128)(2,1)S(1)} %copy-done.2), channel_id=1, source_target_pairs={{0,2},{1,3},{2,0},{3,1},{4,6},{5,7},{6,4},{7,5},{8,10},{9,11},{10,... | collective-permute-start | bytes 442376 | tf_op jit(solution)/shard_map/ppermute | solution.py:249
  10.1 1.5 %collective-permute-start = (bf16[112,768]{1,0:T(8,128)(2,1)S(1)}, bf16[112,768]{1,0:T(8,128)(2,1)S(1)}, u32[]{:S(2)}, u32[]{:S(2)}) collective-permute-start(bf16[112,768]{1,0:T(8,128)(2,1)S(1)} %get-tuple-element.41), channel_id=1, source_target_pairs={{0,4},{1,5},{2,6},{3,7},{4,0},{5,1},{6,2},{7,3},{8,12},{9,13},{10,... | collective-permute-start | bytes 516104 | tf_op jit(solution)/shard_map/ppermute | solution.py:249
  11.6 1.6 %collective-permute-start.1 = (bf16[112,768]{1,0:T(8,128)(2,1)S(1)}, bf16[112,768]{1,0:T(8,128)(2,1)S(1)}, u32[]{:S(2)}, u32[]{:S(2)}) collective-permute-start(bf16[112,768]{1,0:T(8,128)(2,1)S(1)} %get-tuple-element.42), channel_id=1, source_target_pairs={{0,8},{1,9},{2,10},{3,11},{4,12},{5,13},{6,14},{7,15},{8,0},{9,1},... | collective-permute-start | bytes 516104 | tf_op jit(solution)/shard_map/ppermute | solution.py:249
  14.3 1.4 %collective-permute-done.16.refs_2_ = bf16[48,1536]{1,0:T(8,128)(2,1)S(1)} collective-permute-done((bf16[48,1536]{1,0:T(8,128)(2,1)S(1)}, bf16[48,1536]{1,0:T(8,128)(2,1)S(1)}, u32[]{:S(2)}, u32[]{:S(2)}) %collective-permute-start.16) | collective-permute-done | bytes 147488 | tf_op jit(solution)/shard_map/ppermute | solution.py:249
  15.7 1.5 %collective-permute-start.17 = (bf16[48,1536]{1,0:T(8,128)(2,1)S(1)}, bf16[48,1536]{1,0:T(8,128)(2,1)S(1)}, u32[]{:S(2)}, u32[]{:S(2)}) collective-permute-start(bf16[48,1536]{1,0:T(8,128)(2,1)S(1)} %collective-permute-done.16.refs_2_), channel_id=1, source_target_pairs={{0,2},{1,3},{2,0},{3,1},{4,6},{5,7},{6,4},{7,5},{8,10},{9,11},{10,... | collective-permute-start | bytes 442376 | tf_op jit(solution)/shard_map/ppermute | solution.py:249
  17.3 1.8 %shard_map.100 = (s32[2]{0:T(128)S(1)}, s32[2]{0:T(128)S(1)}, f32[33,384]{1,0:T(8,128)S(1)}, f32[1,1536]{1,0:T(1,128)S(1)}) custom-call(s32[1]{0:T(128)} %bitcast.place, s32[144]{0:T(256)S(1)} %reshape.70.packed, f32[34,1536]{1,0:T(8,128)S(1)} %pad_maximum_fusion.small), custom_call_target="tpu_custom_call" | custom-call | bytes 266324 | tf_op jit(solution)/shard_map/pallas_call | solution.py:21
  19.7 2.9 %collective-permute-done.2.refs_3_ = bf16[112,768]{1,0:T(8,128)(2,1)S(1)} collective-permute-done((bf16[112,768]{1,0:T(8,128)(2,1)S(1)}, bf16[112,768]{1,0:T(8,128)(2,1)S(1)}, u32[]{:S(2)}, u32[]{:S(2)}) %collective-permute-start.2) | collective-permute-done | bytes 172064 | tf_op jit(solution)/shard_map/ppermute | solution.py:249
  23.2 0.8 collective-permute-start.3
  24.1 3.1 %collective-permute-start.4 = (bf16[32,1536]{1,0:T(8,128)(2,1)S(1)}, bf16[32,1536]{1,0:T(8,128)(2,1)S(1)}, u32[]{:S(2)}, u32[]{:S(2)}) collective-permute-start(bf16[32,1536]{1,0:T(8,128)(2,1)S(1)} %get-tuple-element.45), channel_id=1, source_target_pairs={{0,20},{1,21},{2,22},{3,23},{4,16},{5,17},{6,18},{7,19},{8,28},{9,... | collective-permute-start | bytes 294920 | tf_op jit(solution)/shard_map/ppermute | solution.py:249
  27.2 2.4 %collective-permute-start.5 = (bf16[32,1536]{1,0:T(8,128)(2,1)S(1)}, bf16[32,1536]{1,0:T(8,128)(2,1)S(1)}, u32[]{:S(2)}, u32[]{:S(2)}) collective-permute-start(bf16[32,1536]{1,0:T(8,128)(2,1)S(1)} %get-tuple-element.48), channel_id=1, source_target_pairs={{0,24},{1,25},{2,26},{3,27},{4,28},{5,29},{6,30},{7,31},{8,16},{9,... | collective-permute-start | bytes 294920 | tf_op jit(solution)/shard_map/ppermute | solution.py:249
  30.3 7.5 %collective-permute-start.6 = (bf16[32,1536]{1,0:T(8,128)(2,1)S(1)}, bf16[32,1536]{1,0:T(8,128)(2,1)S(1)}, u32[]{:S(2)}, u32[]{:S(2)}) collective-permute-start(bf16[32,1536]{1,0:T(8,128)(2,1)S(1)} %get-tuple-element.49), channel_id=1, source_target_pairs={{0,28},{1,29},{2,30},{3,31},{4,24},{5,25},{6,26},{7,27},{8,20},{9,... | collective-permute-start | bytes 294920 | tf_op jit(solution)/shard_map/ppermute | solution.py:249
  39.7 0.9 collective-permute-done.6.refs_7_
  41.2 2.1 %collective-permute-start.13 = (bf16[4,48,768]{2,1,0:T(8,128)(2,1)S(1)}, bf16[4,48,768]{2,1,0:T(8,128)(2,1)S(1)}, u32[]{:S(2)}, u32[]{:S(2)}) collective-permute-start(bf16[4,48,768]{2,1,0:T(8,128)(2,1)S(1)} %shard_map.102.refs_4_), channel_id=1, source_target_pairs={{0,16},{1,17},{2,18},{3,19},{4,20},{5,21},{6,22},{7,23},{8,24},{9,... | collective-permute-start | bytes 884744 | tf_op jit(solution)/shard_map/ppermute | solution.py:249
  43.4 0.9 copy-done.4
  44.3 0.9 copy-done.6
  45.1 1.1 %shard_map.103 = (bf16[2,32,1536]{2,1,0:T(8,128)(2,1)S(1)}, bf16[2,32,1536]{2,1,0:T(8,128)(2,1)S(1)}) custom-call(s32[1]{0:T(128)} %bitcast.place, s32[2]{0:T(128)S(1)} %get-tuple-element.38.sources, s32[2]{0:T(128)S(1)} %get-tuple-element.37.lens, f32[1,1536]{1,0:T(1,128)S(1)} %get-tuple-element.39.gain, bf16[112,768]{1,0:T(8,128)(2,1)S(1)} %get-tuple-element.50.refs_0_, ...), custom_call_target="tpu_custom_call" | custom-call | bytes 1480724 | tf_op jit(solution)/shard_map/pallas_call | solution.py:21
  46.2 10.3 %collective-permute-done.13.refs_5_ = bf16[4,48,768]{2,1,0:T(8,128)(2,1)S(1)} collective-permute-done((bf16[4,48,768]{2,1,0:T(8,128)(2,1)S(1)}, bf16[4,48,768]{2,1,0:T(8,128)(2,1)S(1)}, u32[]{:S(2)}, u32[]{:S(2)}) %collective-permute-start.13) | collective-permute-done | bytes 294944 | tf_op jit(solution)/shard_map/ppermute | solution.py:249
  56.5 2.2 %collective-permute-start.14 = (bf16[4,48,768]{2,1,0:T(8,128)(2,1)S(1)}, bf16[4,48,768]{2,1,0:T(8,128)(2,1)S(1)}, u32[]{:S(2)}, u32[]{:S(2)}) collective-permute-start(bf16[4,48,768]{2,1,0:T(8,128)(2,1)S(1)} %collective-permute-done.13.refs_5_), channel_id=1, source_target_pairs={{0,2},{1,3},{2,0},{3,1},{4,6},{5,7},{6,4},{7,5},{8,10},{9,11},{10,... | collective-permute-start | bytes 884744 | tf_op jit(solution)/shard_map/ppermute | solution.py:249
  58.8 1.3 %collective-permute-start.11 = (bf16[2,32,1536]{2,1,0:T(8,128)(2,1)S(1)}, bf16[2,32,1536]{2,1,0:T(8,128)(2,1)S(1)}, u32[]{:S(2)}, u32[]{:S(2)}) collective-permute-start(bf16[2,32,1536]{2,1,0:T(8,128)(2,1)S(1)} %get-tuple-element.60.refs_0_), channel_id=1, source_target_pairs={{0,8},{1,9},{2,10},{3,11},{4,12},{5,13},{6,14},{7,15},{8,0},{9,1},... | collective-permute-start | bytes 589832 | tf_op jit(solution)/shard_map/ppermute | solution.py:249
  60.0 2.2 %collective-permute-start.10 = (bf16[2,32,1536]{2,1,0:T(8,128)(2,1)S(1)}, bf16[2,32,1536]{2,1,0:T(8,128)(2,1)S(1)}, u32[]{:S(2)}, u32[]{:S(2)}) collective-permute-start(bf16[2,32,1536]{2,1,0:T(8,128)(2,1)S(1)} %get-tuple-element.60.refs_0_), channel_id=1, source_target_pairs={{0,4},{1,5},{2,6},{3,7},{4,0},{5,1},{6,2},{7,3},{8,12},{9,13},{10,... | collective-permute-start | bytes 589832 | tf_op jit(solution)/shard_map/ppermute | solution.py:249
  62.2 5.2 %collective-permute-done.12.refs_3_ = bf16[2,32,1536]{2,1,0:T(8,128)(2,1)S(1)} collective-permute-done((bf16[2,32,1536]{2,1,0:T(8,128)(2,1)S(1)}, bf16[2,32,1536]{2,1,0:T(8,128)(2,1)S(1)}, u32[]{:S(2)}, u32[]{:S(2)}) %collective-permute-start.12) | collective-permute-done | bytes 196640 | tf_op jit(solution)/shard_map/ppermute | solution.py:249
  67.4 1.8 %collective-permute-done.11.refs_2_ = bf16[2,32,1536]{2,1,0:T(8,128)(2,1)S(1)} collective-permute-done((bf16[2,32,1536]{2,1,0:T(8,128)(2,1)S(1)}, bf16[2,32,1536]{2,1,0:T(8,128)(2,1)S(1)}, u32[]{:S(2)}, u32[]{:S(2)}) %collective-permute-start.11) | collective-permute-done | bytes 196640 | tf_op jit(solution)/shard_map/ppermute | solution.py:249
  69.2 1.7 %collective-permute-done.10.refs_1_ = bf16[2,32,1536]{2,1,0:T(8,128)(2,1)S(1)} collective-permute-done((bf16[2,32,1536]{2,1,0:T(8,128)(2,1)S(1)}, bf16[2,32,1536]{2,1,0:T(8,128)(2,1)S(1)}, u32[]{:S(2)}, u32[]{:S(2)}) %collective-permute-start.10) | collective-permute-done | bytes 196640 | tf_op jit(solution)/shard_map/ppermute | solution.py:249
  71.1 1.4 %collective-permute-done.20.refs_12_ = bf16[4,48,768]{2,1,0:T(8,128)(2,1)S(1)} collective-permute-done((bf16[4,48,768]{2,1,0:T(8,128)(2,1)S(1)}, bf16[4,48,768]{2,1,0:T(8,128)(2,1)S(1)}, u32[]{:S(2)}, u32[]{:S(2)}) %collective-permute-start.20) | collective-permute-done | bytes 294944 | tf_op jit(solution)/shard_map/ppermute | solution.py:249
  72.5 3.7 %shard_map.105 = (f32[2,32,1536]{2,1,0:T(8,128)S(1)}, bf16[2,32,1536]{2,1,0:T(8,128)(2,1)S(1)}, bf16[2,32,1536]{2,1,0:T(8,128)(2,1)S(1)}, bf16[2,32,1536]{2,1,0:T(8,128)(2,1)S(1)}) custom-call(s32[8,5]{1,0:T(8,128)S(1)} %pad_add_fusion.1.where, bf16[2,32,1536]{2,1,0:T(8,128)(2,1)S(1)} %get-tuple-element.58.kept, f32[33,384]{1,0:T(8,128)S(1)} %copy-done.8, ...), custom_call_target="tpu_custom_call" | custom-call | flops 905969664 | bytes 10471072 | tf_op jit(solution)/shard_map/pallas_call | solution.py:21
  77.1 2.6 %collective-permute-start.23 = (bf16[2,32,1536]{2,1,0:T(8,128)(2,1)S(1)}, bf16[2,32,1536]{2,1,0:T(8,128)(2,1)S(1)}, u32[]{:S(2)}, u32[]{:S(2)}) collective-permute-start(bf16[2,32,1536]{2,1,0:T(8,128)(2,1)S(1)} %get-tuple-element.68), channel_id=1, source_target_pairs={{0,12},{1,13},{2,14},{3,15},{4,8},{5,9},{6,10},{7,11},{8,4},{9,5},... | collective-permute-start | bytes 589832 | tf_op jit(solution)/shard_map/ppermute | solution.py:249
  79.8 3.4 %collective-permute-done.21 = bf16[2,32,1536]{2,1,0:T(8,128)(2,1)S(1)} collective-permute-done((bf16[2,32,1536]{2,1,0:T(8,128)(2,1)S(1)}, bf16[2,32,1536]{2,1,0:T(8,128)(2,1)S(1)}, u32[]{:S(2)}, u32[]{:S(2)}) %collective-permute-start.21) | collective-permute-done | bytes 196640 | tf_op jit(solution)/shard_map/ppermute | solution.py:249
  83.2 1.5 %collective-permute-done.22 = bf16[2,32,1536]{2,1,0:T(8,128)(2,1)S(1)} collective-permute-done((bf16[2,32,1536]{2,1,0:T(8,128)(2,1)S(1)}, bf16[2,32,1536]{2,1,0:T(8,128)(2,1)S(1)}, u32[]{:S(2)}, u32[]{:S(2)}) %collective-permute-start.22) | collective-permute-done | bytes 196640 | tf_op jit(solution)/shard_map/ppermute | solution.py:249
  84.7 3.9 %collective-permute-done.23 = bf16[2,32,1536]{2,1,0:T(8,128)(2,1)S(1)} collective-permute-done((bf16[2,32,1536]{2,1,0:T(8,128)(2,1)S(1)}, bf16[2,32,1536]{2,1,0:T(8,128)(2,1)S(1)}, u32[]{:S(2)}, u32[]{:S(2)}) %collective-permute-start.23) | collective-permute-done | bytes 196640 | tf_op jit(solution)/shard_map/ppermute | solution.py:249
  (66 shorter events, 10.1 us)
Async XLA Ops:
  1.6 1.1 %copy-start = (bf16[1,6,32,1536]{3,2,1,0:T(8,128)(2,1)S(1)}, bf16[1,6,32,1536]{3,2,1,0:T(8,128)(2,1)}, u32[]{:S(2)}) copy-start(bf16[1,6,32,1536]{3,2,1,0:T(8,128)(2,1)} %param.10) | copy-start | bytes 1769476
  2.7 1.0 %copy-start.1 = (bf16[48,3072]{1,0:T(8,128)(2,1)S(1)}, bf16[48,3072]{1,0:T(8,128)(2,1)}, u32[]{:S(2)}) copy-start(bf16[48,3072]{1,0:T(8,128)(2,1)} %weights.1) | copy-start | bytes 884740
  3.6 0.9 %copy-start.2 = (bf16[48,1536]{1,0:T(8,128)(2,1)S(1)}, bf16[48,1536]{1,0:T(8,128)(2,1)}, u32[]{:S(2)}) copy-start(bf16[48,1536]{1,0:T(8,128)(2,1)} %refs_0_) | copy-start | bytes 442372
  3.6 13.6 %copy-start.9 = (f32[31,1536]{1,0:T(8,128)S(1)}, f32[31,1536]{1,0:T(8,128)}, u32[]{:S(2)}) copy-start(f32[31,1536]{1,0:T(8,128)} %param.13) | copy-start | bytes 571396
  4.3 9.2 %copy-start.10 = (f32[1536]{0:T(1024)S(1)}, f32[1536]{0:T(1024)}, u32[]{:S(2)}) copy-start(f32[1536]{0:T(1024)} %param.11) | copy-start | bytes 18436
  4.4 9.2 %copy-start.11 = (f32[1536]{0:T(1024)S(1)}, f32[1536]{0:T(1024)}, u32[]{:S(2)}) copy-start(f32[1536]{0:T(1024)} %param.14) | copy-start | bytes 18436
  4.5 11.1 %collective-permute-start.16 = (bf16[48,1536]{1,0:T(8,128)(2,1)S(1)}, bf16[48,1536]{1,0:T(8,128)(2,1)S(1)}, u32[]{:S(2)}, u32[]{:S(2)}) collective-permute-start(bf16[48,1536]{1,0:T(8,128)(2,1)S(1)} %copy-done.2), channel_id=1, source_target_pairs={{0,16},{1,17},{2,18},{3,19},{4,20},{5,21},{6,22},{7,23},{8,24},{9,... | collective-permute-start | bytes 442376 | tf_op jit(solution)/shard_map/ppermute | solution.py:249
  8.6 15.4 %collective-permute-start.15 = (bf16[48,1536]{1,0:T(8,128)(2,1)S(1)}, bf16[48,1536]{1,0:T(8,128)(2,1)S(1)}, u32[]{:S(2)}, u32[]{:S(2)}) collective-permute-start(bf16[48,1536]{1,0:T(8,128)(2,1)S(1)} %copy-done.2), channel_id=1, source_target_pairs={{0,2},{1,3},{2,0},{3,1},{4,6},{5,7},{6,4},{7,5},{8,10},{9,11},{10,... | collective-permute-start | bytes 442376 | tf_op jit(solution)/shard_map/ppermute | solution.py:249
  10.1 9.6 %collective-permute-start = (bf16[112,768]{1,0:T(8,128)(2,1)S(1)}, bf16[112,768]{1,0:T(8,128)(2,1)S(1)}, u32[]{:S(2)}, u32[]{:S(2)}) collective-permute-start(bf16[112,768]{1,0:T(8,128)(2,1)S(1)} %get-tuple-element.41), channel_id=1, source_target_pairs={{0,4},{1,5},{2,6},{3,7},{4,0},{5,1},{6,2},{7,3},{8,12},{9,13},{10,... | collective-permute-start | bytes 516104 | tf_op jit(solution)/shard_map/ppermute | solution.py:249
  11.6 8.1 %collective-permute-start.1 = (bf16[112,768]{1,0:T(8,128)(2,1)S(1)}, bf16[112,768]{1,0:T(8,128)(2,1)S(1)}, u32[]{:S(2)}, u32[]{:S(2)}) collective-permute-start(bf16[112,768]{1,0:T(8,128)(2,1)S(1)} %get-tuple-element.42), channel_id=1, source_target_pairs={{0,8},{1,9},{2,10},{3,11},{4,12},{5,13},{6,14},{7,15},{8,0},{9,1},... | collective-permute-start | bytes 516104 | tf_op jit(solution)/shard_map/ppermute | solution.py:249
  13.2 9.4 %collective-permute-start.2 = (bf16[112,768]{1,0:T(8,128)(2,1)S(1)}, bf16[112,768]{1,0:T(8,128)(2,1)S(1)}, u32[]{:S(2)}, u32[]{:S(2)}) collective-permute-start(bf16[112,768]{1,0:T(8,128)(2,1)S(1)} %get-tuple-element.43), channel_id=1, source_target_pairs={{0,12},{1,13},{2,14},{3,15},{4,8},{5,9},{6,10},{7,11},{8,4},{9,5},... | collective-permute-start | bytes 516104 | tf_op jit(solution)/shard_map/ppermute | solution.py:249
  15.7 8.3 %collective-permute-start.17 = (bf16[48,1536]{1,0:T(8,128)(2,1)S(1)}, bf16[48,1536]{1,0:T(8,128)(2,1)S(1)}, u32[]{:S(2)}, u32[]{:S(2)}) collective-permute-start(bf16[48,1536]{1,0:T(8,128)(2,1)S(1)} %collective-permute-done.16.refs_2_), channel_id=1, source_target_pairs={{0,2},{1,3},{2,0},{3,1},{4,6},{5,7},{6,4},{7,5},{8,10},{9,11},{10,... | collective-permute-start | bytes 442376 | tf_op jit(solution)/shard_map/ppermute | solution.py:249
  22.6 16.0 %collective-permute-start.8 = (bf16[4,48,768]{2,1,0:T(8,128)(2,1)S(1)}, bf16[4,48,768]{2,1,0:T(8,128)(2,1)S(1)}, u32[]{:S(2)}, u32[]{:S(2)}) collective-permute-start(bf16[4,48,768]{2,1,0:T(8,128)(2,1)S(1)} %shard_map.102.refs_4_), channel_id=1, source_target_pairs={{0,2},{1,3},{2,0},{3,1},{4,6},{5,7},{6,4},{7,5},{8,10},{9,11},{10,... | collective-permute-start | bytes 884744 | tf_op jit(solution)/shard_map/ppermute | solution.py:249
  23.2 7.2 %collective-permute-start.3 = (bf16[32,1536]{1,0:T(8,128)(2,1)S(1)}, bf16[32,1536]{1,0:T(8,128)(2,1)S(1)}, u32[]{:S(2)}, u32[]{:S(2)}) collective-permute-start(bf16[32,1536]{1,0:T(8,128)(2,1)S(1)} %get-tuple-element.44), channel_id=1, source_target_pairs={{0,16},{1,17},{2,18},{3,19},{4,20},{5,21},{6,22},{7,23},{8,24},{9,... | collective-permute-start | bytes 294920 | tf_op jit(solution)/shard_map/ppermute | solution.py:249
  24.1 36.0 %collective-permute-start.19 = (bf16[8,48,768]{2,1,0:T(8,128)(2,1)S(1)}, bf16[8,48,768]{2,1,0:T(8,128)(2,1)S(1)}, u32[]{:S(2)}, u32[]{:S(2)}) collective-permute-start(bf16[8,48,768]{2,1,0:T(8,128)(2,1)S(1)} %shard_map.104.refs_8_), channel_id=1, source_target_pairs={{0,1},{1,0},{2,3},{3,2},{4,5},{5,4},{6,7},{7,6},{8,9},{9,8},{10,11... | collective-permute-start | bytes 1769480 | tf_op jit(solution)/shard_map/ppermute | solution.py:249
  24.1 14.4 %collective-permute-start.4 = (bf16[32,1536]{1,0:T(8,128)(2,1)S(1)}, bf16[32,1536]{1,0:T(8,128)(2,1)S(1)}, u32[]{:S(2)}, u32[]{:S(2)}) collective-permute-start(bf16[32,1536]{1,0:T(8,128)(2,1)S(1)} %get-tuple-element.45), channel_id=1, source_target_pairs={{0,20},{1,21},{2,22},{3,23},{4,16},{5,17},{6,18},{7,19},{8,28},{9,... | collective-permute-start | bytes 294920 | tf_op jit(solution)/shard_map/ppermute | solution.py:249
  27.2 11.8 %collective-permute-start.5 = (bf16[32,1536]{1,0:T(8,128)(2,1)S(1)}, bf16[32,1536]{1,0:T(8,128)(2,1)S(1)}, u32[]{:S(2)}, u32[]{:S(2)}) collective-permute-start(bf16[32,1536]{1,0:T(8,128)(2,1)S(1)} %get-tuple-element.48), channel_id=1, source_target_pairs={{0,24},{1,25},{2,26},{3,27},{4,28},{5,29},{6,30},{7,31},{8,16},{9,... | collective-permute-start | bytes 294920 | tf_op jit(solution)/shard_map/ppermute | solution.py:249
  30.3 10.2 %collective-permute-start.6 = (bf16[32,1536]{1,0:T(8,128)(2,1)S(1)}, bf16[32,1536]{1,0:T(8,128)(2,1)S(1)}, u32[]{:S(2)}, u32[]{:S(2)}) collective-permute-start(bf16[32,1536]{1,0:T(8,128)(2,1)S(1)} %get-tuple-element.49), channel_id=1, source_target_pairs={{0,28},{1,29},{2,30},{3,31},{4,24},{5,25},{6,26},{7,27},{8,20},{9,... | collective-permute-start | bytes 294920 | tf_op jit(solution)/shard_map/ppermute | solution.py:249
  38.5 4.8 %collective-permute-start.7 = (bf16[4,48,768]{2,1,0:T(8,128)(2,1)S(1)}, bf16[4,48,768]{2,1,0:T(8,128)(2,1)S(1)}, u32[]{:S(2)}, u32[]{:S(2)}) collective-permute-start(bf16[4,48,768]{2,1,0:T(8,128)(2,1)S(1)} %shard_map.102.refs_4_), channel_id=1, source_target_pairs={{0,1},{1,0},{2,3},{3,2},{4,5},{5,4},{6,7},{7,6},{8,9},{9,8},{10,11... | collective-permute-start | bytes 884744 | tf_op jit(solution)/shard_map/ppermute | solution.py:249
  38.6 4.8 %collective-permute-start.9 = (bf16[4,48,768]{2,1,0:T(8,128)(2,1)S(1)}, bf16[4,48,768]{2,1,0:T(8,128)(2,1)S(1)}, u32[]{:S(2)}, u32[]{:S(2)}) collective-permute-start(bf16[4,48,768]{2,1,0:T(8,128)(2,1)S(1)} %collective-permute-done.8.refs_6_), channel_id=1, source_target_pairs={{0,1},{1,0},{2,3},{3,2},{4,5},{5,4},{6,7},{7,6},{8,9},{9,8},{10,11... | collective-permute-start | bytes 884744 | tf_op jit(solution)/shard_map/ppermute | solution.py:249
  41.2 15.3 %collective-permute-start.13 = (bf16[4,48,768]{2,1,0:T(8,128)(2,1)S(1)}, bf16[4,48,768]{2,1,0:T(8,128)(2,1)S(1)}, u32[]{:S(2)}, u32[]{:S(2)}) collective-permute-start(bf16[4,48,768]{2,1,0:T(8,128)(2,1)S(1)} %shard_map.102.refs_4_), channel_id=1, source_target_pairs={{0,16},{1,17},{2,18},{3,19},{4,20},{5,21},{6,22},{7,23},{8,24},{9,... | collective-permute-start | bytes 884744 | tf_op jit(solution)/shard_map/ppermute | solution.py:249
  43.4 0.9 %copy-start.4 = (bf16[32,1536]{1,0:T(8,128)(2,1)S(1)}, bf16[32,1536]{1,0:T(8,128)(2,1)}, u32[]{:S(2)}) copy-start(bf16[32,1536]{1,0:T(8,128)(2,1)} %copy-done.3) | copy-start | bytes 294916
  45.1 27.3 %copy-start.8 = (f32[33,384]{1,0:T(8,128)S(1)}, f32[33,384]{1,0:T(8,128)}, u32[]{:S(2)}) copy-start(f32[33,384]{1,0:T(8,128)} %copy-done.7) | copy-start | bytes 152068
  56.5 14.4 %collective-permute-start.18 = (bf16[4,48,768]{2,1,0:T(8,128)(2,1)S(1)}, bf16[4,48,768]{2,1,0:T(8,128)(2,1)S(1)}, u32[]{:S(2)}, u32[]{:S(2)}) collective-permute-start(bf16[4,48,768]{2,1,0:T(8,128)(2,1)S(1)} %collective-permute-done.13.refs_5_), channel_id=1, source_target_pairs={{0,1},{1,0},{2,3},{3,2},{4,5},{5,4},{6,7},{7,6},{8,9},{9,8},{10,11... | collective-permute-start | bytes 884744 | tf_op jit(solution)/shard_map/ppermute | solution.py:249
  56.5 14.4 %collective-permute-start.14 = (bf16[4,48,768]{2,1,0:T(8,128)(2,1)S(1)}, bf16[4,48,768]{2,1,0:T(8,128)(2,1)S(1)}, u32[]{:S(2)}, u32[]{:S(2)}) collective-permute-start(bf16[4,48,768]{2,1,0:T(8,128)(2,1)S(1)} %collective-permute-done.13.refs_5_), channel_id=1, source_target_pairs={{0,2},{1,3},{2,0},{3,1},{4,6},{5,7},{6,4},{7,5},{8,10},{9,11},{10,... | collective-permute-start | bytes 884744 | tf_op jit(solution)/shard_map/ppermute | solution.py:249
  58.7 8.7 %collective-permute-start.12 = (bf16[2,32,1536]{2,1,0:T(8,128)(2,1)S(1)}, bf16[2,32,1536]{2,1,0:T(8,128)(2,1)S(1)}, u32[]{:S(2)}, u32[]{:S(2)}) collective-permute-start(bf16[2,32,1536]{2,1,0:T(8,128)(2,1)S(1)} %get-tuple-element.60.refs_0_), channel_id=1, source_target_pairs={{0,12},{1,13},{2,14},{3,15},{4,8},{5,9},{6,10},{7,11},{8,4},{9,5},... | collective-permute-start | bytes 589832 | tf_op jit(solution)/shard_map/ppermute | solution.py:249
  58.8 10.5 %collective-permute-start.11 = (bf16[2,32,1536]{2,1,0:T(8,128)(2,1)S(1)}, bf16[2,32,1536]{2,1,0:T(8,128)(2,1)S(1)}, u32[]{:S(2)}, u32[]{:S(2)}) collective-permute-start(bf16[2,32,1536]{2,1,0:T(8,128)(2,1)S(1)} %get-tuple-element.60.refs_0_), channel_id=1, source_target_pairs={{0,8},{1,9},{2,10},{3,11},{4,12},{5,13},{6,14},{7,15},{8,0},{9,1},... | collective-permute-start | bytes 589832 | tf_op jit(solution)/shard_map/ppermute | solution.py:249
  60.0 10.9 %collective-permute-start.10 = (bf16[2,32,1536]{2,1,0:T(8,128)(2,1)S(1)}, bf16[2,32,1536]{2,1,0:T(8,128)(2,1)S(1)}, u32[]{:S(2)}, u32[]{:S(2)}) collective-permute-start(bf16[2,32,1536]{2,1,0:T(8,128)(2,1)S(1)} %get-tuple-element.60.refs_0_), channel_id=1, source_target_pairs={{0,4},{1,5},{2,6},{3,7},{4,0},{5,1},{6,2},{7,3},{8,12},{9,13},{10,... | collective-permute-start | bytes 589832 | tf_op jit(solution)/shard_map/ppermute | solution.py:249
  70.9 1.6 %collective-permute-start.20 = (bf16[4,48,768]{2,1,0:T(8,128)(2,1)S(1)}, bf16[4,48,768]{2,1,0:T(8,128)(2,1)S(1)}, u32[]{:S(2)}, u32[]{:S(2)}) collective-permute-start(bf16[4,48,768]{2,1,0:T(8,128)(2,1)S(1)} %collective-permute-done.14.refs_7_), channel_id=1, source_target_pairs={{0,1},{1,0},{2,3},{3,2},{4,5},{5,4},{6,7},{7,6},{8,9},{9,8},{10,11... | collective-permute-start | bytes 884744 | tf_op jit(solution)/shard_map/ppermute | solution.py:249
  76.2 7.0 %collective-permute-start.21 = (bf16[2,32,1536]{2,1,0:T(8,128)(2,1)S(1)}, bf16[2,32,1536]{2,1,0:T(8,128)(2,1)S(1)}, u32[]{:S(2)}, u32[]{:S(2)}) collective-permute-start(bf16[2,32,1536]{2,1,0:T(8,128)(2,1)S(1)} %get-tuple-element.66), channel_id=1, source_target_pairs={{0,4},{1,5},{2,6},{3,7},{4,0},{5,1},{6,2},{7,3},{8,12},{9,13},{10,... | collective-permute-start | bytes 589832 | tf_op jit(solution)/shard_map/ppermute | solution.py:249
  76.9 7.8 %collective-permute-start.22 = (bf16[2,32,1536]{2,1,0:T(8,128)(2,1)S(1)}, bf16[2,32,1536]{2,1,0:T(8,128)(2,1)S(1)}, u32[]{:S(2)}, u32[]{:S(2)}) collective-permute-start(bf16[2,32,1536]{2,1,0:T(8,128)(2,1)S(1)} %get-tuple-element.67), channel_id=1, source_target_pairs={{0,8},{1,9},{2,10},{3,11},{4,12},{5,13},{6,14},{7,15},{8,0},{9,1},... | collective-permute-start | bytes 589832 | tf_op jit(solution)/shard_map/ppermute | solution.py:249
  77.1 11.5 %collective-permute-start.23 = (bf16[2,32,1536]{2,1,0:T(8,128)(2,1)S(1)}, bf16[2,32,1536]{2,1,0:T(8,128)(2,1)S(1)}, u32[]{:S(2)}, u32[]{:S(2)}) collective-permute-start(bf16[2,32,1536]{2,1,0:T(8,128)(2,1)S(1)} %get-tuple-element.68), channel_id=1, source_target_pairs={{0,12},{1,13},{2,14},{3,15},{4,8},{5,9},{6,10},{7,11},{8,4},{9,5},... | collective-permute-start | bytes 589832 | tf_op jit(solution)/shard_map/ppermute | solution.py:249
  (7 other events, 4.9 us)

commit v10 on v9

--- a/solution.py
+++ b/solution.py
@@ -330,9 +330,6 @@
         [VMEM, VMEM],
         (place, sources, lens, gain, *near, *gated(far, crossed)),
     )
-    for shift in ins:
-        if shift not in early:
-            ins[shift] = gated(ins[shift], normed)
     share_chips(ins, True)
     normed = quad_swap([normed] * QUAD)
     chip_mask = (fsdp_count - 1) ^ 1

time: 89.7 us -> 86.9 us (0.969)
  waiting for transfers between devices: 35.6 us -> 31.9 us
    ppermute x24, waiting for transfers between devices: 35.6 us -> 31.9 us  [swap(): lax.ppermute(array, ('dp', 'fsdp'), [(at, at ^ mask) for at in range(devi...]
where the time goes in v10:
time: 86.9 us; the launch traced here: 86.6 us
  starting transfers between devices  37.8 us (43%)
  waiting for transfers between devices  31.9 us (37%)
  Pallas kernels  7.65 us (9%)
  local copies, waits for them, and re-layouts  7.29 us (8%)
  other arithmetic  1.75 us (2%)
    ppermute x24, starting transfers between devices, swap(): lax.ppermute(array, ('dp', 'fsdp'), [(at, at ^ mask) for at in range(devi...  37.8 us
    ppermute x24, waiting for transfers between devices, swap(): lax.ppermute(array, ('dp', 'fsdp'), [(at, at ^ mask) for at in range(devi...  31.9 us
    pallas_call x6, Pallas kernels, call(): pl.pallas_call(kernel, out_shape=out_shape, in_specs=in_specs, out_specs=...  7.65 us
    unnamed x30, local copies, waits for them, and re-layouts  7.08 us
  transfers between devices with their start and end apart: 24, of which 13 were waited for; matrix products, arithmetic and copies ran while one was open for 0% of the time, Pallas kernels for 3%

profile of v10, /device:TPU:0, one launch (start us, length us, event | category | flops | bytes accessed | tf_op | source)
XLA Modules:
  0.0 86.6 jit_solution(11440530950065589046)
XLA Ops:
  1.6 1.1 %copy-done = bf16[1,6,32,1536]{3,2,1,0:T(8,128)(2,1)S(1)} copy-done((bf16[1,6,32,1536]{3,2,1,0:T(8,128)(2,1)S(1)}, bf16[1,6,32,1536]{3,2,1,0:T(8,128)(2,1)}, u32[]{:S(2)}) %copy-start) | copy-done | bytes 589848
  2.7 1.0 %copy-done.1 = bf16[48,3072]{1,0:T(8,128)(2,1)S(1)} copy-done((bf16[48,3072]{1,0:T(8,128)(2,1)S(1)}, bf16[48,3072]{1,0:T(8,128)(2,1)}, u32[]{:S(2)}) %copy-start.1) | copy-done | bytes 294936
  4.4 3.0 %collective-permute-start = (bf16[112,768]{1,0:T(8,128)(2,1)S(1)}, bf16[112,768]{1,0:T(8,128)(2,1)S(1)}, u32[]{:S(2)}, u32[]{:S(2)}) collective-permute-start(bf16[112,768]{1,0:T(8,128)(2,1)S(1)} %get-tuple-element.40), channel_id=1, source_target_pairs={{0,4},{1,5},{2,6},{3,7},{4,0},{5,1},{6,2},{7,3},{8,12},{9,13},{10,... | collective-permute-start | bytes 516104 | tf_op jit(solution)/shard_map/ppermute | solution.py:249
  7.4 1.6 %collective-permute-start.1 = (bf16[112,768]{1,0:T(8,128)(2,1)S(1)}, bf16[112,768]{1,0:T(8,128)(2,1)S(1)}, u32[]{:S(2)}, u32[]{:S(2)}) collective-permute-start(bf16[112,768]{1,0:T(8,128)(2,1)S(1)} %get-tuple-element.41), channel_id=1, source_target_pairs={{0,8},{1,9},{2,10},{3,11},{4,12},{5,13},{6,14},{7,15},{8,0},{9,1},... | collective-permute-start | bytes 516104 | tf_op jit(solution)/shard_map/ppermute | solution.py:249
  9.0 3.0 %collective-permute-start.3 = (bf16[32,1536]{1,0:T(8,128)(2,1)S(1)}, bf16[32,1536]{1,0:T(8,128)(2,1)S(1)}, u32[]{:S(2)}, u32[]{:S(2)}) collective-permute-start(bf16[32,1536]{1,0:T(8,128)(2,1)S(1)} %get-tuple-element.43), channel_id=1, source_target_pairs={{0,16},{1,17},{2,18},{3,19},{4,20},{5,21},{6,22},{7,23},{8,24},{9,... | collective-permute-start | bytes 294920 | tf_op jit(solution)/shard_map/ppermute | solution.py:249
  12.0 1.3 %collective-permute-start.4 = (bf16[32,1536]{1,0:T(8,128)(2,1)S(1)}, bf16[32,1536]{1,0:T(8,128)(2,1)S(1)}, u32[]{:S(2)}, u32[]{:S(2)}) collective-permute-start(bf16[32,1536]{1,0:T(8,128)(2,1)S(1)} %get-tuple-element.44), channel_id=1, source_target_pairs={{0,20},{1,21},{2,22},{3,23},{4,16},{5,17},{6,18},{7,19},{8,28},{9,... | collective-permute-start | bytes 294920 | tf_op jit(solution)/shard_map/ppermute | solution.py:249
  14.0 2.7 %collective-permute-start.16 = (bf16[48,1536]{1,0:T(8,128)(2,1)S(1)}, bf16[48,1536]{1,0:T(8,128)(2,1)S(1)}, u32[]{:S(2)}, u32[]{:S(2)}) collective-permute-start(bf16[48,1536]{1,0:T(8,128)(2,1)S(1)} %copy-done.2), channel_id=1, source_target_pairs={{0,16},{1,17},{2,18},{3,19},{4,20},{5,21},{6,22},{7,23},{8,24},{9,... | collective-permute-start | bytes 442376 | tf_op jit(solution)/shard_map/ppermute | solution.py:249
  16.6 3.5 %collective-permute-done.1.refs_2_ = bf16[112,768]{1,0:T(8,128)(2,1)S(1)} collective-permute-done((bf16[112,768]{1,0:T(8,128)(2,1)S(1)}, bf16[112,768]{1,0:T(8,128)(2,1)S(1)}, u32[]{:S(2)}, u32[]{:S(2)}) %collective-permute-start.1) | collective-permute-done | bytes 172064 | tf_op jit(solution)/shard_map/ppermute | solution.py:249
  20.1 3.0 %collective-permute-start.5 = (bf16[32,1536]{1,0:T(8,128)(2,1)S(1)}, bf16[32,1536]{1,0:T(8,128)(2,1)S(1)}, u32[]{:S(2)}, u32[]{:S(2)}) collective-permute-start(bf16[32,1536]{1,0:T(8,128)(2,1)S(1)} %get-tuple-element.47), channel_id=1, source_target_pairs={{0,24},{1,25},{2,26},{3,27},{4,28},{5,29},{6,30},{7,31},{8,16},{9,... | collective-permute-start | bytes 294920 | tf_op jit(solution)/shard_map/ppermute | solution.py:249
  23.1 3.1 %collective-permute-start.6 = (bf16[32,1536]{1,0:T(8,128)(2,1)S(1)}, bf16[32,1536]{1,0:T(8,128)(2,1)S(1)}, u32[]{:S(2)}, u32[]{:S(2)}) collective-permute-start(bf16[32,1536]{1,0:T(8,128)(2,1)S(1)} %get-tuple-element.48), channel_id=1, source_target_pairs={{0,28},{1,29},{2,30},{3,31},{4,24},{5,25},{6,26},{7,27},{8,20},{9,... | collective-permute-start | bytes 294920 | tf_op jit(solution)/shard_map/ppermute | solution.py:249
  26.3 1.8 %shard_map.100 = (s32[2]{0:T(128)S(1)}, s32[2]{0:T(128)S(1)}, f32[33,384]{1,0:T(8,128)S(1)}, f32[1,1536]{1,0:T(1,128)S(1)}) custom-call(s32[1]{0:T(128)} %bitcast.place, s32[144]{0:T(256)S(1)} %reshape.70.packed, f32[34,1536]{1,0:T(8,128)S(1)} %pad_maximum_fusion.small), custom_call_target="tpu_custom_call" | custom-call | bytes 266324 | tf_op jit(solution)/shard_map/pallas_call | solution.py:21
  28.7 1.6 %collective-permute-start.8 = (bf16[4,48,768]{2,1,0:T(8,128)(2,1)S(1)}, bf16[4,48,768]{2,1,0:T(8,128)(2,1)S(1)}, u32[]{:S(2)}, u32[]{:S(2)}) collective-permute-start(bf16[4,48,768]{2,1,0:T(8,128)(2,1)S(1)} %shard_map.102.refs_4_), channel_id=1, source_target_pairs={{0,2},{1,3},{2,0},{3,1},{4,6},{5,7},{6,4},{7,5},{8,10},{9,11},{10,... | collective-permute-start | bytes 884744 | tf_op jit(solution)/shard_map/ppermute | solution.py:249
  32.4 7.3 %collective-permute-start.13 = (bf16[4,48,768]{2,1,0:T(8,128)(2,1)S(1)}, bf16[4,48,768]{2,1,0:T(8,128)(2,1)S(1)}, u32[]{:S(2)}, u32[]{:S(2)}) collective-permute-start(bf16[4,48,768]{2,1,0:T(8,128)(2,1)S(1)} %shard_map.102.refs_4_), channel_id=1, source_target_pairs={{0,16},{1,17},{2,18},{3,19},{4,20},{5,21},{6,22},{7,23},{8,24},{9,... | collective-permute-start | bytes 884744 | tf_op jit(solution)/shard_map/ppermute | solution.py:249
  39.7 1.5 %collective-permute-start.15 = (bf16[48,1536]{1,0:T(8,128)(2,1)S(1)}, bf16[48,1536]{1,0:T(8,128)(2,1)S(1)}, u32[]{:S(2)}, u32[]{:S(2)}) collective-permute-start(bf16[48,1536]{1,0:T(8,128)(2,1)S(1)} %copy-done.2), channel_id=1, source_target_pairs={{0,2},{1,3},{2,0},{3,1},{4,6},{5,7},{6,4},{7,5},{8,10},{9,11},{10,... | collective-permute-start | bytes 442376 | tf_op jit(solution)/shard_map/ppermute | solution.py:249
  41.7 3.1 %collective-permute-done.15.refs_1_ = bf16[48,1536]{1,0:T(8,128)(2,1)S(1)} collective-permute-done((bf16[48,1536]{1,0:T(8,128)(2,1)S(1)}, bf16[48,1536]{1,0:T(8,128)(2,1)S(1)}, u32[]{:S(2)}, u32[]{:S(2)}) %collective-permute-start.15) | collective-permute-done | bytes 147488 | tf_op jit(solution)/shard_map/ppermute | solution.py:249
  44.8 1.6 %collective-permute-done.17.refs_3_ = bf16[48,1536]{1,0:T(8,128)(2,1)S(1)} collective-permute-done((bf16[48,1536]{1,0:T(8,128)(2,1)S(1)}, bf16[48,1536]{1,0:T(8,128)(2,1)S(1)}, u32[]{:S(2)}, u32[]{:S(2)}) %collective-permute-start.17) | collective-permute-done | bytes 147488 | tf_op jit(solution)/shard_map/ppermute | solution.py:249
  47.1 4.1 %collective-permute-done.13.refs_5_ = bf16[4,48,768]{2,1,0:T(8,128)(2,1)S(1)} collective-permute-done((bf16[4,48,768]{2,1,0:T(8,128)(2,1)S(1)}, bf16[4,48,768]{2,1,0:T(8,128)(2,1)S(1)}, u32[]{:S(2)}, u32[]{:S(2)}) %collective-permute-start.13) | collective-permute-done | bytes 294944 | tf_op jit(solution)/shard_map/ppermute | solution.py:249
  51.2 1.5 %collective-permute-start.14 = (bf16[4,48,768]{2,1,0:T(8,128)(2,1)S(1)}, bf16[4,48,768]{2,1,0:T(8,128)(2,1)S(1)}, u32[]{:S(2)}, u32[]{:S(2)}) collective-permute-start(bf16[4,48,768]{2,1,0:T(8,128)(2,1)S(1)} %collective-permute-done.13.refs_5_), channel_id=1, source_target_pairs={{0,2},{1,3},{2,0},{3,1},{4,6},{5,7},{6,4},{7,5},{8,10},{9,11},{10,... | collective-permute-start | bytes 884744 | tf_op jit(solution)/shard_map/ppermute | solution.py:249
  53.6 0.9 %copy-done.6 = bf16[32,1536]{1,0:T(8,128)(2,1)S(1)} copy-done((bf16[32,1536]{1,0:T(8,128)(2,1)S(1)}, bf16[32,1536]{1,0:T(8,128)(2,1)}, u32[]{:S(2)}) %copy-start.6) | copy-done | bytes 98328
  54.5 1.1 %shard_map.103 = (bf16[2,32,1536]{2,1,0:T(8,128)(2,1)S(1)}, bf16[2,32,1536]{2,1,0:T(8,128)(2,1)S(1)}) custom-call(s32[1]{0:T(128)} %bitcast.place, s32[2]{0:T(128)S(1)} %get-tuple-element.37.sources, s32[2]{0:T(128)S(1)} %get-tuple-element.36.lens, f32[1,1536]{1,0:T(1,128)S(1)} %get-tuple-element.38.gain, bf16[112,768]{1,0:T(8,128)(2,1)S(1)} %get-tuple-element.49.refs_0_, ...), custom_call_target="tpu_custom_call" | custom-call | bytes 1480724 | tf_op jit(solution)/shard_map/pallas_call | solution.py:21
  55.6 2.5 %collective-permute-start.11 = (bf16[2,32,1536]{2,1,0:T(8,128)(2,1)S(1)}, bf16[2,32,1536]{2,1,0:T(8,128)(2,1)S(1)}, u32[]{:S(2)}, u32[]{:S(2)}) collective-permute-start(bf16[2,32,1536]{2,1,0:T(8,128)(2,1)S(1)} %get-tuple-element.59.refs_0_), channel_id=1, source_target_pairs={{0,8},{1,9},{2,10},{3,11},{4,12},{5,13},{6,14},{7,15},{8,0},{9,1},... | collective-permute-start | bytes 589832 | tf_op jit(solution)/shard_map/ppermute | solution.py:249
  58.1 1.0 %collective-permute-start.10 = (bf16[2,32,1536]{2,1,0:T(8,128)(2,1)S(1)}, bf16[2,32,1536]{2,1,0:T(8,128)(2,1)S(1)}, u32[]{:S(2)}, u32[]{:S(2)}) collective-permute-start(bf16[2,32,1536]{2,1,0:T(8,128)(2,1)S(1)} %get-tuple-element.59.refs_0_), channel_id=1, source_target_pairs={{0,4},{1,5},{2,6},{3,7},{4,0},{5,1},{6,2},{7,3},{8,12},{9,13},{10,... | collective-permute-start | bytes 589832 | tf_op jit(solution)/shard_map/ppermute | solution.py:249
  59.1 1.5 %collective-permute-done.14.refs_7_ = bf16[4,48,768]{2,1,0:T(8,128)(2,1)S(1)} collective-permute-done((bf16[4,48,768]{2,1,0:T(8,128)(2,1)S(1)}, bf16[4,48,768]{2,1,0:T(8,128)(2,1)S(1)}, u32[]{:S(2)}, u32[]{:S(2)}) %collective-permute-start.14) | collective-permute-done | bytes 294944 | tf_op jit(solution)/shard_map/ppermute | solution.py:249
  60.6 3.7 %collective-permute-done.12.refs_3_ = bf16[2,32,1536]{2,1,0:T(8,128)(2,1)S(1)} collective-permute-done((bf16[2,32,1536]{2,1,0:T(8,128)(2,1)S(1)}, bf16[2,32,1536]{2,1,0:T(8,128)(2,1)S(1)}, u32[]{:S(2)}, u32[]{:S(2)}) %collective-permute-start.12) | collective-permute-done | bytes 196640 | tf_op jit(solution)/shard_map/ppermute | solution.py:249
  64.3 3.1 %collective-permute-done.11.refs_2_ = bf16[2,32,1536]{2,1,0:T(8,128)(2,1)S(1)} collective-permute-done((bf16[2,32,1536]{2,1,0:T(8,128)(2,1)S(1)}, bf16[2,32,1536]{2,1,0:T(8,128)(2,1)S(1)}, u32[]{:S(2)}, u32[]{:S(2)}) %collective-permute-start.11) | collective-permute-done | bytes 196640 | tf_op jit(solution)/shard_map/ppermute | solution.py:249
  67.9 1.4 %collective-permute-done.20.refs_12_ = bf16[4,48,768]{2,1,0:T(8,128)(2,1)S(1)} collective-permute-done((bf16[4,48,768]{2,1,0:T(8,128)(2,1)S(1)}, bf16[4,48,768]{2,1,0:T(8,128)(2,1)S(1)}, u32[]{:S(2)}, u32[]{:S(2)}) %collective-permute-start.20) | collective-permute-done | bytes 294944 | tf_op jit(solution)/shard_map/ppermute | solution.py:249
  69.3 4.0 %shard_map.105 = (f32[2,32,1536]{2,1,0:T(8,128)S(1)}, bf16[2,32,1536]{2,1,0:T(8,128)(2,1)S(1)}, bf16[2,32,1536]{2,1,0:T(8,128)(2,1)S(1)}, bf16[2,32,1536]{2,1,0:T(8,128)(2,1)S(1)}) custom-call(s32[8,5]{1,0:T(8,128)S(1)} %pad_add_fusion.1.where, bf16[2,32,1536]{2,1,0:T(8,128)(2,1)S(1)} %get-tuple-element.57.kept, f32[33,384]{1,0:T(8,128)S(1)} %copy-done.8, ...), custom_call_target="tpu_custom_call" | custom-call | flops 905969664 | bytes 10471072 | tf_op jit(solution)/shard_map/pallas_call | solution.py:21
  73.4 1.1 %collective-permute-start.21 = (bf16[2,32,1536]{2,1,0:T(8,128)(2,1)S(1)}, bf16[2,32,1536]{2,1,0:T(8,128)(2,1)S(1)}, u32[]{:S(2)}, u32[]{:S(2)}) collective-permute-start(bf16[2,32,1536]{2,1,0:T(8,128)(2,1)S(1)} %get-tuple-element.64), channel_id=1, source_target_pairs={{0,4},{1,5},{2,6},{3,7},{4,0},{5,1},{6,2},{7,3},{8,12},{9,13},{10,... | collective-permute-start | bytes 589832 | tf_op jit(solution)/shard_map/ppermute | solution.py:249
  74.5 2.5 %collective-permute-start.23 = (bf16[2,32,1536]{2,1,0:T(8,128)(2,1)S(1)}, bf16[2,32,1536]{2,1,0:T(8,128)(2,1)S(1)}, u32[]{:S(2)}, u32[]{:S(2)}) collective-permute-start(bf16[2,32,1536]{2,1,0:T(8,128)(2,1)S(1)} %get-tuple-element.66), channel_id=1, source_target_pairs={{0,12},{1,13},{2,14},{3,15},{4,8},{5,9},{6,10},{7,11},{8,4},{9,5},... | collective-permute-start | bytes 589832 | tf_op jit(solution)/shard_map/ppermute | solution.py:249
  77.0 3.4 %collective-permute-done.21 = bf16[2,32,1536]{2,1,0:T(8,128)(2,1)S(1)} collective-permute-done((bf16[2,32,1536]{2,1,0:T(8,128)(2,1)S(1)}, bf16[2,32,1536]{2,1,0:T(8,128)(2,1)S(1)}, u32[]{:S(2)}, u32[]{:S(2)}) %collective-permute-start.21) | collective-permute-done | bytes 196640 | tf_op jit(solution)/shard_map/ppermute | solution.py:249
  80.4 1.9 %collective-permute-done.22 = bf16[2,32,1536]{2,1,0:T(8,128)(2,1)S(1)} collective-permute-done((bf16[2,32,1536]{2,1,0:T(8,128)(2,1)S(1)}, bf16[2,32,1536]{2,1,0:T(8,128)(2,1)S(1)}, u32[]{:S(2)}, u32[]{:S(2)}) %collective-permute-start.22) | collective-permute-done | bytes 196640 | tf_op jit(solution)/shard_map/ppermute | solution.py:249
  82.3 3.5 %collective-permute-done.23 = bf16[2,32,1536]{2,1,0:T(8,128)(2,1)S(1)} collective-permute-done((bf16[2,32,1536]{2,1,0:T(8,128)(2,1)S(1)}, bf16[2,32,1536]{2,1,0:T(8,128)(2,1)S(1)}, u32[]{:S(2)}, u32[]{:S(2)}) %collective-permute-start.23) | collective-permute-done | bytes 196640 | tf_op jit(solution)/shard_map/ppermute | solution.py:249
  (66 shorter events, 9.4 us)
Async XLA Ops:
  1.6 1.1 %copy-start = (bf16[1,6,32,1536]{3,2,1,0:T(8,128)(2,1)S(1)}, bf16[1,6,32,1536]{3,2,1,0:T(8,128)(2,1)}, u32[]{:S(2)}) copy-start(bf16[1,6,32,1536]{3,2,1,0:T(8,128)(2,1)} %param.10) | copy-start | bytes 1769476
  2.7 1.0 %copy-start.1 = (bf16[48,3072]{1,0:T(8,128)(2,1)S(1)}, bf16[48,3072]{1,0:T(8,128)(2,1)}, u32[]{:S(2)}) copy-start(bf16[48,3072]{1,0:T(8,128)(2,1)} %weights.1) | copy-start | bytes 884740
  3.6 10.4 %copy-start.2 = (bf16[48,1536]{1,0:T(8,128)(2,1)S(1)}, bf16[48,1536]{1,0:T(8,128)(2,1)}, u32[]{:S(2)}) copy-start(bf16[48,1536]{1,0:T(8,128)(2,1)} %refs_0_) | copy-start | bytes 442372
  3.6 22.6 %copy-start.9 = (f32[31,1536]{1,0:T(8,128)S(1)}, f32[31,1536]{1,0:T(8,128)}, u32[]{:S(2)}) copy-start(f32[31,1536]{1,0:T(8,128)} %param.13) | copy-start | bytes 571396
  4.3 8.9 %copy-start.10 = (f32[1536]{0:T(1024)S(1)}, f32[1536]{0:T(1024)}, u32[]{:S(2)}) copy-start(f32[1536]{0:T(1024)} %param.11) | copy-start | bytes 18436
  4.4 9.6 %collective-permute-start = (bf16[112,768]{1,0:T(8,128)(2,1)S(1)}, bf16[112,768]{1,0:T(8,128)(2,1)S(1)}, u32[]{:S(2)}, u32[]{:S(2)}) collective-permute-start(bf16[112,768]{1,0:T(8,128)(2,1)S(1)} %get-tuple-element.40), channel_id=1, source_target_pairs={{0,4},{1,5},{2,6},{3,7},{4,0},{5,1},{6,2},{7,3},{8,12},{9,13},{10,... | collective-permute-start | bytes 516104 | tf_op jit(solution)/shard_map/ppermute | solution.py:249
  7.4 12.7 %collective-permute-start.1 = (bf16[112,768]{1,0:T(8,128)(2,1)S(1)}, bf16[112,768]{1,0:T(8,128)(2,1)S(1)}, u32[]{:S(2)}, u32[]{:S(2)}) collective-permute-start(bf16[112,768]{1,0:T(8,128)(2,1)S(1)} %get-tuple-element.41), channel_id=1, source_target_pairs={{0,8},{1,9},{2,10},{3,11},{4,12},{5,13},{6,14},{7,15},{8,0},{9,1},... | collective-permute-start | bytes 516104 | tf_op jit(solution)/shard_map/ppermute | solution.py:249
  9.0 14.2 %collective-permute-start.2 = (bf16[112,768]{1,0:T(8,128)(2,1)S(1)}, bf16[112,768]{1,0:T(8,128)(2,1)S(1)}, u32[]{:S(2)}, u32[]{:S(2)}) collective-permute-start(bf16[112,768]{1,0:T(8,128)(2,1)S(1)} %get-tuple-element.42), channel_id=1, source_target_pairs={{0,12},{1,13},{2,14},{3,15},{4,8},{5,9},{6,10},{7,11},{8,4},{9,5},... | collective-permute-start | bytes 516104 | tf_op jit(solution)/shard_map/ppermute | solution.py:249
  9.0 4.3 %copy-start.11 = (f32[1536]{0:T(1024)S(1)}, f32[1536]{0:T(1024)}, u32[]{:S(2)}) copy-start(f32[1536]{0:T(1024)} %param.14) | copy-start | bytes 18436
  9.0 19.7 %collective-permute-start.3 = (bf16[32,1536]{1,0:T(8,128)(2,1)S(1)}, bf16[32,1536]{1,0:T(8,128)(2,1)S(1)}, u32[]{:S(2)}, u32[]{:S(2)}) collective-permute-start(bf16[32,1536]{1,0:T(8,128)(2,1)S(1)} %get-tuple-element.43), channel_id=1, source_target_pairs={{0,16},{1,17},{2,18},{3,19},{4,20},{5,21},{6,22},{7,23},{8,24},{9,... | collective-permute-start | bytes 294920 | tf_op jit(solution)/shard_map/ppermute | solution.py:249
  12.0 19.1 %collective-permute-start.4 = (bf16[32,1536]{1,0:T(8,128)(2,1)S(1)}, bf16[32,1536]{1,0:T(8,128)(2,1)S(1)}, u32[]{:S(2)}, u32[]{:S(2)}) collective-permute-start(bf16[32,1536]{1,0:T(8,128)(2,1)S(1)} %get-tuple-element.44), channel_id=1, source_target_pairs={{0,20},{1,21},{2,22},{3,23},{4,16},{5,17},{6,18},{7,19},{8,28},{9,... | collective-permute-start | bytes 294920 | tf_op jit(solution)/shard_map/ppermute | solution.py:249
  14.0 27.2 %collective-permute-start.16 = (bf16[48,1536]{1,0:T(8,128)(2,1)S(1)}, bf16[48,1536]{1,0:T(8,128)(2,1)S(1)}, u32[]{:S(2)}, u32[]{:S(2)}) collective-permute-start(bf16[48,1536]{1,0:T(8,128)(2,1)S(1)} %copy-done.2), channel_id=1, source_target_pairs={{0,16},{1,17},{2,18},{3,19},{4,20},{5,21},{6,22},{7,23},{8,24},{9,... | collective-permute-start | bytes 442376 | tf_op jit(solution)/shard_map/ppermute | solution.py:249
  20.1 11.0 %collective-permute-start.5 = (bf16[32,1536]{1,0:T(8,128)(2,1)S(1)}, bf16[32,1536]{1,0:T(8,128)(2,1)S(1)}, u32[]{:S(2)}, u32[]{:S(2)}) collective-permute-start(bf16[32,1536]{1,0:T(8,128)(2,1)S(1)} %get-tuple-element.47), channel_id=1, source_target_pairs={{0,24},{1,25},{2,26},{3,27},{4,28},{5,29},{6,30},{7,31},{8,16},{9,... | collective-permute-start | bytes 294920 | tf_op jit(solution)/shard_map/ppermute | solution.py:249
  23.1 8.6 %collective-permute-start.6 = (bf16[32,1536]{1,0:T(8,128)(2,1)S(1)}, bf16[32,1536]{1,0:T(8,128)(2,1)S(1)}, u32[]{:S(2)}, u32[]{:S(2)}) collective-permute-start(bf16[32,1536]{1,0:T(8,128)(2,1)S(1)} %get-tuple-element.48), channel_id=1, source_target_pairs={{0,28},{1,29},{2,30},{3,31},{4,24},{5,25},{6,26},{7,27},{8,20},{9,... | collective-permute-start | bytes 294920 | tf_op jit(solution)/shard_map/ppermute | solution.py:249
  28.7 18.3 %collective-permute-start.8 = (bf16[4,48,768]{2,1,0:T(8,128)(2,1)S(1)}, bf16[4,48,768]{2,1,0:T(8,128)(2,1)S(1)}, u32[]{:S(2)}, u32[]{:S(2)}) collective-permute-start(bf16[4,48,768]{2,1,0:T(8,128)(2,1)S(1)} %shard_map.102.refs_4_), channel_id=1, source_target_pairs={{0,2},{1,3},{2,0},{3,1},{4,6},{5,7},{6,4},{7,5},{8,10},{9,11},{10,... | collective-permute-start | bytes 884744 | tf_op jit(solution)/shard_map/ppermute | solution.py:249
  32.4 18.8 %collective-permute-start.13 = (bf16[4,48,768]{2,1,0:T(8,128)(2,1)S(1)}, bf16[4,48,768]{2,1,0:T(8,128)(2,1)S(1)}, u32[]{:S(2)}, u32[]{:S(2)}) collective-permute-start(bf16[4,48,768]{2,1,0:T(8,128)(2,1)S(1)} %shard_map.102.refs_4_), channel_id=1, source_target_pairs={{0,16},{1,17},{2,18},{3,19},{4,20},{5,21},{6,22},{7,23},{8,24},{9,... | collective-permute-start | bytes 884744 | tf_op jit(solution)/shard_map/ppermute | solution.py:249
  39.7 5.1 %collective-permute-start.15 = (bf16[48,1536]{1,0:T(8,128)(2,1)S(1)}, bf16[48,1536]{1,0:T(8,128)(2,1)S(1)}, u32[]{:S(2)}, u32[]{:S(2)}) collective-permute-start(bf16[48,1536]{1,0:T(8,128)(2,1)S(1)} %copy-done.2), channel_id=1, source_target_pairs={{0,2},{1,3},{2,0},{3,1},{4,6},{5,7},{6,4},{7,5},{8,10},{9,11},{10,... | collective-permute-start | bytes 442376 | tf_op jit(solution)/shard_map/ppermute | solution.py:249
  41.2 5.2 %collective-permute-start.17 = (bf16[48,1536]{1,0:T(8,128)(2,1)S(1)}, bf16[48,1536]{1,0:T(8,128)(2,1)S(1)}, u32[]{:S(2)}, u32[]{:S(2)}) collective-permute-start(bf16[48,1536]{1,0:T(8,128)(2,1)S(1)} %collective-permute-done.16.refs_2_), channel_id=1, source_target_pairs={{0,2},{1,3},{2,0},{3,1},{4,6},{5,7},{6,4},{7,5},{8,10},{9,11},{10,... | collective-permute-start | bytes 442376 | tf_op jit(solution)/shard_map/ppermute | solution.py:249
  46.4 14.2 %collective-permute-start.19 = (bf16[8,48,768]{2,1,0:T(8,128)(2,1)S(1)}, bf16[8,48,768]{2,1,0:T(8,128)(2,1)S(1)}, u32[]{:S(2)}, u32[]{:S(2)}) collective-permute-start(bf16[8,48,768]{2,1,0:T(8,128)(2,1)S(1)} %shard_map.104.refs_8_), channel_id=1, source_target_pairs={{0,1},{1,0},{2,3},{3,2},{4,5},{5,4},{6,7},{7,6},{8,9},{9,8},{10,11... | collective-permute-start | bytes 1769480 | tf_op jit(solution)/shard_map/ppermute | solution.py:249
  46.5 6.2 %collective-permute-start.7 = (bf16[4,48,768]{2,1,0:T(8,128)(2,1)S(1)}, bf16[4,48,768]{2,1,0:T(8,128)(2,1)S(1)}, u32[]{:S(2)}, u32[]{:S(2)}) collective-permute-start(bf16[4,48,768]{2,1,0:T(8,128)(2,1)S(1)} %shard_map.102.refs_4_), channel_id=1, source_target_pairs={{0,1},{1,0},{2,3},{3,2},{4,5},{5,4},{6,7},{7,6},{8,9},{9,8},{10,11... | collective-permute-start | bytes 884744 | tf_op jit(solution)/shard_map/ppermute | solution.py:249
  47.0 5.7 %collective-permute-start.9 = (bf16[4,48,768]{2,1,0:T(8,128)(2,1)S(1)}, bf16[4,48,768]{2,1,0:T(8,128)(2,1)S(1)}, u32[]{:S(2)}, u32[]{:S(2)}) collective-permute-start(bf16[4,48,768]{2,1,0:T(8,128)(2,1)S(1)} %collective-permute-done.8.refs_6_), channel_id=1, source_target_pairs={{0,1},{1,0},{2,3},{3,2},{4,5},{5,4},{6,7},{7,6},{8,9},{9,8},{10,11... | collective-permute-start | bytes 884744 | tf_op jit(solution)/shard_map/ppermute | solution.py:249
  51.2 6.9 %collective-permute-start.18 = (bf16[4,48,768]{2,1,0:T(8,128)(2,1)S(1)}, bf16[4,48,768]{2,1,0:T(8,128)(2,1)}, u32[]{:S(2)}, u32[]{:S(2)}) collective-permute-start(bf16[4,48,768]{2,1,0:T(8,128)(2,1)S(1)} %collective-permute-done.13.refs_5_), channel_id=1, source_target_pairs={{0,1},{1,0},{2,3},{3,2},{4,5},{5,4},{6,7},{7,6},{8,9},{9,8},{10,11... | collective-permute-start | bytes 884744 | tf_op jit(solution)/shard_map/ppermute | solution.py:249
  51.2 9.4 %collective-permute-start.14 = (bf16[4,48,768]{2,1,0:T(8,128)(2,1)S(1)}, bf16[4,48,768]{2,1,0:T(8,128)(2,1)S(1)}, u32[]{:S(2)}, u32[]{:S(2)}) collective-permute-start(bf16[4,48,768]{2,1,0:T(8,128)(2,1)S(1)} %collective-permute-done.13.refs_5_), channel_id=1, source_target_pairs={{0,2},{1,3},{2,0},{3,1},{4,6},{5,7},{6,4},{7,5},{8,10},{9,11},{10,... | collective-permute-start | bytes 884744 | tf_op jit(solution)/shard_map/ppermute | solution.py:249
  52.7 0.9 %copy-start.4 = (bf16[32,1536]{1,0:T(8,128)(2,1)S(1)}, bf16[32,1536]{1,0:T(8,128)(2,1)}, u32[]{:S(2)}) copy-start(bf16[32,1536]{1,0:T(8,128)(2,1)} %copy-done.3) | copy-start | bytes 294916
  54.5 14.9 %copy-start.8 = (f32[33,384]{1,0:T(8,128)S(1)}, f32[33,384]{1,0:T(8,128)}, u32[]{:S(2)}) copy-start(f32[33,384]{1,0:T(8,128)} %copy-done.7) | copy-start | bytes 152068
  55.5 8.7 %collective-permute-start.12 = (bf16[2,32,1536]{2,1,0:T(8,128)(2,1)S(1)}, bf16[2,32,1536]{2,1,0:T(8,128)(2,1)S(1)}, u32[]{:S(2)}, u32[]{:S(2)}) collective-permute-start(bf16[2,32,1536]{2,1,0:T(8,128)(2,1)S(1)} %get-tuple-element.59.refs_0_), channel_id=1, source_target_pairs={{0,12},{1,13},{2,14},{3,15},{4,8},{5,9},{6,10},{7,11},{8,4},{9,5},... | collective-permute-start | bytes 589832 | tf_op jit(solution)/shard_map/ppermute | solution.py:249
  55.6 11.7 %collective-permute-start.11 = (bf16[2,32,1536]{2,1,0:T(8,128)(2,1)S(1)}, bf16[2,32,1536]{2,1,0:T(8,128)(2,1)S(1)}, u32[]{:S(2)}, u32[]{:S(2)}) collective-permute-start(bf16[2,32,1536]{2,1,0:T(8,128)(2,1)S(1)} %get-tuple-element.59.refs_0_), channel_id=1, source_target_pairs={{0,8},{1,9},{2,10},{3,11},{4,12},{5,13},{6,14},{7,15},{8,0},{9,1},... | collective-permute-start | bytes 589832 | tf_op jit(solution)/shard_map/ppermute | solution.py:249
  58.1 9.6 %collective-permute-start.10 = (bf16[2,32,1536]{2,1,0:T(8,128)(2,1)S(1)}, bf16[2,32,1536]{2,1,0:T(8,128)(2,1)S(1)}, u32[]{:S(2)}, u32[]{:S(2)}) collective-permute-start(bf16[2,32,1536]{2,1,0:T(8,128)(2,1)S(1)} %get-tuple-element.59.refs_0_), channel_id=1, source_target_pairs={{0,4},{1,5},{2,6},{3,7},{4,0},{5,1},{6,2},{7,3},{8,12},{9,13},{10,... | collective-permute-start | bytes 589832 | tf_op jit(solution)/shard_map/ppermute | solution.py:249
  67.8 1.6 %collective-permute-start.20 = (bf16[4,48,768]{2,1,0:T(8,128)(2,1)S(1)}, bf16[4,48,768]{2,1,0:T(8,128)(2,1)S(1)}, u32[]{:S(2)}, u32[]{:S(2)}) collective-permute-start(bf16[4,48,768]{2,1,0:T(8,128)(2,1)S(1)} %collective-permute-done.14.refs_7_), channel_id=1, source_target_pairs={{0,1},{1,0},{2,3},{3,2},{4,5},{5,4},{6,7},{7,6},{8,9},{9,8},{10,11... | collective-permute-start | bytes 884744 | tf_op jit(solution)/shard_map/ppermute | solution.py:249
  73.4 7.0 %collective-permute-start.21 = (bf16[2,32,1536]{2,1,0:T(8,128)(2,1)S(1)}, bf16[2,32,1536]{2,1,0:T(8,128)(2,1)S(1)}, u32[]{:S(2)}, u32[]{:S(2)}) collective-permute-start(bf16[2,32,1536]{2,1,0:T(8,128)(2,1)S(1)} %get-tuple-element.64), channel_id=1, source_target_pairs={{0,4},{1,5},{2,6},{3,7},{4,0},{5,1},{6,2},{7,3},{8,12},{9,13},{10,... | collective-permute-start | bytes 589832 | tf_op jit(solution)/shard_map/ppermute | solution.py:249
  74.5 7.8 %collective-permute-start.22 = (bf16[2,32,1536]{2,1,0:T(8,128)(2,1)S(1)}, bf16[2,32,1536]{2,1,0:T(8,128)(2,1)S(1)}, u32[]{:S(2)}, u32[]{:S(2)}) collective-permute-start(bf16[2,32,1536]{2,1,0:T(8,128)(2,1)S(1)} %get-tuple-element.65), channel_id=1, source_target_pairs={{0,8},{1,9},{2,10},{3,11},{4,12},{5,13},{6,14},{7,15},{8,0},{9,1},... | collective-permute-start | bytes 589832 | tf_op jit(solution)/shard_map/ppermute | solution.py:249
  74.5 11.3 %collective-permute-start.23 = (bf16[2,32,1536]{2,1,0:T(8,128)(2,1)S(1)}, bf16[2,32,1536]{2,1,0:T(8,128)(2,1)S(1)}, u32[]{:S(2)}, u32[]{:S(2)}) collective-permute-start(bf16[2,32,1536]{2,1,0:T(8,128)(2,1)S(1)} %get-tuple-element.66), channel_id=1, source_target_pairs={{0,12},{1,13},{2,14},{3,15},{4,8},{5,9},{6,10},{7,11},{8,4},{9,5},... | collective-permute-start | bytes 589832 | tf_op jit(solution)/shard_map/ppermute | solution.py:249
  (7 other events, 4.9 us)

commit v11 on v8

--- a/solution.py
+++ b/solution.py
@@ -85,21 +85,26 @@
         out[start:, :] = buf[jnp.bitwise_xor(lax.rem(me, QUAD), number)]
 
 
-def fetch(out, number, ref, far):
+def fetch(out, number, ref, start):
     long, width = out.shape[1:]
     wide = ref.shape[1]
     for half in range(width // wide):
-        start = (far * (width // wide) + half) * long
-        out[number, :, half * wide : half * wide + wide] = ref[start : start + long, :]
-
-
-def merge_kernel(sources, place, packed, *refs):
+        rows = ref[pl.ds(start + half * long, long), :]
+        out[number, :, half * wide : half * wide + wide] = rows
+
+
+def merge_kernel(sources, long, place, packed, *refs):
     arrived, outs, piece = refs[:QUAD], refs[QUAD:-1], refs[-1]
     tables = Tables(packed, sources)
     me = place[0]
-    depth, wide = piece.shape[1:]
+    depth = piece.shape[1]
+    size = (arrived[0].shape[0] - depth) * QUAD // sources
+    for number, ref in enumerate(arrived):
+        columns = ref[ref.shape[0] - depth :, :]
+        piece[number] = columns
+        for out in outs:
+            out[number * depth : (number + 1) * depth, :] = columns
     for far, out in enumerate(outs, 1):
-        long = out.shape[1]
         for number, ref in enumerate(arrived):
             source = jnp.bitwise_xor(me, number)
             target = jnp.bitwise_xor(me, far * QUAD)
@@ -110,10 +115,8 @@
 
             @pl.when(start >= 0)
             def _():
-                fetch(out, start // long, ref, far)
-
-    for number, ref in enumerate(arrived):
-        piece[number] = ref[ref.shape[0] - depth :, :]
+                at = pl.multiple_of(start // long * size + QUAD * depth, 8)
+                out[pl.ds(at, size), :] = ref[far * size : (far + 1) * size, :]
 
 
 def stack_kernel(*refs):
@@ -160,8 +163,9 @@
             table[...] = jnp.concatenate(parts, axis=1)
 
 
-def norm_kernel(place, sources, lens, gain, *refs):
+def norm_kernel(first, place, sources, lens, gain, *refs):
     near, far, (kept, normed) = refs[:QUAD], refs[QUAD:-2], refs[-2:]
+    size = kept.shape[1] * kept.shape[2] // near[0].shape[1]
     for number in range(kept.shape[0]):
         shift = jnp.bitwise_xor(sources[number], place[0])
         for other, ref in enumerate(near):
@@ -174,7 +178,7 @@
 
             @pl.when(shift // QUAD == other)
             def _():
-                kept[number] = ref[number]
+                fetch(kept, number, ref, first + number * size)
 
         wide = kept[number].astype(F32)
         mean = jnp.mean(wide, axis=1, keepdims=True)
@@ -285,18 +289,7 @@
 
     count = width // wide
 
-    outs = {0: w_out}
-
-    def share_chips(parts, first):
-        for bit in chip_bits:
-            for shift in [shift for shift in parts if (shift >= fsdp_count) == first]:
-                parts[shift ^ bit] = swap(parts[shift], fsdp=bit)
-
-    for mask in range(1, highs):
-        outs[mask * fsdp_count] = swap(w_out, high=mask)
-    share_chips(outs, False)
-
-    near = call(
+    sent = call(
         functools.partial(send_kernel, dp_count),
         [like(BF16, highs * count * long + depth, wide)] * QUAD,
         [SMEM, SMEM, VMEM, VMEM],
@@ -304,7 +297,20 @@
         (place, packed, w_in, frames[0]),
         [like(BF16, QUAD, depth, wide)],
     )
-    near = quad_swap(near)
+    near = quad_swap(sent)
+
+    w_out = gated(w_out, sent)
+    outs = {0: w_out}
+
+    def share_chips(parts, first):
+        for bit in chip_bits:
+            for shift in [shift for shift in parts if (shift >= fsdp_count) == first]:
+                parts[shift ^ bit] = swap(parts[shift], fsdp=bit)
+
+    for mask in range(1, highs):
+        outs[mask * fsdp_count] = swap(w_out, high=mask)
+    share_chips(outs, False)
+
     sources, lens, table, gain = call(
         functools.partial(table_kernel, dp_count, long),
         [like(jnp.int32, recv)] * 2 + [like(F32, taps + 2, chans), like(F32, 1, width)],
@@ -314,8 +320,9 @@
     )
     utts = like(BF16, recv, long, width)
     *far, own_in = call(
-        functools.partial(merge_kernel, dp_count),
-        [utts] * (highs - 1) + [like(BF16, QUAD, depth, wide)],
+        functools.partial(merge_kernel, dp_count, long),
+        [like(BF16, QUAD * depth + recv * count * long, wide)] * (highs - 1)
+        + [like(BF16, QUAD, depth, wide)],
         [SMEM] * 2 + [VMEM] * QUAD,
         [VMEM] * highs,
         (gated(place, (lens, gain, outs)), packed, *near),
@@ -323,7 +330,6 @@
     far = [swap(part, high=mask) for mask, part in enumerate(far, 1)]
 
     ins = {0: own_in}
-    far_in = [swap(own_in, high=mask) for mask in range(1, highs)]
     share_chips(ins, False)
     early = list(ins)
     share_chips(outs, True)
@@ -337,10 +343,10 @@
     )
     crossed = {shift: swap(ins[shift], fsdp=1) for shift in early}
     crossed_out = swap(stacked, fsdp=1)
-    for mask, part in enumerate(gated(far_in, far), 1):
-        ins[mask * fsdp_count] = part
+    for mask, part in enumerate(far, 1):
+        ins[mask * fsdp_count] = part[: QUAD * depth].reshape(QUAD, depth, wide)
     kept, normed = call(
-        norm_kernel,
+        functools.partial(norm_kernel, QUAD * depth),
         [utts, utts],
         [SMEM] * 3 + [VMEM] * (QUAD + highs),
         [VMEM, VMEM],

time: 84.5 us -> 84.1 us (level)
  waiting for transfers between devices: 47.4 us -> 46.5 us
    ppermute x21 -> x20, waiting for transfers between devices: 47.4 us -> 46.5 us  [swap(): lax.ppermute(array, ('dp', 'fsdp'), [(at, at ^ mask) for at in range(devi...]
    ppermute x21 -> x20, starting transfers between devices: 21.9 us -> 22.4 us  [swap(): lax.ppermute(array, ('dp', 'fsdp'), [(at, at ^ mask) for at in range(devi...]
  transfers between devices with their start and end apart: 21 -> 20, of which waited for: 13 -> 12; matrix products, arithmetic and copies ran while one was open for 1% -> 0% of each run, Pallas kernels for 6% -> 5%
where the time goes in v11:
time: 84.1 us; the launch traced here: 83.8 us
  waiting for transfers between devices  46.5 us (55%)
  starting transfers between devices  22.4 us (27%)
  Pallas kernels  9.16 us (11%)
  local copies, waits for them, and re-layouts  3.82 us (5%)
  other arithmetic  1.76 us (2%)
    ppermute x20, waiting for transfers between devices, swap(): lax.ppermute(array, ('dp', 'fsdp'), [(at, at ^ mask) for at in range(devi...  46.5 us
    ppermute x20, starting transfers between devices, swap(): lax.ppermute(array, ('dp', 'fsdp'), [(at, at ^ mask) for at in range(devi...  22.4 us
    pallas_call x6, Pallas kernels, call(): pl.pallas_call(kernel, out_shape=out_shape, in_specs=in_specs, out_specs=...  9.16 us
    unnamed x18, local copies, waits for them, and re-layouts  3.59 us
  transfers between devices with their start and end apart: 20, of which 12 were waited for; matrix products, arithmetic and copies ran while one was open for 0% of the time, Pallas kernels for 5%

profile of v11, /device:TPU:0, one launch (start us, length us, event | category | flops | bytes accessed | tf_op | source)
XLA Modules:
  0.0 83.8 jit_solution(11657929985788187102)
XLA Ops:
  0.7 0.7 pad_add_fusion
  1.6 1.1 %copy-done = bf16[1,6,32,1536]{3,2,1,0:T(8,128)(2,1)S(1)} copy-done((bf16[1,6,32,1536]{3,2,1,0:T(8,128)(2,1)S(1)}, bf16[1,6,32,1536]{3,2,1,0:T(8,128)(2,1)}, u32[]{:S(2)}) %copy-start) | copy-done | bytes 589848
  2.7 1.0 %copy-done.1 = bf16[48,3072]{1,0:T(8,128)(2,1)S(1)} copy-done((bf16[48,3072]{1,0:T(8,128)(2,1)S(1)}, bf16[48,3072]{1,0:T(8,128)(2,1)}, u32[]{:S(2)}) %copy-start.1) | copy-done | bytes 294936
  3.6 0.7 shard_map.101
  4.5 4.0 %collective-permute-start.4 = (bf16[48,1536]{1,0:T(8,128)(2,1)S(1)}, bf16[48,1536]{1,0:T(8,128)(2,1)S(1)}, u32[]{:S(2)}, u32[]{:S(2)}) collective-permute-start(bf16[48,1536]{1,0:T(8,128)(2,1)S(1)} %copy-done.2), channel_id=1, source_target_pairs={{0,16},{1,17},{2,18},{3,19},{4,20},{5,21},{6,22},{7,23},{8,24},{9,... | collective-permute-start | bytes 442376 | tf_op jit(solution)/shard_map/ppermute | solution.py:276
  8.6 1.5 %collective-permute-start = (bf16[176,768]{1,0:T(8,128)(2,1)S(1)}, bf16[176,768]{1,0:T(8,128)(2,1)S(1)}, u32[]{:S(2)}, u32[]{:S(2)}) collective-permute-start(bf16[176,768]{1,0:T(8,128)(2,1)S(1)} %get-tuple-element.29), channel_id=1, source_target_pairs={{0,4},{1,5},{2,6},{3,7},{4,0},{5,1},{6,2},{7,3},{8,12},{9,13},{10,... | collective-permute-start | bytes 811016 | tf_op jit(solution)/shard_map/ppermute | solution.py:276
  10.1 1.6 %collective-permute-start.1 = (bf16[176,768]{1,0:T(8,128)(2,1)S(1)}, bf16[176,768]{1,0:T(8,128)(2,1)S(1)}, u32[]{:S(2)}, u32[]{:S(2)}) collective-permute-start(bf16[176,768]{1,0:T(8,128)(2,1)S(1)} %get-tuple-element.30), channel_id=1, source_target_pairs={{0,8},{1,9},{2,10},{3,11},{4,12},{5,13},{6,14},{7,15},{8,0},{9,1},... | collective-permute-start | bytes 811016 | tf_op jit(solution)/shard_map/ppermute | solution.py:276
  12.1 1.5 %collective-permute-start.3 = (bf16[48,1536]{1,0:T(8,128)(2,1)S(1)}, bf16[48,1536]{1,0:T(8,128)(2,1)S(1)}, u32[]{:S(2)}, u32[]{:S(2)}) collective-permute-start(bf16[48,1536]{1,0:T(8,128)(2,1)S(1)} %copy-done.2), channel_id=1, source_target_pairs={{0,2},{1,3},{2,0},{3,1},{4,6},{5,7},{6,4},{7,5},{8,10},{9,11},{10,... | collective-permute-start | bytes 442376 | tf_op jit(solution)/shard_map/ppermute | solution.py:276
  14.3 1.4 %collective-permute-done.4.refs_2_ = bf16[48,1536]{1,0:T(8,128)(2,1)S(1)} collective-permute-done((bf16[48,1536]{1,0:T(8,128)(2,1)S(1)}, bf16[48,1536]{1,0:T(8,128)(2,1)S(1)}, u32[]{:S(2)}, u32[]{:S(2)}) %collective-permute-start.4) | collective-permute-done | bytes 147488 | tf_op jit(solution)/shard_map/ppermute | solution.py:276
  15.7 1.5 %collective-permute-start.9 = (bf16[48,1536]{1,0:T(8,128)(2,1)S(1)}, bf16[48,1536]{1,0:T(8,128)(2,1)S(1)}, u32[]{:S(2)}, u32[]{:S(2)}) collective-permute-start(bf16[48,1536]{1,0:T(8,128)(2,1)S(1)} %collective-permute-done.4.refs_2_), channel_id=1, source_target_pairs={{0,2},{1,3},{2,0},{3,1},{4,6},{5,7},{6,4},{7,5},{8,10},{9,11},{10,... | collective-permute-start | bytes 442376 | tf_op jit(solution)/shard_map/ppermute | solution.py:276
  17.3 1.8 %shard_map.100 = (s32[2]{0:T(128)S(1)}, s32[2]{0:T(128)S(1)}, f32[33,384]{1,0:T(8,128)S(1)}, f32[1,1536]{1,0:T(1,128)S(1)}) custom-call(s32[1]{0:T(128)} %bitcast.place, s32[144]{0:T(256)S(1)} %reshape.73.packed, f32[34,1536]{1,0:T(8,128)S(1)} %pad_maximum_fusion.small), custom_call_target="tpu_custom_call" | custom-call | bytes 266324 | tf_op jit(solution)/shard_map/pallas_call | solution.py:21
  19.1 1.9 %collective-permute-done.1.refs_2_ = bf16[176,768]{1,0:T(8,128)(2,1)S(1)} collective-permute-done((bf16[176,768]{1,0:T(8,128)(2,1)S(1)}, bf16[176,768]{1,0:T(8,128)(2,1)S(1)}, u32[]{:S(2)}, u32[]{:S(2)}) %collective-permute-start.1) | collective-permute-done | bytes 270368 | tf_op jit(solution)/shard_map/ppermute | solution.py:276
  20.9 4.6 %collective-permute-done.2.refs_3_ = bf16[176,768]{1,0:T(8,128)(2,1)S(1)} collective-permute-done((bf16[176,768]{1,0:T(8,128)(2,1)S(1)}, bf16[176,768]{1,0:T(8,128)(2,1)S(1)}, u32[]{:S(2)}, u32[]{:S(2)}) %collective-permute-start.2) | collective-permute-done | bytes 270368 | tf_op jit(solution)/shard_map/ppermute | solution.py:276
  25.5 1.5 %shard_map.102 = (bf16[320,768]{1,0:T(8,128)(2,1)}, bf16[4,48,768]{2,1,0:T(8,128)(2,1)S(1)}) custom-call(s32[1]{0:T(128)} %bitcast.place, s32[144]{0:T(256)S(1)} %reshape.73.packed, bf16[176,768]{1,0:T(8,128)(2,1)S(1)} %get-tuple-element.28.refs_0_, bf16[176,768]{1,0:T(8,128)(2,1)S(1)} %collective-permute-done.refs_1_, ...), custom_call_target="tpu_custom_call" | custom-call | bytes 1868356 | tf_op jit(solution)/shard_map/pallas_call | solution.py:21
  27.0 1.1 %collective-permute-start.5 = (bf16[320,768]{1,0:T(8,128)(2,1)}, bf16[320,768]{1,0:T(8,128)(2,1)S(1)}, u32[]{:S(2)}, u32[]{:S(2)}) collective-permute-start(bf16[320,768]{1,0:T(8,128)(2,1)} %get-tuple-element.34), channel_id=1, source_target_pairs={{0,16},{1,17},{2,18},{3,19},{4,20},{5,21},{6,22},{7,23},{8,24},{9,... | collective-permute-start | bytes 1474568 | tf_op jit(solution)/shard_map/ppermute | solution.py:276
  28.1 1.5 %collective-permute-start.7 = (bf16[4,48,768]{2,1,0:T(8,128)(2,1)S(1)}, bf16[4,48,768]{2,1,0:T(8,128)(2,1)S(1)}, u32[]{:S(2)}, u32[]{:S(2)}) collective-permute-start(bf16[4,48,768]{2,1,0:T(8,128)(2,1)S(1)} %get-tuple-element.35.refs_4_), channel_id=1, source_target_pairs={{0,2},{1,3},{2,0},{3,1},{4,6},{5,7},{6,4},{7,5},{8,10},{9,11},{10,... | collective-permute-start | bytes 884744 | tf_op jit(solution)/shard_map/ppermute | solution.py:276
  30.2 5.5 %collective-permute-done.7.refs_5_ = bf16[4,48,768]{2,1,0:T(8,128)(2,1)S(1)} collective-permute-done((bf16[4,48,768]{2,1,0:T(8,128)(2,1)S(1)}, bf16[4,48,768]{2,1,0:T(8,128)(2,1)S(1)}, u32[]{:S(2)}, u32[]{:S(2)}) %collective-permute-start.7) | collective-permute-done | bytes 294944 | tf_op jit(solution)/shard_map/ppermute | solution.py:276
  35.7 14.4 %collective-permute-done.5.refs_4_ = bf16[320,768]{1,0:T(8,128)(2,1)S(1)} collective-permute-done((bf16[320,768]{1,0:T(8,128)(2,1)}, bf16[320,768]{1,0:T(8,128)(2,1)S(1)}, u32[]{:S(2)}, u32[]{:S(2)}) %collective-permute-start.5) | collective-permute-done | bytes 491552 | tf_op jit(solution)/shard_map/ppermute | solution.py:276
  50.2 1.6 %collective-permute-start.14 = (bf16[4,48,768]{2,1,0:T(8,128)(2,1)S(1)}, bf16[4,48,768]{2,1,0:T(8,128)(2,1)S(1)}, u32[]{:S(2)}, u32[]{:S(2)}) collective-permute-start(bf16[4,48,768]{2,1,0:T(8,128)(2,1)S(1)} %bitcast.5), channel_id=1, source_target_pairs={{0,2},{1,3},{2,0},{3,1},{4,6},{5,7},{6,4},{7,5},{8,10},{9,11},{10,... | collective-permute-start | bytes 884744 | tf_op jit(solution)/shard_map/ppermute | solution.py:276
  51.8 1.0 %shard_map.104 = (bf16[2,32,1536]{2,1,0:T(8,128)(2,1)S(1)}, bf16[2,32,1536]{2,1,0:T(8,128)(2,1)S(1)}) custom-call(s32[1]{0:T(128)} %bitcast.place, s32[2]{0:T(128)S(1)} %get-tuple-element.26.sources, s32[2]{0:T(128)S(1)} %get-tuple-element.25.lens, f32[1,1536]{1,0:T(1,128)S(1)} %get-tuple-element.27.gain, bf16[176,768]{1,0:T(8,128)(2,1)S(1)} %get-tuple-element.28.refs_0_, ...), custom_call_target="tpu_custom_call" | custom-call | bytes 1972244 | tf_op jit(solution)/shard_map/pallas_call | solution.py:21
  52.9 3.2 %collective-permute-start.12 = (bf16[2,32,1536]{2,1,0:T(8,128)(2,1)S(1)}, bf16[2,32,1536]{2,1,0:T(8,128)(2,1)S(1)}, u32[]{:S(2)}, u32[]{:S(2)}) collective-permute-start(bf16[2,32,1536]{2,1,0:T(8,128)(2,1)S(1)} %get-tuple-element.39.refs_0_), channel_id=1, source_target_pairs={{0,8},{1,9},{2,10},{3,11},{4,12},{5,13},{6,14},{7,15},{8,0},{9,1},... | collective-permute-start | bytes 589832 | tf_op jit(solution)/shard_map/ppermute | solution.py:276
  56.4 1.5 %collective-permute-done.14.refs_7_ = bf16[4,48,768]{2,1,0:T(8,128)(2,1)S(1)} collective-permute-done((bf16[4,48,768]{2,1,0:T(8,128)(2,1)S(1)}, bf16[4,48,768]{2,1,0:T(8,128)(2,1)S(1)}, u32[]{:S(2)}, u32[]{:S(2)}) %collective-permute-start.14) | collective-permute-done | bytes 294944 | tf_op jit(solution)/shard_map/ppermute | solution.py:276
  57.9 3.4 %collective-permute-done.13.refs_3_ = bf16[2,32,1536]{2,1,0:T(8,128)(2,1)S(1)} collective-permute-done((bf16[2,32,1536]{2,1,0:T(8,128)(2,1)S(1)}, bf16[2,32,1536]{2,1,0:T(8,128)(2,1)S(1)}, u32[]{:S(2)}, u32[]{:S(2)}) %collective-permute-start.13) | collective-permute-done | bytes 196640 | tf_op jit(solution)/shard_map/ppermute | solution.py:276
  61.3 3.7 %collective-permute-done.12.refs_2_ = bf16[2,32,1536]{2,1,0:T(8,128)(2,1)S(1)} collective-permute-done((bf16[2,32,1536]{2,1,0:T(8,128)(2,1)S(1)}, bf16[2,32,1536]{2,1,0:T(8,128)(2,1)S(1)}, u32[]{:S(2)}, u32[]{:S(2)}) %collective-permute-start.12) | collective-permute-done | bytes 196640 | tf_op jit(solution)/shard_map/ppermute | solution.py:276
  65.1 1.4 %collective-permute-done.16.refs_12_ = bf16[4,48,768]{2,1,0:T(8,128)(2,1)S(1)} collective-permute-done((bf16[4,48,768]{2,1,0:T(8,128)(2,1)S(1)}, bf16[4,48,768]{2,1,0:T(8,128)(2,1)S(1)}, u32[]{:S(2)}, u32[]{:S(2)}) %collective-permute-start.16) | collective-permute-done | bytes 294944 | tf_op jit(solution)/shard_map/ppermute | solution.py:276
  66.5 4.1 %shard_map.105 = (f32[2,32,1536]{2,1,0:T(8,128)S(1)}, bf16[2,32,1536]{2,1,0:T(8,128)(2,1)S(1)}, bf16[2,32,1536]{2,1,0:T(8,128)(2,1)S(1)}, bf16[2,32,1536]{2,1,0:T(8,128)(2,1)S(1)}) custom-call(s32[8,5]{1,0:T(8,128)S(1)} %pad_add_fusion.1.where, bf16[2,32,1536]{2,1,0:T(8,128)(2,1)S(1)} %get-tuple-element.37.kept, f32[33,384]{1,0:T(8,128)S(1)} %get-tuple-element.38.table, ...), custom_call_target="tpu_custom_call" | custom-call | flops 905969664 | bytes 10471072 | tf_op jit(solution)/shard_map/pallas_call | solution.py:21
  70.6 1.5 %collective-permute-start.17 = (bf16[2,32,1536]{2,1,0:T(8,128)(2,1)S(1)}, bf16[2,32,1536]{2,1,0:T(8,128)(2,1)S(1)}, u32[]{:S(2)}, u32[]{:S(2)}) collective-permute-start(bf16[2,32,1536]{2,1,0:T(8,128)(2,1)S(1)} %get-tuple-element.42), channel_id=1, source_target_pairs={{0,4},{1,5},{2,6},{3,7},{4,0},{5,1},{6,2},{7,3},{8,12},{9,13},{10,... | collective-permute-start | bytes 589832 | tf_op jit(solution)/shard_map/ppermute | solution.py:276
  72.1 2.1 %collective-permute-start.19 = (bf16[2,32,1536]{2,1,0:T(8,128)(2,1)S(1)}, bf16[2,32,1536]{2,1,0:T(8,128)(2,1)S(1)}, u32[]{:S(2)}, u32[]{:S(2)}) collective-permute-start(bf16[2,32,1536]{2,1,0:T(8,128)(2,1)S(1)} %get-tuple-element.44), channel_id=1, source_target_pairs={{0,12},{1,13},{2,14},{3,15},{4,8},{5,9},{6,10},{7,11},{8,4},{9,5},... | collective-permute-start | bytes 589832 | tf_op jit(solution)/shard_map/ppermute | solution.py:276
  74.2 3.4 %collective-permute-done.17 = bf16[2,32,1536]{2,1,0:T(8,128)(2,1)S(1)} collective-permute-done((bf16[2,32,1536]{2,1,0:T(8,128)(2,1)S(1)}, bf16[2,32,1536]{2,1,0:T(8,128)(2,1)S(1)}, u32[]{:S(2)}, u32[]{:S(2)}) %collective-permute-start.17) | collective-permute-done | bytes 196640 | tf_op jit(solution)/shard_map/ppermute | solution.py:276
  77.6 2.3 %collective-permute-done.18 = bf16[2,32,1536]{2,1,0:T(8,128)(2,1)S(1)} collective-permute-done((bf16[2,32,1536]{2,1,0:T(8,128)(2,1)S(1)}, bf16[2,32,1536]{2,1,0:T(8,128)(2,1)S(1)}, u32[]{:S(2)}, u32[]{:S(2)}) %collective-permute-start.18) | collective-permute-done | bytes 196640 | tf_op jit(solution)/shard_map/ppermute | solution.py:276
  79.9 3.1 %collective-permute-done.19 = bf16[2,32,1536]{2,1,0:T(8,128)(2,1)S(1)} collective-permute-done((bf16[2,32,1536]{2,1,0:T(8,128)(2,1)S(1)}, bf16[2,32,1536]{2,1,0:T(8,128)(2,1)S(1)}, u32[]{:S(2)}, u32[]{:S(2)}) %collective-permute-start.19) | collective-permute-done | bytes 196640 | tf_op jit(solution)/shard_map/ppermute | solution.py:276
  83.0 0.8 fusion
  (47 shorter events, 3.4 us)
Async XLA Ops:
  0.0 0.7 copy-start.8
  0.0 0.7 copy-start.7
  1.6 1.1 %copy-start = (bf16[1,6,32,1536]{3,2,1,0:T(8,128)(2,1)S(1)}, bf16[1,6,32,1536]{3,2,1,0:T(8,128)(2,1)}, u32[]{:S(2)}) copy-start(bf16[1,6,32,1536]{3,2,1,0:T(8,128)(2,1)} %param.10) | copy-start | bytes 1769476
  2.7 1.0 %copy-start.1 = (bf16[48,3072]{1,0:T(8,128)(2,1)S(1)}, bf16[48,3072]{1,0:T(8,128)(2,1)}, u32[]{:S(2)}) copy-start(bf16[48,3072]{1,0:T(8,128)(2,1)} %weights.1) | copy-start | bytes 884740
  3.6 0.9 %copy-start.2 = (bf16[48,1536]{1,0:T(8,128)(2,1)S(1)}, bf16[48,1536]{1,0:T(8,128)(2,1)}, u32[]{:S(2)}) copy-start(bf16[48,1536]{1,0:T(8,128)(2,1)} %refs_0_) | copy-start | bytes 442372
  3.6 9.9 %copy-start.4 = (f32[1536]{0:T(1024)S(1)}, f32[1536]{0:T(1024)}, u32[]{:S(2)}) copy-start(f32[1536]{0:T(1024)} %param.11) | copy-start | bytes 18436
  3.6 13.6 %copy-start.3 = (f32[31,1536]{1,0:T(8,128)S(1)}, f32[31,1536]{1,0:T(8,128)}, u32[]{:S(2)}) copy-start(f32[31,1536]{1,0:T(8,128)} %param.13) | copy-start | bytes 571396
  4.3 9.2 %copy-start.5 = (f32[1536]{0:T(1024)S(1)}, f32[1536]{0:T(1024)}, u32[]{:S(2)}) copy-start(f32[1536]{0:T(1024)} %param.14) | copy-start | bytes 18436
  4.5 11.2 %collective-permute-start.4 = (bf16[48,1536]{1,0:T(8,128)(2,1)S(1)}, bf16[48,1536]{1,0:T(8,128)(2,1)S(1)}, u32[]{:S(2)}, u32[]{:S(2)}) collective-permute-start(bf16[48,1536]{1,0:T(8,128)(2,1)S(1)} %copy-done.2), channel_id=1, source_target_pairs={{0,16},{1,17},{2,18},{3,19},{4,20},{5,21},{6,22},{7,23},{8,24},{9,... | collective-permute-start | bytes 442376 | tf_op jit(solution)/shard_map/ppermute | solution.py:276
  8.6 10.5 %collective-permute-start = (bf16[176,768]{1,0:T(8,128)(2,1)S(1)}, bf16[176,768]{1,0:T(8,128)(2,1)S(1)}, u32[]{:S(2)}, u32[]{:S(2)}) collective-permute-start(bf16[176,768]{1,0:T(8,128)(2,1)S(1)} %get-tuple-element.29), channel_id=1, source_target_pairs={{0,4},{1,5},{2,6},{3,7},{4,0},{5,1},{6,2},{7,3},{8,12},{9,13},{10,... | collective-permute-start | bytes 811016 | tf_op jit(solution)/shard_map/ppermute | solution.py:276
  10.1 10.9 %collective-permute-start.1 = (bf16[176,768]{1,0:T(8,128)(2,1)S(1)}, bf16[176,768]{1,0:T(8,128)(2,1)S(1)}, u32[]{:S(2)}, u32[]{:S(2)}) collective-permute-start(bf16[176,768]{1,0:T(8,128)(2,1)S(1)} %get-tuple-element.30), channel_id=1, source_target_pairs={{0,8},{1,9},{2,10},{3,11},{4,12},{5,13},{6,14},{7,15},{8,0},{9,1},... | collective-permute-start | bytes 811016 | tf_op jit(solution)/shard_map/ppermute | solution.py:276
  11.7 13.9 %collective-permute-start.2 = (bf16[176,768]{1,0:T(8,128)(2,1)S(1)}, bf16[176,768]{1,0:T(8,128)(2,1)S(1)}, u32[]{:S(2)}, u32[]{:S(2)}) collective-permute-start(bf16[176,768]{1,0:T(8,128)(2,1)S(1)} %get-tuple-element.31), channel_id=1, source_target_pairs={{0,12},{1,13},{2,14},{3,15},{4,8},{5,9},{6,10},{7,11},{8,4},{9,5},... | collective-permute-start | bytes 811016 | tf_op jit(solution)/shard_map/ppermute | solution.py:276
  12.1 7.0 %collective-permute-start.3 = (bf16[48,1536]{1,0:T(8,128)(2,1)S(1)}, bf16[48,1536]{1,0:T(8,128)(2,1)S(1)}, u32[]{:S(2)}, u32[]{:S(2)}) collective-permute-start(bf16[48,1536]{1,0:T(8,128)(2,1)S(1)} %copy-done.2), channel_id=1, source_target_pairs={{0,2},{1,3},{2,0},{3,1},{4,6},{5,7},{6,4},{7,5},{8,10},{9,11},{10,... | collective-permute-start | bytes 442376 | tf_op jit(solution)/shard_map/ppermute | solution.py:276
  13.6 0.7 copy-start.6
  15.7 13.9 %collective-permute-start.9 = (bf16[48,1536]{1,0:T(8,128)(2,1)S(1)}, bf16[48,1536]{1,0:T(8,128)(2,1)S(1)}, u32[]{:S(2)}, u32[]{:S(2)}) collective-permute-start(bf16[48,1536]{1,0:T(8,128)(2,1)S(1)} %collective-permute-done.4.refs_2_), channel_id=1, source_target_pairs={{0,2},{1,3},{2,0},{3,1},{4,6},{5,7},{6,4},{7,5},{8,10},{9,11},{10,... | collective-permute-start | bytes 442376 | tf_op jit(solution)/shard_map/ppermute | solution.py:276
  27.0 23.1 %collective-permute-start.5 = (bf16[320,768]{1,0:T(8,128)(2,1)}, bf16[320,768]{1,0:T(8,128)(2,1)S(1)}, u32[]{:S(2)}, u32[]{:S(2)}) collective-permute-start(bf16[320,768]{1,0:T(8,128)(2,1)} %get-tuple-element.34), channel_id=1, source_target_pairs={{0,16},{1,17},{2,18},{3,19},{4,20},{5,21},{6,22},{7,23},{8,24},{9,... | collective-permute-start | bytes 1474568 | tf_op jit(solution)/shard_map/ppermute | solution.py:276
  28.1 7.6 %collective-permute-start.7 = (bf16[4,48,768]{2,1,0:T(8,128)(2,1)S(1)}, bf16[4,48,768]{2,1,0:T(8,128)(2,1)S(1)}, u32[]{:S(2)}, u32[]{:S(2)}) collective-permute-start(bf16[4,48,768]{2,1,0:T(8,128)(2,1)S(1)} %get-tuple-element.35.refs_4_), channel_id=1, source_target_pairs={{0,2},{1,3},{2,0},{3,1},{4,6},{5,7},{6,4},{7,5},{8,10},{9,11},{10,... | collective-permute-start | bytes 884744 | tf_op jit(solution)/shard_map/ppermute | solution.py:276
  29.6 22.1 %collective-permute-start.10 = (bf16[8,48,768]{2,1,0:T(8,128)(2,1)S(1)}, bf16[8,48,768]{2,1,0:T(8,128)(2,1)S(1)}, u32[]{:S(2)}, u32[]{:S(2)}) collective-permute-start(bf16[8,48,768]{2,1,0:T(8,128)(2,1)S(1)} %shard_map.103.refs_8_), channel_id=1, source_target_pairs={{0,1},{1,0},{2,3},{3,2},{4,5},{5,4},{6,7},{7,6},{8,9},{9,8},{10,11... | collective-permute-start | bytes 1769480 | tf_op jit(solution)/shard_map/ppermute | solution.py:276
  29.7 22.0 %collective-permute-start.6 = (bf16[4,48,768]{2,1,0:T(8,128)(2,1)S(1)}, bf16[4,48,768]{2,1,0:T(8,128)(2,1)}, u32[]{:S(2)}, u32[]{:S(2)}) collective-permute-start(bf16[4,48,768]{2,1,0:T(8,128)(2,1)S(1)} %get-tuple-element.35.refs_4_), channel_id=1, source_target_pairs={{0,1},{1,0},{2,3},{3,2},{4,5},{5,4},{6,7},{7,6},{8,9},{9,8},{10,11... | collective-permute-start | bytes 884744 | tf_op jit(solution)/shard_map/ppermute | solution.py:276
  35.7 16.0 %collective-permute-start.8 = (bf16[4,48,768]{2,1,0:T(8,128)(2,1)S(1)}, bf16[4,48,768]{2,1,0:T(8,128)(2,1)}, u32[]{:S(2)}, u32[]{:S(2)}) collective-permute-start(bf16[4,48,768]{2,1,0:T(8,128)(2,1)S(1)} %collective-permute-done.7.refs_5_), channel_id=1, source_target_pairs={{0,1},{1,0},{2,3},{3,2},{4,5},{5,4},{6,7},{7,6},{8,9},{9,8},{10,11... | collective-permute-start | bytes 884744 | tf_op jit(solution)/shard_map/ppermute | solution.py:276
  50.2 7.7 %collective-permute-start.14 = (bf16[4,48,768]{2,1,0:T(8,128)(2,1)S(1)}, bf16[4,48,768]{2,1,0:T(8,128)(2,1)S(1)}, u32[]{:S(2)}, u32[]{:S(2)}) collective-permute-start(bf16[4,48,768]{2,1,0:T(8,128)(2,1)S(1)} %bitcast.5), channel_id=1, source_target_pairs={{0,2},{1,3},{2,0},{3,1},{4,6},{5,7},{6,4},{7,5},{8,10},{9,11},{10,... | collective-permute-start | bytes 884744 | tf_op jit(solution)/shard_map/ppermute | solution.py:276
  52.8 8.4 %collective-permute-start.13 = (bf16[2,32,1536]{2,1,0:T(8,128)(2,1)S(1)}, bf16[2,32,1536]{2,1,0:T(8,128)(2,1)S(1)}, u32[]{:S(2)}, u32[]{:S(2)}) collective-permute-start(bf16[2,32,1536]{2,1,0:T(8,128)(2,1)S(1)} %get-tuple-element.39.refs_0_), channel_id=1, source_target_pairs={{0,12},{1,13},{2,14},{3,15},{4,8},{5,9},{6,10},{7,11},{8,4},{9,5},... | collective-permute-start | bytes 589832 | tf_op jit(solution)/shard_map/ppermute | solution.py:276
  52.9 12.0 %collective-permute-start.12 = (bf16[2,32,1536]{2,1,0:T(8,128)(2,1)S(1)}, bf16[2,32,1536]{2,1,0:T(8,128)(2,1)S(1)}, u32[]{:S(2)}, u32[]{:S(2)}) collective-permute-start(bf16[2,32,1536]{2,1,0:T(8,128)(2,1)S(1)} %get-tuple-element.39.refs_0_), channel_id=1, source_target_pairs={{0,8},{1,9},{2,10},{3,11},{4,12},{5,13},{6,14},{7,15},{8,0},{9,1},... | collective-permute-start | bytes 589832 | tf_op jit(solution)/shard_map/ppermute | solution.py:276
  56.1 8.8 %collective-permute-start.11 = (bf16[2,32,1536]{2,1,0:T(8,128)(2,1)S(1)}, bf16[2,32,1536]{2,1,0:T(8,128)(2,1)S(1)}, u32[]{:S(2)}, u32[]{:S(2)}) collective-permute-start(bf16[2,32,1536]{2,1,0:T(8,128)(2,1)S(1)} %get-tuple-element.39.refs_0_), channel_id=1, source_target_pairs={{0,4},{1,5},{2,6},{3,7},{4,0},{5,1},{6,2},{7,3},{8,12},{9,13},{10,... | collective-permute-start | bytes 589832 | tf_op jit(solution)/shard_map/ppermute | solution.py:276
  56.4 8.7 %collective-permute-start.15 = (bf16[4,48,768]{2,1,0:T(8,128)(2,1)S(1)}, bf16[4,48,768]{2,1,0:T(8,128)(2,1)S(1)}, u32[]{:S(2)}, u32[]{:S(2)}) collective-permute-start(bf16[4,48,768]{2,1,0:T(8,128)(2,1)S(1)} %bitcast.6), channel_id=1, source_target_pairs={{0,1},{1,0},{2,3},{3,2},{4,5},{5,4},{6,7},{7,6},{8,9},{9,8},{10,11... | collective-permute-start | bytes 884744 | tf_op jit(solution)/shard_map/ppermute | solution.py:276
  64.9 1.6 %collective-permute-start.16 = (bf16[4,48,768]{2,1,0:T(8,128)(2,1)S(1)}, bf16[4,48,768]{2,1,0:T(8,128)(2,1)S(1)}, u32[]{:S(2)}, u32[]{:S(2)}) collective-permute-start(bf16[4,48,768]{2,1,0:T(8,128)(2,1)S(1)} %collective-permute-done.14.refs_7_), channel_id=1, source_target_pairs={{0,1},{1,0},{2,3},{3,2},{4,5},{5,4},{6,7},{7,6},{8,9},{9,8},{10,11... | collective-permute-start | bytes 884744 | tf_op jit(solution)/shard_map/ppermute | solution.py:276
  70.6 7.0 %collective-permute-start.17 = (bf16[2,32,1536]{2,1,0:T(8,128)(2,1)S(1)}, bf16[2,32,1536]{2,1,0:T(8,128)(2,1)S(1)}, u32[]{:S(2)}, u32[]{:S(2)}) collective-permute-start(bf16[2,32,1536]{2,1,0:T(8,128)(2,1)S(1)} %get-tuple-element.42), channel_id=1, source_target_pairs={{0,4},{1,5},{2,6},{3,7},{4,0},{5,1},{6,2},{7,3},{8,12},{9,13},{10,... | collective-permute-start | bytes 589832 | tf_op jit(solution)/shard_map/ppermute | solution.py:276
  72.1 7.8 %collective-permute-start.18 = (bf16[2,32,1536]{2,1,0:T(8,128)(2,1)S(1)}, bf16[2,32,1536]{2,1,0:T(8,128)(2,1)S(1)}, u32[]{:S(2)}, u32[]{:S(2)}) collective-permute-start(bf16[2,32,1536]{2,1,0:T(8,128)(2,1)S(1)} %get-tuple-element.43), channel_id=1, source_target_pairs={{0,8},{1,9},{2,10},{3,11},{4,12},{5,13},{6,14},{7,15},{8,0},{9,1},... | collective-permute-start | bytes 589832 | tf_op jit(solution)/shard_map/ppermute | solution.py:276
  72.1 10.9 %collective-permute-start.19 = (bf16[2,32,1536]{2,1,0:T(8,128)(2,1)S(1)}, bf16[2,32,1536]{2,1,0:T(8,128)(2,1)S(1)}, u32[]{:S(2)}, u32[]{:S(2)}) collective-permute-start(bf16[2,32,1536]{2,1,0:T(8,128)(2,1)S(1)} %get-tuple-element.44), channel_id=1, source_target_pairs={{0,12},{1,13},{2,14},{3,15},{4,8},{5,9},{6,10},{7,11},{8,4},{9,5},... | collective-permute-start | bytes 589832 | tf_op jit(solution)/shard_map/ppermute | solution.py:276

commit v12 on v7

--- a/solution.py
+++ b/solution.py
@@ -79,7 +79,7 @@
     arrived, outs = refs[:QUAD], refs[QUAD:]
     tables = Tables(packed, sources)
     me = place[0]
-    for far, out in enumerate(outs, 1):
+    for far, out in enumerate(outs):
         long = out.shape[1]
         for number, ref in enumerate(arrived):
             source = jnp.bitwise_xor(me, number)
@@ -133,18 +133,12 @@
 
 
 def norm_kernel(place, sources, lens, gain, *refs):
-    near, far, (kept, normed) = refs[:QUAD], refs[QUAD:-2], refs[-2:]
+    arrived, (kept, normed) = refs[:-2], refs[-2:]
     for number in range(kept.shape[0]):
-        shift = jnp.bitwise_xor(sources[number], place[0])
-        for other, ref in enumerate(near):
+        shift = jnp.bitwise_xor(sources[number], place[0]) // QUAD
+        for other, ref in enumerate(arrived):
 
             @pl.when(shift == other)
-            def _():
-                kept[number] = ref[0]
-
-        for other, ref in enumerate(far, 1):
-
-            @pl.when(shift // QUAD == other)
             def _():
                 kept[number] = ref[number]
 
@@ -287,28 +281,30 @@
         (place, packed, small),
     )
     utts = like(BF16, recv, long, width)
-    far = call(
+    held, *far = call(
         functools.partial(merge_kernel, dp_count),
-        [utts] * (highs - 1),
+        [utts] * highs,
         [SMEM] * 2 + [VMEM] * QUAD,
-        [VMEM] * (highs - 1),
+        [VMEM] * highs,
         (gated(place, (lens, gain)), packed, *near),
     )
+    merged = far
     far = [swap(part, high=mask) for mask, part in enumerate(far, 1)]
 
     halves = [w_out[:, at : at + wide] for at in range(0, width, wide)]
     pieces = [jnp.stack(columns + halves)]
     shifts = [mask * fsdp_count for mask in range(highs)]
-    pieces += gated([swap(pieces[0], high=mask) for mask in range(1, highs)], far)
     chip_first = [swap(pieces[0], fsdp=bit) for bit in chip_bits[:1]]
+    crossing = [swap(pieces[0], high=mask) for mask in range(1, highs)]
+    pieces += gated(crossing, (merged, chip_first))
     early = [swap(part, fsdp=1) for part in pieces[:1] + chip_first]
     far = gated(far, early)
     kept, normed = call(
         norm_kernel,
         [utts, utts],
-        [SMEM] * 3 + [VMEM] * (QUAD + highs),
+        [SMEM] * 3 + [VMEM] * (1 + highs),
         [VMEM, VMEM],
-        (place, sources, lens, gain, *near, *far),
+        (place, sources, lens, gain, held, *far),
     )
     for bit in chip_bits:
         first = chip_first if bit == chip_bits[0] else []

time: 80.3 us -> 78.5 us (0.978)
  waiting for transfers between devices: 39.1 us -> 37.1 us
  other arithmetic: 1.76 us -> 2.69 us
  local copies, waits for them, and re-layouts: 5.27 us -> 4.36 us
    ppermute x20, waiting for transfers between devices: 39.1 us -> 37.1 us  [swap(): lax.ppermute(array, ('dp', 'fsdp'), [(at, at ^ mask) for at in range(devi...]
    concatenate x1, other arithmetic: 0.03 us -> 0.96 us  [shards(): jnp.concatenate([depth_kernel, bn_scale[None], bn_shift[None], ln_gain[No...]
    unnamed x29 -> x23, local copies, waits for them, and re-layouts: 4.97 us -> 4.06 us
  transfers between devices with their start and end apart: 20 -> 20, of which waited for: 13 -> 12; matrix products, arithmetic and copies ran while one was open for 0% -> 2% of each run, Pallas kernels for 5% -> 5%
where the time goes in v12:
time: 78.5 us; the launch traced here: 78.1 us
  waiting for transfers between devices  37.1 us (47%)
  starting transfers between devices  25.8 us (33%)
  Pallas kernels  7.99 us (10%)
  local copies, waits for them, and re-layouts  4.36 us (6%)
  other arithmetic  2.69 us (3%)
    ppermute x20, waiting for transfers between devices, swap(): lax.ppermute(array, ('dp', 'fsdp'), [(at, at ^ mask) for at in range(devi...  37.1 us
    ppermute x20, starting transfers between devices, swap(): lax.ppermute(array, ('dp', 'fsdp'), [(at, at ^ mask) for at in range(devi...  25.8 us
    pallas_call x6, Pallas kernels, call(): pl.pallas_call(kernel, out_shape=out_shape, in_specs=in_specs, out_specs=...  7.99 us
    unnamed x23, local copies, waits for them, and re-layouts  4.06 us
  transfers between devices with their start and end apart: 20, of which 12 were waited for; matrix products, arithmetic and copies ran while one was open for 2% of the time, Pallas kernels for 5%

profile of v12, /device:TPU:0, one launch (start us, length us, event | category | flops | bytes accessed | tf_op | source)
XLA Modules:
  0.0 78.1 jit_solution(13173554497430479828)
XLA Ops:
  0.7 0.7 pad_add_fusion
  1.6 1.1 %copy-done = bf16[1,6,32,1536]{3,2,1,0:T(8,128)(2,1)S(1)} copy-done((bf16[1,6,32,1536]{3,2,1,0:T(8,128)(2,1)S(1)}, bf16[1,6,32,1536]{3,2,1,0:T(8,128)(2,1)}, u32[]{:S(2)}) %copy-start) | copy-done | bytes 589848
  3.3 3.0 %collective-permute-start = (bf16[2,32,1536]{2,1,0:T(8,128)(2,1)S(1)}, bf16[2,32,1536]{2,1,0:T(8,128)(2,1)S(1)}, u32[]{:S(2)}, u32[]{:S(2)}) collective-permute-start(bf16[2,32,1536]{2,1,0:T(8,128)(2,1)S(1)} %get-tuple-element.38), channel_id=1, source_target_pairs={{0,4},{1,5},{2,6},{3,7},{4,0},{5,1},{6,2},{7,3},{8,12},{9,13},{10,... | collective-permute-start | bytes 589832 | tf_op jit(solution)/shard_map/ppermute | solution.py:235
  6.8 1.8 %collective-permute-start.5 = (bf16[48,768]{1,0:T(8,128)(2,1)S(1)}, bf16[48,768]{1,0:T(8,128)(2,1)S(1)}, u32[]{:S(2)}, u32[]{:S(2)}) collective-permute-start(bf16[48,768]{1,0:T(8,128)(2,1)S(1)} %get-tuple-element.45), channel_id=1, source_target_pairs={{0,8},{1,9},{2,10},{3,11},{4,12},{5,13},{6,14},{7,15},{8,0},{9,1},... | collective-permute-start | bytes 221192 | tf_op jit(solution)/shard_map/ppermute | solution.py:235
  8.7 1.4 %collective-permute-start.6 = (bf16[48,768]{1,0:T(8,128)(2,1)S(1)}, bf16[48,768]{1,0:T(8,128)(2,1)S(1)}, u32[]{:S(2)}, u32[]{:S(2)}) collective-permute-start(bf16[48,768]{1,0:T(8,128)(2,1)S(1)} %get-tuple-element.46), channel_id=1, source_target_pairs={{0,12},{1,13},{2,14},{3,15},{4,8},{5,9},{6,10},{7,11},{8,4},{9,5},... | collective-permute-start | bytes 221192 | tf_op jit(solution)/shard_map/ppermute | solution.py:235
  10.1 4.4 %collective-permute-done.4 = bf16[48,768]{1,0:T(8,128)(2,1)S(1)} collective-permute-done((bf16[48,768]{1,0:T(8,128)(2,1)S(1)}, bf16[48,768]{1,0:T(8,128)(2,1)S(1)}, u32[]{:S(2)}, u32[]{:S(2)}) %collective-permute-start.4) | collective-permute-done | bytes 73760 | tf_op jit(solution)/shard_map/ppermute | solution.py:235
  14.5 0.9 %copy-done.2 = bf16[48,1536]{1,0:T(8,128)(2,1)S(1)} copy-done((bf16[48,1536]{1,0:T(8,128)(2,1)S(1)}, bf16[48,1536]{1,0:T(8,128)(2,1)}, u32[]{:S(2)}) %copy-start.2) | copy-done | bytes 147480
  15.4 1.8 %collective-permute-start.8 = (bf16[6,48,768]{2,1,0:T(8,128)(2,1)S(1)}, bf16[6,48,768]{2,1,0:T(8,128)(2,1)S(1)}, u32[]{:S(2)}, u32[]{:S(2)}) collective-permute-start(bf16[6,48,768]{2,1,0:T(8,128)(2,1)S(1)} %bitcast_dynamic-update-slice_fusion.refs_4_), channel_id=1, source_target_pairs={{0,2},{1,3},{2,0},{3,1},{4,6},{5,7},{6,4},{7,5},{8,10},{9,11},{10,... | collective-permute-start | bytes 1327112 | tf_op jit(solution)/shard_map/ppermute | solution.py:235
  17.2 2.6 %collective-permute-start.13 = (bf16[6,48,768]{2,1,0:T(8,128)(2,1)S(1)}, bf16[6,48,768]{2,1,0:T(8,128)(2,1)S(1)}, u32[]{:S(2)}, u32[]{:S(2)}) collective-permute-start(bf16[6,48,768]{2,1,0:T(8,128)(2,1)S(1)} %bitcast_dynamic-update-slice_fusion.refs_4_), channel_id=1, source_target_pairs={{0,16},{1,17},{2,18},{3,19},{4,20},{5,21},{6,22},{7,23},{8,24},{9,... | collective-permute-start | bytes 1327112 | tf_op jit(solution)/shard_map/ppermute | solution.py:235
  19.7 1.6 %collective-permute-start.1 = (bf16[2,32,1536]{2,1,0:T(8,128)(2,1)S(1)}, bf16[2,32,1536]{2,1,0:T(8,128)(2,1)S(1)}, u32[]{:S(2)}, u32[]{:S(2)}) collective-permute-start(bf16[2,32,1536]{2,1,0:T(8,128)(2,1)S(1)} %get-tuple-element.39), channel_id=1, source_target_pairs={{0,8},{1,9},{2,10},{3,11},{4,12},{5,13},{6,14},{7,15},{8,0},{9,1},... | collective-permute-start | bytes 589832 | tf_op jit(solution)/shard_map/ppermute | solution.py:235
  21.3 1.4 %collective-permute-start.2 = (bf16[2,32,1536]{2,1,0:T(8,128)(2,1)S(1)}, bf16[2,32,1536]{2,1,0:T(8,128)(2,1)S(1)}, u32[]{:S(2)}, u32[]{:S(2)}) collective-permute-start(bf16[2,32,1536]{2,1,0:T(8,128)(2,1)S(1)} %get-tuple-element.40), channel_id=1, source_target_pairs={{0,12},{1,13},{2,14},{3,15},{4,8},{5,9},{6,10},{7,11},{8,4},{9,5},... | collective-permute-start | bytes 589832 | tf_op jit(solution)/shard_map/ppermute | solution.py:235
  24.2 1.9 %collective-permute-done.8.refs_6_ = bf16[6,48,768]{2,1,0:T(8,128)(2,1)S(1)} collective-permute-done((bf16[6,48,768]{2,1,0:T(8,128)(2,1)S(1)}, bf16[6,48,768]{2,1,0:T(8,128)(2,1)S(1)}, u32[]{:S(2)}, u32[]{:S(2)}) %collective-permute-start.8) | collective-permute-done | bytes 442400 | tf_op jit(solution)/shard_map/ppermute | solution.py:235
  26.0 1.0 %pad_maximum_fusion.small = f32[34,1536]{1,0:T(8,128)S(1)} fusion(f32[1,1536]{1,0:T(1,128)S(1)} %broadcast_in_dim.38, f32[1,1536]{1,0:T(1,128)S(1)} %broadcast_in_dim.37, f32[1,1536]{1,0:T(1,128)S(1)} %broadcast_in_dim.36, f32[31,1536]{1,0:T(8,128)} %param.14), kind=kLoop, calls=%fused_computation.1 | loop fusion | flops 156672 | bytes 417792 | tf_op jit(solution)/shard_map/concatenate | solution.py:245
  27.0 1.8 %shard_map.109 = (s32[2]{0:T(128)S(1)}, s32[2]{0:T(128)S(1)}, f32[33,384]{1,0:T(8,128)S(1)}, f32[1,1536]{1,0:T(1,128)S(1)}) custom-call(s32[1]{0:T(128)} %bitcast.place, s32[144]{0:T(256)S(1)} %reshape.34.packed, f32[34,1536]{1,0:T(8,128)S(1)} %pad_maximum_fusion.small), custom_call_target="tpu_custom_call" | custom-call | bytes 266324 | tf_op jit(solution)/shard_map/pallas_call | solution.py:21
  28.8 4.8 %collective-permute-done.1.refs_2_ = bf16[2,32,1536]{2,1,0:T(8,128)(2,1)S(1)} collective-permute-done((bf16[2,32,1536]{2,1,0:T(8,128)(2,1)S(1)}, bf16[2,32,1536]{2,1,0:T(8,128)(2,1)S(1)}, u32[]{:S(2)}, u32[]{:S(2)}) %collective-permute-start.1) | collective-permute-done | bytes 196640 | tf_op jit(solution)/shard_map/ppermute | solution.py:235
  33.6 2.1 %collective-permute-done.2.refs_3_ = bf16[2,32,1536]{2,1,0:T(8,128)(2,1)S(1)} collective-permute-done((bf16[2,32,1536]{2,1,0:T(8,128)(2,1)S(1)}, bf16[2,32,1536]{2,1,0:T(8,128)(2,1)S(1)}, u32[]{:S(2)}, u32[]{:S(2)}) %collective-permute-start.2) | collective-permute-done | bytes 196640 | tf_op jit(solution)/shard_map/ppermute | solution.py:235
  35.7 0.7 shard_map.111
  36.5 4.2 %collective-permute-start.3 = (bf16[2,32,1536]{2,1,0:T(8,128)(2,1)S(1)}, bf16[2,32,1536]{2,1,0:T(8,128)(2,1)S(1)}, u32[]{:S(2)}, u32[]{:S(2)}) collective-permute-start(bf16[2,32,1536]{2,1,0:T(8,128)(2,1)S(1)} %get-tuple-element.42), channel_id=1, source_target_pairs={{0,16},{1,17},{2,18},{3,19},{4,20},{5,21},{6,22},{7,23},{8,24},{9,... | collective-permute-start | bytes 589832 | tf_op jit(solution)/shard_map/ppermute | solution.py:235
  41.3 6.1 %collective-permute-done.3.refs_1_ = bf16[2,32,1536]{2,1,0:T(8,128)(2,1)S(1)} collective-permute-done((bf16[2,32,1536]{2,1,0:T(8,128)(2,1)S(1)}, bf16[2,32,1536]{2,1,0:T(8,128)(2,1)S(1)}, u32[]{:S(2)}, u32[]{:S(2)}) %collective-permute-start.3) | collective-permute-done | bytes 196640 | tf_op jit(solution)/shard_map/ppermute | solution.py:235
  47.4 1.0 %shard_map.113 = (bf16[2,32,1536]{2,1,0:T(8,128)(2,1)S(1)}, bf16[2,32,1536]{2,1,0:T(8,128)(2,1)S(1)}) custom-call(s32[1]{0:T(128)} %bitcast.place, s32[2]{0:T(128)S(1)} %get-tuple-element.34.sources, s32[2]{0:T(128)S(1)} %get-tuple-element.33.lens, f32[1,1536]{1,0:T(1,128)S(1)} %get-tuple-element.35.gain, ...), custom_call_target="tpu_custom_call" | custom-call | bytes 792596 | tf_op jit(solution)/shard_map/pallas_call | solution.py:21
  48.6 1.9 %collective-permute-start.11 = (bf16[2,32,1536]{2,1,0:T(8,128)(2,1)S(1)}, bf16[2,32,1536]{2,1,0:T(8,128)(2,1)S(1)}, u32[]{:S(2)}, u32[]{:S(2)}) collective-permute-start(bf16[2,32,1536]{2,1,0:T(8,128)(2,1)S(1)} %get-tuple-element.54.refs_0_), channel_id=1, source_target_pairs={{0,8},{1,9},{2,10},{3,11},{4,12},{5,13},{6,14},{7,15},{8,0},{9,1},... | collective-permute-start | bytes 589832 | tf_op jit(solution)/shard_map/ppermute | solution.py:235
  50.5 1.5 %collective-permute-start.10 = (bf16[2,32,1536]{2,1,0:T(8,128)(2,1)S(1)}, bf16[2,32,1536]{2,1,0:T(8,128)(2,1)S(1)}, u32[]{:S(2)}, u32[]{:S(2)}) collective-permute-start(bf16[2,32,1536]{2,1,0:T(8,128)(2,1)S(1)} %get-tuple-element.54.refs_0_), channel_id=1, source_target_pairs={{0,4},{1,5},{2,6},{3,7},{4,0},{5,1},{6,2},{7,3},{8,12},{9,13},{10,... | collective-permute-start | bytes 589832 | tf_op jit(solution)/shard_map/ppermute | solution.py:235
  52.0 5.2 %collective-permute-done.12.refs_3_ = bf16[2,32,1536]{2,1,0:T(8,128)(2,1)S(1)} collective-permute-done((bf16[2,32,1536]{2,1,0:T(8,128)(2,1)S(1)}, bf16[2,32,1536]{2,1,0:T(8,128)(2,1)S(1)}, u32[]{:S(2)}, u32[]{:S(2)}) %collective-permute-start.12) | collective-permute-done | bytes 196640 | tf_op jit(solution)/shard_map/ppermute | solution.py:235
  57.3 1.2 %collective-permute-done.11.refs_2_ = bf16[2,32,1536]{2,1,0:T(8,128)(2,1)S(1)} collective-permute-done((bf16[2,32,1536]{2,1,0:T(8,128)(2,1)S(1)}, bf16[2,32,1536]{2,1,0:T(8,128)(2,1)S(1)}, u32[]{:S(2)}, u32[]{:S(2)}) %collective-permute-start.11) | collective-permute-done | bytes 196640 | tf_op jit(solution)/shard_map/ppermute | solution.py:235
  58.5 0.9 %collective-permute-done.10.refs_1_ = bf16[2,32,1536]{2,1,0:T(8,128)(2,1)S(1)} collective-permute-done((bf16[2,32,1536]{2,1,0:T(8,128)(2,1)S(1)}, bf16[2,32,1536]{2,1,0:T(8,128)(2,1)S(1)}, u32[]{:S(2)}, u32[]{:S(2)}) %collective-permute-start.10) | collective-permute-done | bytes 196640 | tf_op jit(solution)/shard_map/ppermute | solution.py:235
  59.6 1.6 %collective-permute-done.16.refs_11_ = bf16[6,48,768]{2,1,0:T(8,128)(2,1)S(1)} collective-permute-done((bf16[6,48,768]{2,1,0:T(8,128)(2,1)S(1)}, bf16[6,48,768]{2,1,0:T(8,128)(2,1)S(1)}, u32[]{:S(2)}, u32[]{:S(2)}) %collective-permute-start.16) | collective-permute-done | bytes 442400 | tf_op jit(solution)/shard_map/ppermute | solution.py:235
  61.2 3.7 %shard_map.114 = (f32[2,32,1536]{2,1,0:T(8,128)S(1)}, bf16[2,32,1536]{2,1,0:T(8,128)(2,1)S(1)}, bf16[2,32,1536]{2,1,0:T(8,128)(2,1)S(1)}, bf16[2,32,1536]{2,1,0:T(8,128)(2,1)S(1)}) custom-call(s32[8,5]{1,0:T(8,128)S(1)} %pad_add_fusion.1.where, bf16[2,32,1536]{2,1,0:T(8,128)(2,1)S(1)} %get-tuple-element.52.kept, f32[33,384]{1,0:T(8,128)S(1)} %get-tuple-element.53.table, ...), custom_call_target="tpu_custom_call" | custom-call | flops 905969664 | bytes 10471072 | tf_op jit(solution)/shard_map/pallas_call | solution.py:21
  66.1 2.4 %collective-permute-start.19 = (bf16[2,32,1536]{2,1,0:T(8,128)(2,1)S(1)}, bf16[2,32,1536]{2,1,0:T(8,128)(2,1)S(1)}, u32[]{:S(2)}, u32[]{:S(2)}) collective-permute-start(bf16[2,32,1536]{2,1,0:T(8,128)(2,1)S(1)} %get-tuple-element.60), channel_id=1, source_target_pairs={{0,12},{1,13},{2,14},{3,15},{4,8},{5,9},{6,10},{7,11},{8,4},{9,5},... | collective-permute-start | bytes 589832 | tf_op jit(solution)/shard_map/ppermute | solution.py:235
  68.5 3.4 %collective-permute-done.17 = bf16[2,32,1536]{2,1,0:T(8,128)(2,1)S(1)} collective-permute-done((bf16[2,32,1536]{2,1,0:T(8,128)(2,1)S(1)}, bf16[2,32,1536]{2,1,0:T(8,128)(2,1)S(1)}, u32[]{:S(2)}, u32[]{:S(2)}) %collective-permute-start.17) | collective-permute-done | bytes 196640 | tf_op jit(solution)/shard_map/ppermute | solution.py:235
  71.9 1.4 %collective-permute-done.18 = bf16[2,32,1536]{2,1,0:T(8,128)(2,1)S(1)} collective-permute-done((bf16[2,32,1536]{2,1,0:T(8,128)(2,1)S(1)}, bf16[2,32,1536]{2,1,0:T(8,128)(2,1)S(1)}, u32[]{:S(2)}, u32[]{:S(2)}) %collective-permute-start.18) | collective-permute-done | bytes 196640 | tf_op jit(solution)/shard_map/ppermute | solution.py:235
  73.3 4.0 %collective-permute-done.19 = bf16[2,32,1536]{2,1,0:T(8,128)(2,1)S(1)} collective-permute-done((bf16[2,32,1536]{2,1,0:T(8,128)(2,1)S(1)}, bf16[2,32,1536]{2,1,0:T(8,128)(2,1)S(1)}, u32[]{:S(2)}, u32[]{:S(2)}) %collective-permute-start.19) | collective-permute-done | bytes 196640 | tf_op jit(solution)/shard_map/ppermute | solution.py:235
  77.3 0.8 %fusion = bf16[1,2,32,1536]{3,2,1,0:T(8,128)(2,1)} fusion(bf16[2,32,1536]{2,1,0:T(8,128)(2,1)S(1)} %collective-permute-done.19, bf16[2,32,1536]{2,1,0:T(8,128)(2,1)S(1)} %collective-permute-done.18, f32[2,32,1536]{2,1,0:T(8,128)S(1)} %get-tuple-element.57, bf16[2,32,1536]{2,1,0:T(8,128)(2,1)S(1)} %collective-permute-done.17, ...), kind=kLoop, calls=%fused_computation.2 | loop fusion | flops 786432 | bytes 1179712 | tf_op jit(solution)/shard_map/broadcast_in_dim | solution.py:354
  (53 shorter events, 5.7 us)
Async XLA Ops:
  0.0 0.7 copy-start.7
  0.0 0.7 copy-start.6
  1.6 1.1 %copy-start = (bf16[1,6,32,1536]{3,2,1,0:T(8,128)(2,1)S(1)}, bf16[1,6,32,1536]{3,2,1,0:T(8,128)(2,1)}, u32[]{:S(2)}) copy-start(bf16[1,6,32,1536]{3,2,1,0:T(8,128)(2,1)} %param.11) | copy-start | bytes 1769476
  2.7 3.7 %copy-start.1 = (bf16[48,3072]{1,0:T(8,128)(2,1)S(1)}, bf16[48,3072]{1,0:T(8,128)(2,1)}, u32[]{:S(2)}) copy-start(bf16[48,3072]{1,0:T(8,128)(2,1)} %weights.1) | copy-start | bytes 884740
  3.3 11.1 %collective-permute-start = (bf16[2,32,1536]{2,1,0:T(8,128)(2,1)S(1)}, bf16[2,32,1536]{2,1,0:T(8,128)(2,1)S(1)}, u32[]{:S(2)}, u32[]{:S(2)}) collective-permute-start(bf16[2,32,1536]{2,1,0:T(8,128)(2,1)S(1)} %get-tuple-element.38), channel_id=1, source_target_pairs={{0,4},{1,5},{2,6},{3,7},{4,0},{5,1},{6,2},{7,3},{8,12},{9,13},{10,... | collective-permute-start | bytes 589832 | tf_op jit(solution)/shard_map/ppermute | solution.py:235
  6.5 7.9 %collective-permute-start.4 = (bf16[48,768]{1,0:T(8,128)(2,1)S(1)}, bf16[48,768]{1,0:T(8,128)(2,1)S(1)}, u32[]{:S(2)}, u32[]{:S(2)}) collective-permute-start(bf16[48,768]{1,0:T(8,128)(2,1)S(1)} %get-tuple-element.44), channel_id=1, source_target_pairs={{0,4},{1,5},{2,6},{3,7},{4,0},{5,1},{6,2},{7,3},{8,12},{9,13},{10,... | collective-permute-start | bytes 221192 | tf_op jit(solution)/shard_map/ppermute | solution.py:235
  6.8 7.6 %collective-permute-start.5 = (bf16[48,768]{1,0:T(8,128)(2,1)S(1)}, bf16[48,768]{1,0:T(8,128)(2,1)S(1)}, u32[]{:S(2)}, u32[]{:S(2)}) collective-permute-start(bf16[48,768]{1,0:T(8,128)(2,1)S(1)} %get-tuple-element.45), channel_id=1, source_target_pairs={{0,8},{1,9},{2,10},{3,11},{4,12},{5,13},{6,14},{7,15},{8,0},{9,1},... | collective-permute-start | bytes 221192 | tf_op jit(solution)/shard_map/ppermute | solution.py:235
  8.7 5.8 %collective-permute-start.6 = (bf16[48,768]{1,0:T(8,128)(2,1)S(1)}, bf16[48,768]{1,0:T(8,128)(2,1)S(1)}, u32[]{:S(2)}, u32[]{:S(2)}) collective-permute-start(bf16[48,768]{1,0:T(8,128)(2,1)S(1)} %get-tuple-element.46), channel_id=1, source_target_pairs={{0,12},{1,13},{2,14},{3,15},{4,8},{5,9},{6,10},{7,11},{8,4},{9,5},... | collective-permute-start | bytes 221192 | tf_op jit(solution)/shard_map/ppermute | solution.py:235
  14.4 0.9 %copy-start.2 = (bf16[48,1536]{1,0:T(8,128)(2,1)S(1)}, bf16[48,1536]{1,0:T(8,128)(2,1)}, u32[]{:S(2)}) copy-start(bf16[48,1536]{1,0:T(8,128)(2,1)} %param.17) | copy-start | bytes 442372
  15.4 10.6 %collective-permute-start.8 = (bf16[6,48,768]{2,1,0:T(8,128)(2,1)S(1)}, bf16[6,48,768]{2,1,0:T(8,128)(2,1)S(1)}, u32[]{:S(2)}, u32[]{:S(2)}) collective-permute-start(bf16[6,48,768]{2,1,0:T(8,128)(2,1)S(1)} %bitcast_dynamic-update-slice_fusion.refs_4_), channel_id=1, source_target_pairs={{0,2},{1,3},{2,0},{3,1},{4,6},{5,7},{6,4},{7,5},{8,10},{9,11},{10,... | collective-permute-start | bytes 1327112 | tf_op jit(solution)/shard_map/ppermute | solution.py:235
  17.2 23.5 %collective-permute-start.13 = (bf16[6,48,768]{2,1,0:T(8,128)(2,1)S(1)}, bf16[6,48,768]{2,1,0:T(8,128)(2,1)S(1)}, u32[]{:S(2)}, u32[]{:S(2)}) collective-permute-start(bf16[6,48,768]{2,1,0:T(8,128)(2,1)S(1)} %bitcast_dynamic-update-slice_fusion.refs_4_), channel_id=1, source_target_pairs={{0,16},{1,17},{2,18},{3,19},{4,20},{5,21},{6,22},{7,23},{8,24},{9,... | collective-permute-start | bytes 1327112 | tf_op jit(solution)/shard_map/ppermute | solution.py:235
  19.7 13.8 %collective-permute-start.1 = (bf16[2,32,1536]{2,1,0:T(8,128)(2,1)S(1)}, bf16[2,32,1536]{2,1,0:T(8,128)(2,1)S(1)}, u32[]{:S(2)}, u32[]{:S(2)}) collective-permute-start(bf16[2,32,1536]{2,1,0:T(8,128)(2,1)S(1)} %get-tuple-element.39), channel_id=1, source_target_pairs={{0,8},{1,9},{2,10},{3,11},{4,12},{5,13},{6,14},{7,15},{8,0},{9,1},... | collective-permute-start | bytes 589832 | tf_op jit(solution)/shard_map/ppermute | solution.py:235
  21.3 14.4 %collective-permute-start.2 = (bf16[2,32,1536]{2,1,0:T(8,128)(2,1)S(1)}, bf16[2,32,1536]{2,1,0:T(8,128)(2,1)S(1)}, u32[]{:S(2)}, u32[]{:S(2)}) collective-permute-start(bf16[2,32,1536]{2,1,0:T(8,128)(2,1)S(1)} %get-tuple-element.40), channel_id=1, source_target_pairs={{0,12},{1,13},{2,14},{3,15},{4,8},{5,9},{6,10},{7,11},{8,4},{9,5},... | collective-permute-start | bytes 589832 | tf_op jit(solution)/shard_map/ppermute | solution.py:235
  22.7 0.7 copy-start.3
  22.7 0.7 copy-start.4
  23.4 0.7 copy-start.5
  24.1 23.3 %collective-permute-start.7 = (bf16[6,48,768]{2,1,0:T(8,128)(2,1)S(1)}, bf16[6,48,768]{2,1,0:T(8,128)(2,1)S(1)}, u32[]{:S(2)}, u32[]{:S(2)}) collective-permute-start(bf16[6,48,768]{2,1,0:T(8,128)(2,1)S(1)} %bitcast_dynamic-update-slice_fusion.refs_4_), channel_id=1, source_target_pairs={{0,1},{1,0},{2,3},{3,2},{4,5},{5,4},{6,7},{7,6},{8,9},{9,8},{10,11... | collective-permute-start | bytes 1327112 | tf_op jit(solution)/shard_map/ppermute | solution.py:235
  26.0 21.4 %collective-permute-start.9 = (bf16[6,48,768]{2,1,0:T(8,128)(2,1)S(1)}, bf16[6,48,768]{2,1,0:T(8,128)(2,1)S(1)}, u32[]{:S(2)}, u32[]{:S(2)}) collective-permute-start(bf16[6,48,768]{2,1,0:T(8,128)(2,1)S(1)} %collective-permute-done.8.refs_6_), channel_id=1, source_target_pairs={{0,1},{1,0},{2,3},{3,2},{4,5},{5,4},{6,7},{7,6},{8,9},{9,8},{10,11... | collective-permute-start | bytes 1327112 | tf_op jit(solution)/shard_map/ppermute | solution.py:235
  36.5 4.8 %copy-start.8 = (s32[8]{0:T(128)S(1)}, s32[8]{0:T(128)}, u32[]{:S(2)}) copy-start(s32[8]{0:T(128)} %constant.58.clone) | copy-start | bytes 100
  36.5 11.0 %collective-permute-start.3 = (bf16[2,32,1536]{2,1,0:T(8,128)(2,1)S(1)}, bf16[2,32,1536]{2,1,0:T(8,128)(2,1)S(1)}, u32[]{:S(2)}, u32[]{:S(2)}) collective-permute-start(bf16[2,32,1536]{2,1,0:T(8,128)(2,1)S(1)} %get-tuple-element.42), channel_id=1, source_target_pairs={{0,16},{1,17},{2,18},{3,19},{4,20},{5,21},{6,22},{7,23},{8,24},{9,... | collective-permute-start | bytes 589832 | tf_op jit(solution)/shard_map/ppermute | solution.py:235
  40.7 11.4 %collective-permute-start.14 = (bf16[6,48,768]{2,1,0:T(8,128)(2,1)S(1)}, bf16[6,48,768]{2,1,0:T(8,128)(2,1)S(1)}, u32[]{:S(2)}, u32[]{:S(2)}) collective-permute-start(bf16[6,48,768]{2,1,0:T(8,128)(2,1)S(1)} %collective-permute-done.13.refs_5_), channel_id=1, source_target_pairs={{0,2},{1,3},{2,0},{3,1},{4,6},{5,7},{6,4},{7,5},{8,10},{9,11},{10,... | collective-permute-start | bytes 1327112 | tf_op jit(solution)/shard_map/ppermute | solution.py:235
  48.5 8.8 %collective-permute-start.12 = (bf16[2,32,1536]{2,1,0:T(8,128)(2,1)S(1)}, bf16[2,32,1536]{2,1,0:T(8,128)(2,1)S(1)}, u32[]{:S(2)}, u32[]{:S(2)}) collective-permute-start(bf16[2,32,1536]{2,1,0:T(8,128)(2,1)S(1)} %get-tuple-element.54.refs_0_), channel_id=1, source_target_pairs={{0,12},{1,13},{2,14},{3,15},{4,8},{5,9},{6,10},{7,11},{8,4},{9,5},... | collective-permute-start | bytes 589832 | tf_op jit(solution)/shard_map/ppermute | solution.py:235
  48.6 9.8 %collective-permute-start.11 = (bf16[2,32,1536]{2,1,0:T(8,128)(2,1)S(1)}, bf16[2,32,1536]{2,1,0:T(8,128)(2,1)S(1)}, u32[]{:S(2)}, u32[]{:S(2)}) collective-permute-start(bf16[2,32,1536]{2,1,0:T(8,128)(2,1)S(1)} %get-tuple-element.54.refs_0_), channel_id=1, source_target_pairs={{0,8},{1,9},{2,10},{3,11},{4,12},{5,13},{6,14},{7,15},{8,0},{9,1},... | collective-permute-start | bytes 589832 | tf_op jit(solution)/shard_map/ppermute | solution.py:235
  50.5 8.9 %collective-permute-start.10 = (bf16[2,32,1536]{2,1,0:T(8,128)(2,1)S(1)}, bf16[2,32,1536]{2,1,0:T(8,128)(2,1)S(1)}, u32[]{:S(2)}, u32[]{:S(2)}) collective-permute-start(bf16[2,32,1536]{2,1,0:T(8,128)(2,1)S(1)} %get-tuple-element.54.refs_0_), channel_id=1, source_target_pairs={{0,4},{1,5},{2,6},{3,7},{4,0},{5,1},{6,2},{7,3},{8,12},{9,13},{10,... | collective-permute-start | bytes 589832 | tf_op jit(solution)/shard_map/ppermute | solution.py:235
  52.0 7.5 %collective-permute-start.15 = (bf16[6,48,768]{2,1,0:T(8,128)(2,1)S(1)}, bf16[6,48,768]{2,1,0:T(8,128)(2,1)S(1)}, u32[]{:S(2)}, u32[]{:S(2)}) collective-permute-start(bf16[6,48,768]{2,1,0:T(8,128)(2,1)S(1)} %collective-permute-done.13.refs_5_), channel_id=1, source_target_pairs={{0,1},{1,0},{2,3},{3,2},{4,5},{5,4},{6,7},{7,6},{8,9},{9,8},{10,11... | collective-permute-start | bytes 1327112 | tf_op jit(solution)/shard_map/ppermute | solution.py:235
  59.4 1.8 %collective-permute-start.16 = (bf16[6,48,768]{2,1,0:T(8,128)(2,1)S(1)}, bf16[6,48,768]{2,1,0:T(8,128)(2,1)S(1)}, u32[]{:S(2)}, u32[]{:S(2)}) collective-permute-start(bf16[6,48,768]{2,1,0:T(8,128)(2,1)S(1)} %collective-permute-done.14.refs_7_), channel_id=1, source_target_pairs={{0,1},{1,0},{2,3},{3,2},{4,5},{5,4},{6,7},{7,6},{8,9},{9,8},{10,11... | collective-permute-start | bytes 1327112 | tf_op jit(solution)/shard_map/ppermute | solution.py:235
  64.9 7.0 %collective-permute-start.17 = (bf16[2,32,1536]{2,1,0:T(8,128)(2,1)S(1)}, bf16[2,32,1536]{2,1,0:T(8,128)(2,1)S(1)}, u32[]{:S(2)}, u32[]{:S(2)}) collective-permute-start(bf16[2,32,1536]{2,1,0:T(8,128)(2,1)S(1)} %get-tuple-element.58), channel_id=1, source_target_pairs={{0,4},{1,5},{2,6},{3,7},{4,0},{5,1},{6,2},{7,3},{8,12},{9,13},{10,... | collective-permute-start | bytes 589832 | tf_op jit(solution)/shard_map/ppermute | solution.py:235
  65.5 7.8 %collective-permute-start.18 = (bf16[2,32,1536]{2,1,0:T(8,128)(2,1)S(1)}, bf16[2,32,1536]{2,1,0:T(8,128)(2,1)S(1)}, u32[]{:S(2)}, u32[]{:S(2)}) collective-permute-start(bf16[2,32,1536]{2,1,0:T(8,128)(2,1)S(1)} %get-tuple-element.59), channel_id=1, source_target_pairs={{0,8},{1,9},{2,10},{3,11},{4,12},{5,13},{6,14},{7,15},{8,0},{9,1},... | collective-permute-start | bytes 589832 | tf_op jit(solution)/shard_map/ppermute | solution.py:235
  66.1 11.2 %collective-permute-start.19 = (bf16[2,32,1536]{2,1,0:T(8,128)(2,1)S(1)}, bf16[2,32,1536]{2,1,0:T(8,128)(2,1)S(1)}, u32[]{:S(2)}, u32[]{:S(2)}) collective-permute-start(bf16[2,32,1536]{2,1,0:T(8,128)(2,1)S(1)} %get-tuple-element.60), channel_id=1, source_target_pairs={{0,12},{1,13},{2,14},{3,15},{4,8},{5,9},{6,10},{7,11},{8,4},{9,5},... | collective-permute-start | bytes 589832 | tf_op jit(solution)/shard_map/ppermute | solution.py:235

commit v13 on v12

--- a/solution.py
+++ b/solution.py
@@ -294,11 +294,12 @@
     halves = [w_out[:, at : at + wide] for at in range(0, width, wide)]
     pieces = [jnp.stack(columns + halves)]
     shifts = [mask * fsdp_count for mask in range(highs)]
-    chip_first = [swap(pieces[0], fsdp=bit) for bit in chip_bits[:1]]
+    waiting = gated(pieces[0], merged)
+    chip_first = [swap(waiting, fsdp=bit) for bit in chip_bits[:1]]
     crossing = [swap(pieces[0], high=mask) for mask in range(1, highs)]
     pieces += gated(crossing, (merged, chip_first))
     early = [swap(part, fsdp=1) for part in pieces[:1] + chip_first]
-    far = gated(far, early)
+    far = gated(far, early[:1])
     kept, normed = call(
         norm_kernel,
         [utts, utts],

time: 78.5 us -> 81.7 us (1.041)
  waiting for transfers between devices: 37.1 us -> 47.8 us
  starting transfers between devices: 25.8 us -> 20.4 us
  other arithmetic: 2.69 us -> 1.08 us
    ppermute x20, waiting for transfers between devices: 37.1 us -> 47.8 us  [swap(): lax.ppermute(array, ('dp', 'fsdp'), [(at, at ^ mask) for at in range(devi...]
    ppermute x20, starting transfers between devices: 25.8 us -> 20.4 us  [swap(): lax.ppermute(array, ('dp', 'fsdp'), [(at, at ^ mask) for at in range(devi...]
    concatenate x1, other arithmetic: 0.96 us -> 0.04 us  [shards(): jnp.concatenate([depth_kernel, bn_scale[None], bn_shift[None], ln_gain[No...]
    unnamed x23 -> x27, local copies, waits for them, and re-layouts: 4.06 us -> 3.64 us
  transfers between devices with their start and end apart: 20 -> 20, of which waited for: 12 -> 13; matrix products, arithmetic and copies ran while one was open for 2% -> 1% of each run, Pallas kernels for 5% -> 4%
where the time goes in v13:
time: 81.7 us; the launch traced here: 81.4 us
  waiting for transfers between devices  47.8 us (59%)
  starting transfers between devices  20.4 us (25%)
  Pallas kernels  7.99 us (10%)
  local copies, waits for them, and re-layouts  3.93 us (5%)
  other arithmetic  1.08 us (1%)
    ppermute x20, waiting for transfers between devices, swap(): lax.ppermute(array, ('dp', 'fsdp'), [(at, at ^ mask) for at in range(devi...  47.8 us
    ppermute x20, starting transfers between devices, swap(): lax.ppermute(array, ('dp', 'fsdp'), [(at, at ^ mask) for at in range(devi...  20.4 us
    pallas_call x6, Pallas kernels, call(): pl.pallas_call(kernel, out_shape=out_shape, in_specs=in_specs, out_specs=...  7.99 us
    unnamed x27, local copies, waits for them, and re-layouts  3.64 us
  transfers between devices with their start and end apart: 20, of which 13 were waited for; matrix products, arithmetic and copies ran while one was open for 1% of the time, Pallas kernels for 4%

profile of v13, /device:TPU:0, one launch (start us, length us, event | category | flops | bytes accessed | tf_op | source)
XLA Modules:
  0.0 81.4 jit_solution(3717129602016357482)
XLA Ops:
  0.0 1.0 %copy-done.1 = bf16[48,3072]{1,0:T(8,128)(2,1)S(1)} copy-done((bf16[48,3072]{1,0:T(8,128)(2,1)S(1)}, bf16[48,3072]{1,0:T(8,128)(2,1)}, u32[]{:S(2)}) %copy-start.1) | copy-done | bytes 294936
  1.1 3.0 %collective-permute-start.4 = (bf16[48,768]{1,0:T(8,128)(2,1)S(1)}, bf16[48,768]{1,0:T(8,128)(2,1)S(1)}, u32[]{:S(2)}, u32[]{:S(2)}) collective-permute-start(bf16[48,768]{1,0:T(8,128)(2,1)S(1)} %get-tuple-element.45), channel_id=1, source_target_pairs={{0,4},{1,5},{2,6},{3,7},{4,0},{5,1},{6,2},{7,3},{8,12},{9,13},{10,... | collective-permute-start | bytes 221192 | tf_op jit(solution)/shard_map/ppermute | solution.py:235
  4.2 1.6 %collective-permute-start.5 = (bf16[48,768]{1,0:T(8,128)(2,1)S(1)}, bf16[48,768]{1,0:T(8,128)(2,1)S(1)}, u32[]{:S(2)}, u32[]{:S(2)}) collective-permute-start(bf16[48,768]{1,0:T(8,128)(2,1)S(1)} %get-tuple-element.46), channel_id=1, source_target_pairs={{0,8},{1,9},{2,10},{3,11},{4,12},{5,13},{6,14},{7,15},{8,0},{9,1},... | collective-permute-start | bytes 221192 | tf_op jit(solution)/shard_map/ppermute | solution.py:235
  6.0 1.1 %copy-done = bf16[1,6,32,1536]{3,2,1,0:T(8,128)(2,1)S(1)} copy-done((bf16[1,6,32,1536]{3,2,1,0:T(8,128)(2,1)S(1)}, bf16[1,6,32,1536]{3,2,1,0:T(8,128)(2,1)}, u32[]{:S(2)}) %copy-start) | copy-done | bytes 589848
  7.7 2.0 %collective-permute-start = (bf16[2,32,1536]{2,1,0:T(8,128)(2,1)S(1)}, bf16[2,32,1536]{2,1,0:T(8,128)(2,1)S(1)}, u32[]{:S(2)}, u32[]{:S(2)}) collective-permute-start(bf16[2,32,1536]{2,1,0:T(8,128)(2,1)S(1)} %get-tuple-element.39), channel_id=1, source_target_pairs={{0,4},{1,5},{2,6},{3,7},{4,0},{5,1},{6,2},{7,3},{8,12},{9,13},{10,... | collective-permute-start | bytes 589832 | tf_op jit(solution)/shard_map/ppermute | solution.py:235
  9.7 1.6 %collective-permute-start.1 = (bf16[2,32,1536]{2,1,0:T(8,128)(2,1)S(1)}, bf16[2,32,1536]{2,1,0:T(8,128)(2,1)S(1)}, u32[]{:S(2)}, u32[]{:S(2)}) collective-permute-start(bf16[2,32,1536]{2,1,0:T(8,128)(2,1)S(1)} %get-tuple-element.40), channel_id=1, source_target_pairs={{0,8},{1,9},{2,10},{3,11},{4,12},{5,13},{6,14},{7,15},{8,0},{9,1},... | collective-permute-start | bytes 589832 | tf_op jit(solution)/shard_map/ppermute | solution.py:235
  11.3 0.7 copy-done.6
  12.0 1.8 %shard_map.109 = (s32[2]{0:T(128)S(1)}, s32[2]{0:T(128)S(1)}, f32[33,384]{1,0:T(8,128)S(1)}, f32[1,1536]{1,0:T(1,128)S(1)}) custom-call(s32[1]{0:T(128)} %bitcast.place, s32[144]{0:T(256)S(1)} %reshape.34.packed, f32[34,1536]{1,0:T(8,128)S(1)} %pad_maximum_fusion.small), custom_call_target="tpu_custom_call" | custom-call | bytes 266324 | tf_op jit(solution)/shard_map/pallas_call | solution.py:21
  14.0 0.7 collective-permute-done.refs_1_
  14.7 0.9 %copy-done.3 = bf16[48,1536]{1,0:T(8,128)(2,1)S(1)} copy-done((bf16[48,1536]{1,0:T(8,128)(2,1)S(1)}, bf16[48,1536]{1,0:T(8,128)(2,1)}, u32[]{:S(2)}) %copy-start.3) | copy-done | bytes 147480
  15.9 4.6 %collective-permute-done.2.refs_3_ = bf16[2,32,1536]{2,1,0:T(8,128)(2,1)S(1)} collective-permute-done((bf16[2,32,1536]{2,1,0:T(8,128)(2,1)S(1)}, bf16[2,32,1536]{2,1,0:T(8,128)(2,1)S(1)}, u32[]{:S(2)}, u32[]{:S(2)}) %collective-permute-start.2) | collective-permute-done | bytes 196640 | tf_op jit(solution)/shard_map/ppermute | solution.py:235
  20.5 0.8 shard_map.111
  21.2 1.6 %collective-permute-start.12 = (bf16[6,48,768]{2,1,0:T(8,128)(2,1)S(1)}, bf16[6,48,768]{2,1,0:T(8,128)(2,1)S(1)}, u32[]{:S(2)}, u32[]{:S(2)}) collective-permute-start(bf16[6,48,768]{2,1,0:T(8,128)(2,1)S(1)} %bitcast_dynamic-update-slice_fusion.refs_4_), channel_id=1, source_target_pairs={{0,2},{1,3},{2,0},{3,1},{4,6},{5,7},{6,4},{7,5},{8,10},{9,11},{10,... | collective-permute-start | bytes 1327112 | tf_op jit(solution)/shard_map/ppermute | solution.py:235
  22.8 2.6 %collective-permute-start.11 = (bf16[6,48,768]{2,1,0:T(8,128)(2,1)S(1)}, bf16[6,48,768]{2,1,0:T(8,128)(2,1)S(1)}, u32[]{:S(2)}, u32[]{:S(2)}) collective-permute-start(bf16[6,48,768]{2,1,0:T(8,128)(2,1)S(1)} %bitcast_dynamic-update-slice_fusion.refs_4_), channel_id=1, source_target_pairs={{0,16},{1,17},{2,18},{3,19},{4,20},{5,21},{6,22},{7,23},{8,24},{9,... | collective-permute-start | bytes 1327112 | tf_op jit(solution)/shard_map/ppermute | solution.py:235
  25.7 4.9 %collective-permute-done.12.refs_6_ = bf16[6,48,768]{2,1,0:T(8,128)(2,1)S(1)} collective-permute-done((bf16[6,48,768]{2,1,0:T(8,128)(2,1)S(1)}, bf16[6,48,768]{2,1,0:T(8,128)(2,1)S(1)}, u32[]{:S(2)}, u32[]{:S(2)}) %collective-permute-start.12) | collective-permute-done | bytes 442400 | tf_op jit(solution)/shard_map/ppermute | solution.py:235
  30.7 16.8 %collective-permute-done.11.refs_5_ = bf16[6,48,768]{2,1,0:T(8,128)(2,1)S(1)} collective-permute-done((bf16[6,48,768]{2,1,0:T(8,128)(2,1)S(1)}, bf16[6,48,768]{2,1,0:T(8,128)(2,1)S(1)}, u32[]{:S(2)}, u32[]{:S(2)}) %collective-permute-start.11) | collective-permute-done | bytes 442400 | tf_op jit(solution)/shard_map/ppermute | solution.py:235
  48.1 2.5 %collective-permute-done.3.refs_1_ = bf16[2,32,1536]{2,1,0:T(8,128)(2,1)S(1)} collective-permute-done((bf16[2,32,1536]{2,1,0:T(8,128)(2,1)S(1)}, bf16[2,32,1536]{2,1,0:T(8,128)(2,1)S(1)}, u32[]{:S(2)}, u32[]{:S(2)}) %collective-permute-start.3) | collective-permute-done | bytes 196640 | tf_op jit(solution)/shard_map/ppermute | solution.py:235
  50.7 1.0 %shard_map.113 = (bf16[2,32,1536]{2,1,0:T(8,128)(2,1)S(1)}, bf16[2,32,1536]{2,1,0:T(8,128)(2,1)S(1)}) custom-call(s32[1]{0:T(128)} %bitcast.place, s32[2]{0:T(128)S(1)} %get-tuple-element.35.sources, s32[2]{0:T(128)S(1)} %get-tuple-element.34.lens, f32[1,1536]{1,0:T(1,128)S(1)} %get-tuple-element.36.gain, ...), custom_call_target="tpu_custom_call" | custom-call | bytes 792596 | tf_op jit(solution)/shard_map/pallas_call | solution.py:21
  51.7 1.1 %collective-permute-start.10 = (bf16[2,32,1536]{2,1,0:T(8,128)(2,1)S(1)}, bf16[2,32,1536]{2,1,0:T(8,128)(2,1)S(1)}, u32[]{:S(2)}, u32[]{:S(2)}) collective-permute-start(bf16[2,32,1536]{2,1,0:T(8,128)(2,1)S(1)} %get-tuple-element.55.refs_0_), channel_id=1, source_target_pairs={{0,12},{1,13},{2,14},{3,15},{4,8},{5,9},{6,10},{7,11},{8,4},{9,5},... | collective-permute-start | bytes 589832 | tf_op jit(solution)/shard_map/ppermute | solution.py:235
  52.8 1.4 %collective-permute-start.9 = (bf16[2,32,1536]{2,1,0:T(8,128)(2,1)S(1)}, bf16[2,32,1536]{2,1,0:T(8,128)(2,1)S(1)}, u32[]{:S(2)}, u32[]{:S(2)}) collective-permute-start(bf16[2,32,1536]{2,1,0:T(8,128)(2,1)S(1)} %get-tuple-element.55.refs_0_), channel_id=1, source_target_pairs={{0,8},{1,9},{2,10},{3,11},{4,12},{5,13},{6,14},{7,15},{8,0},{9,1},... | collective-permute-start | bytes 589832 | tf_op jit(solution)/shard_map/ppermute | solution.py:235
  54.2 1.1 %collective-permute-start.8 = (bf16[2,32,1536]{2,1,0:T(8,128)(2,1)S(1)}, bf16[2,32,1536]{2,1,0:T(8,128)(2,1)S(1)}, u32[]{:S(2)}, u32[]{:S(2)}) collective-permute-start(bf16[2,32,1536]{2,1,0:T(8,128)(2,1)S(1)} %get-tuple-element.55.refs_0_), channel_id=1, source_target_pairs={{0,4},{1,5},{2,6},{3,7},{4,0},{5,1},{6,2},{7,3},{8,12},{9,13},{10,... | collective-permute-start | bytes 589832 | tf_op jit(solution)/shard_map/ppermute | solution.py:235
  55.3 5.2 %collective-permute-done.10.refs_3_ = bf16[2,32,1536]{2,1,0:T(8,128)(2,1)S(1)} collective-permute-done((bf16[2,32,1536]{2,1,0:T(8,128)(2,1)S(1)}, bf16[2,32,1536]{2,1,0:T(8,128)(2,1)S(1)}, u32[]{:S(2)}, u32[]{:S(2)}) %collective-permute-start.10) | collective-permute-done | bytes 196640 | tf_op jit(solution)/shard_map/ppermute | solution.py:235
  60.5 1.2 %collective-permute-done.9.refs_2_ = bf16[2,32,1536]{2,1,0:T(8,128)(2,1)S(1)} collective-permute-done((bf16[2,32,1536]{2,1,0:T(8,128)(2,1)S(1)}, bf16[2,32,1536]{2,1,0:T(8,128)(2,1)S(1)}, u32[]{:S(2)}, u32[]{:S(2)}) %collective-permute-start.9) | collective-permute-done | bytes 196640 | tf_op jit(solution)/shard_map/ppermute | solution.py:235
  61.7 1.1 %collective-permute-done.8.refs_1_ = bf16[2,32,1536]{2,1,0:T(8,128)(2,1)S(1)} collective-permute-done((bf16[2,32,1536]{2,1,0:T(8,128)(2,1)S(1)}, bf16[2,32,1536]{2,1,0:T(8,128)(2,1)S(1)}, u32[]{:S(2)}, u32[]{:S(2)}) %collective-permute-start.8) | collective-permute-done | bytes 196640 | tf_op jit(solution)/shard_map/ppermute | solution.py:235
  62.9 1.6 %collective-permute-done.16.refs_11_ = bf16[6,48,768]{2,1,0:T(8,128)(2,1)S(1)} collective-permute-done((bf16[6,48,768]{2,1,0:T(8,128)(2,1)S(1)}, bf16[6,48,768]{2,1,0:T(8,128)(2,1)S(1)}, u32[]{:S(2)}, u32[]{:S(2)}) %collective-permute-start.16) | collective-permute-done | bytes 442400 | tf_op jit(solution)/shard_map/ppermute | solution.py:235
  64.6 3.7 %shard_map.114 = (f32[2,32,1536]{2,1,0:T(8,128)S(1)}, bf16[2,32,1536]{2,1,0:T(8,128)(2,1)S(1)}, bf16[2,32,1536]{2,1,0:T(8,128)(2,1)S(1)}, bf16[2,32,1536]{2,1,0:T(8,128)(2,1)S(1)}) custom-call(s32[8,5]{1,0:T(8,128)S(1)} %pad_add_fusion.1.where, bf16[2,32,1536]{2,1,0:T(8,128)(2,1)S(1)} %get-tuple-element.53.kept, f32[33,384]{1,0:T(8,128)S(1)} %get-tuple-element.54.table, ...), custom_call_target="tpu_custom_call" | custom-call | flops 905969664 | bytes 10471072 | tf_op jit(solution)/shard_map/pallas_call | solution.py:21
  68.9 2.0 %collective-permute-start.18 = (bf16[2,32,1536]{2,1,0:T(8,128)(2,1)S(1)}, bf16[2,32,1536]{2,1,0:T(8,128)(2,1)S(1)}, u32[]{:S(2)}, u32[]{:S(2)}) collective-permute-start(bf16[2,32,1536]{2,1,0:T(8,128)(2,1)S(1)} %get-tuple-element.61), channel_id=1, source_target_pairs={{0,8},{1,9},{2,10},{3,11},{4,12},{5,13},{6,14},{7,15},{8,0},{9,1},... | collective-permute-start | bytes 589832 | tf_op jit(solution)/shard_map/ppermute | solution.py:235
  70.9 0.9 %collective-permute-start.19 = (bf16[2,32,1536]{2,1,0:T(8,128)(2,1)S(1)}, bf16[2,32,1536]{2,1,0:T(8,128)(2,1)S(1)}, u32[]{:S(2)}, u32[]{:S(2)}) collective-permute-start(bf16[2,32,1536]{2,1,0:T(8,128)(2,1)S(1)} %get-tuple-element.62), channel_id=1, source_target_pairs={{0,12},{1,13},{2,14},{3,15},{4,8},{5,9},{6,10},{7,11},{8,4},{9,5},... | collective-permute-start | bytes 589832 | tf_op jit(solution)/shard_map/ppermute | solution.py:235
  71.9 3.4 %collective-permute-done.17 = bf16[2,32,1536]{2,1,0:T(8,128)(2,1)S(1)} collective-permute-done((bf16[2,32,1536]{2,1,0:T(8,128)(2,1)S(1)}, bf16[2,32,1536]{2,1,0:T(8,128)(2,1)S(1)}, u32[]{:S(2)}, u32[]{:S(2)}) %collective-permute-start.17) | collective-permute-done | bytes 196640 | tf_op jit(solution)/shard_map/ppermute | solution.py:235
  75.2 1.4 %collective-permute-done.18 = bf16[2,32,1536]{2,1,0:T(8,128)(2,1)S(1)} collective-permute-done((bf16[2,32,1536]{2,1,0:T(8,128)(2,1)S(1)}, bf16[2,32,1536]{2,1,0:T(8,128)(2,1)S(1)}, u32[]{:S(2)}, u32[]{:S(2)}) %collective-permute-start.18) | collective-permute-done | bytes 196640 | tf_op jit(solution)/shard_map/ppermute | solution.py:235
  76.6 4.0 %collective-permute-done.19 = bf16[2,32,1536]{2,1,0:T(8,128)(2,1)S(1)} collective-permute-done((bf16[2,32,1536]{2,1,0:T(8,128)(2,1)S(1)}, bf16[2,32,1536]{2,1,0:T(8,128)(2,1)S(1)}, u32[]{:S(2)}, u32[]{:S(2)}) %collective-permute-start.19) | collective-permute-done | bytes 196640 | tf_op jit(solution)/shard_map/ppermute | solution.py:235
  80.6 0.8 fusion
  (57 shorter events, 3.4 us)
Async XLA Ops:
  0.0 1.0 %copy-start.1 = (bf16[48,3072]{1,0:T(8,128)(2,1)S(1)}, bf16[48,3072]{1,0:T(8,128)(2,1)}, u32[]{:S(2)}) copy-start(bf16[48,3072]{1,0:T(8,128)(2,1)} %weights.1) | copy-start | bytes 884740
  1.0 4.8 %copy-start.8 = (s32[1,8,6]{1,0,2:T(1,128)S(1)}, s32[1,8,6]{1,0,2:T(1,128)}, u32[]{:S(2)}) copy-start(s32[1,8,6]{1,0,2:T(1,128)} %param.19) | copy-start | bytes 580
  1.0 4.8 %copy-start.9 = (s32[1,8,6]{1,0,2:T(1,128)S(1)}, s32[1,8,6]{1,0,2:T(1,128)}, u32[]{:S(2)}) copy-start(s32[1,8,6]{1,0,2:T(1,128)} %param.18) | copy-start | bytes 580
  1.1 4.6 %copy-start.7 = (s32[1,8,6]{1,0,2:T(1,128)S(1)}, s32[1,8,6]{1,0,2:T(1,128)}, u32[]{:S(2)}) copy-start(s32[1,8,6]{1,0,2:T(1,128)} %param.20) | copy-start | bytes 580
  1.1 12.7 %collective-permute-start.4 = (bf16[48,768]{1,0:T(8,128)(2,1)S(1)}, bf16[48,768]{1,0:T(8,128)(2,1)S(1)}, u32[]{:S(2)}, u32[]{:S(2)}) collective-permute-start(bf16[48,768]{1,0:T(8,128)(2,1)S(1)} %get-tuple-element.45), channel_id=1, source_target_pairs={{0,4},{1,5},{2,6},{3,7},{4,0},{5,1},{6,2},{7,3},{8,12},{9,13},{10,... | collective-permute-start | bytes 221192 | tf_op jit(solution)/shard_map/ppermute | solution.py:235
  4.2 9.8 %collective-permute-start.5 = (bf16[48,768]{1,0:T(8,128)(2,1)S(1)}, bf16[48,768]{1,0:T(8,128)(2,1)S(1)}, u32[]{:S(2)}, u32[]{:S(2)}) collective-permute-start(bf16[48,768]{1,0:T(8,128)(2,1)S(1)} %get-tuple-element.46), channel_id=1, source_target_pairs={{0,8},{1,9},{2,10},{3,11},{4,12},{5,13},{6,14},{7,15},{8,0},{9,1},... | collective-permute-start | bytes 221192 | tf_op jit(solution)/shard_map/ppermute | solution.py:235
  5.7 8.2 %collective-permute-start.6 = (bf16[48,768]{1,0:T(8,128)(2,1)S(1)}, bf16[48,768]{1,0:T(8,128)(2,1)S(1)}, u32[]{:S(2)}, u32[]{:S(2)}) collective-permute-start(bf16[48,768]{1,0:T(8,128)(2,1)S(1)} %get-tuple-element.47), channel_id=1, source_target_pairs={{0,12},{1,13},{2,14},{3,15},{4,8},{5,9},{6,10},{7,11},{8,4},{9,5},... | collective-permute-start | bytes 221192 | tf_op jit(solution)/shard_map/ppermute | solution.py:235
  6.0 1.1 %copy-start = (bf16[1,6,32,1536]{3,2,1,0:T(8,128)(2,1)S(1)}, bf16[1,6,32,1536]{3,2,1,0:T(8,128)(2,1)}, u32[]{:S(2)}) copy-start(bf16[1,6,32,1536]{3,2,1,0:T(8,128)(2,1)} %param.11) | copy-start | bytes 1769476
  7.1 4.2 %copy-start.4 = (f32[1536]{0:T(1024)S(1)}, f32[1536]{0:T(1024)}, u32[]{:S(2)}) copy-start(f32[1536]{0:T(1024)} %param.12) | copy-start | bytes 18436
  7.1 4.9 %copy-start.2 = (f32[31,1536]{1,0:T(8,128)S(1)}, f32[31,1536]{1,0:T(8,128)}, u32[]{:S(2)}) copy-start(f32[31,1536]{1,0:T(8,128)} %param.14) | copy-start | bytes 571396
  7.7 3.6 %copy-start.5 = (f32[1536]{0:T(1024)S(1)}, f32[1536]{0:T(1024)}, u32[]{:S(2)}) copy-start(f32[1536]{0:T(1024)} %param.15) | copy-start | bytes 18436
  7.7 6.9 %collective-permute-start = (bf16[2,32,1536]{2,1,0:T(8,128)(2,1)S(1)}, bf16[2,32,1536]{2,1,0:T(8,128)(2,1)S(1)}, u32[]{:S(2)}, u32[]{:S(2)}) collective-permute-start(bf16[2,32,1536]{2,1,0:T(8,128)(2,1)S(1)} %get-tuple-element.39), channel_id=1, source_target_pairs={{0,4},{1,5},{2,6},{3,7},{4,0},{5,1},{6,2},{7,3},{8,12},{9,13},{10,... | collective-permute-start | bytes 589832 | tf_op jit(solution)/shard_map/ppermute | solution.py:235
  9.7 6.2 %collective-permute-start.1 = (bf16[2,32,1536]{2,1,0:T(8,128)(2,1)S(1)}, bf16[2,32,1536]{2,1,0:T(8,128)(2,1)S(1)}, u32[]{:S(2)}, u32[]{:S(2)}) collective-permute-start(bf16[2,32,1536]{2,1,0:T(8,128)(2,1)S(1)} %get-tuple-element.40), channel_id=1, source_target_pairs={{0,8},{1,9},{2,10},{3,11},{4,12},{5,13},{6,14},{7,15},{8,0},{9,1},... | collective-permute-start | bytes 589832 | tf_op jit(solution)/shard_map/ppermute | solution.py:235
  11.3 0.7 copy-start.6
  13.8 6.6 %collective-permute-start.2 = (bf16[2,32,1536]{2,1,0:T(8,128)(2,1)S(1)}, bf16[2,32,1536]{2,1,0:T(8,128)(2,1)S(1)}, u32[]{:S(2)}, u32[]{:S(2)}) collective-permute-start(bf16[2,32,1536]{2,1,0:T(8,128)(2,1)S(1)} %get-tuple-element.41), channel_id=1, source_target_pairs={{0,12},{1,13},{2,14},{3,15},{4,8},{5,9},{6,10},{7,11},{8,4},{9,5},... | collective-permute-start | bytes 589832 | tf_op jit(solution)/shard_map/ppermute | solution.py:235
  14.7 0.9 %copy-start.3 = (bf16[48,1536]{1,0:T(8,128)(2,1)S(1)}, bf16[48,1536]{1,0:T(8,128)(2,1)}, u32[]{:S(2)}) copy-start(bf16[48,1536]{1,0:T(8,128)(2,1)} %param.17) | copy-start | bytes 442372
  21.2 9.4 %collective-permute-start.12 = (bf16[6,48,768]{2,1,0:T(8,128)(2,1)S(1)}, bf16[6,48,768]{2,1,0:T(8,128)(2,1)S(1)}, u32[]{:S(2)}, u32[]{:S(2)}) collective-permute-start(bf16[6,48,768]{2,1,0:T(8,128)(2,1)S(1)} %bitcast_dynamic-update-slice_fusion.refs_4_), channel_id=1, source_target_pairs={{0,2},{1,3},{2,0},{3,1},{4,6},{5,7},{6,4},{7,5},{8,10},{9,11},{10,... | collective-permute-start | bytes 1327112 | tf_op jit(solution)/shard_map/ppermute | solution.py:235
  22.8 24.7 %collective-permute-start.11 = (bf16[6,48,768]{2,1,0:T(8,128)(2,1)S(1)}, bf16[6,48,768]{2,1,0:T(8,128)(2,1)S(1)}, u32[]{:S(2)}, u32[]{:S(2)}) collective-permute-start(bf16[6,48,768]{2,1,0:T(8,128)(2,1)S(1)} %bitcast_dynamic-update-slice_fusion.refs_4_), channel_id=1, source_target_pairs={{0,16},{1,17},{2,18},{3,19},{4,20},{5,21},{6,22},{7,23},{8,24},{9,... | collective-permute-start | bytes 1327112 | tf_op jit(solution)/shard_map/ppermute | solution.py:235
  25.4 25.3 %collective-permute-start.7 = (bf16[6,48,768]{2,1,0:T(8,128)(2,1)S(1)}, bf16[6,48,768]{2,1,0:T(8,128)(2,1)S(1)}, u32[]{:S(2)}, u32[]{:S(2)}) collective-permute-start(bf16[6,48,768]{2,1,0:T(8,128)(2,1)S(1)} %bitcast_dynamic-update-slice_fusion.refs_4_), channel_id=1, source_target_pairs={{0,1},{1,0},{2,3},{3,2},{4,5},{5,4},{6,7},{7,6},{8,9},{9,8},{10,11... | collective-permute-start | bytes 1327112 | tf_op jit(solution)/shard_map/ppermute | solution.py:235
  25.4 22.7 %copy-start.10 = (s32[8]{0:T(128)S(1)}, s32[8]{0:T(128)}, u32[]{:S(2)}) copy-start(s32[8]{0:T(128)} %constant.58.clone) | copy-start | bytes 100
  25.4 25.3 %collective-permute-start.3 = (bf16[2,32,1536]{2,1,0:T(8,128)(2,1)S(1)}, bf16[2,32,1536]{2,1,0:T(8,128)(2,1)S(1)}, u32[]{:S(2)}, u32[]{:S(2)}) collective-permute-start(bf16[2,32,1536]{2,1,0:T(8,128)(2,1)S(1)} %get-tuple-element.43), channel_id=1, source_target_pairs={{0,16},{1,17},{2,18},{3,19},{4,20},{5,21},{6,22},{7,23},{8,24},{9,... | collective-permute-start | bytes 589832 | tf_op jit(solution)/shard_map/ppermute | solution.py:235
  47.5 15.3 %collective-permute-start.13 = (bf16[6,48,768]{2,1,0:T(8,128)(2,1)S(1)}, bf16[6,48,768]{2,1,0:T(8,128)(2,1)S(1)}, u32[]{:S(2)}, u32[]{:S(2)}) collective-permute-start(bf16[6,48,768]{2,1,0:T(8,128)(2,1)S(1)} %collective-permute-done.11.refs_5_), channel_id=1, source_target_pairs={{0,2},{1,3},{2,0},{3,1},{4,6},{5,7},{6,4},{7,5},{8,10},{9,11},{10,... | collective-permute-start | bytes 1327112 | tf_op jit(solution)/shard_map/ppermute | solution.py:235
  51.7 8.8 %collective-permute-start.10 = (bf16[2,32,1536]{2,1,0:T(8,128)(2,1)S(1)}, bf16[2,32,1536]{2,1,0:T(8,128)(2,1)S(1)}, u32[]{:S(2)}, u32[]{:S(2)}) collective-permute-start(bf16[2,32,1536]{2,1,0:T(8,128)(2,1)S(1)} %get-tuple-element.55.refs_0_), channel_id=1, source_target_pairs={{0,12},{1,13},{2,14},{3,15},{4,8},{5,9},{6,10},{7,11},{8,4},{9,5},... | collective-permute-start | bytes 589832 | tf_op jit(solution)/shard_map/ppermute | solution.py:235
  52.8 8.8 %collective-permute-start.9 = (bf16[2,32,1536]{2,1,0:T(8,128)(2,1)S(1)}, bf16[2,32,1536]{2,1,0:T(8,128)(2,1)S(1)}, u32[]{:S(2)}, u32[]{:S(2)}) collective-permute-start(bf16[2,32,1536]{2,1,0:T(8,128)(2,1)S(1)} %get-tuple-element.55.refs_0_), channel_id=1, source_target_pairs={{0,8},{1,9},{2,10},{3,11},{4,12},{5,13},{6,14},{7,15},{8,0},{9,1},... | collective-permute-start | bytes 589832 | tf_op jit(solution)/shard_map/ppermute | solution.py:235
  54.2 8.6 %collective-permute-start.8 = (bf16[2,32,1536]{2,1,0:T(8,128)(2,1)S(1)}, bf16[2,32,1536]{2,1,0:T(8,128)(2,1)S(1)}, u32[]{:S(2)}, u32[]{:S(2)}) collective-permute-start(bf16[2,32,1536]{2,1,0:T(8,128)(2,1)S(1)} %get-tuple-element.55.refs_0_), channel_id=1, source_target_pairs={{0,4},{1,5},{2,6},{3,7},{4,0},{5,1},{6,2},{7,3},{8,12},{9,13},{10,... | collective-permute-start | bytes 589832 | tf_op jit(solution)/shard_map/ppermute | solution.py:235
  55.3 7.7 %collective-permute-start.14 = (bf16[6,48,768]{2,1,0:T(8,128)(2,1)S(1)}, bf16[6,48,768]{2,1,0:T(8,128)(2,1)S(1)}, u32[]{:S(2)}, u32[]{:S(2)}) collective-permute-start(bf16[6,48,768]{2,1,0:T(8,128)(2,1)S(1)} %collective-permute-done.11.refs_5_), channel_id=1, source_target_pairs={{0,1},{1,0},{2,3},{3,2},{4,5},{5,4},{6,7},{7,6},{8,9},{9,8},{10,11... | collective-permute-start | bytes 1327112 | tf_op jit(solution)/shard_map/ppermute | solution.py:235
  60.5 2.4 %collective-permute-start.15 = (bf16[6,48,768]{2,1,0:T(8,128)(2,1)S(1)}, bf16[6,48,768]{2,1,0:T(8,128)(2,1)S(1)}, u32[]{:S(2)}, u32[]{:S(2)}) collective-permute-start(bf16[6,48,768]{2,1,0:T(8,128)(2,1)S(1)} %collective-permute-done.12.refs_6_), channel_id=1, source_target_pairs={{0,1},{1,0},{2,3},{3,2},{4,5},{5,4},{6,7},{7,6},{8,9},{9,8},{10,11... | collective-permute-start | bytes 1327112 | tf_op jit(solution)/shard_map/ppermute | solution.py:235
  62.8 1.8 %collective-permute-start.16 = (bf16[6,48,768]{2,1,0:T(8,128)(2,1)S(1)}, bf16[6,48,768]{2,1,0:T(8,128)(2,1)S(1)}, u32[]{:S(2)}, u32[]{:S(2)}) collective-permute-start(bf16[6,48,768]{2,1,0:T(8,128)(2,1)S(1)} %collective-permute-done.13.refs_7_), channel_id=1, source_target_pairs={{0,1},{1,0},{2,3},{3,2},{4,5},{5,4},{6,7},{7,6},{8,9},{9,8},{10,11... | collective-permute-start | bytes 1327112 | tf_op jit(solution)/shard_map/ppermute | solution.py:235
  68.2 7.0 %collective-permute-start.17 = (bf16[2,32,1536]{2,1,0:T(8,128)(2,1)S(1)}, bf16[2,32,1536]{2,1,0:T(8,128)(2,1)S(1)}, u32[]{:S(2)}, u32[]{:S(2)}) collective-permute-start(bf16[2,32,1536]{2,1,0:T(8,128)(2,1)S(1)} %get-tuple-element.60), channel_id=1, source_target_pairs={{0,4},{1,5},{2,6},{3,7},{4,0},{5,1},{6,2},{7,3},{8,12},{9,13},{10,... | collective-permute-start | bytes 589832 | tf_op jit(solution)/shard_map/ppermute | solution.py:235
  68.9 7.8 %collective-permute-start.18 = (bf16[2,32,1536]{2,1,0:T(8,128)(2,1)S(1)}, bf16[2,32,1536]{2,1,0:T(8,128)(2,1)S(1)}, u32[]{:S(2)}, u32[]{:S(2)}) collective-permute-start(bf16[2,32,1536]{2,1,0:T(8,128)(2,1)S(1)} %get-tuple-element.61), channel_id=1, source_target_pairs={{0,8},{1,9},{2,10},{3,11},{4,12},{5,13},{6,14},{7,15},{8,0},{9,1},... | collective-permute-start | bytes 589832 | tf_op jit(solution)/shard_map/ppermute | solution.py:235
  70.9 9.8 %collective-permute-start.19 = (bf16[2,32,1536]{2,1,0:T(8,128)(2,1)S(1)}, bf16[2,32,1536]{2,1,0:T(8,128)(2,1)S(1)}, u32[]{:S(2)}, u32[]{:S(2)}) collective-permute-start(bf16[2,32,1536]{2,1,0:T(8,128)(2,1)S(1)} %get-tuple-element.62), channel_id=1, source_target_pairs={{0,12},{1,13},{2,14},{3,15},{4,8},{5,9},{6,10},{7,11},{8,4},{9,5},... | collective-permute-start | bytes 589832 | tf_op jit(solution)/shard_map/ppermute | solution.py:235
